TPU v7x, 32 devices: a whole 2x2x4 slice. The times are simulated.
32 devices in a mesh: grp: 2 (over y), inst: 8 (over z, x), tp: 2 (over core).
Axes of the slice: x: 2, y: 2, z: 4, core: 2. Of those that a mesh axis runs over, the one named last changes fastest.
Arguments:
- queries: bfloat16 [8192, 12288], P(('grp', 'inst'), 'tp'), parts along dimension 0, may hold values from -330 to 330
- keys_values: bfloat16 [8192, 2048], P(('grp', 'inst')), parts along dimension 0, may hold values from -5 to 5
- out_weight: bfloat16 [12288, 12288], P('tp', 'inst'), may hold values from -0.0546875 to 0.0546875
- lengths: int32 [16, 4], P(('grp', 'inst')), parts along dimension 0, may hold values from 1 to 256, 512 in all within a row
- placement: int32 [64], P('grp'), parts along dimension 0, may hold values from 0 to 1
- page_table: int32 [64, 16], P('grp'), parts along dimension 0, may hold values from 0 to 127, as said below
Outputs:
- projected: bfloat16 [8192, 12288], P(('grp', 'inst', 'tp')), parts along dimension 0
- cache: bfloat16 [2048, 16, 2048], P(('grp', 'inst'), None, 'tp'), parts along dimension 0
There are 2 independent parts, one for each index of `grp`. A program takes and returns all parts, laid end to end along the dimension named above; an argument that names none is the same for every part. Nothing has to cross between parts.
Inputs may be any that keep to these rules, and one draw needn't show every extreme that they name: `page_table`: pages of different requests, or of different p // 4, with equal p % 4 hold different slots.
All inputs are finite; a program needn't handle non-finite values.
Results may differ from a plain program's by a relative error of at most 0.013.
Values may be sent and summed in bfloat16 or wider, within the bound.
No kernel may reach another device: no remote copies, remote signals or barrier semaphores. Data moves between devices by JAX's collectives and lax.ppermute only.
A program may use at most 512 MiB of HBM per device.

v0:
```python
import jax
import jax.numpy as jnp
from jax import lax
from jax.sharding import PartitionSpec as P

NH = 96
KVH = 8
HD = 128
PAGE = 16
OWNERS = 4
REQ_INST = 4
MAXLEN = 256
QUARTERS = 4


def per_device(queries, keys_values, out_weight, lengths, placement, page_table):
    tok_rows = queries.shape[0]
    tp_count = lax.axis_size("tp")
    tp_here = lax.axis_index("tp")
    inst_count = lax.axis_size("inst")
    inst_here = lax.axis_index("inst")
    local_heads = queries.shape[1] // HD
    full_group = NH // KVH
    kv_heads = max(1, local_heads // full_group)
    first_kv = tp_here * local_heads // full_group
    head_pairs = lax.dynamic_slice_in_dim(keys_values, first_kv * 2 * HD, kv_heads * 2 * HD, 1)
    pair_rows = head_pairs.reshape(tok_rows, kv_heads, 2, HD)
    group_size = local_heads // kv_heads
    query_rows = queries.reshape(tok_rows, local_heads, HD)
    lens_row = lengths[0]
    ends = jnp.cumsum(lens_row)
    positions = jnp.arange(tok_rows, dtype=jnp.int32)
    segment = jnp.sum((positions[:, None] >= ends[None, :]).astype(jnp.int32), axis=1)
    allowed = (segment[:, None] == segment[None, :]) & (positions[None, :] <= positions[:, None])
    keys_full = jnp.repeat(pair_rows[:, :, 0], group_size, axis=1)
    vals_full = jnp.repeat(pair_rows[:, :, 1], group_size, axis=1)
    scores = jnp.einsum(
        "qhd,khd->hqk", query_rows, keys_full, preferred_element_type=jnp.float32
    ) * (1.0 / HD**0.5)
    scores = jnp.where(allowed[None], scores, -1e30)
    top_score = jnp.max(scores, axis=2, keepdims=True)
    expo = jnp.exp(scores - top_score)
    probs = (expo / jnp.sum(expo, axis=2, keepdims=True)).astype(jnp.bfloat16)
    mixed = jnp.einsum("hqk,khd->qhd", probs, vals_full, preferred_element_type=jnp.float32)
    attended = mixed.astype(jnp.bfloat16).reshape(tok_rows, local_heads * HD)
    kv_width = keys_values.shape[1] // tp_count
    own_columns = lax.dynamic_slice_in_dim(keys_values, tp_here * kv_width, kv_width, 1)
    starts = ends - lens_row
    offsets = jnp.arange(MAXLEN, dtype=jnp.int32)
    rows_taken = jnp.clip(starts[:, None] + offsets[None, :], 0, tok_rows - 1)
    live = offsets[None, :] < lens_row[:, None]
    taken = jnp.take(own_columns, rows_taken.reshape(-1), axis=0).reshape(
        REQ_INST, MAXLEN, kv_width
    )
    padded = jnp.where(live[:, :, None], taken, jnp.zeros_like(taken))
    pages = padded.reshape(REQ_INST, QUARTERS, OWNERS, PAGE, kv_width).transpose(2, 0, 1, 3, 4)
    decode_count = inst_count // OWNERS
    request_ids = inst_here * REQ_INST + jnp.arange(REQ_INST, dtype=jnp.int32)
    dest_inst = jnp.take(placement, request_ids, axis=0)
    hit = dest_inst[None, :] == jnp.arange(decode_count, dtype=jnp.int32)[:, None]
    outgoing = jnp.where(
        hit[:, None, :, None, None, None], pages[None], jnp.zeros_like(pages[None])
    )
    outgoing = outgoing.reshape(inst_count, REQ_INST, QUARTERS, PAGE, kv_width)
    incoming = lax.all_to_all(outgoing, "inst", split_axis=0, concat_axis=0, tiled=True)
    slot_count = page_table.shape[0] * QUARTERS
    residue = inst_here % OWNERS
    my_decode = inst_here // OWNERS
    slot_table = page_table.reshape(page_table.shape[0], QUARTERS, OWNERS)
    my_slots = lax.dynamic_index_in_dim(slot_table, residue, axis=2, keepdims=False)
    valid = placement == my_decode
    target = jnp.where(valid[:, None], my_slots, slot_count).reshape(-1)
    cache = (
        jnp.zeros((slot_count, PAGE, kv_width), jnp.bfloat16)
        .at[target]
        .set(incoming.reshape(-1, PAGE, kv_width), mode="drop")
    )
    rows_dev = tok_rows // tp_count
    everyone = lax.all_gather(attended, "inst", axis=0, tiled=True)
    head_cols = everyone.shape[1]
    reordered = (
        everyone.reshape(inst_count, tp_count, rows_dev, head_cols)
        .transpose(1, 0, 2, 3)
        .reshape(-1, head_cols)
    )
    summed = lax.psum_scatter(
        jnp.dot(reordered, out_weight, preferred_element_type=jnp.float32).astype(jnp.bfloat16),
        "tp",
        scatter_dimension=0,
        tiled=True,
    )
    shares = summed.reshape(inst_count, rows_dev, out_weight.shape[1])
    returned = lax.all_to_all(shares, "inst", split_axis=0, concat_axis=2, tiled=True)
    projected = returned.reshape(rows_dev, inst_count * out_weight.shape[1])
    return (projected, cache)


def solution(mesh):
    return jax.shard_map(
        per_device,
        mesh=mesh,
        in_specs=(
            P(("grp", "inst"), "tp"),
            P(("grp", "inst"), None),
            P("tp", "inst"),
            P(("grp", "inst"), None),
            P("grp"),
            P("grp", None),
        ),
        out_specs=(P(("grp", "inst", "tp"), None), P(("grp", "inst"), None, "tp")),
        check_vma=False,
    )
```

profile of v0, /device:TPU:0, one launch (start us, length us, event | category | flops | bytes accessed | tf_op | source)
XLA Modules:
  0.0 1458.3 jit_solution(15535543738988859804)
XLA Ops:
  7.2 0.0 copy-start
  7.2 0.0 copy-start.3
  7.2 0.0 all-gather.2.cloned.1.call-start
  7.3 2.7 constant_dynamic-slice_fusion
  10.0 0.5 copy.43
  10.5 0.1 fusion.15
  10.6 0.3 copy.33
  10.9 0.0 copy-done.3
  10.9 0.2 reduce-window.7
  11.0 0.0 copy-start.5
  11.0 0.1 convert_reduce_fusion
  11.1 0.2 fusion.10
  11.3 4.2 broadcast_in_dim.110
  15.5 22.3 %fusion.6 = f32[48,512,512]{2,1,0:T(8,128)} fusion(bf16[512,48,128]{2,0,1:T(8,128)(2,1)} %bitcast.74, bf16[512,6144]{1,0:T(8,128)(2,1)} %param.6), kind=kOutput, calls=%fused_computation.13 | convolution fusion | flops 3221225472 | bytes 62914560 | tf_op jit(solution)/shard_map/qhd,khd->hqk/dot_general | solution.py:37
  37.8 0.0 copy-done.5
  37.8 49.2 %fusion.16 = (f32[48,512]{1,0:T(8,128)S(1)}, f32[48,512,512]{1,2,0:T(8,128)}) fusion(f32[48,512,512]{2,1,0:T(8,128)} %fusion.6, pred[512,512]{0,1:T(8,128)(4,1)S(1)} %fusion.10), kind=kOutput, calls=%fused_computation.47 | output fusion | flops 75497984 | bytes 101023744 | tf_op jit(solution)/shard_map/sub | solution.py:42
  87.0 3.5 broadcast_in_dim.108
  90.4 22.2 %fusion.9 = bf16[48,128,512]{2,1,0:T(8,128)(2,1)} fusion(bf16[512,48,128]{0,2,1:T(8,128)(2,1)} %bitcast.80, f32[48,512,512]{1,2,0:T(8,128)} %get-tuple-element.7, f32[48,512]{1,0:T(8,128)S(1)} %get-tuple-element.6), kind=kOutput, calls=%fused_computation.17 | convolution fusion | flops 3249537024 | bytes 63012864 | tf_op jit(solution)/shard_map/hqk,khd->qhd/dot_general | solution.py:44
  112.7 8.6 copy.36
  121.3 0.0 all-gather.2.cloned.1.call-update
  121.3 0.2 reduce-scatter.2.cloned.1.call-start
  121.5 954.9 %all-gather.2.cloned.1.call-done = bf16[4096,6144]{1,0:T(8,128)(2,1)} async-done(((bf16[512,6144]{1,0:T(8,128)(2,1)}), bf16[4096,6144]{1,0:T(8,128)(2,1)}) %all-gather.2.cloned.1.call-update) | async-done | bytes 50331664 | tf_op jit(solution)/shard_map/all_gather | solution.py:79
  1076.5 33.2 %copy.37 = bf16[2,8,256,6144]{3,2,1,0:T(8,128)(2,1)} copy(bf16[2,8,256,6144]{3,2,0,1:T(8,128)(2,1)} %bitcast.72) | data formatting | bytes 100663296 | tf_op jit(solution)/shard_map/transpose | solution.py:83
  1109.7 87.6 %convolution_convert_fusion = bf16[4096,1536]{1,0:T(8,128)(2,1)} fusion(bf16[4096,6144]{1,0:T(8,128)(2,1)} %bitcast.73, bf16[6144,1536]{1,0:T(8,128)(2,1)} %param.8), kind=kOutput, calls=%fused_computation.12 | convolution fusion | flops 77315702784 | bytes 81788928 | tf_op jit(solution)/shard_map/dot_general | solution.py:87
  1197.3 0.0 copy-start.4
  1197.3 0.0 copy-start.6
  1197.3 0.0 copy-start.2
  1197.3 0.0 reduce-scatter.2.cloned.1.call-update
  1197.3 0.6 copy-done.4
  1198.0 0.0 copy-done.6
  1198.0 0.1 clamp_bitcast_fusion
  1198.1 0.4 copy-done.2
  1198.6 4.1 gather_fusion.1
  1202.6 0.0 copy-done.1
  1202.7 0.6 gather_fusion
  1203.3 0.1 compare_and_fusion
  1203.5 1.9 bitcast_select_fusion.4
  1205.4 97.8 %all_to_all.20 = bf16[8,4,4,16,1024]{4,3,2,1,0:T(8,128)(2,1)} all-to-all(bf16[8,4,4,16,1024]{4,3,2,1,0:T(8,128)(2,1)S(1)} %bitcast_select_fusion.4), channel_id=1, replica_groups=mesh['grp'=2,'inst'=8,'tp'=2] {'inst'}, dimensions={0} | all-to-all | bytes 8388608 | tf_op jit(solution)/shard_map/all_to_all | solution.py:65
  1303.2 4.7 all-to-all-start
  1308.0 0.0 copy-done
  1308.0 0.1 copy.44
  1308.1 0.1 squeeze.13
  1308.2 0.1 broadcast_in_dim.113
  1308.3 0.1 broadcast_in_dim.114
  1308.4 2.5 broadcast_in_dim.112
  1311.0 19.0 %scatter_fusion = bf16[128,16,1024]{2,1,0:T(8,128)(2,1)} fusion(bf16[128,16,1024]{2,1,0:T(8,128)(2,1)} %broadcast_in_dim.112, s32[128]{0:T(128)S(1)} %fusion.11, bf16[128,16,1024]{2,1,0:T(8,128)(2,1)} %bitcast.75), kind=kCustom, calls=%fused_computation.2 | custom fusion | bytes 12583424 | tf_op jit(solution)/shard_map/scatter | solution.py:76
  1330.0 115.2 %all-to-all-done = bf16[8,256,1536]{2,1,0:T(8,128)(2,1)} async-done(((bf16[8,256,1536]{2,1,0:T(8,128)(2,1)}), bf16[8,256,1536]{2,1,0:T(8,128)(2,1)}, u32[]{:S(2)}, u32[]{:S(2)}) %all-to-all-start) | async-done | bytes 6291488 | tf_op jit(solution)/shard_map/all_to_all | solution.py:93
  1445.1 6.3 copy.46
  (15 shorter events, 0.1 us)
Async XLA Ops:
  7.2 1300.8 %copy-start = (s32[32,16]{0,1:T(8,128)S(1)}, s32[32,16]{0,1:T(8,128)}, u32[]{:S(2)}) copy-start(s32[32,16]{0,1:T(8,128)} %param.11) | copy-start | bytes 6148
  7.2 3.7 copy-start.3
  7.2 1069.3 %all-gather.2.cloned.1.call-start = ((), (), s32[]{:S(2)}) async-start(), calls=%async_computation.3 | async-start | bytes 56623104 | tf_op jit(solution)/shard_map/all_gather | solution.py:79
  11.0 26.7 %copy-start.5 = (s32[4,1]{0,1:T(1,128)}, s32[4,1]{0,1:T(1,128)S(1)}, u32[]{:S(2)}) copy-start(s32[4,1]{0,1:T(1,128)S(1)} %reduce-window.7) | copy-start | bytes 52
  121.3 1181.9 %reduce-scatter.2.cloned.1.call-start = ((), (), s32[]{:S(2)}) async-start(), calls=%async_computation.4 | async-start | bytes 18874368 | tf_op jit(solution)/shard_map/reduce_scatter | solution.py:86
  1197.3 0.7 copy-start.4
  1197.3 0.7 copy-start.6
  1197.3 1.2 copy-start.2
  1198.6 4.1 copy-start.1
  1303.2 141.9 %all-to-all-start = ((bf16[8,256,1536]{2,1,0:T(8,128)(2,1)}), bf16[8,256,1536]{2,1,0:T(8,128)(2,1)}, u32[]{:S(2)}, u32[]{:S(2)}) async-start(bf16[8,256,1536]{2,1,0:T(8,128)(2,1)} %bitcast.77), calls=%async_computation.1 | async-start | bytes 12582912 | tf_op jit(solution)/shard_map/all_to_all | solution.py:93
Sparse Core Ops, SparseCore 0:
  121.4 955.0 all-gather.1
  1197.5 21.4 reduce-scatter.1
where the time goes:
time: 1460 us
  waiting for transfers between devices  1070 us (73%)
  matrix products  132 us (9%)
  blocking collectives  97.8 us (7%)
  local copies, waits for them, and re-layouts  87.1 us (6%)
  other arithmetic  51.8 us (4%)
    all_gather x1, waiting for transfers between devices, per_device(): everyone = lax.all_gather(attended, 'inst', axis=0, tiled=True)  955 us
    all_to_all x1, waiting for transfers between devices, per_device(): lax.all_to_all(shares, 'inst', split_axis=0, concat_axis=2, tiled=True)  115 us
    all_to_all x1, blocking collectives, per_device(): lax.all_to_all(outgoing, 'inst', split_axis=0, concat_axis=0, tiled=True)  97.8 us
    dot_general x1, matrix products, per_device(): jnp.dot(reordered, out_weight, preferred_element_type=jnp.float32)  87.6 us
    sub x1, other arithmetic, per_device(): expo = jnp.exp(scores - top_score)  49.2 us
    transpose x1, local copies, waits for them, and re-layouts, per_device(): reordered = everyone.reshape(inst_count, tp_count, rows_dev, head_cols).t...  33.2 us
  transfers between devices with their start and end apart: 3, of which 2 were waited for; matrix products, arithmetic and copies ran while one was open for 2% of the time, Pallas kernels for 0%

commit v1 on v0

v1 whole, which is shorter than its diff:
```python
import functools

import jax
import jax.numpy as jnp
from jax import lax
from jax.experimental import pallas as pl
from jax.experimental.pallas import tpu as pltpu
from jax.sharding import PartitionSpec as P

NH = 96
KVH = 8
HD = 128
PAGE = 16
OWNERS = 4
REQ_INST = 4
MAXLEN = 256
QUARTERS = 4
ROWS = 128
LOG2E = 1.4426950408889634

SIDE, NEXT, FAR = 1, 2, 4
PIECES = (256, 256, 128, 128)


def attention_kernel(info, q_ref, k_ref, v_ref, o_ref, *, heads, row_blocks, window):
    for block in range(row_blocks):
        place = info[0] * row_blocks + block
        first = pl.multiple_of(jnp.maximum(place - (window // ROWS - 1), 0) * ROWS, ROWS)
        row = place * ROWS + lax.broadcasted_iota(jnp.int32, (ROWS, window), 0)
        col = first + lax.broadcasted_iota(jnp.int32, (ROWS, window), 1)
        begin = jnp.zeros_like(row)
        for j in range(REQ_INST):
            begin = jnp.where(row >= info[2 + j], info[2 + j], begin)
        bias = jnp.where((col <= row) & (col >= begin), 0.0, -1e30)
        keys = k_ref[pl.ds(first, window), :]
        vals = v_ref[pl.ds(first, window), :]
        vals = jnp.concatenate([vals, jnp.ones_like(vals)], axis=1)
        rows = slice(block * ROWS, (block + 1) * ROWS)
        for head in range(heads):
            cols = slice(head * HD, (head + 1) * HD)
            scores = lax.dot_general(
                q_ref[rows, cols], keys, (((1,), (1,)), ((), ())),
                preferred_element_type=jnp.float32,
            )
            scores = scores * (LOG2E / HD**0.5) + bias
            expo = jnp.exp2(scores - jnp.max(scores, axis=1, keepdims=True))
            mixed = jnp.dot(expo.astype(jnp.bfloat16), vals, preferred_element_type=jnp.float32)
            o_ref[rows, cols] = (mixed[:, :HD] / mixed[:, HD:]).astype(jnp.bfloat16)


def attention(queries, keys_values, ends, first_kv, chunk, chunk_rows):
    tok_rows, width = queries.shape
    local_heads = width // HD
    kv_heads = max(1, local_heads // (NH // KVH))
    heads = local_heads // kv_heads
    window = min(ROWS + MAXLEN, tok_rows)
    info = jnp.concatenate([jnp.stack([chunk, first_kv]).astype(jnp.int32), ends])
    work = chunk_rows * window * width
    return pl.pallas_call(
        functools.partial(
            attention_kernel, heads=heads, row_blocks=chunk_rows // ROWS, window=window
        ),
        grid_spec=pltpu.PrefetchScalarGridSpec(
            num_scalar_prefetch=1,
            grid=(kv_heads,),
            in_specs=[
                pl.BlockSpec((chunk_rows, heads * HD), lambda g, info: (info[0], g)),
                pl.BlockSpec((tok_rows, HD), lambda g, info: (0, 2 * (info[1] + g))),
                pl.BlockSpec((tok_rows, HD), lambda g, info: (0, 2 * (info[1] + g) + 1)),
            ],
            out_specs=pl.BlockSpec((chunk_rows, heads * HD), lambda g, info: (0, g)),
        ),
        out_shape=jax.ShapeDtypeStruct((chunk_rows, width), jnp.bfloat16),
        compiler_params=pltpu.CompilerParams(vmem_limit_bytes=32 << 20),
        cost_estimate=pl.CostEstimate(
            flops=6 * work, bytes_accessed=4 * chunk_rows * width, transcendentals=work // HD
        ),
        name="attention",
    )(info, queries, keys_values, keys_values)


def place_kernel(offsets, *refs, count):
    pieces, out, sems = refs[:count], refs[count], refs[count + 1]
    copies = []
    for n, piece in enumerate(pieces):
        width = piece.shape[1]
        start = pl.multiple_of(offsets[n], 128)
        copies.append(
            pltpu.make_async_copy(piece, out.at[:, pl.ds(start, width)], sems.at[n])
        )
    for copy in copies:
        copy.start()
    for copy in copies:
        copy.wait()


def place(pieces, offsets, columns):
    rows = pieces[0].shape[0]
    return pl.pallas_call(
        functools.partial(place_kernel, count=len(pieces)),
        grid_spec=pltpu.PrefetchScalarGridSpec(
            num_scalar_prefetch=1,
            grid=(),
            in_specs=[pl.BlockSpec(memory_space=pl.ANY)] * len(pieces),
            out_specs=pl.BlockSpec(memory_space=pl.ANY),
            scratch_shapes=[pltpu.SemaphoreType.DMA((len(pieces),))],
        ),
        out_shape=jax.ShapeDtypeStruct((rows, columns), pieces[0].dtype),
        cost_estimate=pl.CostEstimate(
            flops=0, bytes_accessed=4 * rows * columns, transcendentals=0
        ),
        name="place",
    )(jnp.stack(offsets).astype(jnp.int32), *pieces)


def hop(array, mask):
    count = lax.axis_size("inst")
    return lax.ppermute(array, "inst", [(i, i ^ mask) for i in range(count)])


def swap(array, axis):
    return lax.ppermute(array, axis, [(0, 1), (1, 0)])


def dot(left, right):
    return jnp.dot(left, right, preferred_element_type=jnp.float32)


def group_sum(parts, weight):
    if lax.axis_size("tp") == 2:
        given, kept = parts
        other = swap(dot(given, weight).astype(jnp.bfloat16), "tp")
        return (dot(kept, weight) + other.astype(jnp.float32)).astype(jnp.bfloat16)
    (rows,) = parts
    term = dot(rows, weight).astype(jnp.bfloat16)
    return lax.psum_scatter(term, "tp", scatter_dimension=0, tiled=True)


def fill_cache(keys_values, lengths, placement, page_table):
    tok_rows = keys_values.shape[0]
    tp_count = lax.axis_size("tp")
    inst_count = lax.axis_size("inst")
    inst_here = lax.axis_index("inst")
    kv_width = keys_values.shape[1] // tp_count
    held = lax.dynamic_slice_in_dim(keys_values, lax.axis_index("tp") * kv_width, kv_width, 1)
    for mask in (FAR, NEXT, SIDE):
        held = jnp.concatenate([held, hop(held, mask)], axis=0)
    order = [0]
    for mask in (FAR, NEXT, SIDE):
        order = order + [at ^ mask for at in order]
    block_of = jnp.asarray([order.index(i) for i in range(inst_count)], jnp.int32)

    lens = lax.all_gather(lengths, "inst", axis=0, tiled=True)
    starts = jnp.cumsum(lens, axis=1) - lens
    requests = page_table.shape[0]
    slot_count = requests * QUARTERS
    residue = inst_here % OWNERS
    slots = lax.dynamic_index_in_dim(
        page_table.reshape(requests, QUARTERS, OWNERS), residue, axis=2, keepdims=False
    )
    valid = placement == inst_here // OWNERS
    target = jnp.where(valid[:, None], slots, slot_count).reshape(-1)
    inst_of = jnp.arange(requests, dtype=jnp.int32) // REQ_INST
    base = jnp.take(block_of, inst_of ^ inst_here) * tok_rows + starts.reshape(-1)
    offset = (jnp.arange(QUARTERS, dtype=jnp.int32) * OWNERS + residue) * PAGE
    page_base = (base[:, None] + offset[None, :]).reshape(-1)
    page_live = jnp.clip(lens.reshape(-1)[:, None] - offset[None, :], 0, PAGE).reshape(-1)
    match = target[None, :] == jnp.arange(slot_count, dtype=jnp.int32)[:, None]
    slot_base = jnp.sum(jnp.where(match, page_base[None, :], 0), axis=1)
    slot_live = jnp.sum(jnp.where(match, page_live[None, :], 0), axis=1)
    within = jnp.arange(PAGE, dtype=jnp.int32)
    live = within[None, :] < slot_live[:, None]
    rows = jnp.where(live, slot_base[:, None] + within[None, :], 0)
    taken = jnp.take(held, rows.reshape(-1), axis=0, mode="clip")
    taken = taken.reshape(slot_count, PAGE, kv_width)
    return jnp.where(live[:, :, None], taken, jnp.zeros_like(taken))


def per_device(queries, keys_values, out_weight, lengths, placement, page_table):
    tok_rows = queries.shape[0]
    tp_count = lax.axis_size("tp")
    tp_here = lax.axis_index("tp")
    inst_count = lax.axis_size("inst")
    inst_here = lax.axis_index("inst")
    grp_here = lax.axis_index("grp")
    local_heads = queries.shape[1] // HD
    first_kv = tp_here * local_heads // (NH // KVH)
    ends = jnp.cumsum(lengths[0])
    depth, own_cols = out_weight.shape
    half_cols = own_cols // 2

    chunks = [1 - tp_here, tp_here] if tp_count == 2 else [jnp.int32(0)]
    chunk_rows = tok_rows // len(chunks)
    attended = [
        attention(queries, keys_values, ends, first_kv, chunk, chunk_rows) for chunk in chunks
    ]
    blocks = {0: attended}
    blocks[NEXT] = [hop(rows, NEXT) for rows in attended]
    blocks[SIDE] = [hop(rows, SIDE) for rows in attended]
    blocks[NEXT | SIDE] = [hop(rows, SIDE) for rows in blocks[NEXT]]
    masks = (0, NEXT, SIDE, NEXT | SIDE)

    arrived = []
    at = 0
    for n, width in enumerate(PIECES):
        piece = lax.dynamic_slice(
            out_weight, (jnp.int32(0), grp_here * half_cols + at), (depth, width)
        )
        if n >= 2:
            piece, _ = lax.optimization_barrier((piece, arrived[n - 2][0]))
        along = hop(piece, FAR)
        arrived.append((along, swap(along, "grp"), at, width))
        at += width

    pieces, offsets = [], []

    def hand_out(shares, column_of):
        for mask in masks:
            share = shares[mask]
            pieces.append(hop(share, mask) if mask else share)
            offsets.append(column_of(inst_here ^ mask))

    hand_out(
        {mask: group_sum(blocks[mask], out_weight) for mask in masks},
        lambda inst: inst * own_cols,
    )
    stacked = [
        jnp.concatenate([blocks[mask][c] for mask in masks], axis=0) for c in range(len(chunks))
    ]
    rows_dev = tok_rows // tp_count
    for along, across, at, width in arrived:
        for weight, half in ((along, grp_here), (across, 1 - grp_here)):
            if tp_count == 2:
                total = group_sum(stacked, weight)
                shares = {
                    mask: total[n * rows_dev : (n + 1) * rows_dev] for n, mask in enumerate(masks)
                }
            else:
                shares = {mask: group_sum(blocks[mask], weight) for mask in masks}
            hand_out(
                shares,
                lambda inst, half=half, at=at: (inst ^ FAR) * own_cols + half * half_cols + at,
            )
    projected = place(pieces, offsets, inst_count * own_cols)
    cache = fill_cache(keys_values, lengths, placement, page_table)
    return (projected, cache)


def solution(mesh):
    return jax.shard_map(
        per_device,
        mesh=mesh,
        in_specs=(
            P(("grp", "inst"), "tp"),
            P(("grp", "inst"), None),
            P("tp", "inst"),
            P(("grp", "inst"), None),
            P("grp"),
            P("grp", None),
        ),
        out_specs=(P(("grp", "inst", "tp"), None), P(("grp", "inst"), None, "tp")),
        check_vma=False,
    )
```

time: 1460 us -> 1050 us (0.72)
  waiting for transfers between devices: 1070 us -> 379 us
  Pallas kernels: 0 us -> 214 us
  starting transfers between devices: 5 us -> 76.5 us
  blocking collectives: 97.8 us -> 150 us
  local copies, waits for them, and re-layouts: 87.1 us -> 44.6 us
  other arithmetic: 51.8 us -> 30.5 us
    all_gather x1 -> x0, waiting for transfers between devices: 955 us -> none  [per_device(): everyone = lax.all_gather(attended, 'inst', axis=0, tiled=True)]
    ppermute x0 -> x56, waiting for transfers between devices: none -> 379 us  [the longest x40 267 us: hop(): return lax.ppermute(array, 'inst', [(i, i ^ mask) for i in range(count)])]
    pallas_call x0 -> x3, Pallas kernels: none -> 214 us  [the longest x1 193 us: place(): pl.pallas_call(functools.partial(place_kernel, count=len(pieces)), grid_s...]
    all_gather x0 -> x1, blocking collectives: none -> 150 us  [fill_cache(): lens = lax.all_gather(lengths, 'inst', axis=0, tiled=True)]
    all_to_all x1 -> x0, waiting for transfers between devices: 115 us -> none  [per_device(): lax.all_to_all(shares, 'inst', split_axis=0, concat_axis=2, tiled=True)]
    all_to_all x1 -> x0, blocking collectives: 97.8 us -> none  [per_device(): lax.all_to_all(outgoing, 'inst', split_axis=0, concat_axis=0, tiled=True)]
    ppermute x0 -> x56, starting transfers between devices: none -> 76.5 us  [the longest x40 68.8 us: hop(): return lax.ppermute(array, 'inst', [(i, i ^ mask) for i in range(count)])]
    sub x2 -> x1, other arithmetic: 49.2 us -> 0.01 us  [fill_cache(): starts = jnp.cumsum(lens, axis=1) - lens]
  transfers between devices with their start and end apart: 3 -> 56, of which waited for: 2 -> 14; matrix products, arithmetic and copies ran while one was open for 2% -> 20% of each run, Pallas kernels for 0% -> 1%
where the time goes in v1:
time: 1050 us; the launch traced here: 1040 us
  waiting for transfers between devices  379 us (36%)
  Pallas kernels  214 us (20%)
  blocking collectives  150 us (14%)
  matrix products  145 us (14%)
  starting transfers between devices  76.5 us (7%)
  local copies, waits for them, and re-layouts  44.6 us (4%)
  other arithmetic  30.5 us (3%)
    ppermute x40, waiting for transfers between devices, hop(): return lax.ppermute(array, 'inst', [(i, i ^ mask) for i in range(count)])  267 us
    pallas_call x1, Pallas kernels, place(): pl.pallas_call(functools.partial(place_kernel, count=len(pieces)), grid_s...  193 us
    all_gather x1, blocking collectives, fill_cache(): lens = lax.all_gather(lengths, 'inst', axis=0, tiled=True)  150 us
    dot_general x24, matrix products, dot(): return jnp.dot(left, right, preferred_element_type=jnp.float32)  145 us
    ppermute x16, waiting for transfers between devices, swap(): return lax.ppermute(array, axis, [(0, 1), (1, 0)])  111 us
    ppermute x40, starting transfers between devices, hop(): return lax.ppermute(array, 'inst', [(i, i ^ mask) for i in range(count)])  68.8 us
    pallas_call x2, Pallas kernels, attention(): pl.pallas_call(functools.partial(attention_kernel, heads=heads, row_block...  21.5 us
  transfers between devices with their start and end apart: 56, of which 14 were waited for; matrix products, arithmetic and copies ran while one was open for 20% of the time, Pallas kernels for 1%

profile of v1, /device:TPU:0, one launch (start us, length us, event | category | flops | bytes accessed | tf_op | source)
XLA Modules:
  0.0 1041.6 jit_solution(12122034144915054905)
XLA Ops:
  6.0 11.1 %attention.3 = bf16[256,6144]{1,0:T(8,128)(2,1)} custom-call(s32[6]{0:T(128)S(1)} %get-tuple-element.46.info, bf16[512,6144]{1,0:T(8,128)(2,1)S(1)} %copy-done.4, bf16[512,2048]{1,0:T(8,128)(2,1)S(1)} %copy-done.2, bf16[512,2048]{1,0:T(8,128)(2,1)S(1)} %copy-done.2), custom_call_target="tpu_custom_call" | custom-call | flops 3623878656 | bytes 6291456 | tf_op jit(solution)/shard_map/attention/pallas_call | solution.py:59
  17.1 3.0 collective-permute-start.2
  21.6 10.7 %convolution_convert_fusion.3 = bf16[256,1536]{1,0:T(8,128)(2,1)} fusion(bf16[256,6144]{1,0:T(8,128)(2,1)} %attention.3, bf16[6144,1536]{1,0:T(8,128)(2,1)} %param.9), kind=kOutput, calls=%fused_computation.13 | convolution fusion | flops 4832231424 | bytes 22806528 | tf_op jit(solution)/shard_map/dot_general | solution.py:126
  32.3 6.2 constant_dynamic-slice_fusion.4
  41.6 150.5 %all-gather = s32[8,1,4]{2,1,0:T(1,128)S(1)} all-gather(s32[1,1,4]{2,1,0:T(1,128)S(1)} %bitcast.104), channel_id=1, replica_groups=mesh['grp'=2,'inst'=8,'tp'=2] {'inst'}, dimensions={0}, use_global_device_ids=true | all-gather | bytes 144 | tf_op jit(solution)/shard_map/all_gather | solution.py:153
  194.6 3.8 constant_dynamic-slice_fusion.2
  200.6 22.0 %collective-permute-done.53 = bf16[512,1024]{1,0:T(8,128)(2,1)} collective-permute-done((bf16[512,1024]{1,0:T(8,128)(2,1)S(1)}, bf16[512,1024]{1,0:T(8,128)(2,1)}, u32[]{:S(2)}, u32[]{:S(2)}) %collective-permute-start.53) | collective-permute-done | bytes 1048608 | tf_op jit(solution)/shard_map/ppermute | solution.py:118
  225.4 17.8 %collective-permute-start.54 = (bf16[1024,1024]{1,0:T(8,128)(2,1)}, bf16[1024,1024]{1,0:T(8,128)(2,1)S(1)}, u32[]{:S(2)}, u32[]{:S(2)}) collective-permute-start(bf16[1024,1024]{1,0:T(8,128)(2,1)} %pad_maximum_fusion.4), channel_id=1, source_target_pairs={{0,4},{2,6},{4,0},{6,2},{8,12},{10,14},{12,8},{14,10},{1,5},{3,7},... | collective-permute-start | bytes 6291464 | tf_op jit(solution)/shard_map/ppermute | solution.py:118
  246.6 10.4 attention.2
  257.1 10.4 add_convert_fusion.refs_0_
  267.5 56.2 %collective-permute-done.54 = bf16[1024,1024]{1,0:T(8,128)(2,1)S(1)} collective-permute-done((bf16[1024,1024]{1,0:T(8,128)(2,1)}, bf16[1024,1024]{1,0:T(8,128)(2,1)S(1)}, u32[]{:S(2)}, u32[]{:S(2)}) %collective-permute-start.54) | collective-permute-done | bytes 2097184 | tf_op jit(solution)/shard_map/ppermute | solution.py:118
  324.8 3.3 pad_maximum_fusion.3
  330.1 7.0 convolution_convert_fusion.2
  337.3 7.0 convolution_convert_fusion.1
  344.3 85.3 %collective-permute-done.23 = bf16[6144,256]{1,0:T(8,128)(2,1)} collective-permute-done((bf16[6144,256]{1,0:T(8,128)(2,1)}, bf16[6144,256]{1,0:T(8,128)(2,1)}, u32[]{:S(2)}, u32[]{:S(2)}) %collective-permute-start.23) | collective-permute-done | bytes 3145760 | tf_op jit(solution)/shard_map/ppermute | solution.py:118
  430.4 8.2 fusion
  442.8 7.1 fusion.1
  450.0 79.4 %collective-permute-done.10 = bf16[256,6144]{1,0:T(8,128)(2,1)} collective-permute-done((bf16[256,6144]{1,0:T(8,128)(2,1)}, bf16[256,6144]{1,0:T(8,128)(2,1)}, u32[]{:S(2)}, u32[]{:S(2)}) %collective-permute-start.10) | collective-permute-done | bytes 3145760 | tf_op jit(solution)/shard_map/ppermute | solution.py:118
  530.8 6.2 pad_maximum_fusion.1
  537.0 6.1 convolution_convert_fusion.7
  543.1 5.3 convolution_convert_fusion.5
  549.0 19.8 %collective-permute-done.43 = bf16[6144,128]{1,0:T(8,128)(2,1)} collective-permute-done((bf16[6144,128]{1,0:T(8,128)(2,1)}, bf16[6144,128]{1,0:T(8,128)(2,1)}, u32[]{:S(2)}, u32[]{:S(2)}) %collective-permute-start.43) | collective-permute-done | bytes 1572896 | tf_op jit(solution)/shard_map/ppermute | solution.py:118
  570.3 30.2 %collective-permute-done.18 = bf16[6144,256]{1,0:T(8,128)(2,1)S(1)} collective-permute-done((bf16[6144,256]{1,0:T(8,128)(2,1)}, bf16[6144,256]{1,0:T(8,128)(2,1)S(1)}, u32[]{:S(2)}, u32[]{:S(2)}) %collective-permute-start.18) | collective-permute-done | bytes 3145760 | tf_op jit(solution)/shard_map/ppermute | solution.py:122
  602.1 4.2 convolution_convert_fusion.6
  606.3 5.5 convolution_convert_fusion.11
  611.8 5.7 convolution_convert_fusion.9
  617.5 71.4 %collective-permute-done.38 = bf16[6144,128]{1,0:T(8,128)(2,1)S(1)} collective-permute-done((bf16[6144,128]{1,0:T(8,128)(2,1)}, bf16[6144,128]{1,0:T(8,128)(2,1)S(1)}, u32[]{:S(2)}, u32[]{:S(2)}) %collective-permute-start.38) | collective-permute-done | bytes 1572896 | tf_op jit(solution)/shard_map/ppermute | solution.py:122
  688.9 3.1 collective-permute-start.4
  692.1 4.1 convolution_convert_fusion.10
  696.2 9.6 collective-permute-done.48
  707.0 4.1 convolution_convert_fusion.8
  711.1 10.6 %convolution_convert_fusion = bf16[256,1536]{1,0:T(8,128)(2,1)} fusion(bf16[256,6144]{1,0:T(8,128)(2,1)} %collective-permute-done.10, bf16[6144,1536]{1,0:T(8,128)(2,1)} %param.9), kind=kOutput, calls=%fused_computation.10 | convolution fusion | flops 4832231424 | bytes 22806528 | tf_op jit(solution)/shard_map/dot_general | solution.py:126
  721.7 3.4 convolution_convert_fusion.4
  725.7 4.8 pad_maximum_fusion
  730.6 5.1 fusion.10
  736.2 3.5 fusion.9
  739.9 5.1 fusion.8
  746.1 4.0 fusion.7
  752.1 5.3 fusion.6
  757.9 3.4 fusion.5
  761.5 5.3 fusion.4
  766.9 3.2 collective-permute-start.35
  770.1 3.6 fusion.3
  801.0 10.2 fusion.2
  816.5 6.4 pad_maximum_fusion.2
  823.0 15.4 %gather_fusion.1 = bf16[2048,1024]{1,0:T(8,128)(2,1)} fusion(bf16[4096,1024]{1,0:T(8,128)(2,1)} %pad_maximum_fusion.2, s32[2048]{0:T(1024)S(1)} %copy-done.39), kind=kCustom, calls=%fused_computation.1 | custom fusion | bytes 8396800 | tf_op jit(solution)/shard_map/jit(_take)/gather | solution.py:174
  843.7 3.8 broadcast_select_fusion
  848.7 192.7 %place.1 = bf16[256,12288]{1,0:T(8,128)(2,1)} custom-call(s32[36]{0:T(128)} %stack.157.offsets, bf16[256,1536]{1,0:T(8,128)(2,1)} %add_convert_fusion.refs_0_, bf16[256,1536]{1,0:T(8,128)(2,1)} %copy-done.11, bf16[256,1536]{1,0:T(8,128)(2,1)} %copy-done.12, bf16[256,1536]{1,0:T(8,128)(2,1)} %copy-done.13, bf16[256,256]{1,0:T(8,128)(2,1)} %get-tuple-element.27.refs_4_, ...), custom_call_target="tpu_custom_call" | custom-call | bytes 12582912 | tf_op jit(solution)/shard_map/place/pallas_call | solution.py:99
  (258 shorter events, 79.4 us)
Async XLA Ops:
  17.1 311.7 %collective-permute-start.2 = (bf16[256,6144]{1,0:T(8,128)(2,1)}, bf16[256,6144]{1,0:T(8,128)(2,1)}, u32[]{:S(2)}, u32[]{:S(2)}) collective-permute-start(bf16[256,6144]{1,0:T(8,128)(2,1)} %attention.3), channel_id=1, source_target_pairs={{0,4},{2,6},{4,0},{6,2},{8,12},{10,14},{12,8},{14,10},{1,5},{3,7},... | collective-permute-start | bytes 9437192 | tf_op jit(solution)/shard_map/ppermute | solution.py:118
  20.1 317.1 %collective-permute-start.6 = (bf16[256,6144]{1,0:T(8,128)(2,1)}, bf16[256,6144]{1,0:T(8,128)(2,1)}, u32[]{:S(2)}, u32[]{:S(2)}) collective-permute-start(bf16[256,6144]{1,0:T(8,128)(2,1)} %attention.3), channel_id=1, source_target_pairs={{0,2},{2,0},{4,6},{6,4},{8,10},{10,8},{12,14},{14,12},{1,3},{3,1},... | collective-permute-start | bytes 9437192 | tf_op jit(solution)/shard_map/ppermute | solution.py:118
  32.3 224.8 %collective-permute-start = (bf16[256,1536]{1,0:T(8,128)(2,1)}, bf16[256,1536]{1,0:T(8,128)(2,1)}, u32[]{:S(2)}, u32[]{:S(2)}) collective-permute-start(bf16[256,1536]{1,0:T(8,128)(2,1)} %convolution_convert_fusion.3), channel_id=1, source_target_pairs={{0,1},{1,0},{2,3},{3,2},{4,5},{5,4},{6,7},{7,6},{8,9},{9,8},{10,11... | collective-permute-start | bytes 2359304 | tf_op jit(solution)/shard_map/ppermute | solution.py:122
  38.5 289.6 %collective-permute-start.13 = (bf16[6144,256]{1,0:T(8,128)(2,1)}, bf16[6144,256]{1,0:T(8,128)(2,1)}, u32[]{:S(2)}, u32[]{:S(2)}) collective-permute-start(bf16[6144,256]{1,0:T(8,128)(2,1)} %get-tuple-element.11), channel_id=1, source_target_pairs={{0,8},{2,10},{4,12},{6,14},{8,0},{10,2},{12,4},{14,6},{1,9},{3,11}... | collective-permute-start | bytes 9437192 | tf_op jit(solution)/shard_map/ppermute | solution.py:118
  41.2 181.4 %collective-permute-start.53 = (bf16[512,1024]{1,0:T(8,128)(2,1)S(1)}, bf16[512,1024]{1,0:T(8,128)(2,1)}, u32[]{:S(2)}, u32[]{:S(2)}) collective-permute-start(bf16[512,1024]{1,0:T(8,128)(2,1)S(1)} %constant_dynamic-slice_fusion), channel_id=1, source_target_pairs={{0,8},{2,10},{4,12},{6,14},{8,0},{10,2},{12,4},{14,6},{1,9},{3,11}... | collective-permute-start | bytes 3145736 | tf_op jit(solution)/shard_map/ppermute | solution.py:118
  225.4 98.3 %collective-permute-start.54 = (bf16[1024,1024]{1,0:T(8,128)(2,1)}, bf16[1024,1024]{1,0:T(8,128)(2,1)S(1)}, u32[]{:S(2)}, u32[]{:S(2)}) collective-permute-start(bf16[1024,1024]{1,0:T(8,128)(2,1)} %pad_maximum_fusion.4), channel_id=1, source_target_pairs={{0,4},{2,6},{4,0},{6,2},{8,12},{10,14},{12,8},{14,10},{1,5},{3,7},... | collective-permute-start | bytes 6291464 | tf_op jit(solution)/shard_map/ppermute | solution.py:118
  257.0 172.6 %collective-permute-start.1 = (bf16[256,6144]{1,0:T(8,128)(2,1)S(1)}, bf16[256,6144]{1,0:T(8,128)(2,1)}, u32[]{:S(2)}, u32[]{:S(2)}) collective-permute-start(bf16[256,6144]{1,0:T(8,128)(2,1)S(1)} %attention.2), channel_id=1, source_target_pairs={{0,4},{2,6},{4,0},{6,2},{8,12},{10,14},{12,8},{14,10},{1,5},{3,7},... | collective-permute-start | bytes 9437192 | tf_op jit(solution)/shard_map/ppermute | solution.py:118
  323.7 105.9 %collective-permute-start.23 = (bf16[6144,256]{1,0:T(8,128)(2,1)}, bf16[6144,256]{1,0:T(8,128)(2,1)}, u32[]{:S(2)}, u32[]{:S(2)}) collective-permute-start(bf16[6144,256]{1,0:T(8,128)(2,1)} %get-tuple-element.10), channel_id=1, source_target_pairs={{0,8},{2,10},{4,12},{6,14},{8,0},{10,2},{12,4},{14,6},{1,9},{3,11}... | collective-permute-start | bytes 9437192 | tf_op jit(solution)/shard_map/ppermute | solution.py:118
  328.1 110.5 %collective-permute-start.5 = (bf16[256,6144]{1,0:T(8,128)(2,1)S(1)}, bf16[256,6144]{1,0:T(8,128)(2,1)S(1)}, u32[]{:S(2)}, u32[]{:S(2)}) collective-permute-start(bf16[256,6144]{1,0:T(8,128)(2,1)S(1)} %attention.2), channel_id=1, source_target_pairs={{0,2},{2,0},{4,6},{6,4},{8,10},{10,8},{12,14},{14,12},{1,3},{3,1},... | collective-permute-start | bytes 9437192 | tf_op jit(solution)/shard_map/ppermute | solution.py:118
  328.7 486.6 %collective-permute-start.55 = (bf16[2048,1024]{1,0:T(8,128)(2,1)}, bf16[2048,1024]{1,0:T(8,128)(2,1)}, u32[]{:S(2)}, u32[]{:S(2)}) collective-permute-start(bf16[2048,1024]{1,0:T(8,128)(2,1)} %pad_maximum_fusion.3), channel_id=1, source_target_pairs={{0,2},{2,0},{4,6},{6,4},{8,10},{10,8},{12,14},{14,12},{1,3},{3,1},... | collective-permute-start | bytes 12582920 | tf_op jit(solution)/shard_map/ppermute | solution.py:118
  337.2 92.5 %collective-permute-start.3 = (bf16[256,1536]{1,0:T(8,128)(2,1)S(1)}, bf16[256,1536]{1,0:T(8,128)(2,1)S(1)}, u32[]{:S(2)}, u32[]{:S(2)}) collective-permute-start(bf16[256,1536]{1,0:T(8,128)(2,1)S(1)} %convolution_convert_fusion.2), channel_id=1, source_target_pairs={{0,1},{1,0},{2,3},{3,2},{4,5},{5,4},{6,7},{7,6},{8,9},{9,8},{10,11... | collective-permute-start | bytes 2359304 | tf_op jit(solution)/shard_map/ppermute | solution.py:122
  429.6 11.8 %collective-permute-start.7 = (bf16[256,1536]{1,0:T(8,128)(2,1)S(1)}, bf16[256,1536]{1,0:T(8,128)(2,1)}, u32[]{:S(2)}, u32[]{:S(2)}) collective-permute-start(bf16[256,1536]{1,0:T(8,128)(2,1)S(1)} %convolution_convert_fusion.1), channel_id=1, source_target_pairs={{0,1},{1,0},{2,3},{3,2},{4,5},{5,4},{6,7},{7,6},{8,9},{9,8},{10,11... | collective-permute-start | bytes 2359304 | tf_op jit(solution)/shard_map/ppermute | solution.py:122
  429.6 118.8 %collective-permute-start.33 = (bf16[6144,128]{1,0:T(8,128)(2,1)}, bf16[6144,128]{1,0:T(8,128)(2,1)}, u32[]{:S(2)}, u32[]{:S(2)}) collective-permute-start(bf16[6144,128]{1,0:T(8,128)(2,1)} %get-tuple-element.4), channel_id=1, source_target_pairs={{0,8},{2,10},{4,12},{6,14},{8,0},{10,2},{12,4},{14,6},{1,9},{3,11}... | collective-permute-start | bytes 4718600 | tf_op jit(solution)/shard_map/ppermute | solution.py:118
  429.7 99.6 %collective-permute-start.10 = (bf16[256,6144]{1,0:T(8,128)(2,1)}, bf16[256,6144]{1,0:T(8,128)(2,1)}, u32[]{:S(2)}, u32[]{:S(2)}) collective-permute-start(bf16[256,6144]{1,0:T(8,128)(2,1)} %collective-permute-done.2), channel_id=1, source_target_pairs={{0,2},{2,0},{4,6},{6,4},{8,10},{10,8},{12,14},{14,12},{1,3},{3,1},... | collective-permute-start | bytes 9437192 | tf_op jit(solution)/shard_map/ppermute | solution.py:118
  438.6 130.2 %collective-permute-start.43 = (bf16[6144,128]{1,0:T(8,128)(2,1)}, bf16[6144,128]{1,0:T(8,128)(2,1)}, u32[]{:S(2)}, u32[]{:S(2)}) collective-permute-start(bf16[6144,128]{1,0:T(8,128)(2,1)} %get-tuple-element.5), channel_id=1, source_target_pairs={{0,8},{2,10},{4,12},{6,14},{8,0},{10,2},{12,4},{14,6},{1,9},{3,11}... | collective-permute-start | bytes 4718600 | tf_op jit(solution)/shard_map/ppermute | solution.py:118
  441.5 283.7 %collective-permute-start.9 = (bf16[256,6144]{1,0:T(8,128)(2,1)}, bf16[256,6144]{1,0:T(8,128)(2,1)S(1)}, u32[]{:S(2)}, u32[]{:S(2)}) collective-permute-start(bf16[256,6144]{1,0:T(8,128)(2,1)} %collective-permute-done.1), channel_id=1, source_target_pairs={{0,2},{2,0},{4,6},{6,4},{8,10},{10,8},{12,14},{14,12},{1,3},{3,1},... | collective-permute-start | bytes 9437192 | tf_op jit(solution)/shard_map/ppermute | solution.py:118
  529.3 71.2 %collective-permute-start.18 = (bf16[6144,256]{1,0:T(8,128)(2,1)}, bf16[6144,256]{1,0:T(8,128)(2,1)S(1)}, u32[]{:S(2)}, u32[]{:S(2)}) collective-permute-start(bf16[6144,256]{1,0:T(8,128)(2,1)} %collective-permute-done.13), channel_id=1, source_target_pairs={{0,16},{16,0},{1,17},{17,1},{2,18},{18,2},{3,19},{19,3},{4,20},{20... | collective-permute-start | bytes 9437192 | tf_op jit(solution)/shard_map/ppermute | solution.py:122
  548.4 173.3 %collective-permute-start.28 = (bf16[6144,256]{1,0:T(8,128)(2,1)}, bf16[6144,256]{1,0:T(8,128)(2,1)S(1)}, u32[]{:S(2)}, u32[]{:S(2)}) collective-permute-start(bf16[6144,256]{1,0:T(8,128)(2,1)} %collective-permute-done.23), channel_id=1, source_target_pairs={{0,16},{16,0},{1,17},{17,1},{2,18},{18,2},{3,19},{19,3},{4,20},{20... | collective-permute-start | bytes 9437192 | tf_op jit(solution)/shard_map/ppermute | solution.py:122
  568.8 120.1 %collective-permute-start.38 = (bf16[6144,128]{1,0:T(8,128)(2,1)}, bf16[6144,128]{1,0:T(8,128)(2,1)S(1)}, u32[]{:S(2)}, u32[]{:S(2)}) collective-permute-start(bf16[6144,128]{1,0:T(8,128)(2,1)} %collective-permute-done.33), channel_id=1, source_target_pairs={{0,16},{16,0},{1,17},{17,1},{2,18},{18,2},{3,19},{19,3},{4,20},{20... | collective-permute-start | bytes 4718600 | tf_op jit(solution)/shard_map/ppermute | solution.py:122
  600.6 105.2 %collective-permute-start.48 = (bf16[6144,128]{1,0:T(8,128)(2,1)}, bf16[6144,128]{1,0:T(8,128)(2,1)S(1)}, u32[]{:S(2)}, u32[]{:S(2)}) collective-permute-start(bf16[6144,128]{1,0:T(8,128)(2,1)} %collective-permute-done.43), channel_id=1, source_target_pairs={{0,16},{16,0},{1,17},{17,1},{2,18},{18,2},{3,19},{19,3},{4,20},{20... | collective-permute-start | bytes 4718600 | tf_op jit(solution)/shard_map/ppermute | solution.py:122
  688.9 84.7 %collective-permute-start.4 = (bf16[256,1536]{1,0:T(8,128)(2,1)}, bf16[256,1536]{1,0:T(8,128)(2,1)S(1)}, u32[]{:S(2)}, u32[]{:S(2)}) collective-permute-start(bf16[256,1536]{1,0:T(8,128)(2,1)} %fusion), channel_id=1, source_target_pairs={{0,4},{2,6},{4,0},{6,2},{8,12},{10,14},{12,8},{14,10},{1,5},{3,7},... | collective-permute-start | bytes 2359304 | tf_op jit(solution)/shard_map/ppermute | solution.py:118
  705.8 68.8 %collective-permute-start.8 = (bf16[256,1536]{1,0:T(8,128)(2,1)}, bf16[256,1536]{1,0:T(8,128)(2,1)S(1)}, u32[]{:S(2)}, u32[]{:S(2)}) collective-permute-start(bf16[256,1536]{1,0:T(8,128)(2,1)} %fusion.1), channel_id=1, source_target_pairs={{0,2},{2,0},{4,6},{6,4},{8,10},{10,8},{12,14},{14,12},{1,3},{3,1},... | collective-permute-start | bytes 2359304 | tf_op jit(solution)/shard_map/ppermute | solution.py:118
  721.7 76.1 %collective-permute-start.11 = (bf16[256,1536]{1,0:T(8,128)(2,1)}, bf16[256,1536]{1,0:T(8,128)(2,1)S(1)}, u32[]{:S(2)}, u32[]{:S(2)}) collective-permute-start(bf16[256,1536]{1,0:T(8,128)(2,1)} %convolution_convert_fusion), channel_id=1, source_target_pairs={{0,1},{1,0},{2,3},{3,2},{4,5},{5,4},{6,7},{7,6},{8,9},{9,8},{10,11... | collective-permute-start | bytes 2359304 | tf_op jit(solution)/shard_map/ppermute | solution.py:122
  725.2 5.4 collective-permute-start.34
  739.7 5.9 collective-permute-start.49
  745.7 6.3 collective-permute-start.14
  752.0 5.4 collective-permute-start.19
  761.4 5.5 collective-permute-start.29
  766.9 9.0 collective-permute-start.35
  774.6 5.5 collective-permute-start.37
  778.0 5.5 collective-permute-start.41
  781.1 5.7 collective-permute-start.45
  785.3 5.5 collective-permute-start.47
  788.7 5.6 collective-permute-start.51
  790.8 5.7 collective-permute-start.52
  792.1 19.2 %collective-permute-start.15 = (bf16[256,256]{1,0:T(8,128)(2,1)S(1)}, bf16[256,256]{1,0:T(8,128)(2,1)S(1)}, u32[]{:S(2)}, u32[]{:S(2)}) collective-permute-start(bf16[256,256]{1,0:T(8,128)(2,1)S(1)} %get-tuple-element.26), channel_id=1, source_target_pairs={{0,4},{2,6},{4,0},{6,2},{8,12},{10,14},{12,8},{14,10},{1,5},{3,7},... | collective-permute-start | bytes 393224 | tf_op jit(solution)/shard_map/ppermute | solution.py:118
  794.9 17.0 %collective-permute-start.16 = (bf16[256,256]{1,0:T(8,128)(2,1)S(1)}, bf16[256,256]{1,0:T(8,128)(2,1)S(1)}, u32[]{:S(2)}, u32[]{:S(2)}) collective-permute-start(bf16[256,256]{1,0:T(8,128)(2,1)S(1)} %get-tuple-element.25), channel_id=1, source_target_pairs={{0,2},{2,0},{4,6},{6,4},{8,10},{10,8},{12,14},{14,12},{1,3},{3,1},... | collective-permute-start | bytes 393224 | tf_op jit(solution)/shard_map/ppermute | solution.py:118
  797.1 15.9 %collective-permute-start.17 = (bf16[256,256]{1,0:T(8,128)(2,1)S(1)}, bf16[256,256]{1,0:T(8,128)(2,1)S(1)}, u32[]{:S(2)}, u32[]{:S(2)}) collective-permute-start(bf16[256,256]{1,0:T(8,128)(2,1)S(1)} %get-tuple-element.24), channel_id=1, source_target_pairs={{0,6},{2,4},{4,2},{6,0},{8,14},{10,12},{12,10},{14,8},{1,7},{3,5},... | collective-permute-start | bytes 393224 | tf_op jit(solution)/shard_map/ppermute | solution.py:118
  798.7 16.2 %collective-permute-start.20 = (bf16[256,256]{1,0:T(8,128)(2,1)S(1)}, bf16[256,256]{1,0:T(8,128)(2,1)S(1)}, u32[]{:S(2)}, u32[]{:S(2)}) collective-permute-start(bf16[256,256]{1,0:T(8,128)(2,1)S(1)} %get-tuple-element.22), channel_id=1, source_target_pairs={{0,4},{2,6},{4,0},{6,2},{8,12},{10,14},{12,8},{14,10},{1,5},{3,7},... | collective-permute-start | bytes 393224 | tf_op jit(solution)/shard_map/ppermute | solution.py:118
  811.3 27.1 %collective-permute-start.21 = (bf16[256,256]{1,0:T(8,128)(2,1)S(1)}, bf16[256,256]{1,0:T(8,128)(2,1)S(1)}, u32[]{:S(2)}, u32[]{:S(2)}) collective-permute-start(bf16[256,256]{1,0:T(8,128)(2,1)S(1)} %get-tuple-element.21), channel_id=1, source_target_pairs={{0,2},{2,0},{4,6},{6,4},{8,10},{10,8},{12,14},{14,12},{1,3},{3,1},... | collective-permute-start | bytes 393224 | tf_op jit(solution)/shard_map/ppermute | solution.py:118
  811.9 28.3 %collective-permute-start.22 = (bf16[256,256]{1,0:T(8,128)(2,1)S(1)}, bf16[256,256]{1,0:T(8,128)(2,1)S(1)}, u32[]{:S(2)}, u32[]{:S(2)}) collective-permute-start(bf16[256,256]{1,0:T(8,128)(2,1)S(1)} %get-tuple-element.20), channel_id=1, source_target_pairs={{0,6},{2,4},{4,2},{6,0},{8,14},{10,12},{12,10},{14,8},{1,7},{3,5},... | collective-permute-start | bytes 393224 | tf_op jit(solution)/shard_map/ppermute | solution.py:118
  813.0 28.1 %collective-permute-start.25 = (bf16[256,256]{1,0:T(8,128)(2,1)S(1)}, bf16[256,256]{1,0:T(8,128)(2,1)S(1)}, u32[]{:S(2)}, u32[]{:S(2)}) collective-permute-start(bf16[256,256]{1,0:T(8,128)(2,1)S(1)} %get-tuple-element.18), channel_id=1, source_target_pairs={{0,4},{2,6},{4,0},{6,2},{8,12},{10,14},{12,8},{14,10},{1,5},{3,7},... | collective-permute-start | bytes 393224 | tf_op jit(solution)/shard_map/ppermute | solution.py:118
  814.9 27.0 %collective-permute-start.26 = (bf16[256,256]{1,0:T(8,128)(2,1)S(1)}, bf16[256,256]{1,0:T(8,128)(2,1)S(1)}, u32[]{:S(2)}, u32[]{:S(2)}) collective-permute-start(bf16[256,256]{1,0:T(8,128)(2,1)S(1)} %get-tuple-element.17), channel_id=1, source_target_pairs={{0,2},{2,0},{4,6},{6,4},{8,10},{10,8},{12,14},{14,12},{1,3},{3,1},... | collective-permute-start | bytes 393224 | tf_op jit(solution)/shard_map/ppermute | solution.py:118
  815.4 32.4 %collective-permute-start.12 = (bf16[256,1536]{1,0:T(8,128)(2,1)}, bf16[256,1536]{1,0:T(8,128)(2,1)S(1)}, u32[]{:S(2)}, u32[]{:S(2)}) collective-permute-start(bf16[256,1536]{1,0:T(8,128)(2,1)} %fusion.2), channel_id=1, source_target_pairs={{0,6},{2,4},{4,2},{6,0},{8,14},{10,12},{12,10},{14,8},{1,7},{3,5},... | collective-permute-start | bytes 2359304 | tf_op jit(solution)/shard_map/ppermute | solution.py:118
  838.4 9.1 collective-permute-start.27
  840.2 7.4 collective-permute-start.30
  841.1 6.4 collective-permute-start.31
  841.9 5.9 collective-permute-start.32
  (66 other events, 1956.1 us)

commit v2 on v1

v2 whole, which is shorter than its diff:
```python
import functools

import jax
import jax.numpy as jnp
from jax import lax
from jax.experimental import pallas as pl
from jax.experimental.pallas import tpu as pltpu
from jax.sharding import PartitionSpec as P

NH = 96
KVH = 8
HD = 128
PAGE = 16
OWNERS = 4
REQ_INST = 4
MAXLEN = 256
QUARTERS = 4
ROWS = 128
LOG2E = 1.4426950408889634

SIDE, NEXT, FAR = 1, 2, 4
MASKS = (0, NEXT, SIDE, NEXT | SIDE)
WIDTH = 128
LIGHT = pl.CostEstimate(flops=0, bytes_accessed=0, transcendentals=0)


def attention_kernel(info, q_ref, k_ref, v_ref, o_ref, *, heads, row_blocks, window):
    for block in range(row_blocks):
        place = info[0] * row_blocks + block
        first = pl.multiple_of(jnp.maximum(place - (window // ROWS - 1), 0) * ROWS, ROWS)
        row = place * ROWS + lax.broadcasted_iota(jnp.int32, (ROWS, window), 0)
        col = first + lax.broadcasted_iota(jnp.int32, (ROWS, window), 1)
        begin = jnp.zeros_like(row)
        for j in range(REQ_INST):
            begin = jnp.where(row >= info[2 + j], info[2 + j], begin)
        bias = jnp.where((col <= row) & (col >= begin), 0.0, -1e30)
        keys = k_ref[pl.ds(first, window), :]
        vals = v_ref[pl.ds(first, window), :]
        vals = jnp.concatenate([vals, jnp.ones_like(vals)], axis=1)
        rows = slice(block * ROWS, (block + 1) * ROWS)
        for head in range(heads):
            cols = slice(head * HD, (head + 1) * HD)
            scores = lax.dot_general(
                q_ref[rows, cols], keys, (((1,), (1,)), ((), ())),
                preferred_element_type=jnp.float32,
            )
            scores = scores * (LOG2E / HD**0.5) + bias
            expo = jnp.exp2(scores - jnp.max(scores, axis=1, keepdims=True))
            mixed = jnp.dot(expo.astype(jnp.bfloat16), vals, preferred_element_type=jnp.float32)
            o_ref[rows, cols] = (mixed[:, :HD] / mixed[:, HD:]).astype(jnp.bfloat16)


def attention(queries, keys_values, ends, first_kv, chunk, chunk_rows, part, parts):
    tok_rows, width = queries.shape
    local_heads = width // HD
    kv_heads = max(1, local_heads // (NH // KVH))
    heads = local_heads // kv_heads
    steps = kv_heads // parts
    window = min(ROWS + MAXLEN, tok_rows)
    first_kv = first_kv + part * steps
    info = jnp.concatenate([jnp.stack([chunk, first_kv]).astype(jnp.int32), ends])
    return pl.pallas_call(
        functools.partial(
            attention_kernel, heads=heads, row_blocks=chunk_rows // ROWS, window=window
        ),
        grid_spec=pltpu.PrefetchScalarGridSpec(
            num_scalar_prefetch=1,
            grid=(steps,),
            in_specs=[
                pl.BlockSpec(
                    (chunk_rows, heads * HD), lambda g, info: (info[0], part * steps + g)
                ),
                pl.BlockSpec((tok_rows, HD), lambda g, info: (0, 2 * (info[1] + g))),
                pl.BlockSpec((tok_rows, HD), lambda g, info: (0, 2 * (info[1] + g) + 1)),
            ],
            out_specs=pl.BlockSpec((chunk_rows, heads * HD), lambda g, info: (0, g)),
        ),
        out_shape=jax.ShapeDtypeStruct((chunk_rows, width // parts), jnp.bfloat16),
        compiler_params=pltpu.CompilerParams(vmem_limit_bytes=32 << 20),
        cost_estimate=LIGHT,
        name="attention",
    )(info, queries, keys_values, keys_values)


def place_kernel(offsets, *refs, segments):
    out = refs[-1]
    for n, (source, at, width) in enumerate(segments):
        start = pl.multiple_of(offsets[n], 128)
        out[:, pl.ds(start, width)] = refs[source][:, at : at + width]


def place(pieces, segments, offsets, columns):
    rows = pieces[0].shape[0]
    block = 64 if rows % 64 == 0 else rows
    return pl.pallas_call(
        functools.partial(place_kernel, segments=segments),
        grid_spec=pltpu.PrefetchScalarGridSpec(
            num_scalar_prefetch=1,
            grid=(rows // block,),
            in_specs=[
                pl.BlockSpec((block, piece.shape[1]), lambda i, offsets: (i, 0))
                for piece in pieces
            ],
            out_specs=pl.BlockSpec((block, columns), lambda i, offsets: (i, 0)),
        ),
        out_shape=jax.ShapeDtypeStruct((rows, columns), pieces[0].dtype),
        compiler_params=pltpu.CompilerParams(vmem_limit_bytes=32 << 20),
        cost_estimate=LIGHT,
        name="place",
    )(jnp.stack(offsets).astype(jnp.int32), *pieces)


def cache_kernel(page_of, pages_ref, o_ref):
    slots = o_ref.shape[0]
    first = pl.program_id(0) * slots
    for n in range(slots):
        page = page_of[first + n]
        start = pl.multiple_of(jnp.maximum(page, 0) * PAGE, PAGE)
        rows = pages_ref[pl.ds(start, PAGE), :]
        o_ref[n] = jnp.where(page >= 0, rows, jnp.zeros_like(rows))


def cache_of(pages, page_of):
    rows, width = pages.shape
    count = page_of.shape[0]
    block = 16 if count % 16 == 0 else count
    return pl.pallas_call(
        cache_kernel,
        grid_spec=pltpu.PrefetchScalarGridSpec(
            num_scalar_prefetch=1,
            grid=(count // block,),
            in_specs=[pl.BlockSpec((rows, width), lambda i, page_of: (0, 0))],
            out_specs=pl.BlockSpec((block, PAGE, width), lambda i, page_of: (i, 0, 0)),
        ),
        out_shape=jax.ShapeDtypeStruct((count, PAGE, width), pages.dtype),
        compiler_params=pltpu.CompilerParams(vmem_limit_bytes=32 << 20),
        cost_estimate=LIGHT,
        name="cache",
    )(page_of, pages)


def hop(array, mask):
    count = lax.axis_size("inst")
    return lax.ppermute(array, "inst", [(i, i ^ mask) for i in range(count)])


def swap(array, axis):
    return lax.ppermute(array, axis, [(0, 1), (1, 0)])


def product_kernel(*refs, heights, parts, groups, summed):
    step = pl.program_id(0)
    lefts, refs = refs[: heights * parts], refs[heights * parts :]
    out = refs[-1]
    rows, depth = lefts[0].shape

    def group_of(rights):
        def compute():
            for height in range(heights):
                total = None
                for part in range(parts):
                    span = slice(part * depth, (part + 1) * depth)
                    right = jnp.concatenate([ref[span, :] for ref in rights], axis=1)
                    term = jnp.dot(
                        lefts[height * parts + part][...], right,
                        preferred_element_type=jnp.float32,
                    )
                    total = term if total is None else total + term
                at = slice(height * rows, (height + 1) * rows)
                if summed:
                    total = total + refs[-2][at, :].astype(jnp.float32)
                out[at, :] = total.astype(out.dtype)
        return compute

    first = 0
    for steps, count in groups:
        compute = group_of(refs[:count])
        refs = refs[count:]
        if len(groups) == 1:
            compute()
        else:
            pl.when((step >= first) & (step < first + steps))(compute)
        first += steps


def product(lefts, rights, other=None):
    rows, depth = lefts[0][0].shape
    block = 2 * WIDTH
    operands, specs, groups = [], [], []
    for left in lefts:
        for part in left:
            operands.append(part)
            specs.append(pl.BlockSpec((rows, depth), lambda n: (0, 0)))
    first = 0
    for right in rights:
        if isinstance(right, tuple):
            steps = 1
            for piece in right:
                operands.append(piece)
                specs.append(pl.BlockSpec(piece.shape, lambda n: (0, 0)))
            groups.append((1, len(right)))
        else:
            steps = right.shape[1] // block
            operands.append(right)
            specs.append(
                pl.BlockSpec(
                    (right.shape[0], block),
                    lambda n, first=first, steps=steps: (0, jnp.clip(n - first, 0, steps - 1)),
                )
            )
            groups.append((steps, 1))
        first += steps
    height = rows * len(lefts)
    out_spec = pl.BlockSpec((height, block), lambda n: (0, n))
    if other is not None:
        operands.append(other)
        specs.append(out_spec)
    return pl.pallas_call(
        functools.partial(
            product_kernel, heights=len(lefts), parts=len(lefts[0]), groups=groups,
            summed=other is not None,
        ),
        grid=(first,),
        in_specs=specs,
        out_specs=out_spec,
        out_shape=jax.ShapeDtypeStruct((height, first * block), operands[0].dtype),
        compiler_params=pltpu.CompilerParams(vmem_limit_bytes=56 << 20),
        cost_estimate=LIGHT,
        name="product",
    )(*operands)


def after(array, *earlier):
    return lax.optimization_barrier((array,) + earlier)[0]


def data_pages(tok_rows):
    span = PAGE * OWNERS
    return (tok_rows + REQ_INST * (span - 1)) // span


def packing(lens, residue):
    page_counts = (lens + (PAGE - 1)) // PAGE
    counts = jnp.maximum(page_counts - residue + (OWNERS - 1), 0) // OWNERS
    return counts, jnp.cumsum(counts, axis=-1) - counts


def packed_pages(held, lens, residues, tok_rows):
    limit = data_pages(tok_rows)
    starts = jnp.cumsum(lens) - lens
    residues = jnp.stack(residues)[:, None]
    counts, firsts = packing(lens[None, :], residues)
    slot = jnp.arange(limit + 1, dtype=jnp.int32)
    step = slot[None, :, None] - firsts[:, None, :]
    mine = (step >= 0) & (step < counts[:, None, :])
    offset = (step * OWNERS + residues[:, :, None]) * PAGE
    base = jnp.sum(jnp.where(mine, starts[None, None, :] + offset, 0), axis=2)
    live = jnp.sum(jnp.where(mine, jnp.minimum(lens[None, None, :] - offset, PAGE), 0), axis=2)
    base = jnp.where(slot[None, :] == limit, tok_rows, base)
    live = jnp.where(slot[None, :] == limit, PAGE, live)
    within = jnp.arange(PAGE, dtype=jnp.int32)
    row = jnp.where(
        within[None, None, :] < live[:, :, None], base[:, :, None] + within[None, None, :], -1
    ).reshape(-1)
    chosen = row[:, None] == jnp.arange(held.shape[0], dtype=jnp.int32)[None, :]
    pages = jnp.dot(chosen.astype(held.dtype), held, preferred_element_type=jnp.float32)
    return pages.astype(held.dtype).reshape(residues.shape[0], (limit + 1) * PAGE, held.shape[1])


def slot_pages(lens, placement, page_table, block_of, limit):
    inst_here = lax.axis_index("inst")
    residue = inst_here % OWNERS
    requests = page_table.shape[0]
    slot_count = requests * QUARTERS
    counts, firsts = packing(lens, residue)
    slots = lax.dynamic_index_in_dim(
        page_table.reshape(requests, QUARTERS, OWNERS), residue, axis=2, keepdims=False
    )
    step = jnp.arange(QUARTERS, dtype=jnp.int32)
    valid = (placement == inst_here // OWNERS)[:, None] & (step[None, :] < counts.reshape(-1)[:, None])
    page = (firsts + block_of[:, None] * (limit + 1)).reshape(-1)[:, None] + step[None, :]
    target = jnp.where(valid, slots, slot_count).reshape(-1)
    match = target[None, :] == jnp.arange(slot_count, dtype=jnp.int32)[:, None]
    return jnp.sum(jnp.where(match, page.reshape(-1)[None, :] + 1, 0), axis=1) - 1


def per_device(queries, keys_values, out_weight, lengths, placement, page_table):
    tok_rows = queries.shape[0]
    tp_count = lax.axis_size("tp")
    tp_here = lax.axis_index("tp")
    inst_count = lax.axis_size("inst")
    inst_here = lax.axis_index("inst")
    grp_here = lax.axis_index("grp")
    side_here = inst_here % 2
    next_here = inst_here // NEXT % 2
    local_heads = queries.shape[1] // HD
    first_kv = tp_here * local_heads // (NH // KVH)
    ends = jnp.cumsum(lengths[0])
    depth, own_cols = out_weight.shape
    half_cols = own_cols // 2
    kv_width = keys_values.shape[1] // tp_count

    pairs = half_cols // WIDTH

    gate = ()

    def gated(array):
        return after(array, *gate) if gate else array

    def cut(n, *earlier):
        weight = after(out_weight, *earlier) if earlier else out_weight
        return lax.dynamic_slice(
            weight, (jnp.int32(0), grp_here * half_cols + n * WIDTH), (depth, WIDTH)
        )

    pieces, segments, offsets = [], [], []
    own_columns = [(own_cols, lambda inst: inst * own_cols)]

    def pair_columns(first, last):
        return [
            (
                WIDTH,
                lambda inst, n=n, half=half: (
                    (inst ^ FAR) * own_cols + half * half_cols + n * WIDTH
                ),
            )
            for n in range(first, last)
            for half in (grp_here, 1 - grp_here)
        ]

    def hand_out(mask, share, columns):
        at = 0
        for width, column_of in columns:
            segments.append((len(pieces), at, width))
            offsets.append(column_of(inst_here ^ mask))
            at += width
        pieces.append(hop(share, mask) if mask else share)
        return pieces[-1]

    kv_parts = 2 if local_heads % (2 * (NH // KVH)) == 0 else 1
    blocks = {mask: [] for mask in MASKS}

    def begin_sum(masks, rights):
        lefts = [list(blocks[mask]) for mask in masks]
        lefts[0][0] = gated(lefts[0][0])
        return masks, rights, product([left[:kv_parts] for left in lefts], rights)

    def end_sum(begun, *earlier):
        masks, rights, given = begun
        given = after(given, *earlier) if earlier else given
        if tp_count == 2:
            lefts = [blocks[mask][kv_parts:] for mask in masks]
            total = product(lefts, rights, swap(given, "tp"))
        else:
            total = given
        rows = total.shape[0] // len(masks)
        shares = {mask: total[n * rows : (n + 1) * rows] for n, mask in enumerate(masks)}
        if tp_count != 2:
            for mask in masks:
                shares[mask] = lax.psum_scatter(
                    shares[mask], "tp", scatter_dimension=0, tiled=True
                )
        return total, shares

    def group_sum(masks, rights, *earlier):
        return end_sum(begin_sum(masks, rights), *earlier)

    sliced, along, across = [cut(0)], [], []
    along.append(hop(sliced[0], FAR))
    held = lax.dynamic_slice_in_dim(
        after(keys_values, sliced[0]), tp_here * kv_width, kv_width, 1
    )
    lens_rows = jnp.zeros((PAGE, kv_width), held.dtype)
    lens_rows = lens_rows.at[0, :REQ_INST].set(lengths[0].astype(held.dtype))
    held = jnp.concatenate([held, lens_rows], axis=0)
    held_far = hop(held, FAR)
    chunks = [1 - tp_here, tp_here] if tp_count == 2 else [jnp.int32(0)]
    own = blocks[0]
    ready = held
    for chunk in chunks:
        for part in range(kv_parts):
            ready = attention(
                after(queries, ready), keys_values, ends, first_kv, chunk,
                tok_rows // len(chunks), part, kv_parts,
            )
            own.append(ready)

    def spread(name, arrays, mask):
        sent = [hop(gated(array), mask) for array in arrays]
        blocks[name] += sent
        return tuple(sent)

    moved = spread(NEXT, own[:1], NEXT) + spread(SIDE, own[:2], SIDE)
    for n in range(1, pairs):
        ready = cut(n, ready)
        sliced.append(ready)
    gate = moved + (along[0], held_far, ready)

    def weights():
        n = len(across)
        across.append(swap(gated(along[n]), "grp"))
        if n + 1 < pairs:
            along.append(hop(gated(sliced[n + 1]), FAR))
        return (across[-1], along[-1])

    moved = weights() + spread(NEXT, own[1:2], NEXT) + spread(SIDE, own[2:], SIDE)
    held_far = gated(held_far)
    pages_given, pages_kept = (
        jnp.stack(
            [
                packed_pages(rows, lens, residues, tok_rows)
                for rows, lens in (
                    (held, lengths[0]),
                    (held_far, held_far[tok_rows, :REQ_INST].astype(jnp.int32)),
                )
            ]
        )
        for residues in ([1 - side_here, 3 - side_here], [side_here, 2 + side_here])
    )
    ready, own_shares = group_sum((0,), [out_weight], moved[0])
    gate = moved + (pages_given, pages_kept, ready)

    near = blocks[NEXT]
    moved = weights() + spread(NEXT, own[2:3], NEXT) + spread(NEXT | SIDE, near[:2], SIDE)
    ready, shares = group_sum((SIDE,), [out_weight], moved[0])
    own_shares.update(shares)
    gate = moved + (ready,)

    def pair(n):
        return (along[n], across[n])

    moved = weights() + spread(NEXT, own[3:], NEXT) + spread(NEXT | SIDE, near[2:3], SIDE)
    pages_side = hop(gated(pages_given), SIDE)
    ready, shares = group_sum((0, SIDE), [pair(0), pair(1)], moved[0])
    gate = moved + (pages_side, ready)

    first_columns = own_columns + pair_columns(0, 2)
    moved = weights() + spread(NEXT | SIDE, near[3:], SIDE)
    moved += (
        hand_out(SIDE, gated(jnp.concatenate([own_shares[SIDE], shares[SIDE]], axis=1)), first_columns),
    )
    hand_out(0, own_shares[0], own_columns)
    hand_out(0, shares[0], pair_columns(0, 2))
    pages = gated(jnp.concatenate([pages_kept, pages_side], axis=0))
    pages_next = hop(
        lax.dynamic_index_in_dim(pages, 1 - next_here, axis=1, keepdims=False), NEXT
    )
    pages = lax.dynamic_index_in_dim(pages, next_here, axis=1, keepdims=False)
    ready, shares = group_sum((NEXT,), [out_weight, pair(0), pair(1)], moved[0])
    gate = moved + (pages_next, ready)

    moved = weights() + (hand_out(NEXT, gated(shares[NEXT]), first_columns),)
    begun = begin_sum((NEXT | SIDE,), [out_weight, pair(0), pair(1), pair(2), pair(3)])
    begun_near = begin_sum((SIDE, NEXT, 0), [pair(2), pair(3)])
    far_shares = end_sum(begun, begun_near[2], *moved)[1]
    shares = end_sum(begun_near, *moved)[1]
    pages = jnp.concatenate([pages, gated(pages_next)], axis=0)
    order = [mask ^ far for mask in (0, SIDE) for far in (0, FAR)]
    order = order + [at ^ NEXT for at in order]
    block_of = jnp.asarray([order.index(i) for i in range(inst_count)], jnp.int32)
    block_of = jnp.take(block_of, jnp.arange(inst_count, dtype=jnp.int32) ^ inst_here)
    limit = data_pages(tok_rows)
    lens = jnp.take(pages[:, limit * PAGE, :REQ_INST].astype(jnp.int32), block_of, axis=0)
    page_of = slot_pages(lens, placement, page_table, block_of, limit)
    cache = cache_of(pages.reshape(-1, kv_width), page_of)
    gate = moved + (begun_near[2],)

    moved = weights()
    hand_out(NEXT | SIDE, gated(far_shares[NEXT | SIDE]), own_columns + pair_columns(0, 4))
    for mask in (NEXT, SIDE, 0):
        hand_out(mask, gated(shares[mask]), pair_columns(2, 4))
    masks = (NEXT | SIDE, NEXT, SIDE, 0)
    ready, shares = group_sum(masks, [pair(4)])
    for mask in masks:
        hand_out(mask, shares[mask], pair_columns(4, 5))
    gate = moved + (ready,)
    ready, shares = group_sum(masks, [pair(5)])
    for mask in masks:
        hand_out(mask, shares[mask], pair_columns(5, 6))
    projected = place(pieces, segments, offsets, inst_count * own_cols)
    return (projected, cache)


def solution(mesh):
    return jax.shard_map(
        per_device,
        mesh=mesh,
        in_specs=(
            P(("grp", "inst"), "tp"),
            P(("grp", "inst"), None),
            P("tp", "inst"),
            P(("grp", "inst"), None),
            P("grp"),
            P("grp", None),
        ),
        out_specs=(P(("grp", "inst", "tp"), None), P(("grp", "inst"), None, "tp")),
        check_vma=False,
    )
```

time: 1050 us -> 611 us (0.58)
  blocking collectives: 150 us -> 0 us
  matrix products: 145 us -> 7.46 us
  waiting for transfers between devices: 379 us -> 260 us
  starting transfers between devices: 76.5 us -> 50.1 us
  Pallas kernels: 214 us -> 233 us
  other arithmetic: 30.5 us -> 11.5 us
    all_gather x1 -> x0, blocking collectives: 150 us -> none  [fill_cache(): lens = lax.all_gather(lengths, 'inst', axis=0, tiled=True)]
    dot_general x24 -> x4, matrix products: 145 us -> 7.46 us  [packed_pages(): jnp.dot(chosen.astype(held.dtype), held, preferred_element_type=jnp.float32)]
    ppermute x40 -> x32, waiting for transfers between devices: 267 us -> 194 us  [hop(): return lax.ppermute(array, 'inst', [(i, i ^ mask) for i in range(count)])]
    ppermute x16 -> x14, waiting for transfers between devices: 111 us -> 66 us  [swap(): return lax.ppermute(array, axis, [(0, 1), (1, 0)])]
    ppermute x40 -> x32, starting transfers between devices: 68.8 us -> 39 us  [hop(): return lax.ppermute(array, 'inst', [(i, i ^ mask) for i in range(count)])]
    concatenate x5, other arithmetic: 23.4 us -> 4.74 us  [the longest x2 2.4 us: per_device(): pages = jnp.concatenate([pages, gated(pages_next)], axis=0)]
    pallas_call x1 -> x18, Pallas kernels: 193 us -> 209 us  [the longest x16 201 us: product(): pl.pallas_call(functools.partial(product_kernel, heights=len(lefts), part...]
    gather x2, local copies, waits for them, and re-layouts: 16.1 us -> 1.2 us  [the longest x1 0.64 us: per_device(): jnp.take(block_of, jnp.arange(inst_count, dtype=jnp.int32) ^ inst_here)]
  transfers between devices with their start and end apart: 56 -> 46, of which waited for: 14 -> 24; matrix products, arithmetic and copies ran while one was open for 20% -> 6% of each run, Pallas kernels for 1% -> 38%
where the time goes in v2:
time: 611 us; the launch traced here: 602 us
  waiting for transfers between devices  260 us (43%)
  Pallas kernels  233 us (38%)
  starting transfers between devices  50.1 us (8%)
  local copies, waits for them, and re-layouts  37.3 us (6%)
  other arithmetic  11.5 us (2%)
  matrix products  7.46 us (1%)
    pallas_call x16, Pallas kernels, product(): pl.pallas_call(functools.partial(product_kernel, heights=len(lefts), part...  201 us
    ppermute x32, waiting for transfers between devices, hop(): return lax.ppermute(array, 'inst', [(i, i ^ mask) for i in range(count)])  194 us
    ppermute x14, waiting for transfers between devices, swap(): return lax.ppermute(array, axis, [(0, 1), (1, 0)])  66 us
    ppermute x32, starting transfers between devices, hop(): return lax.ppermute(array, 'inst', [(i, i ^ mask) for i in range(count)])  39 us
    pallas_call x4, Pallas kernels, attention(): pl.pallas_call(functools.partial(attention_kernel, heads=heads, row_block...  24.5 us
    dynamic_slice x6, local copies, waits for them, and re-layouts, cut(): lax.dynamic_slice(weight, (jnp.int32(0), grp_here * half_cols + n * WIDTH...  16.4 us
    unnamed x70, local copies, waits for them, and re-layouts  13.3 us
  transfers between devices with their start and end apart: 46, of which 24 were waited for; matrix products, arithmetic and copies ran while one was open for 6% of the time, Pallas kernels for 38%

profile of v2, /device:TPU:0, one launch (start us, length us, event | category | flops | bytes accessed | tf_op | source)
XLA Modules:
  0.0 601.5 jit_solution(7618640594587049737)
XLA Ops:
  1.4 2.8 constant_dynamic-slice_fusion.7
  5.4 4.1 collective-permute-start.4
  9.7 2.8 copy-done.3
  12.5 6.4 %attention.4.refs_0_.refs_4_.refs_6_ = bf16[256,3072]{1,0:T(8,128)(2,1)} custom-call(s32[6]{0:T(128)S(1)} %get-tuple-element.180.info, bf16[512,6144]{1,0:T(8,128)(2,1)S(1)} %copy-done.3, bf16[512,2048]{1,0:T(8,128)(2,1)S(1)} %copy-done.2, bf16[512,2048]{1,0:T(8,128)(2,1)S(1)} %copy-done.2), custom_call_target="tpu_custom_call" | custom-call | tf_op jit(solution)/shard_map/attention/pallas_call | solution.py:62
  22.4 6.3 %attention.5.refs_1_.refs_5_.refs_7_ = bf16[256,3072]{1,0:T(8,128)(2,1)} custom-call(s32[6]{0:T(128)S(1)} %get-tuple-element.181.info, bf16[512,6144]{1,0:T(8,128)(2,1)S(1)} %copy-done.3, bf16[512,2048]{1,0:T(8,128)(2,1)S(1)} %copy-done.2, bf16[512,2048]{1,0:T(8,128)(2,1)S(1)} %copy-done.2), custom_call_target="tpu_custom_call" | custom-call | tf_op jit(solution)/shard_map/attention/pallas_call | solution.py:62
  29.3 2.8 copy-done.4
  32.1 6.3 %attention.6.refs_0_.refs_4_.refs_6_ = bf16[256,3072]{1,0:T(8,128)(2,1)} custom-call(s32[6]{0:T(128)S(1)} %add_add_fusion.1.info, bf16[512,6144]{1,0:T(8,128)(2,1)S(1)} %copy-done.4, bf16[512,2048]{1,0:T(8,128)(2,1)S(1)} %copy-done.2, bf16[512,2048]{1,0:T(8,128)(2,1)S(1)} %copy-done.2), custom_call_target="tpu_custom_call" | custom-call | tf_op jit(solution)/shard_map/attention/pallas_call | solution.py:62
  38.4 5.5 attention.7.refs_1_.refs_5_.refs_7_
  50.3 2.8 constant_dynamic-slice_fusion.3
  53.1 2.7 constant_dynamic-slice_fusion.2
  55.8 2.8 constant_dynamic-slice_fusion.1
  58.6 30.2 %collective-permute-done.2.refs_1_.refs_3_.refs_5_ = bf16[256,3072]{1,0:T(8,128)(2,1)} collective-permute-done((bf16[256,3072]{1,0:T(8,128)(2,1)}, bf16[256,3072]{1,0:T(8,128)(2,1)}, u32[]{:S(2)}, u32[]{:S(2)}) %collective-permute-start.2) | collective-permute-done | bytes 1572896 | tf_op jit(solution)/shard_map/ppermute | solution.py:144
  90.0 34.0 %collective-permute-done.3.refs_4_.refs_3_ = bf16[6144,128]{1,0:T(8,128)(2,1)} collective-permute-done((bf16[6144,128]{1,0:T(8,128)(2,1)}, bf16[6144,128]{1,0:T(8,128)(2,1)}, u32[]{:S(2)}, u32[]{:S(2)}) %collective-permute-start.3) | collective-permute-done | bytes 1572896 | tf_op jit(solution)/shard_map/ppermute | solution.py:144
  130.7 4.0 collective-permute-start.9
  135.6 12.4 %product.16 = bf16[256,1536]{1,0:T(8,128)(2,1)} custom-call(bf16[256,3072]{1,0:T(8,128)(2,1)} %attention.4.refs_0_.refs_4_.refs_6_, bf16[256,3072]{1,0:T(8,128)(2,1)} %attention.5.refs_1_.refs_5_.refs_7_, bf16[6144,1536]{1,0:T(8,128)(2,1)} %refs_2_.15), custom_call_target="tpu_custom_call" | custom-call | tf_op jit(solution)/shard_map/product/pallas_call | solution.py:218
  151.0 13.4 %collective-permute-done.7.refs_5_.refs_4_ = bf16[6144,128]{1,0:T(8,128)(2,1)S(1)} collective-permute-done((bf16[6144,128]{1,0:T(8,128)(2,1)}, bf16[6144,128]{1,0:T(8,128)(2,1)S(1)}, u32[]{:S(2)}, u32[]{:S(2)}) %collective-permute-start.7) | collective-permute-done | bytes 1572896 | tf_op jit(solution)/shard_map/ppermute | solution.py:148
  167.7 2.9 convolution_convert_fusion
  171.5 11.9 %product.17.refs_1_ = bf16[256,1536]{1,0:T(8,128)(2,1)} custom-call(bf16[256,3072]{1,0:T(8,128)(2,1)} %attention.6.refs_0_.refs_4_.refs_6_, bf16[256,3072]{1,0:T(8,128)(2,1)} %copy-done.5, bf16[6144,1536]{1,0:T(8,128)(2,1)} %refs_2_.15, bf16[256,1536]{1,0:T(8,128)(2,1)} %copy-done.29), custom_call_target="tpu_custom_call" | custom-call | tf_op jit(solution)/shard_map/product/pallas_call | solution.py:218
  183.4 13.3 %collective-permute-done.6.refs_1_.refs_3_.refs_5_ = bf16[256,3072]{1,0:T(8,128)(2,1)} collective-permute-done((bf16[256,3072]{1,0:T(8,128)(2,1)S(1)}, bf16[256,3072]{1,0:T(8,128)(2,1)}, u32[]{:S(2)}, u32[]{:S(2)}) %collective-permute-start.6) | collective-permute-done | bytes 1572896 | tf_op jit(solution)/shard_map/ppermute | solution.py:144
  196.7 3.5 collective-permute-done.8.refs_6_.refs_5_
  206.8 11.8 %product.18 = bf16[256,1536]{1,0:T(8,128)(2,1)} custom-call(bf16[256,3072]{1,0:T(8,128)(2,1)} %collective-permute-done.1.refs_0_.refs_2_.refs_4_, bf16[256,3072]{1,0:T(8,128)(2,1)} %collective-permute-done.2.refs_1_.refs_3_.refs_5_, bf16[6144,1536]{1,0:T(8,128)(2,1)} %refs_2_.15), custom_call_target="tpu_custom_call" | custom-call | tf_op jit(solution)/shard_map/product/pallas_call | solution.py:218
  218.6 16.1 %collective-permute-done.11.refs_7_.refs_6_ = bf16[6144,128]{1,0:T(8,128)(2,1)S(1)} collective-permute-done((bf16[6144,128]{1,0:T(8,128)(2,1)}, bf16[6144,128]{1,0:T(8,128)(2,1)S(1)}, u32[]{:S(2)}, u32[]{:S(2)}) %collective-permute-start.11) | collective-permute-done | bytes 1572896 | tf_op jit(solution)/shard_map/ppermute | solution.py:148
  237.3 11.9 %product.19 = bf16[256,1536]{1,0:T(8,128)(2,1)} custom-call(bf16[256,3072]{1,0:T(8,128)(2,1)} %collective-permute-done.5.refs_0_.refs_2_.refs_4_, bf16[256,3072]{1,0:T(8,128)(2,1)} %collective-permute-done.6.refs_1_.refs_3_.refs_5_, bf16[6144,1536]{1,0:T(8,128)(2,1)} %refs_2_.15, bf16[256,1536]{1,0:T(8,128)(2,1)} %collective-permute-done.12.refs_3_), custom_call_target="tpu_custom_call" | custom-call | tf_op jit(solution)/shard_map/product/pallas_call | solution.py:218
  249.2 20.9 %collective-permute-done.13.refs_7_.refs_6_ = bf16[6144,128]{1,0:T(8,128)(2,1)S(1)} collective-permute-done((bf16[6144,128]{1,0:T(8,128)(2,1)}, bf16[6144,128]{1,0:T(8,128)(2,1)S(1)}, u32[]{:S(2)}, u32[]{:S(2)}) %collective-permute-start.13) | collective-permute-done | bytes 1572896 | tf_op jit(solution)/shard_map/ppermute | solution.py:144
  278.8 9.0 %product.20 = bf16[512,512]{1,0:T(8,128)(2,1)} custom-call(bf16[256,3072]{1,0:T(8,128)(2,1)} %attention.4.refs_0_.refs_4_.refs_6_, bf16[256,3072]{1,0:T(8,128)(2,1)} %attention.5.refs_1_.refs_5_.refs_7_, bf16[256,3072]{1,0:T(8,128)(2,1)} %collective-permute-done.1.refs_0_.refs_2_.refs_4_, bf16[256,3072]{1,0:T(8,128)(2,1)} %collective-permute-done.2.refs_1_.refs_3_.refs_5_, ...), custom_call_target="tpu_custom_call" | custom-call | tf_op jit(solution)/shard_map/product/pallas_call | solution.py:218
  287.7 19.1 %collective-permute-done.17.refs_8_.refs_7_ = bf16[6144,128]{1,0:T(8,128)(2,1)S(1)} collective-permute-done((bf16[6144,128]{1,0:T(8,128)(2,1)S(1)}, bf16[6144,128]{1,0:T(8,128)(2,1)S(1)}, u32[]{:S(2)}, u32[]{:S(2)}) %collective-permute-start.17) | collective-permute-done | bytes 1572896 | tf_op jit(solution)/shard_map/ppermute | solution.py:148
  309.8 9.2 %product.21 = bf16[512,512]{1,0:T(8,128)(2,1)} custom-call(bf16[256,3072]{1,0:T(8,128)(2,1)} %attention.6.refs_0_.refs_4_.refs_6_, bf16[256,3072]{1,0:T(8,128)(2,1)} %copy-done.5, bf16[256,3072]{1,0:T(8,128)(2,1)} %collective-permute-done.5.refs_0_.refs_2_.refs_4_, bf16[256,3072]{1,0:T(8,128)(2,1)} %collective-permute-done.6.refs_1_.refs_3_.refs_5_, ...), custom_call_target="tpu_custom_call" | custom-call | tf_op jit(solution)/shard_map/product/pallas_call | solution.py:218
  319.0 23.6 %collective-permute-done.19.refs_9_.refs_8_ = bf16[6144,128]{1,0:T(8,128)(2,1)S(1)} collective-permute-done((bf16[6144,128]{1,0:T(8,128)(2,1)}, bf16[6144,128]{1,0:T(8,128)(2,1)S(1)}, u32[]{:S(2)}, u32[]{:S(2)}) %collective-permute-start.19) | collective-permute-done | bytes 1572896 | tf_op jit(solution)/shard_map/ppermute | solution.py:144
  342.6 3.4 collective-permute-done.22
  353.7 15.7 %product.22 = bf16[256,2048]{1,0:T(8,128)(2,1)} custom-call(bf16[256,3072]{1,0:T(8,128)(2,1)} %collective-permute-done.refs_0_.refs_2_, bf16[256,3072]{1,0:T(8,128)(2,1)} %collective-permute-done.9.refs_1_.refs_3_, bf16[6144,1536]{1,0:T(8,128)(2,1)} %refs_2_.15, bf16[6144,128]{1,0:T(8,128)(2,1)} %collective-permute-done.3.refs_4_.refs_3_, ...), custom_call_target="tpu_custom_call" | custom-call | tf_op jit(solution)/shard_map/product/pallas_call | solution.py:218
  369.4 11.2 %collective-permute-done.24.refs_10_.refs_9_ = bf16[6144,128]{1,0:T(8,128)(2,1)} collective-permute-done((bf16[6144,128]{1,0:T(8,128)(2,1)S(1)}, bf16[6144,128]{1,0:T(8,128)(2,1)}, u32[]{:S(2)}, u32[]{:S(2)}) %collective-permute-start.24) | collective-permute-done | bytes 1572896 | tf_op jit(solution)/shard_map/ppermute | solution.py:148
  384.5 15.9 %product.23 = bf16[256,2048]{1,0:T(8,128)(2,1)} custom-call(bf16[256,3072]{1,0:T(8,128)(2,1)} %copy-done.16, bf16[256,3072]{1,0:T(8,128)(2,1)} %collective-permute-done.20.refs_1_.refs_3_, bf16[6144,1536]{1,0:T(8,128)(2,1)} %refs_2_.15, bf16[6144,128]{1,0:T(8,128)(2,1)} %collective-permute-done.3.refs_4_.refs_3_, bf16[6144,128]{1,0:T(8,128)(2,1)} %copy-done.11, ...), custom_call_target="tpu_custom_call" | custom-call | tf_op jit(solution)/shard_map/product/pallas_call | solution.py:218
  400.4 7.6 %collective-permute-done.23.refs_0_ = bf16[256,2048]{1,0:T(8,128)(2,1)S(1)} collective-permute-done((bf16[256,2048]{1,0:T(8,128)(2,1)S(1)}, bf16[256,2048]{1,0:T(8,128)(2,1)S(1)}, u32[]{:S(2)}, u32[]{:S(2)}) %collective-permute-start.23) | collective-permute-done | bytes 1048608 | tf_op jit(solution)/shard_map/ppermute | solution.py:144
  408.0 8.9 %collective-permute-done.28 = bf16[4,192,1024]{2,1,0:T(8,128)(2,1)S(1)} collective-permute-done((bf16[4,192,1024]{2,1,0:T(8,128)(2,1)}, bf16[4,192,1024]{2,1,0:T(8,128)(2,1)S(1)}, u32[]{:S(2)}, u32[]{:S(2)}) %collective-permute-start.28) | collective-permute-done | bytes 1572896 | tf_op jit(solution)/shard_map/ppermute | solution.py:144
  416.9 33.1 %collective-permute-done.26.refs_8_ = bf16[6144,128]{1,0:T(8,128)(2,1)} collective-permute-done((bf16[6144,128]{1,0:T(8,128)(2,1)}, bf16[6144,128]{1,0:T(8,128)(2,1)}, u32[]{:S(2)}, u32[]{:S(2)}) %collective-permute-start.26) | collective-permute-done | bytes 1572896 | tf_op jit(solution)/shard_map/ppermute | solution.py:144
  450.0 4.6 collective-permute-start.30
  455.9 11.6 %product.25 = bf16[768,512]{1,0:T(8,128)(2,1)} custom-call(bf16[256,3072]{1,0:T(8,128)(2,1)} %collective-permute-done.1.refs_0_.refs_2_.refs_4_, bf16[256,3072]{1,0:T(8,128)(2,1)} %collective-permute-done.2.refs_1_.refs_3_.refs_5_, bf16[256,3072]{1,0:T(8,128)(2,1)} %collective-permute-done.refs_0_.refs_2_, ...), custom_call_target="tpu_custom_call" | custom-call | tf_op jit(solution)/shard_map/product/pallas_call | solution.py:218
  467.5 19.9 %product.24 = bf16[256,2560]{1,0:T(8,128)(2,1)} custom-call(bf16[256,3072]{1,0:T(8,128)(2,1)} %copy-done.19, bf16[256,3072]{1,0:T(8,128)(2,1)} %collective-permute-done.16.refs_1_, bf16[6144,1536]{1,0:T(8,128)(2,1)} %refs_2_.15, bf16[6144,128]{1,0:T(8,128)(2,1)} %collective-permute-done.3.refs_4_.refs_3_, bf16[6144,128]{1,0:T(8,128)(2,1)} %copy-done.11, ...), custom_call_target="tpu_custom_call" | custom-call | tf_op jit(solution)/shard_map/product/pallas_call | solution.py:218
  487.4 11.4 %collective-permute-done.29.refs_3_ = bf16[256,2048]{1,0:T(8,128)(2,1)S(1)} collective-permute-done((bf16[256,2048]{1,0:T(8,128)(2,1)}, bf16[256,2048]{1,0:T(8,128)(2,1)S(1)}, u32[]{:S(2)}, u32[]{:S(2)}) %collective-permute-start.29) | collective-permute-done | bytes 1048608 | tf_op jit(solution)/shard_map/ppermute | solution.py:144
  502.6 9.7 %product.28 = bf16[1024,256]{1,0:T(8,128)(2,1)} custom-call(bf16[256,3072]{1,0:T(8,128)(2,1)} %copy-done.19, bf16[256,3072]{1,0:T(8,128)(2,1)} %collective-permute-done.16.refs_1_, bf16[256,3072]{1,0:T(8,128)(2,1)} %collective-permute-done.refs_0_.refs_2_, bf16[256,3072]{1,0:T(8,128)(2,1)} %collective-permute-done.9.refs_1_.refs_3_, ...), custom_call_target="tpu_custom_call" | custom-call | tf_op jit(solution)/shard_map/product/pallas_call | solution.py:218
  514.1 20.0 %product.26 = bf16[256,2560]{1,0:T(8,128)(2,1)} custom-call(bf16[256,3072]{1,0:T(8,128)(2,1)} %collective-permute-done.21.refs_0_, bf16[256,3072]{1,0:T(8,128)(2,1)} %copy-done.17, bf16[6144,1536]{1,0:T(8,128)(2,1)} %refs_2_.15, bf16[6144,128]{1,0:T(8,128)(2,1)} %collective-permute-done.3.refs_4_.refs_3_, bf16[6144,128]{1,0:T(8,128)(2,1)} %copy-done.11, ...), custom_call_target="tpu_custom_call" | custom-call | tf_op jit(solution)/shard_map/product/pallas_call | solution.py:218
  534.9 10.0 %product.29 = bf16[1024,256]{1,0:T(8,128)(2,1)} custom-call(bf16[256,3072]{1,0:T(8,128)(2,1)} %collective-permute-done.21.refs_0_, bf16[256,3072]{1,0:T(8,128)(2,1)} %copy-done.17, bf16[256,3072]{1,0:T(8,128)(2,1)} %copy-done.16, bf16[256,3072]{1,0:T(8,128)(2,1)} %collective-permute-done.20.refs_1_.refs_3_, ...), custom_call_target="tpu_custom_call" | custom-call | tf_op jit(solution)/shard_map/product/pallas_call | solution.py:218
  544.9 9.8 %product.30 = bf16[1024,256]{1,0:T(8,128)(2,1)} custom-call(bf16[256,3072]{1,0:T(8,128)(2,1)} %copy-done.19, bf16[256,3072]{1,0:T(8,128)(2,1)} %collective-permute-done.16.refs_1_, bf16[256,3072]{1,0:T(8,128)(2,1)} %collective-permute-done.refs_0_.refs_2_, bf16[256,3072]{1,0:T(8,128)(2,1)} %collective-permute-done.9.refs_1_.refs_3_, ...), custom_call_target="tpu_custom_call" | custom-call | tf_op jit(solution)/shard_map/product/pallas_call | solution.py:218
  555.9 12.0 %product.27 = bf16[768,512]{1,0:T(8,128)(2,1)} custom-call(bf16[256,3072]{1,0:T(8,128)(2,1)} %collective-permute-done.5.refs_0_.refs_2_.refs_4_, bf16[256,3072]{1,0:T(8,128)(2,1)} %collective-permute-done.6.refs_1_.refs_3_.refs_5_, bf16[256,3072]{1,0:T(8,128)(2,1)} %copy-done.16, bf16[256,3072]{1,0:T(8,128)(2,1)} %collective-permute-done.20.refs_1_.refs_3_, ...), custom_call_target="tpu_custom_call" | custom-call | tf_op jit(solution)/shard_map/product/pallas_call | solution.py:218
  571.2 2.7 collective-permute-start.38
  573.9 10.0 %product.31 = bf16[1024,256]{1,0:T(8,128)(2,1)} custom-call(bf16[256,3072]{1,0:T(8,128)(2,1)} %collective-permute-done.21.refs_0_, bf16[256,3072]{1,0:T(8,128)(2,1)} %copy-done.17, bf16[256,3072]{1,0:T(8,128)(2,1)} %copy-done.16, bf16[256,3072]{1,0:T(8,128)(2,1)} %collective-permute-done.20.refs_1_.refs_3_, ...), custom_call_target="tpu_custom_call" | custom-call | tf_op jit(solution)/shard_map/product/pallas_call | solution.py:218
  590.9 4.2 cache.1
  597.2 3.8 place.1
  (213 shorter events, 81.7 us)
Async XLA Ops:
  0.6 455.0 %copy-start = (s32[32,16]{0,1:T(8,128)S(1)}, s32[32,16]{0,1:T(8,128)}, u32[]{:S(2)}) copy-start(s32[32,16]{0,1:T(8,128)} %param.14) | copy-start | bytes 6148
  5.4 53.3 %collective-permute-start.4 = (bf16[528,1024]{1,0:T(8,128)(2,1)S(1)}, bf16[528,1024]{1,0:T(8,128)(2,1)}, u32[]{:S(2)}, u32[]{:S(2)}) collective-permute-start(bf16[528,1024]{1,0:T(8,128)(2,1)S(1)} %fusion.1), channel_id=1, source_target_pairs={{0,8},{2,10},{4,12},{6,14},{8,0},{10,2},{12,4},{14,6},{1,9},{3,11}... | collective-permute-start | bytes 3244040 | tf_op jit(solution)/shard_map/ppermute | solution.py:144
  18.9 69.9 %collective-permute-start.1 = (bf16[256,3072]{1,0:T(8,128)(2,1)}, bf16[256,3072]{1,0:T(8,128)(2,1)}, u32[]{:S(2)}, u32[]{:S(2)}) collective-permute-start(bf16[256,3072]{1,0:T(8,128)(2,1)} %attention.4.refs_0_.refs_4_.refs_6_), channel_id=1, source_target_pairs={{0,2},{2,0},{4,6},{6,4},{8,10},{10,8},{12,14},{14,12},{1,3},{3,1},... | collective-permute-start | bytes 4718600 | tf_op jit(solution)/shard_map/ppermute | solution.py:144
  20.4 69.6 %collective-permute-start = (bf16[256,3072]{1,0:T(8,128)(2,1)}, bf16[256,3072]{1,0:T(8,128)(2,1)}, u32[]{:S(2)}, u32[]{:S(2)}) collective-permute-start(bf16[256,3072]{1,0:T(8,128)(2,1)} %attention.4.refs_0_.refs_4_.refs_6_), channel_id=1, source_target_pairs={{0,4},{2,6},{4,0},{6,2},{8,12},{10,14},{12,8},{14,10},{1,5},{3,7},... | collective-permute-start | bytes 4718600 | tf_op jit(solution)/shard_map/ppermute | solution.py:144
  22.0 102.1 %collective-permute-start.3 = (bf16[6144,128]{1,0:T(8,128)(2,1)}, bf16[6144,128]{1,0:T(8,128)(2,1)}, u32[]{:S(2)}, u32[]{:S(2)}) collective-permute-start(bf16[6144,128]{1,0:T(8,128)(2,1)} %constant_dynamic-slice_fusion.7), channel_id=1, source_target_pairs={{0,8},{2,10},{4,12},{6,14},{8,0},{10,2},{12,4},{14,6},{1,9},{3,11}... | collective-permute-start | bytes 4718600 | tf_op jit(solution)/shard_map/ppermute | solution.py:144
  28.7 60.1 %collective-permute-start.2 = (bf16[256,3072]{1,0:T(8,128)(2,1)}, bf16[256,3072]{1,0:T(8,128)(2,1)}, u32[]{:S(2)}, u32[]{:S(2)}) collective-permute-start(bf16[256,3072]{1,0:T(8,128)(2,1)} %attention.5.refs_1_.refs_5_.refs_7_), channel_id=1, source_target_pairs={{0,2},{2,0},{4,6},{6,4},{8,10},{10,8},{12,14},{14,12},{1,3},{3,1},... | collective-permute-start | bytes 4718600 | tf_op jit(solution)/shard_map/ppermute | solution.py:144
  127.1 56.3 %collective-permute-start.5 = (bf16[256,3072]{1,0:T(8,128)(2,1)}, bf16[256,3072]{1,0:T(8,128)(2,1)}, u32[]{:S(2)}, u32[]{:S(2)}) collective-permute-start(bf16[256,3072]{1,0:T(8,128)(2,1)} %attention.6.refs_0_.refs_4_.refs_6_), channel_id=1, source_target_pairs={{0,2},{2,0},{4,6},{6,4},{8,10},{10,8},{12,14},{14,12},{1,3},{3,1},... | collective-permute-start | bytes 4718600 | tf_op jit(solution)/shard_map/ppermute | solution.py:144
  128.6 68.1 %collective-permute-start.6 = (bf16[256,3072]{1,0:T(8,128)(2,1)S(1)}, bf16[256,3072]{1,0:T(8,128)(2,1)}, u32[]{:S(2)}, u32[]{:S(2)}) collective-permute-start(bf16[256,3072]{1,0:T(8,128)(2,1)S(1)} %copy-done.6), channel_id=1, source_target_pairs={{0,2},{2,0},{4,6},{6,4},{8,10},{10,8},{12,14},{14,12},{1,3},{3,1},... | collective-permute-start | bytes 4718600 | tf_op jit(solution)/shard_map/ppermute | solution.py:144
  129.1 35.2 %collective-permute-start.7 = (bf16[6144,128]{1,0:T(8,128)(2,1)}, bf16[6144,128]{1,0:T(8,128)(2,1)S(1)}, u32[]{:S(2)}, u32[]{:S(2)}) collective-permute-start(bf16[6144,128]{1,0:T(8,128)(2,1)} %collective-permute-done.3.refs_4_.refs_3_), channel_id=1, source_target_pairs={{0,16},{16,0},{1,17},{17,1},{2,18},{18,2},{3,19},{19,3},{4,20},{20... | collective-permute-start | bytes 4718600 | tf_op jit(solution)/shard_map/ppermute | solution.py:148
  130.7 69.5 %collective-permute-start.8 = (bf16[6144,128]{1,0:T(8,128)(2,1)}, bf16[6144,128]{1,0:T(8,128)(2,1)}, u32[]{:S(2)}, u32[]{:S(2)}) collective-permute-start(bf16[6144,128]{1,0:T(8,128)(2,1)} %constant_dynamic-slice_fusion.5), channel_id=1, source_target_pairs={{0,8},{2,10},{4,12},{6,14},{8,0},{10,2},{12,4},{14,6},{1,9},{3,11}... | collective-permute-start | bytes 4718600 | tf_op jit(solution)/shard_map/ppermute | solution.py:144
  130.7 69.5 %collective-permute-start.9 = (bf16[256,3072]{1,0:T(8,128)(2,1)}, bf16[256,3072]{1,0:T(8,128)(2,1)}, u32[]{:S(2)}, u32[]{:S(2)}) collective-permute-start(bf16[256,3072]{1,0:T(8,128)(2,1)} %attention.5.refs_1_.refs_5_.refs_7_), channel_id=1, source_target_pairs={{0,4},{2,6},{4,0},{6,2},{8,12},{10,14},{12,8},{14,10},{1,5},{3,7},... | collective-permute-start | bytes 4718600 | tf_op jit(solution)/shard_map/ppermute | solution.py:144
  164.4 6.2 %collective-permute-start.10 = (bf16[256,1536]{1,0:T(8,128)(2,1)S(1)}, bf16[256,1536]{1,0:T(8,128)(2,1)S(1)}, u32[]{:S(2)}, u32[]{:S(2)}) collective-permute-start(bf16[256,1536]{1,0:T(8,128)(2,1)S(1)} %copy-done.28), channel_id=1, source_target_pairs={{0,1},{1,0},{2,3},{3,2},{4,5},{5,4},{6,7},{7,6},{8,9},{9,8},{10,11... | collective-permute-start | bytes 2359304 | tf_op jit(solution)/shard_map/ppermute | solution.py:148
  200.2 34.5 %collective-permute-start.11 = (bf16[6144,128]{1,0:T(8,128)(2,1)}, bf16[6144,128]{1,0:T(8,128)(2,1)S(1)}, u32[]{:S(2)}, u32[]{:S(2)}) collective-permute-start(bf16[6144,128]{1,0:T(8,128)(2,1)} %collective-permute-done.8.refs_6_.refs_5_), channel_id=1, source_target_pairs={{0,16},{16,0},{1,17},{17,1},{2,18},{18,2},{3,19},{19,3},{4,20},{20... | collective-permute-start | bytes 4718600 | tf_op jit(solution)/shard_map/ppermute | solution.py:148
  201.0 69.1 %collective-permute-start.13 = (bf16[6144,128]{1,0:T(8,128)(2,1)}, bf16[6144,128]{1,0:T(8,128)(2,1)S(1)}, u32[]{:S(2)}, u32[]{:S(2)}) collective-permute-start(bf16[6144,128]{1,0:T(8,128)(2,1)} %constant_dynamic-slice_fusion.4), channel_id=1, source_target_pairs={{0,8},{2,10},{4,12},{6,14},{8,0},{10,2},{12,4},{14,6},{1,9},{3,11}... | collective-permute-start | bytes 4718600 | tf_op jit(solution)/shard_map/ppermute | solution.py:144
  203.1 67.4 %collective-permute-start.14 = (bf16[256,3072]{1,0:T(8,128)(2,1)}, bf16[256,3072]{1,0:T(8,128)(2,1)S(1)}, u32[]{:S(2)}, u32[]{:S(2)}) collective-permute-start(bf16[256,3072]{1,0:T(8,128)(2,1)} %attention.6.refs_0_.refs_4_.refs_6_), channel_id=1, source_target_pairs={{0,4},{2,6},{4,0},{6,2},{8,12},{10,14},{12,8},{14,10},{1,5},{3,7},... | collective-permute-start | bytes 4718600 | tf_op jit(solution)/shard_map/ppermute | solution.py:144
  204.8 65.7 %collective-permute-start.15 = (bf16[256,3072]{1,0:T(8,128)(2,1)}, bf16[256,3072]{1,0:T(8,128)(2,1)S(1)}, u32[]{:S(2)}, u32[]{:S(2)}) collective-permute-start(bf16[256,3072]{1,0:T(8,128)(2,1)} %collective-permute-done.refs_0_.refs_2_), channel_id=1, source_target_pairs={{0,2},{2,0},{4,6},{6,4},{8,10},{10,8},{12,14},{14,12},{1,3},{3,1},... | collective-permute-start | bytes 4718600 | tf_op jit(solution)/shard_map/ppermute | solution.py:144
  206.3 66.3 %collective-permute-start.16 = (bf16[256,3072]{1,0:T(8,128)(2,1)}, bf16[256,3072]{1,0:T(8,128)(2,1)}, u32[]{:S(2)}, u32[]{:S(2)}) collective-permute-start(bf16[256,3072]{1,0:T(8,128)(2,1)} %collective-permute-done.9.refs_1_.refs_3_), channel_id=1, source_target_pairs={{0,2},{2,0},{4,6},{6,4},{8,10},{10,8},{12,14},{14,12},{1,3},{3,1},... | collective-permute-start | bytes 4718600 | tf_op jit(solution)/shard_map/ppermute | solution.py:144
  234.7 2.6 collective-permute-start.12
  272.6 34.3 %collective-permute-start.17 = (bf16[6144,128]{1,0:T(8,128)(2,1)S(1)}, bf16[6144,128]{1,0:T(8,128)(2,1)S(1)}, u32[]{:S(2)}, u32[]{:S(2)}) collective-permute-start(bf16[6144,128]{1,0:T(8,128)(2,1)S(1)} %collective-permute-done.13.refs_7_.refs_6_), channel_id=1, source_target_pairs={{0,16},{16,0},{1,17},{17,1},{2,18},{18,2},{3,19},{19,3},{4,20},{20... | collective-permute-start | bytes 4718600 | tf_op jit(solution)/shard_map/ppermute | solution.py:148
  274.1 68.5 %collective-permute-start.19 = (bf16[6144,128]{1,0:T(8,128)(2,1)}, bf16[6144,128]{1,0:T(8,128)(2,1)S(1)}, u32[]{:S(2)}, u32[]{:S(2)}) collective-permute-start(bf16[6144,128]{1,0:T(8,128)(2,1)} %constant_dynamic-slice_fusion.3), channel_id=1, source_target_pairs={{0,8},{2,10},{4,12},{6,14},{8,0},{10,2},{12,4},{14,6},{1,9},{3,11}... | collective-permute-start | bytes 4718600 | tf_op jit(solution)/shard_map/ppermute | solution.py:144
  274.4 68.2 %collective-permute-start.20 = (bf16[256,3072]{1,0:T(8,128)(2,1)S(1)}, bf16[256,3072]{1,0:T(8,128)(2,1)}, u32[]{:S(2)}, u32[]{:S(2)}) collective-permute-start(bf16[256,3072]{1,0:T(8,128)(2,1)S(1)} %copy-done.7), channel_id=1, source_target_pairs={{0,4},{2,6},{4,0},{6,2},{8,12},{10,14},{12,8},{14,10},{1,5},{3,7},... | collective-permute-start | bytes 4718600 | tf_op jit(solution)/shard_map/ppermute | solution.py:144
  276.7 65.8 %collective-permute-start.21 = (bf16[256,3072]{1,0:T(8,128)(2,1)S(1)}, bf16[256,3072]{1,0:T(8,128)(2,1)}, u32[]{:S(2)}, u32[]{:S(2)}) collective-permute-start(bf16[256,3072]{1,0:T(8,128)(2,1)S(1)} %collective-permute-done.14.refs_0_.refs_2_), channel_id=1, source_target_pairs={{0,2},{2,0},{4,6},{6,4},{8,10},{10,8},{12,14},{14,12},{1,3},{3,1},... | collective-permute-start | bytes 4718600 | tf_op jit(solution)/shard_map/ppermute | solution.py:144
  278.2 67.8 %collective-permute-start.22 = (bf16[2,2,192,1024]{3,2,1,0:T(8,128)(2,1)}, bf16[2,2,192,1024]{3,2,1,0:T(8,128)(2,1)}, u32[]{:S(2)}, u32[]{:S(2)}) collective-permute-start(bf16[2,2,192,1024]{3,2,1,0:T(8,128)(2,1)} %pad_maximum_fusion.2), channel_id=1, source_target_pairs={{0,2},{2,0},{4,6},{6,4},{8,10},{10,8},{12,14},{14,12},{1,3},{3,1},... | collective-permute-start | bytes 4718600 | tf_op jit(solution)/shard_map/ppermute | solution.py:144
  306.9 2.1 collective-permute-start.18
  346.0 34.6 %collective-permute-start.24 = (bf16[6144,128]{1,0:T(8,128)(2,1)S(1)}, bf16[6144,128]{1,0:T(8,128)(2,1)}, u32[]{:S(2)}, u32[]{:S(2)}) collective-permute-start(bf16[6144,128]{1,0:T(8,128)(2,1)S(1)} %collective-permute-done.19.refs_9_.refs_8_), channel_id=1, source_target_pairs={{0,16},{16,0},{1,17},{17,1},{2,18},{18,2},{3,19},{19,3},{4,20},{20... | collective-permute-start | bytes 4718600 | tf_op jit(solution)/shard_map/ppermute | solution.py:148
  350.7 66.2 %collective-permute-start.28 = (bf16[4,192,1024]{2,1,0:T(8,128)(2,1)}, bf16[4,192,1024]{2,1,0:T(8,128)(2,1)S(1)}, u32[]{:S(2)}, u32[]{:S(2)}) collective-permute-start(bf16[4,192,1024]{2,1,0:T(8,128)(2,1)} %get-tuple-element.145), channel_id=1, source_target_pairs={{0,4},{2,6},{4,0},{6,2},{8,12},{10,14},{12,8},{14,10},{1,5},{3,7},... | collective-permute-start | bytes 4718600 | tf_op jit(solution)/shard_map/ppermute | solution.py:144
  351.0 99.0 %collective-permute-start.26 = (bf16[6144,128]{1,0:T(8,128)(2,1)}, bf16[6144,128]{1,0:T(8,128)(2,1)}, u32[]{:S(2)}, u32[]{:S(2)}) collective-permute-start(bf16[6144,128]{1,0:T(8,128)(2,1)} %constant_dynamic-slice_fusion.2), channel_id=1, source_target_pairs={{0,8},{2,10},{4,12},{6,14},{8,0},{10,2},{12,4},{14,6},{1,9},{3,11}... | collective-permute-start | bytes 4718600 | tf_op jit(solution)/shard_map/ppermute | solution.py:144
  351.4 98.6 %collective-permute-start.27 = (bf16[256,3072]{1,0:T(8,128)(2,1)}, bf16[256,3072]{1,0:T(8,128)(2,1)S(1)}, u32[]{:S(2)}, u32[]{:S(2)}) collective-permute-start(bf16[256,3072]{1,0:T(8,128)(2,1)} %collective-permute-done.20.refs_1_.refs_3_), channel_id=1, source_target_pairs={{0,2},{2,0},{4,6},{6,4},{8,10},{10,8},{12,14},{14,12},{1,3},{3,1},... | collective-permute-start | bytes 4718600 | tf_op jit(solution)/shard_map/ppermute | solution.py:144
  369.4 86.4 %copy-start.33 = (s32[32]{0:T(128)S(1)}, s32[32]{0:T(128)}, u32[]{:S(2)}) copy-start(s32[32]{0:T(128)} %param.13) | copy-start | bytes 388
  380.7 2.9 collective-permute-start.25
  380.7 27.3 %collective-permute-start.23 = (bf16[256,2048]{1,0:T(8,128)(2,1)S(1)}, bf16[256,2048]{1,0:T(8,128)(2,1)S(1)}, u32[]{:S(2)}, u32[]{:S(2)}) collective-permute-start(bf16[256,2048]{1,0:T(8,128)(2,1)S(1)} %pad_maximum_fusion.4), channel_id=1, source_target_pairs={{0,2},{2,0},{4,6},{6,4},{8,10},{10,8},{12,14},{14,12},{1,3},{3,1},... | collective-permute-start | bytes 3145736 | tf_op jit(solution)/shard_map/ppermute | solution.py:144
  450.0 48.8 %collective-permute-start.30 = (bf16[6144,128]{1,0:T(8,128)(2,1)}, bf16[6144,128]{1,0:T(8,128)(2,1)}, u32[]{:S(2)}, u32[]{:S(2)}) collective-permute-start(bf16[6144,128]{1,0:T(8,128)(2,1)} %collective-permute-done.26.refs_8_), channel_id=1, source_target_pairs={{0,16},{16,0},{1,17},{17,1},{2,18},{18,2},{3,19},{19,3},{4,20},{20... | collective-permute-start | bytes 4718600 | tf_op jit(solution)/shard_map/ppermute | solution.py:148
  454.6 44.2 %collective-permute-start.31 = (bf16[6144,128]{1,0:T(8,128)(2,1)}, bf16[6144,128]{1,0:T(8,128)(2,1)}, u32[]{:S(2)}, u32[]{:S(2)}) collective-permute-start(bf16[6144,128]{1,0:T(8,128)(2,1)} %constant_dynamic-slice_fusion.1), channel_id=1, source_target_pairs={{0,8},{2,10},{4,12},{6,14},{8,0},{10,2},{12,4},{14,6},{1,9},{3,11}... | collective-permute-start | bytes 4718600 | tf_op jit(solution)/shard_map/ppermute | solution.py:144
  454.6 44.2 %collective-permute-start.29 = (bf16[256,2048]{1,0:T(8,128)(2,1)}, bf16[256,2048]{1,0:T(8,128)(2,1)S(1)}, u32[]{:S(2)}, u32[]{:S(2)}) collective-permute-start(bf16[256,2048]{1,0:T(8,128)(2,1)} %product.23), channel_id=1, source_target_pairs={{0,4},{2,6},{4,0},{6,2},{8,12},{10,14},{12,8},{14,10},{1,5},{3,7},... | collective-permute-start | bytes 3145736 | tf_op jit(solution)/shard_map/ppermute | solution.py:144
  498.8 14.2 %collective-permute-start.32 = (bf16[256,2560]{1,0:T(8,128)(2,1)}, bf16[256,2560]{1,0:T(8,128)(2,1)S(1)}, u32[]{:S(2)}, u32[]{:S(2)}) collective-permute-start(bf16[256,2560]{1,0:T(8,128)(2,1)} %product.24), channel_id=1, source_target_pairs={{0,1},{1,0},{2,3},{3,2},{4,5},{5,4},{6,7},{7,6},{8,9},{9,8},{10,11... | collective-permute-start | bytes 3932168 | tf_op jit(solution)/shard_map/ppermute | solution.py:148
  498.8 46.1 %collective-permute-start.41 = (bf16[6144,128]{1,0:T(8,128)(2,1)}, bf16[6144,128]{1,0:T(8,128)(2,1)}, u32[]{:S(2)}, u32[]{:S(2)}) collective-permute-start(bf16[6144,128]{1,0:T(8,128)(2,1)} %collective-permute-done.31.refs_8_), channel_id=1, source_target_pairs={{0,16},{16,0},{1,17},{17,1},{2,18},{18,2},{3,19},{19,3},{4,20},{20... | collective-permute-start | bytes 4718600 | tf_op jit(solution)/shard_map/ppermute | solution.py:148
  512.4 22.6 %collective-permute-start.37 = (bf16[1024,256]{1,0:T(8,128)(2,1)}, bf16[1024,256]{1,0:T(8,128)(2,1)}, u32[]{:S(2)}, u32[]{:S(2)}) collective-permute-start(bf16[1024,256]{1,0:T(8,128)(2,1)} %product.28), channel_id=1, source_target_pairs={{0,1},{1,0},{2,3},{3,2},{4,5},{5,4},{6,7},{7,6},{8,9},{9,8},{10,11... | collective-permute-start | bytes 1572872 | tf_op jit(solution)/shard_map/ppermute | solution.py:148
  512.5 43.4 %collective-permute-start.34 = (bf16[768,512]{1,0:T(8,128)(2,1)}, bf16[768,512]{1,0:T(8,128)(2,1)}, u32[]{:S(2)}, u32[]{:S(2)}) collective-permute-start(bf16[768,512]{1,0:T(8,128)(2,1)} %product.25), channel_id=1, source_target_pairs={{0,1},{1,0},{2,3},{3,2},{4,5},{5,4},{6,7},{7,6},{8,9},{9,8},{10,11... | collective-permute-start | bytes 2359304 | tf_op jit(solution)/shard_map/ppermute | solution.py:148
  534.1 63.1 %collective-permute-start.33 = (bf16[256,2560]{1,0:T(8,128)(2,1)}, bf16[256,2560]{1,0:T(8,128)(2,1)S(1)}, u32[]{:S(2)}, u32[]{:S(2)}) collective-permute-start(bf16[256,2560]{1,0:T(8,128)(2,1)} %product.26), channel_id=1, source_target_pairs={{0,6},{2,4},{4,2},{6,0},{8,14},{10,12},{12,10},{14,8},{1,7},{3,5},... | collective-permute-start | bytes 3932168 | tf_op jit(solution)/shard_map/ppermute | solution.py:144
  554.7 16.5 %collective-permute-start.42 = (bf16[1024,256]{1,0:T(8,128)(2,1)}, bf16[1024,256]{1,0:T(8,128)(2,1)S(1)}, u32[]{:S(2)}, u32[]{:S(2)}) collective-permute-start(bf16[1024,256]{1,0:T(8,128)(2,1)} %product.30), channel_id=1, source_target_pairs={{0,1},{1,0},{2,3},{3,2},{4,5},{5,4},{6,7},{7,6},{8,9},{9,8},{10,11... | collective-permute-start | bytes 1572872 | tf_op jit(solution)/shard_map/ppermute | solution.py:148
  554.8 29.2 %collective-permute-start.40 = (bf16[256,256]{1,0:T(8,128)(2,1)S(1)}, bf16[256,256]{1,0:T(8,128)(2,1)S(1)}, u32[]{:S(2)}, u32[]{:S(2)}) collective-permute-start(bf16[256,256]{1,0:T(8,128)(2,1)S(1)} %get-tuple-element.156), channel_id=1, source_target_pairs={{0,2},{2,0},{4,6},{6,4},{8,10},{10,8},{12,14},{14,12},{1,3},{3,1},... | collective-permute-start | bytes 393224 | tf_op jit(solution)/shard_map/ppermute | solution.py:144
  569.1 18.2 %collective-permute-start.35 = (bf16[256,512]{1,0:T(8,128)(2,1)S(1)}, bf16[256,512]{1,0:T(8,128)(2,1)S(1)}, u32[]{:S(2)}, u32[]{:S(2)}) collective-permute-start(bf16[256,512]{1,0:T(8,128)(2,1)S(1)} %get-tuple-element.115), channel_id=1, source_target_pairs={{0,4},{2,6},{4,0},{6,2},{8,12},{10,14},{12,8},{14,10},{1,5},{3,7},... | collective-permute-start | bytes 786440 | tf_op jit(solution)/shard_map/ppermute | solution.py:144
  571.0 14.7 %collective-permute-start.39 = (bf16[256,256]{1,0:T(8,128)(2,1)S(1)}, bf16[256,256]{1,0:T(8,128)(2,1)S(1)}, u32[]{:S(2)}, u32[]{:S(2)}) collective-permute-start(bf16[256,256]{1,0:T(8,128)(2,1)S(1)} %get-tuple-element.157), channel_id=1, source_target_pairs={{0,4},{2,6},{4,0},{6,2},{8,12},{10,14},{12,8},{14,10},{1,5},{3,7},... | collective-permute-start | bytes 393224 | tf_op jit(solution)/shard_map/ppermute | solution.py:144
  571.2 16.0 %collective-permute-start.38 = (bf16[256,256]{1,0:T(8,128)(2,1)S(1)}, bf16[256,256]{1,0:T(8,128)(2,1)S(1)}, u32[]{:S(2)}, u32[]{:S(2)}) collective-permute-start(bf16[256,256]{1,0:T(8,128)(2,1)S(1)} %get-tuple-element.158), channel_id=1, source_target_pairs={{0,6},{2,4},{4,2},{6,0},{8,14},{10,12},{12,10},{14,8},{1,7},{3,5},... | collective-permute-start | bytes 393224 | tf_op jit(solution)/shard_map/ppermute | solution.py:144
  584.0 11.8 %collective-permute-start.36 = (bf16[256,512]{1,0:T(8,128)(2,1)S(1)}, bf16[256,512]{1,0:T(8,128)(2,1)S(1)}, u32[]{:S(2)}, u32[]{:S(2)}) collective-permute-start(bf16[256,512]{1,0:T(8,128)(2,1)S(1)} %get-tuple-element.116), channel_id=1, source_target_pairs={{0,2},{2,0},{4,6},{6,4},{8,10},{10,8},{12,14},{14,12},{1,3},{3,1},... | collective-permute-start | bytes 786440 | tf_op jit(solution)/shard_map/ppermute | solution.py:144
  585.6 11.5 %collective-permute-start.45 = (bf16[256,256]{1,0:T(8,128)(2,1)S(1)}, bf16[256,256]{1,0:T(8,128)(2,1)S(1)}, u32[]{:S(2)}, u32[]{:S(2)}) collective-permute-start(bf16[256,256]{1,0:T(8,128)(2,1)S(1)} %get-tuple-element.152), channel_id=1, source_target_pairs={{0,2},{2,0},{4,6},{6,4},{8,10},{10,8},{12,14},{14,12},{1,3},{3,1},... | collective-permute-start | bytes 393224 | tf_op jit(solution)/shard_map/ppermute | solution.py:144
  587.2 10.0 %collective-permute-start.44 = (bf16[256,256]{1,0:T(8,128)(2,1)S(1)}, bf16[256,256]{1,0:T(8,128)(2,1)S(1)}, u32[]{:S(2)}, u32[]{:S(2)}) collective-permute-start(bf16[256,256]{1,0:T(8,128)(2,1)S(1)} %get-tuple-element.153), channel_id=1, source_target_pairs={{0,4},{2,6},{4,0},{6,2},{8,12},{10,14},{12,8},{14,10},{1,5},{3,7},... | collective-permute-start | bytes 393224 | tf_op jit(solution)/shard_map/ppermute | solution.py:144
  587.3 9.9 %collective-permute-start.43 = (bf16[256,256]{1,0:T(8,128)(2,1)S(1)}, bf16[256,256]{1,0:T(8,128)(2,1)S(1)}, u32[]{:S(2)}, u32[]{:S(2)}) collective-permute-start(bf16[256,256]{1,0:T(8,128)(2,1)S(1)} %get-tuple-element.154), channel_id=1, source_target_pairs={{0,6},{2,4},{4,2},{6,0},{8,14},{10,12},{12,10},{14,8},{1,7},{3,5},... | collective-permute-start | bytes 393224 | tf_op jit(solution)/shard_map/ppermute | solution.py:144
  (32 other events, 425.7 us)

commit v3 on v2

--- a/solution.py
+++ b/solution.py
@@ -185,19 +185,20 @@
 
 def product(lefts, rights, other=None):
     rows, depth = lefts[0][0].shape
-    block = 2 * WIDTH
+    block = 4 * WIDTH
+    once = pl.Buffered(1)
     operands, specs, groups = [], [], []
     for left in lefts:
         for part in left:
             operands.append(part)
-            specs.append(pl.BlockSpec((rows, depth), lambda n: (0, 0)))
+            specs.append(pl.BlockSpec((rows, depth), lambda n: (0, 0), pipeline_mode=once))
     first = 0
     for right in rights:
         if isinstance(right, tuple):
             steps = 1
             for piece in right:
                 operands.append(piece)
-                specs.append(pl.BlockSpec(piece.shape, lambda n: (0, 0)))
+                specs.append(pl.BlockSpec(piece.shape, lambda n: (0, 0), pipeline_mode=once))
             groups.append((1, len(right)))
         else:
             steps = right.shape[1] // block
@@ -230,6 +231,81 @@
     )(*operands)
 
 
+def tall_kernel(*refs, heights, pieces, steps, summed):
+    lefts, rights = refs[: heights * len(steps)], refs[heights * len(steps) :]
+    out, total = refs[-2:]
+    step = pl.program_id(0)
+    rows = lefts[0].shape[0]
+
+    @pl.when(step == 0)
+    def _():
+        total[...] = jnp.zeros_like(total)
+
+    def add(part):
+        group = rights[part * 2 : part * 2 + 2] if pieces > 1 else rights[:2]
+        right = jnp.concatenate([ref[...] for ref in group], axis=1)
+        for height in range(heights):
+            at = slice(height * rows, (height + 1) * rows)
+            total[at, :] += jnp.dot(
+                lefts[height * len(steps) + part][...], right, preferred_element_type=jnp.float32
+            )
+
+    first = 0
+    for part, count in enumerate(steps):
+        pl.when((step >= first) & (step < first + count))(functools.partial(add, part))
+        first += count
+
+    @pl.when(step == first - 1)
+    def _():
+        result = total[...]
+        if summed:
+            result = result + refs[-3][...].astype(jnp.float32)
+        out[...] = result.astype(out.dtype)
+
+
+def tall_product(lefts, rights, other=None):
+    rows, depth = lefts[0][0].shape
+    parts = len(lefts[0])
+    block = depth // 4 if depth % 512 == 0 else depth
+    count = depth // block
+    steps = (count,) * parts
+
+    def within(part):
+        return lambda k: jnp.clip(k - part * count, 0, count - 1)
+
+    operands, specs = [], []
+    for left in lefts:
+        for part, array in enumerate(left):
+            operands.append(array)
+            specs.append(
+                pl.BlockSpec((rows, block), lambda k, at=within(part): (0, at(k)))
+            )
+    for part, group in enumerate(rights):
+        for array in group:
+            operands.append(array)
+            at = within(part) if len(rights) > 1 else (lambda k: k)
+            specs.append(pl.BlockSpec((block, WIDTH), lambda k, at=at: (at(k), 0)))
+    shape = (rows * len(lefts), 2 * WIDTH)
+    whole = pl.BlockSpec(shape, lambda k: (0, 0))
+    if other is not None:
+        operands.append(other)
+        specs.append(whole)
+    return pl.pallas_call(
+        functools.partial(
+            tall_kernel, heights=len(lefts), pieces=len(rights), steps=steps,
+            summed=other is not None,
+        ),
+        grid=(count * parts,),
+        in_specs=specs,
+        out_specs=whole,
+        out_shape=jax.ShapeDtypeStruct(shape, operands[0].dtype),
+        scratch_shapes=[pltpu.VMEM(shape, jnp.float32)],
+        compiler_params=pltpu.CompilerParams(vmem_limit_bytes=56 << 20),
+        cost_estimate=LIGHT,
+        name="product",
+    )(*operands)
+
+
 def after(array, *earlier):
     return lax.optimization_barrier((array,) + earlier)[0]
 
@@ -340,17 +416,17 @@
     kv_parts = 2 if local_heads % (2 * (NH // KVH)) == 0 else 1
     blocks = {mask: [] for mask in MASKS}
 
-    def begin_sum(masks, rights):
+    def begin_sum(masks, rights, multiply=product):
         lefts = [list(blocks[mask]) for mask in masks]
         lefts[0][0] = gated(lefts[0][0])
-        return masks, rights, product([left[:kv_parts] for left in lefts], rights)
+        return masks, rights, multiply([left[:kv_parts] for left in lefts], rights), multiply
 
     def end_sum(begun, *earlier):
-        masks, rights, given = begun
+        masks, rights, given, multiply = begun
         given = after(given, *earlier) if earlier else given
         if tp_count == 2:
             lefts = [blocks[mask][kv_parts:] for mask in masks]
-            total = product(lefts, rights, swap(given, "tp"))
+            total = multiply(lefts, rights, swap(given, "tp"))
         else:
             total = given
         rows = total.shape[0] // len(masks)
@@ -362,8 +438,8 @@
                 )
         return total, shares
 
-    def group_sum(masks, rights, *earlier):
-        return end_sum(begin_sum(masks, rights), *earlier)
+    def group_sum(masks, rights, *earlier, multiply=product):
+        return end_sum(begin_sum(masks, rights, multiply), *earlier)
 
     sliced, along, across = [cut(0)], [], []
     along.append(hop(sliced[0], FAR))
@@ -426,12 +502,12 @@
     own_shares.update(shares)
     gate = moved + (ready,)
 
-    def pair(n):
-        return (along[n], across[n])
+    def two_pairs(n):
+        return (along[n], across[n], along[n + 1], across[n + 1])
 
     moved = weights() + spread(NEXT, own[3:], NEXT) + spread(NEXT | SIDE, near[2:3], SIDE)
     pages_side = hop(gated(pages_given), SIDE)
-    ready, shares = group_sum((0, SIDE), [pair(0), pair(1)], moved[0])
+    ready, shares = group_sum((0, SIDE), [two_pairs(0)], moved[0])
     gate = moved + (pages_side, ready)
 
     first_columns = own_columns + pair_columns(0, 2)
@@ -446,14 +522,18 @@
         lax.dynamic_index_in_dim(pages, 1 - next_here, axis=1, keepdims=False), NEXT
     )
     pages = lax.dynamic_index_in_dim(pages, next_here, axis=1, keepdims=False)
-    ready, shares = group_sum((NEXT,), [out_weight, pair(0), pair(1)], moved[0])
+    ready, shares = group_sum((NEXT,), [out_weight, two_pairs(0)], moved[0])
     gate = moved + (pages_next, ready)
 
-    moved = weights() + (hand_out(NEXT, gated(shares[NEXT]), first_columns),)
-    begun = begin_sum((NEXT | SIDE,), [out_weight, pair(0), pair(1), pair(2), pair(3)])
-    begun_near = begin_sum((SIDE, NEXT, 0), [pair(2), pair(3)])
-    far_shares = end_sum(begun, begun_near[2], *moved)[1]
-    shares = end_sum(begun_near, *moved)[1]
+    last_piece = [
+        sliced[pairs - 1][part * depth // kv_parts : (part + 1) * depth // kv_parts]
+        for part in range(kv_parts)
+    ]
+    across.append(swap(gated(along[-1]), "grp"))
+    last_along = [hop(gated(last_piece[0]), FAR)]
+    moved = (across[-1], last_along[0], hand_out(NEXT, gated(shares[NEXT]), first_columns))
+    begun = begin_sum((NEXT | SIDE,), [out_weight, two_pairs(0), two_pairs(2)])
+    begun_near = begin_sum((SIDE, NEXT, 0), [two_pairs(2)])
     pages = jnp.concatenate([pages, gated(pages_next)], axis=0)
     order = [mask ^ far for mask in (0, SIDE) for far in (0, FAR)]
     order = order + [at ^ NEXT for at in order]
@@ -463,18 +543,27 @@
     lens = jnp.take(pages[:, limit * PAGE, :REQ_INST].astype(jnp.int32), block_of, axis=0)
     page_of = slot_pages(lens, placement, page_table, block_of, limit)
     cache = cache_of(pages.reshape(-1, kv_width), page_of)
-    gate = moved + (begun_near[2],)
-
-    moved = weights()
+    ready, far_shares = end_sum(begun, begun_near[2], last_along[0])
+    near_ready, shares = end_sum(begun_near, begun[2], last_along[0])
+    last_across = []
+    for part in range(1, kv_parts):
+        last_along.append(hop(after(last_piece[part], last_along[-1], across[-1]), FAR))
+        last_across.append(swap(after(last_along[part - 1], across[-1]), "grp"))
+    gate = moved + (cache, ready, near_ready) + tuple(last_along) + tuple(last_across)
+
+    last_across.append(swap(gated(last_along[-1]), "grp"))
+    moved = (last_across[-1],)
     hand_out(NEXT | SIDE, gated(far_shares[NEXT | SIDE]), own_columns + pair_columns(0, 4))
     for mask in (NEXT, SIDE, 0):
-        hand_out(mask, gated(shares[mask]), pair_columns(2, 4))
+        moved += (hand_out(mask, gated(shares[mask]), pair_columns(2, 4)),)
     masks = (NEXT | SIDE, NEXT, SIDE, 0)
-    ready, shares = group_sum(masks, [pair(4)])
+    ready, shares = group_sum(masks, [(along[4], across[4])], multiply=tall_product)
     for mask in masks:
         hand_out(mask, shares[mask], pair_columns(4, 5))
     gate = moved + (ready,)
-    ready, shares = group_sum(masks, [pair(5)])
+    ready, shares = group_sum(
+        masks, list(zip(last_along, last_across)), multiply=tall_product
+    )
     for mask in masks:
         hand_out(mask, shares[mask], pair_columns(5, 6))
     projected = place(pieces, segments, offsets, inst_count * own_cols)

time: 611 us -> 611 us (level)
  waiting for transfers between devices: 260 us -> 243 us
  local copies, waits for them, and re-layouts: 37.3 us -> 46 us
  Pallas kernels: 233 us -> 241 us
    pallas_call x0 -> x4, Pallas kernels: none -> 43.1 us  [tall_product(): pl.pallas_call(functools.partial(tall_kernel, heights=len(lefts), pieces=...]
    pallas_call x16 -> x12, Pallas kernels: 201 us -> 164 us  [product(): pl.pallas_call(functools.partial(product_kernel, heights=len(lefts), part...]
    ppermute x14 -> x15, waiting for transfers between devices: 66 us -> 57.2 us  [swap(): return lax.ppermute(array, axis, [(0, 1), (1, 0)])]
    ppermute x32 -> x33, waiting for transfers between devices: 194 us -> 186 us  [hop(): return lax.ppermute(array, 'inst', [(i, i ^ mask) for i in range(count)])]
    unnamed x70 -> x96, local copies, waits for them, and re-layouts: 13.3 us -> 21.7 us
    dynamic_slice x6 -> x5, local copies, waits for them, and re-layouts: 16.4 us -> 13.7 us  [cut(): lax.dynamic_slice(weight, (jnp.int32(0), grp_here * half_cols + n * WIDTH...]
    ppermute x32 -> x33, starting transfers between devices: 39 us -> 41.1 us  [hop(): return lax.ppermute(array, 'inst', [(i, i ^ mask) for i in range(count)])]
  transfers between devices with their start and end apart: 46 -> 48, of which waited for: 24 -> 27; matrix products, arithmetic and copies ran while one was open for 6% -> 6% of each run, Pallas kernels for 38% -> 39%
where the time goes in v3:
time: 611 us; the launch traced here: 601 us
  waiting for transfers between devices  243 us (40%)
  Pallas kernels  241 us (39%)
  starting transfers between devices  49.8 us (8%)
  local copies, waits for them, and re-layouts  46 us (8%)
  other arithmetic  12.7 us (2%)
  matrix products  7.49 us (1%)
    ppermute x33, waiting for transfers between devices, hop(): return lax.ppermute(array, 'inst', [(i, i ^ mask) for i in range(count)])  186 us
    pallas_call x12, Pallas kernels, product(): pl.pallas_call(functools.partial(product_kernel, heights=len(lefts), part...  164 us
    ppermute x15, waiting for transfers between devices, swap(): return lax.ppermute(array, axis, [(0, 1), (1, 0)])  57.2 us
    pallas_call x4, Pallas kernels, tall_product(): pl.pallas_call(functools.partial(tall_kernel, heights=len(lefts), pieces=...  43.1 us
    ppermute x33, starting transfers between devices, hop(): return lax.ppermute(array, 'inst', [(i, i ^ mask) for i in range(count)])  41.1 us
    pallas_call x4, Pallas kernels, attention(): pl.pallas_call(functools.partial(attention_kernel, heads=heads, row_block...  24.5 us
    unnamed x96, local copies, waits for them, and re-layouts  21.7 us
    dynamic_slice x5, local copies, waits for them, and re-layouts, cut(): lax.dynamic_slice(weight, (jnp.int32(0), grp_here * half_cols + n * WIDTH...  13.7 us
  transfers between devices with their start and end apart: 48, of which 27 were waited for; matrix products, arithmetic and copies ran while one was open for 6% of the time, Pallas kernels for 39%

profile of v3, /device:TPU:0, one launch (start us, length us, event | category | flops | bytes accessed | tf_op | source)
XLA Modules:
  0.0 601.0 jit_solution(1373028519676538012)
XLA Ops:
  1.4 2.8 constant_dynamic-slice_fusion.8
  5.4 4.1 collective-permute-start.4
  9.7 2.8 copy-done.3
  12.5 6.3 %attention.4.refs_0_.refs_4_.refs_6_ = bf16[256,3072]{1,0:T(8,128)(2,1)} custom-call(s32[6]{0:T(128)S(1)} %get-tuple-element.186.info, bf16[512,6144]{1,0:T(8,128)(2,1)S(1)} %copy-done.3, bf16[512,2048]{1,0:T(8,128)(2,1)S(1)} %copy-done.2, bf16[512,2048]{1,0:T(8,128)(2,1)S(1)} %copy-done.2), custom_call_target="tpu_custom_call" | custom-call | tf_op jit(solution)/shard_map/attention/pallas_call | solution.py:62
  22.3 6.4 %attention.5.refs_1_.refs_5_.refs_7_ = bf16[256,3072]{1,0:T(8,128)(2,1)} custom-call(s32[6]{0:T(128)S(1)} %get-tuple-element.187.info, bf16[512,6144]{1,0:T(8,128)(2,1)S(1)} %copy-done.3, bf16[512,2048]{1,0:T(8,128)(2,1)S(1)} %copy-done.2, bf16[512,2048]{1,0:T(8,128)(2,1)S(1)} %copy-done.2), custom_call_target="tpu_custom_call" | custom-call | tf_op jit(solution)/shard_map/attention/pallas_call | solution.py:62
  29.3 2.8 copy-done.4
  32.0 6.3 %attention.6.refs_0_.refs_4_.refs_6_ = bf16[256,3072]{1,0:T(8,128)(2,1)} custom-call(s32[6]{0:T(128)S(1)} %add_add_fusion.1.info, bf16[512,6144]{1,0:T(8,128)(2,1)S(1)} %copy-done.4, bf16[512,2048]{1,0:T(8,128)(2,1)S(1)} %copy-done.2, bf16[512,2048]{1,0:T(8,128)(2,1)S(1)} %copy-done.2), custom_call_target="tpu_custom_call" | custom-call | tf_op jit(solution)/shard_map/attention/pallas_call | solution.py:62
  38.3 5.5 attention.7.refs_1_.refs_5_.refs_7_
  45.0 2.7 constant_dynamic-slice_fusion.6
  50.3 2.7 constant_dynamic-slice_fusion.4
  53.1 2.8 constant_dynamic-slice_fusion.3
  57.5 31.2 %collective-permute-done.2.refs_1_.refs_3_.refs_5_ = bf16[256,3072]{1,0:T(8,128)(2,1)} collective-permute-done((bf16[256,3072]{1,0:T(8,128)(2,1)}, bf16[256,3072]{1,0:T(8,128)(2,1)}, u32[]{:S(2)}, u32[]{:S(2)}) %collective-permute-start.2) | collective-permute-done | bytes 1572896 | tf_op jit(solution)/shard_map/ppermute | solution.py:144
  90.0 34.1 %collective-permute-done.3.refs_4_.refs_3_ = bf16[6144,128]{1,0:T(8,128)(2,1)} collective-permute-done((bf16[6144,128]{1,0:T(8,128)(2,1)}, bf16[6144,128]{1,0:T(8,128)(2,1)}, u32[]{:S(2)}, u32[]{:S(2)}) %collective-permute-start.3) | collective-permute-done | bytes 1572896 | tf_op jit(solution)/shard_map/ppermute | solution.py:144
  130.7 4.0 collective-permute-start.9
  135.6 23.4 %product.16 = bf16[256,1536]{1,0:T(8,128)(2,1)} custom-call(bf16[256,3072]{1,0:T(8,128)(2,1)} %attention.4.refs_0_.refs_4_.refs_6_, bf16[256,3072]{1,0:T(8,128)(2,1)} %attention.5.refs_1_.refs_5_.refs_7_, bf16[6144,1536]{1,0:T(8,128)(2,1)} %refs_2_.15), custom_call_target="tpu_custom_call" | custom-call | tf_op jit(solution)/shard_map/product/pallas_call | solution.py:219
  167.7 2.9 convolution_convert_fusion
  171.6 11.1 %product.17.refs_1_ = bf16[256,1536]{1,0:T(8,128)(2,1)} custom-call(bf16[256,3072]{1,0:T(8,128)(2,1)} %attention.6.refs_0_.refs_4_.refs_6_, bf16[256,3072]{1,0:T(8,128)(2,1)} %copy-done.5, bf16[6144,1536]{1,0:T(8,128)(2,1)} %refs_2_.15, bf16[256,1536]{1,0:T(8,128)(2,1)} %copy-done.40), custom_call_target="tpu_custom_call" | custom-call | tf_op jit(solution)/shard_map/product/pallas_call | solution.py:219
  182.6 14.1 %collective-permute-done.6.refs_1_.refs_3_.refs_5_ = bf16[256,3072]{1,0:T(8,128)(2,1)} collective-permute-done((bf16[256,3072]{1,0:T(8,128)(2,1)S(1)}, bf16[256,3072]{1,0:T(8,128)(2,1)}, u32[]{:S(2)}, u32[]{:S(2)}) %collective-permute-start.6) | collective-permute-done | bytes 1572896 | tf_op jit(solution)/shard_map/ppermute | solution.py:144
  196.7 3.5 collective-permute-done.8.refs_6_.refs_5_
  206.8 11.0 %product.18 = bf16[256,1536]{1,0:T(8,128)(2,1)} custom-call(bf16[256,3072]{1,0:T(8,128)(2,1)} %collective-permute-done.1.refs_0_.refs_2_.refs_4_, bf16[256,3072]{1,0:T(8,128)(2,1)} %collective-permute-done.2.refs_1_.refs_3_.refs_5_, bf16[6144,1536]{1,0:T(8,128)(2,1)} %refs_2_.15), custom_call_target="tpu_custom_call" | custom-call | tf_op jit(solution)/shard_map/product/pallas_call | solution.py:219
  217.8 16.9 %collective-permute-done.11.refs_7_.refs_6_ = bf16[6144,128]{1,0:T(8,128)(2,1)S(1)} collective-permute-done((bf16[6144,128]{1,0:T(8,128)(2,1)}, bf16[6144,128]{1,0:T(8,128)(2,1)S(1)}, u32[]{:S(2)}, u32[]{:S(2)}) %collective-permute-start.11) | collective-permute-done | bytes 1572896 | tf_op jit(solution)/shard_map/ppermute | solution.py:148
  237.3 11.1 %product.19 = bf16[256,1536]{1,0:T(8,128)(2,1)} custom-call(bf16[256,3072]{1,0:T(8,128)(2,1)} %collective-permute-done.5.refs_0_.refs_2_.refs_4_, bf16[256,3072]{1,0:T(8,128)(2,1)} %collective-permute-done.6.refs_1_.refs_3_.refs_5_, bf16[6144,1536]{1,0:T(8,128)(2,1)} %refs_2_.15, bf16[256,1536]{1,0:T(8,128)(2,1)} %collective-permute-done.12.refs_3_), custom_call_target="tpu_custom_call" | custom-call | tf_op jit(solution)/shard_map/product/pallas_call | solution.py:219
  248.4 21.7 %collective-permute-done.13.refs_7_.refs_6_ = bf16[6144,128]{1,0:T(8,128)(2,1)S(1)} collective-permute-done((bf16[6144,128]{1,0:T(8,128)(2,1)}, bf16[6144,128]{1,0:T(8,128)(2,1)S(1)}, u32[]{:S(2)}, u32[]{:S(2)}) %collective-permute-start.13) | collective-permute-done | bytes 1572896 | tf_op jit(solution)/shard_map/ppermute | solution.py:144
  279.2 8.8 %product.20 = bf16[512,512]{1,0:T(8,128)(2,1)} custom-call(bf16[256,3072]{1,0:T(8,128)(2,1)} %attention.4.refs_0_.refs_4_.refs_6_, bf16[256,3072]{1,0:T(8,128)(2,1)} %attention.5.refs_1_.refs_5_.refs_7_, bf16[256,3072]{1,0:T(8,128)(2,1)} %collective-permute-done.1.refs_0_.refs_2_.refs_4_, bf16[256,3072]{1,0:T(8,128)(2,1)} %collective-permute-done.2.refs_1_.refs_3_.refs_5_, ...), custom_call_target="tpu_custom_call" | custom-call | tf_op jit(solution)/shard_map/product/pallas_call | solution.py:219
  288.0 19.2 %collective-permute-done.17.refs_8_.refs_7_ = bf16[6144,128]{1,0:T(8,128)(2,1)S(1)} collective-permute-done((bf16[6144,128]{1,0:T(8,128)(2,1)S(1)}, bf16[6144,128]{1,0:T(8,128)(2,1)S(1)}, u32[]{:S(2)}, u32[]{:S(2)}) %collective-permute-start.17) | collective-permute-done | bytes 1572896 | tf_op jit(solution)/shard_map/ppermute | solution.py:148
  310.2 8.9 %product.21 = bf16[512,512]{1,0:T(8,128)(2,1)} custom-call(bf16[256,3072]{1,0:T(8,128)(2,1)} %attention.6.refs_0_.refs_4_.refs_6_, bf16[256,3072]{1,0:T(8,128)(2,1)} %copy-done.5, bf16[256,3072]{1,0:T(8,128)(2,1)} %collective-permute-done.5.refs_0_.refs_2_.refs_4_, bf16[256,3072]{1,0:T(8,128)(2,1)} %collective-permute-done.6.refs_1_.refs_3_.refs_5_, ...), custom_call_target="tpu_custom_call" | custom-call | tf_op jit(solution)/shard_map/product/pallas_call | solution.py:219
  319.1 23.8 %collective-permute-done.19.refs_9_.refs_8_ = bf16[6144,128]{1,0:T(8,128)(2,1)S(1)} collective-permute-done((bf16[6144,128]{1,0:T(8,128)(2,1)}, bf16[6144,128]{1,0:T(8,128)(2,1)S(1)}, u32[]{:S(2)}, u32[]{:S(2)}) %collective-permute-start.19) | collective-permute-done | bytes 1572896 | tf_op jit(solution)/shard_map/ppermute | solution.py:144
  343.0 3.7 collective-permute-done.22
  354.9 14.6 %product.22 = bf16[256,2048]{1,0:T(8,128)(2,1)} custom-call(bf16[256,3072]{1,0:T(8,128)(2,1)} %collective-permute-done.refs_0_.refs_2_, bf16[256,3072]{1,0:T(8,128)(2,1)} %collective-permute-done.9.refs_1_.refs_3_, bf16[6144,1536]{1,0:T(8,128)(2,1)} %refs_2_.15, bf16[6144,128]{1,0:T(8,128)(2,1)} %collective-permute-done.3.refs_4_.refs_3_, ...), custom_call_target="tpu_custom_call" | custom-call | tf_op jit(solution)/shard_map/product/pallas_call | solution.py:219
  369.5 11.7 %collective-permute-done.24.refs_10_.refs_9_ = bf16[6144,128]{1,0:T(8,128)(2,1)} collective-permute-done((bf16[6144,128]{1,0:T(8,128)(2,1)S(1)}, bf16[6144,128]{1,0:T(8,128)(2,1)}, u32[]{:S(2)}, u32[]{:S(2)}) %collective-permute-start.24) | collective-permute-done | bytes 1572896 | tf_op jit(solution)/shard_map/ppermute | solution.py:148
  385.1 15.1 %product.23 = bf16[256,2048]{1,0:T(8,128)(2,1)} custom-call(bf16[256,3072]{1,0:T(8,128)(2,1)} %copy-done.27, bf16[256,3072]{1,0:T(8,128)(2,1)} %collective-permute-done.20.refs_1_.refs_3_, bf16[6144,1536]{1,0:T(8,128)(2,1)} %refs_2_.15, bf16[6144,128]{1,0:T(8,128)(2,1)} %collective-permute-done.3.refs_4_.refs_3_, bf16[6144,128]{1,0:T(8,128)(2,1)} %copy-done.22, ...), custom_call_target="tpu_custom_call" | custom-call | tf_op jit(solution)/shard_map/product/pallas_call | solution.py:219
  400.2 8.1 %collective-permute-done.23.refs_0_ = bf16[256,2048]{1,0:T(8,128)(2,1)S(1)} collective-permute-done((bf16[256,2048]{1,0:T(8,128)(2,1)}, bf16[256,2048]{1,0:T(8,128)(2,1)S(1)}, u32[]{:S(2)}, u32[]{:S(2)}) %collective-permute-start.23) | collective-permute-done | bytes 1048608 | tf_op jit(solution)/shard_map/ppermute | solution.py:144
  408.3 9.3 %collective-permute-done.28 = bf16[4,192,1024]{2,1,0:T(8,128)(2,1)} collective-permute-done((bf16[4,192,1024]{2,1,0:T(8,128)(2,1)}, bf16[4,192,1024]{2,1,0:T(8,128)(2,1)}, u32[]{:S(2)}, u32[]{:S(2)}) %collective-permute-start.28) | collective-permute-done | bytes 1572896 | tf_op jit(solution)/shard_map/ppermute | solution.py:144
  417.6 3.0 collective-permute-done.26.refs_8_
  427.3 11.5 %product.25 = bf16[768,512]{1,0:T(8,128)(2,1)} custom-call(bf16[256,3072]{1,0:T(8,128)(2,1)} %collective-permute-done.1.refs_0_.refs_2_.refs_4_, bf16[256,3072]{1,0:T(8,128)(2,1)} %collective-permute-done.2.refs_1_.refs_3_.refs_5_, bf16[256,3072]{1,0:T(8,128)(2,1)} %collective-permute-done.refs_0_.refs_2_, ...), custom_call_target="tpu_custom_call" | custom-call | tf_op jit(solution)/shard_map/product/pallas_call | solution.py:219
  438.8 18.3 %product.24 = bf16[256,2560]{1,0:T(8,128)(2,1)} custom-call(bf16[256,3072]{1,0:T(8,128)(2,1)} %copy-done.29, bf16[256,3072]{1,0:T(8,128)(2,1)} %collective-permute-done.16.refs_1_, bf16[6144,1536]{1,0:T(8,128)(2,1)} %refs_2_.15, bf16[6144,128]{1,0:T(8,128)(2,1)} %collective-permute-done.3.refs_4_.refs_3_, bf16[6144,128]{1,0:T(8,128)(2,1)} %copy-done.22, ...), custom_call_target="tpu_custom_call" | custom-call | tf_op jit(solution)/shard_map/product/pallas_call | solution.py:219
  457.8 2.7 collective-permute-start.34
  463.6 4.3 cache.1
  467.9 11.6 %product.27 = bf16[768,512]{1,0:T(8,128)(2,1)} custom-call(bf16[256,3072]{1,0:T(8,128)(2,1)} %collective-permute-done.5.refs_0_.refs_2_.refs_4_, bf16[256,3072]{1,0:T(8,128)(2,1)} %collective-permute-done.6.refs_1_.refs_3_.refs_5_, bf16[256,3072]{1,0:T(8,128)(2,1)} %copy-done.27, bf16[256,3072]{1,0:T(8,128)(2,1)} %collective-permute-done.20.refs_1_.refs_3_, ...), custom_call_target="tpu_custom_call" | custom-call | tf_op jit(solution)/shard_map/product/pallas_call | solution.py:219
  479.5 18.7 %product.26 = bf16[256,2560]{1,0:T(8,128)(2,1)} custom-call(bf16[256,3072]{1,0:T(8,128)(2,1)} %collective-permute-done.21.refs_0_, bf16[256,3072]{1,0:T(8,128)(2,1)} %collective-permute-done.27.refs_1_, bf16[6144,1536]{1,0:T(8,128)(2,1)} %refs_2_.15, bf16[6144,128]{1,0:T(8,128)(2,1)} %collective-permute-done.3.refs_4_.refs_3_, bf16[6144,128]{1,0:T(8,128)(2,1)} %copy-done.22, ...), custom_call_target="tpu_custom_call" | custom-call | tf_op jit(solution)/shard_map/product/pallas_call | solution.py:219
  499.8 10.6 %product.28 = bf16[1024,256]{1,0:T(8,128)(2,1)} custom-call(bf16[256,3072]{1,0:T(8,128)(2,1)} %copy-done.29, bf16[256,3072]{1,0:T(8,128)(2,1)} %collective-permute-done.16.refs_1_, bf16[256,3072]{1,0:T(8,128)(2,1)} %collective-permute-done.refs_0_.refs_2_, bf16[256,3072]{1,0:T(8,128)(2,1)} %collective-permute-done.9.refs_1_.refs_3_, ...), custom_call_target="tpu_custom_call" | custom-call | tf_op jit(solution)/shard_map/product/pallas_call | solution.py:293
  510.5 3.0 collective-permute-start.36
  515.7 10.8 %product.29 = bf16[1024,256]{1,0:T(8,128)(2,1)} custom-call(bf16[256,3072]{1,0:T(8,128)(2,1)} %collective-permute-done.21.refs_0_, bf16[256,3072]{1,0:T(8,128)(2,1)} %collective-permute-done.27.refs_1_, bf16[256,3072]{1,0:T(8,128)(2,1)} %copy-done.27, bf16[256,3072]{1,0:T(8,128)(2,1)} %collective-permute-done.20.refs_1_.refs_3_, ...), custom_call_target="tpu_custom_call" | custom-call | tf_op jit(solution)/shard_map/product/pallas_call | solution.py:293
  526.5 22.0 %collective-permute-done.37.refs_5_ = bf16[256,512]{1,0:T(8,128)(2,1)S(1)} collective-permute-done((bf16[256,512]{1,0:T(8,128)(2,1)S(1)}, bf16[256,512]{1,0:T(8,128)(2,1)S(1)}, u32[]{:S(2)}, u32[]{:S(2)}) %collective-permute-start.37) | collective-permute-done | bytes 262176 | tf_op jit(solution)/shard_map/ppermute | solution.py:144
  549.7 10.6 %product.30 = bf16[1024,256]{1,0:T(8,128)(2,1)} custom-call(bf16[256,3072]{1,0:T(8,128)(2,1)} %copy-done.29, bf16[256,3072]{1,0:T(8,128)(2,1)} %collective-permute-done.16.refs_1_, bf16[256,3072]{1,0:T(8,128)(2,1)} %collective-permute-done.refs_0_.refs_2_, bf16[256,3072]{1,0:T(8,128)(2,1)} %collective-permute-done.9.refs_1_.refs_3_, ...), custom_call_target="tpu_custom_call" | custom-call | tf_op jit(solution)/shard_map/product/pallas_call | solution.py:293
  565.4 11.0 %product.31 = bf16[1024,256]{1,0:T(8,128)(2,1)} custom-call(bf16[256,3072]{1,0:T(8,128)(2,1)} %collective-permute-done.21.refs_0_, bf16[256,3072]{1,0:T(8,128)(2,1)} %collective-permute-done.27.refs_1_, bf16[256,3072]{1,0:T(8,128)(2,1)} %copy-done.27, bf16[256,3072]{1,0:T(8,128)(2,1)} %collective-permute-done.20.refs_1_.refs_3_, ...), custom_call_target="tpu_custom_call" | custom-call | tf_op jit(solution)/shard_map/product/pallas_call | solution.py:293
  586.3 2.8 collective-permute-done.45.refs_12_
  595.9 4.8 place.1
  (243 shorter events, 100.3 us)
Async XLA Ops:
  5.4 52.2 %collective-permute-start.4 = (bf16[528,1024]{1,0:T(8,128)(2,1)S(1)}, bf16[528,1024]{1,0:T(8,128)(2,1)}, u32[]{:S(2)}, u32[]{:S(2)}) collective-permute-start(bf16[528,1024]{1,0:T(8,128)(2,1)S(1)} %fusion.1), channel_id=1, source_target_pairs={{0,8},{2,10},{4,12},{6,14},{8,0},{10,2},{12,4},{14,6},{1,9},{3,11}... | collective-permute-start | bytes 3244040 | tf_op jit(solution)/shard_map/ppermute | solution.py:144
  18.9 69.9 %collective-permute-start.1 = (bf16[256,3072]{1,0:T(8,128)(2,1)}, bf16[256,3072]{1,0:T(8,128)(2,1)}, u32[]{:S(2)}, u32[]{:S(2)}) collective-permute-start(bf16[256,3072]{1,0:T(8,128)(2,1)} %attention.4.refs_0_.refs_4_.refs_6_), channel_id=1, source_target_pairs={{0,2},{2,0},{4,6},{6,4},{8,10},{10,8},{12,14},{14,12},{1,3},{3,1},... | collective-permute-start | bytes 4718600 | tf_op jit(solution)/shard_map/ppermute | solution.py:144
  20.4 69.6 %collective-permute-start = (bf16[256,3072]{1,0:T(8,128)(2,1)}, bf16[256,3072]{1,0:T(8,128)(2,1)}, u32[]{:S(2)}, u32[]{:S(2)}) collective-permute-start(bf16[256,3072]{1,0:T(8,128)(2,1)} %attention.4.refs_0_.refs_4_.refs_6_), channel_id=1, source_target_pairs={{0,4},{2,6},{4,0},{6,2},{8,12},{10,14},{12,8},{14,10},{1,5},{3,7},... | collective-permute-start | bytes 4718600 | tf_op jit(solution)/shard_map/ppermute | solution.py:144
  22.0 102.1 %collective-permute-start.3 = (bf16[6144,128]{1,0:T(8,128)(2,1)}, bf16[6144,128]{1,0:T(8,128)(2,1)}, u32[]{:S(2)}, u32[]{:S(2)}) collective-permute-start(bf16[6144,128]{1,0:T(8,128)(2,1)} %constant_dynamic-slice_fusion.8), channel_id=1, source_target_pairs={{0,8},{2,10},{4,12},{6,14},{8,0},{10,2},{12,4},{14,6},{1,9},{3,11}... | collective-permute-start | bytes 4718600 | tf_op jit(solution)/shard_map/ppermute | solution.py:144
  28.6 60.1 %collective-permute-start.2 = (bf16[256,3072]{1,0:T(8,128)(2,1)}, bf16[256,3072]{1,0:T(8,128)(2,1)}, u32[]{:S(2)}, u32[]{:S(2)}) collective-permute-start(bf16[256,3072]{1,0:T(8,128)(2,1)} %attention.5.refs_1_.refs_5_.refs_7_), channel_id=1, source_target_pairs={{0,2},{2,0},{4,6},{6,4},{8,10},{10,8},{12,14},{14,12},{1,3},{3,1},... | collective-permute-start | bytes 4718600 | tf_op jit(solution)/shard_map/ppermute | solution.py:144
  127.1 55.5 %collective-permute-start.5 = (bf16[256,3072]{1,0:T(8,128)(2,1)}, bf16[256,3072]{1,0:T(8,128)(2,1)}, u32[]{:S(2)}, u32[]{:S(2)}) collective-permute-start(bf16[256,3072]{1,0:T(8,128)(2,1)} %attention.6.refs_0_.refs_4_.refs_6_), channel_id=1, source_target_pairs={{0,2},{2,0},{4,6},{6,4},{8,10},{10,8},{12,14},{14,12},{1,3},{3,1},... | collective-permute-start | bytes 4718600 | tf_op jit(solution)/shard_map/ppermute | solution.py:144
  128.6 68.1 %collective-permute-start.6 = (bf16[256,3072]{1,0:T(8,128)(2,1)S(1)}, bf16[256,3072]{1,0:T(8,128)(2,1)}, u32[]{:S(2)}, u32[]{:S(2)}) collective-permute-start(bf16[256,3072]{1,0:T(8,128)(2,1)S(1)} %copy-done.6), channel_id=1, source_target_pairs={{0,2},{2,0},{4,6},{6,4},{8,10},{10,8},{12,14},{14,12},{1,3},{3,1},... | collective-permute-start | bytes 4718600 | tf_op jit(solution)/shard_map/ppermute | solution.py:144
  129.1 35.2 %collective-permute-start.7 = (bf16[6144,128]{1,0:T(8,128)(2,1)}, bf16[6144,128]{1,0:T(8,128)(2,1)S(1)}, u32[]{:S(2)}, u32[]{:S(2)}) collective-permute-start(bf16[6144,128]{1,0:T(8,128)(2,1)} %collective-permute-done.3.refs_4_.refs_3_), channel_id=1, source_target_pairs={{0,16},{16,0},{1,17},{17,1},{2,18},{18,2},{3,19},{19,3},{4,20},{20... | collective-permute-start | bytes 4718600 | tf_op jit(solution)/shard_map/ppermute | solution.py:148
  130.7 69.5 %collective-permute-start.8 = (bf16[6144,128]{1,0:T(8,128)(2,1)}, bf16[6144,128]{1,0:T(8,128)(2,1)}, u32[]{:S(2)}, u32[]{:S(2)}) collective-permute-start(bf16[6144,128]{1,0:T(8,128)(2,1)} %constant_dynamic-slice_fusion.6), channel_id=1, source_target_pairs={{0,8},{2,10},{4,12},{6,14},{8,0},{10,2},{12,4},{14,6},{1,9},{3,11}... | collective-permute-start | bytes 4718600 | tf_op jit(solution)/shard_map/ppermute | solution.py:144
  130.7 69.5 %collective-permute-start.9 = (bf16[256,3072]{1,0:T(8,128)(2,1)}, bf16[256,3072]{1,0:T(8,128)(2,1)}, u32[]{:S(2)}, u32[]{:S(2)}) collective-permute-start(bf16[256,3072]{1,0:T(8,128)(2,1)} %attention.5.refs_1_.refs_5_.refs_7_), channel_id=1, source_target_pairs={{0,4},{2,6},{4,0},{6,2},{8,12},{10,14},{12,8},{14,10},{1,5},{3,7},... | collective-permute-start | bytes 4718600 | tf_op jit(solution)/shard_map/ppermute | solution.py:144
  164.4 6.3 %collective-permute-start.10 = (bf16[256,1536]{1,0:T(8,128)(2,1)S(1)}, bf16[256,1536]{1,0:T(8,128)(2,1)S(1)}, u32[]{:S(2)}, u32[]{:S(2)}) collective-permute-start(bf16[256,1536]{1,0:T(8,128)(2,1)S(1)} %copy-done.39), channel_id=1, source_target_pairs={{0,1},{1,0},{2,3},{3,2},{4,5},{5,4},{6,7},{7,6},{8,9},{9,8},{10,11... | collective-permute-start | bytes 2359304 | tf_op jit(solution)/shard_map/ppermute | solution.py:148
  200.2 34.5 %collective-permute-start.11 = (bf16[6144,128]{1,0:T(8,128)(2,1)}, bf16[6144,128]{1,0:T(8,128)(2,1)S(1)}, u32[]{:S(2)}, u32[]{:S(2)}) collective-permute-start(bf16[6144,128]{1,0:T(8,128)(2,1)} %collective-permute-done.8.refs_6_.refs_5_), channel_id=1, source_target_pairs={{0,16},{16,0},{1,17},{17,1},{2,18},{18,2},{3,19},{19,3},{4,20},{20... | collective-permute-start | bytes 4718600 | tf_op jit(solution)/shard_map/ppermute | solution.py:148
  201.0 69.1 %collective-permute-start.13 = (bf16[6144,128]{1,0:T(8,128)(2,1)}, bf16[6144,128]{1,0:T(8,128)(2,1)S(1)}, u32[]{:S(2)}, u32[]{:S(2)}) collective-permute-start(bf16[6144,128]{1,0:T(8,128)(2,1)} %constant_dynamic-slice_fusion.5), channel_id=1, source_target_pairs={{0,8},{2,10},{4,12},{6,14},{8,0},{10,2},{12,4},{14,6},{1,9},{3,11}... | collective-permute-start | bytes 4718600 | tf_op jit(solution)/shard_map/ppermute | solution.py:144
  203.1 67.4 %collective-permute-start.14 = (bf16[256,3072]{1,0:T(8,128)(2,1)}, bf16[256,3072]{1,0:T(8,128)(2,1)S(1)}, u32[]{:S(2)}, u32[]{:S(2)}) collective-permute-start(bf16[256,3072]{1,0:T(8,128)(2,1)} %attention.6.refs_0_.refs_4_.refs_6_), channel_id=1, source_target_pairs={{0,4},{2,6},{4,0},{6,2},{8,12},{10,14},{12,8},{14,10},{1,5},{3,7},... | collective-permute-start | bytes 4718600 | tf_op jit(solution)/shard_map/ppermute | solution.py:144
  204.8 65.7 %collective-permute-start.15 = (bf16[256,3072]{1,0:T(8,128)(2,1)}, bf16[256,3072]{1,0:T(8,128)(2,1)S(1)}, u32[]{:S(2)}, u32[]{:S(2)}) collective-permute-start(bf16[256,3072]{1,0:T(8,128)(2,1)} %collective-permute-done.refs_0_.refs_2_), channel_id=1, source_target_pairs={{0,2},{2,0},{4,6},{6,4},{8,10},{10,8},{12,14},{14,12},{1,3},{3,1},... | collective-permute-start | bytes 4718600 | tf_op jit(solution)/shard_map/ppermute | solution.py:144
  206.2 66.3 %collective-permute-start.16 = (bf16[256,3072]{1,0:T(8,128)(2,1)}, bf16[256,3072]{1,0:T(8,128)(2,1)}, u32[]{:S(2)}, u32[]{:S(2)}) collective-permute-start(bf16[256,3072]{1,0:T(8,128)(2,1)} %collective-permute-done.9.refs_1_.refs_3_), channel_id=1, source_target_pairs={{0,2},{2,0},{4,6},{6,4},{8,10},{10,8},{12,14},{14,12},{1,3},{3,1},... | collective-permute-start | bytes 4718600 | tf_op jit(solution)/shard_map/ppermute | solution.py:144
  234.7 2.6 collective-permute-start.12
  272.6 34.7 %collective-permute-start.17 = (bf16[6144,128]{1,0:T(8,128)(2,1)S(1)}, bf16[6144,128]{1,0:T(8,128)(2,1)S(1)}, u32[]{:S(2)}, u32[]{:S(2)}) collective-permute-start(bf16[6144,128]{1,0:T(8,128)(2,1)S(1)} %collective-permute-done.13.refs_7_.refs_6_), channel_id=1, source_target_pairs={{0,16},{16,0},{1,17},{17,1},{2,18},{18,2},{3,19},{19,3},{4,20},{20... | collective-permute-start | bytes 4718600 | tf_op jit(solution)/shard_map/ppermute | solution.py:148
  274.1 68.8 %collective-permute-start.19 = (bf16[6144,128]{1,0:T(8,128)(2,1)}, bf16[6144,128]{1,0:T(8,128)(2,1)S(1)}, u32[]{:S(2)}, u32[]{:S(2)}) collective-permute-start(bf16[6144,128]{1,0:T(8,128)(2,1)} %constant_dynamic-slice_fusion.4), channel_id=1, source_target_pairs={{0,8},{2,10},{4,12},{6,14},{8,0},{10,2},{12,4},{14,6},{1,9},{3,11}... | collective-permute-start | bytes 4718600 | tf_op jit(solution)/shard_map/ppermute | solution.py:144
  274.5 68.5 %collective-permute-start.20 = (bf16[256,3072]{1,0:T(8,128)(2,1)S(1)}, bf16[256,3072]{1,0:T(8,128)(2,1)}, u32[]{:S(2)}, u32[]{:S(2)}) collective-permute-start(bf16[256,3072]{1,0:T(8,128)(2,1)S(1)} %copy-done.7), channel_id=1, source_target_pairs={{0,4},{2,6},{4,0},{6,2},{8,12},{10,14},{12,8},{14,10},{1,5},{3,7},... | collective-permute-start | bytes 4718600 | tf_op jit(solution)/shard_map/ppermute | solution.py:144
  277.1 65.8 %collective-permute-start.21 = (bf16[256,3072]{1,0:T(8,128)(2,1)}, bf16[256,3072]{1,0:T(8,128)(2,1)}, u32[]{:S(2)}, u32[]{:S(2)}) collective-permute-start(bf16[256,3072]{1,0:T(8,128)(2,1)} %copy-done.27), channel_id=1, source_target_pairs={{0,2},{2,0},{4,6},{6,4},{8,10},{10,8},{12,14},{14,12},{1,3},{3,1},... | collective-permute-start | bytes 4718600 | tf_op jit(solution)/shard_map/ppermute | solution.py:144
  278.6 68.0 %collective-permute-start.22 = (bf16[2,2,192,1024]{3,2,1,0:T(8,128)(2,1)}, bf16[2,2,192,1024]{3,2,1,0:T(8,128)(2,1)}, u32[]{:S(2)}, u32[]{:S(2)}) collective-permute-start(bf16[2,2,192,1024]{3,2,1,0:T(8,128)(2,1)} %pad_maximum_fusion.2), channel_id=1, source_target_pairs={{0,2},{2,0},{4,6},{6,4},{8,10},{10,8},{12,14},{14,12},{1,3},{3,1},... | collective-permute-start | bytes 4718600 | tf_op jit(solution)/shard_map/ppermute | solution.py:144
  307.3 2.1 collective-permute-start.18
  346.6 34.6 %collective-permute-start.24 = (bf16[6144,128]{1,0:T(8,128)(2,1)S(1)}, bf16[6144,128]{1,0:T(8,128)(2,1)}, u32[]{:S(2)}, u32[]{:S(2)}) collective-permute-start(bf16[6144,128]{1,0:T(8,128)(2,1)S(1)} %collective-permute-done.19.refs_9_.refs_8_), channel_id=1, source_target_pairs={{0,16},{16,0},{1,17},{17,1},{2,18},{18,2},{3,19},{19,3},{4,20},{20... | collective-permute-start | bytes 4718600 | tf_op jit(solution)/shard_map/ppermute | solution.py:148
  351.1 66.6 %collective-permute-start.28 = (bf16[4,192,1024]{2,1,0:T(8,128)(2,1)}, bf16[4,192,1024]{2,1,0:T(8,128)(2,1)}, u32[]{:S(2)}, u32[]{:S(2)}) collective-permute-start(bf16[4,192,1024]{2,1,0:T(8,128)(2,1)} %get-tuple-element.151), channel_id=1, source_target_pairs={{0,4},{2,6},{4,0},{6,2},{8,12},{10,14},{12,8},{14,10},{1,5},{3,7},... | collective-permute-start | bytes 4718600 | tf_op jit(solution)/shard_map/ppermute | solution.py:144
  351.3 69.2 %collective-permute-start.26 = (bf16[6144,128]{1,0:T(8,128)(2,1)}, bf16[6144,128]{1,0:T(8,128)(2,1)}, u32[]{:S(2)}, u32[]{:S(2)}) collective-permute-start(bf16[6144,128]{1,0:T(8,128)(2,1)} %constant_dynamic-slice_fusion.3), channel_id=1, source_target_pairs={{0,8},{2,10},{4,12},{6,14},{8,0},{10,2},{12,4},{14,6},{1,9},{3,11}... | collective-permute-start | bytes 4718600 | tf_op jit(solution)/shard_map/ppermute | solution.py:144
  351.7 68.9 %collective-permute-start.27 = (bf16[256,3072]{1,0:T(8,128)(2,1)}, bf16[256,3072]{1,0:T(8,128)(2,1)}, u32[]{:S(2)}, u32[]{:S(2)}) collective-permute-start(bf16[256,3072]{1,0:T(8,128)(2,1)} %collective-permute-done.20.refs_1_.refs_3_), channel_id=1, source_target_pairs={{0,2},{2,0},{4,6},{6,4},{8,10},{10,8},{12,14},{14,12},{1,3},{3,1},... | collective-permute-start | bytes 4718600 | tf_op jit(solution)/shard_map/ppermute | solution.py:144
  354.4 53.9 %collective-permute-start.23 = (bf16[256,2048]{1,0:T(8,128)(2,1)}, bf16[256,2048]{1,0:T(8,128)(2,1)S(1)}, u32[]{:S(2)}, u32[]{:S(2)}) collective-permute-start(bf16[256,2048]{1,0:T(8,128)(2,1)} %pad_maximum_fusion.4), channel_id=1, source_target_pairs={{0,2},{2,0},{4,6},{6,4},{8,10},{10,8},{12,14},{14,12},{1,3},{3,1},... | collective-permute-start | bytes 3145736 | tf_op jit(solution)/shard_map/ppermute | solution.py:144
  381.2 2.9 collective-permute-start.25
  420.6 37.2 %collective-permute-start.32 = (bf16[6144,128]{1,0:T(8,128)(2,1)}, bf16[6144,128]{1,0:T(8,128)(2,1)}, u32[]{:S(2)}, u32[]{:S(2)}) collective-permute-start(bf16[6144,128]{1,0:T(8,128)(2,1)} %collective-permute-done.26.refs_8_), channel_id=1, source_target_pairs={{0,16},{16,0},{1,17},{17,1},{2,18},{18,2},{3,19},{19,3},{4,20},{20... | collective-permute-start | bytes 4718600 | tf_op jit(solution)/shard_map/ppermute | solution.py:148
  424.8 32.3 %collective-permute-start.30 = (bf16[3072,128]{1,0:T(8,128)(2,1)}, bf16[3072,128]{1,0:T(8,128)(2,1)}, u32[]{:S(2)}, u32[]{:S(2)}) collective-permute-start(bf16[3072,128]{1,0:T(8,128)(2,1)} %get-tuple-element.112), channel_id=1, source_target_pairs={{0,8},{2,10},{4,12},{6,14},{8,0},{10,2},{12,4},{14,6},{1,9},{3,11}... | collective-permute-start | bytes 2359304 | tf_op jit(solution)/shard_map/ppermute | solution.py:144
  427.3 70.9 %collective-permute-start.29 = (bf16[256,2048]{1,0:T(8,128)(2,1)}, bf16[256,2048]{1,0:T(8,128)(2,1)S(1)}, u32[]{:S(2)}, u32[]{:S(2)}) collective-permute-start(bf16[256,2048]{1,0:T(8,128)(2,1)} %product.23), channel_id=1, source_target_pairs={{0,4},{2,6},{4,0},{6,2},{8,12},{10,14},{12,8},{14,10},{1,5},{3,7},... | collective-permute-start | bytes 3145736 | tf_op jit(solution)/shard_map/ppermute | solution.py:144
  457.1 22.4 %collective-permute-start.31 = (bf16[256,2560]{1,0:T(8,128)(2,1)}, bf16[256,2560]{1,0:T(8,128)(2,1)}, u32[]{:S(2)}, u32[]{:S(2)}) collective-permute-start(bf16[256,2560]{1,0:T(8,128)(2,1)} %product.24), channel_id=1, source_target_pairs={{0,1},{1,0},{2,3},{3,2},{4,5},{5,4},{6,7},{7,6},{8,9},{9,8},{10,11... | collective-permute-start | bytes 3932168 | tf_op jit(solution)/shard_map/ppermute | solution.py:148
  457.3 10.6 %collective-permute-start.33 = (bf16[768,512]{1,0:T(8,128)(2,1)}, bf16[768,512]{1,0:T(8,128)(2,1)}, u32[]{:S(2)}, u32[]{:S(2)}) collective-permute-start(bf16[768,512]{1,0:T(8,128)(2,1)} %product.25), channel_id=1, source_target_pairs={{0,1},{1,0},{2,3},{3,2},{4,5},{5,4},{6,7},{7,6},{8,9},{9,8},{10,11... | collective-permute-start | bytes 2359304 | tf_op jit(solution)/shard_map/ppermute | solution.py:148
  457.8 40.4 %collective-permute-start.34 = (bf16[3072,128]{1,0:T(8,128)(2,1)}, bf16[3072,128]{1,0:T(8,128)(2,1)S(1)}, u32[]{:S(2)}, u32[]{:S(2)}) collective-permute-start(bf16[3072,128]{1,0:T(8,128)(2,1)} %get-tuple-element.117), channel_id=1, source_target_pairs={{0,8},{2,10},{4,12},{6,14},{8,0},{10,2},{12,4},{14,6},{1,9},{3,11}... | collective-permute-start | bytes 2359304 | tf_op jit(solution)/shard_map/ppermute | solution.py:144
  460.5 37.8 %collective-permute-start.35 = (bf16[3072,128]{1,0:T(8,128)(2,1)}, bf16[3072,128]{1,0:T(8,128)(2,1)}, u32[]{:S(2)}, u32[]{:S(2)}) collective-permute-start(bf16[3072,128]{1,0:T(8,128)(2,1)} %collective-permute-done.30.refs_8_), channel_id=1, source_target_pairs={{0,16},{16,0},{1,17},{17,1},{2,18},{18,2},{3,19},{19,3},{4,20},{20... | collective-permute-start | bytes 2359304 | tf_op jit(solution)/shard_map/ppermute | solution.py:148
  498.2 50.5 %collective-permute-start.43 = (bf16[3072,128]{1,0:T(8,128)(2,1)S(1)}, bf16[3072,128]{1,0:T(8,128)(2,1)S(1)}, u32[]{:S(2)}, u32[]{:S(2)}) collective-permute-start(bf16[3072,128]{1,0:T(8,128)(2,1)S(1)} %collective-permute-done.34.refs_10_), channel_id=1, source_target_pairs={{0,16},{16,0},{1,17},{17,1},{2,18},{18,2},{3,19},{19,3},{4,20},{20... | collective-permute-start | bytes 2359304 | tf_op jit(solution)/shard_map/ppermute | solution.py:148
  510.4 4.4 collective-permute-start.39
  510.5 72.9 %collective-permute-start.36 = (bf16[256,2560]{1,0:T(8,128)(2,1)}, bf16[256,2560]{1,0:T(8,128)(2,1)S(1)}, u32[]{:S(2)}, u32[]{:S(2)}) collective-permute-start(bf16[256,2560]{1,0:T(8,128)(2,1)} %product.26), channel_id=1, source_target_pairs={{0,6},{2,4},{4,2},{6,0},{8,14},{10,12},{12,10},{14,8},{1,7},{3,5},... | collective-permute-start | bytes 3932168 | tf_op jit(solution)/shard_map/ppermute | solution.py:144
  514.3 34.2 %collective-permute-start.37 = (bf16[256,512]{1,0:T(8,128)(2,1)S(1)}, bf16[256,512]{1,0:T(8,128)(2,1)S(1)}, u32[]{:S(2)}, u32[]{:S(2)}) collective-permute-start(bf16[256,512]{1,0:T(8,128)(2,1)S(1)} %get-tuple-element.120), channel_id=1, source_target_pairs={{0,4},{2,6},{4,0},{6,2},{8,12},{10,14},{12,8},{14,10},{1,5},{3,7},... | collective-permute-start | bytes 786440 | tf_op jit(solution)/shard_map/ppermute | solution.py:144
  514.3 34.4 %collective-permute-start.38 = (bf16[256,512]{1,0:T(8,128)(2,1)S(1)}, bf16[256,512]{1,0:T(8,128)(2,1)S(1)}, u32[]{:S(2)}, u32[]{:S(2)}) collective-permute-start(bf16[256,512]{1,0:T(8,128)(2,1)S(1)} %get-tuple-element.121), channel_id=1, source_target_pairs={{0,2},{2,0},{4,6},{6,4},{8,10},{10,8},{12,14},{14,12},{1,3},{3,1},... | collective-permute-start | bytes 786440 | tf_op jit(solution)/shard_map/ppermute | solution.py:144
  560.3 4.3 collective-permute-start.44
  561.1 18.5 %collective-permute-start.42 = (bf16[256,256]{1,0:T(8,128)(2,1)S(1)}, bf16[256,256]{1,0:T(8,128)(2,1)S(1)}, u32[]{:S(2)}, u32[]{:S(2)}) collective-permute-start(bf16[256,256]{1,0:T(8,128)(2,1)S(1)} %get-tuple-element.162), channel_id=1, source_target_pairs={{0,2},{2,0},{4,6},{6,4},{8,10},{10,8},{12,14},{14,12},{1,3},{3,1},... | collective-permute-start | bytes 393224 | tf_op jit(solution)/shard_map/ppermute | solution.py:144
  562.3 20.0 %collective-permute-start.41 = (bf16[256,256]{1,0:T(8,128)(2,1)S(1)}, bf16[256,256]{1,0:T(8,128)(2,1)S(1)}, u32[]{:S(2)}, u32[]{:S(2)}) collective-permute-start(bf16[256,256]{1,0:T(8,128)(2,1)S(1)} %get-tuple-element.163), channel_id=1, source_target_pairs={{0,4},{2,6},{4,0},{6,2},{8,12},{10,14},{12,8},{14,10},{1,5},{3,7},... | collective-permute-start | bytes 393224 | tf_op jit(solution)/shard_map/ppermute | solution.py:144
  564.3 19.1 %collective-permute-start.40 = (bf16[256,256]{1,0:T(8,128)(2,1)}, bf16[256,256]{1,0:T(8,128)(2,1)}, u32[]{:S(2)}, u32[]{:S(2)}) collective-permute-start(bf16[256,256]{1,0:T(8,128)(2,1)} %get-tuple-element.164), channel_id=1, source_target_pairs={{0,6},{2,4},{4,2},{6,0},{8,14},{10,12},{12,10},{14,8},{1,7},{3,5},... | collective-permute-start | bytes 393224 | tf_op jit(solution)/shard_map/ppermute | solution.py:144
  578.4 5.4 collective-permute-start.47
  580.3 6.0 collective-permute-start.46
  583.0 6.2 %collective-permute-start.45 = (bf16[256,256]{1,0:T(8,128)(2,1)}, bf16[256,256]{1,0:T(8,128)(2,1)}, u32[]{:S(2)}, u32[]{:S(2)}) collective-permute-start(bf16[256,256]{1,0:T(8,128)(2,1)} %get-tuple-element.160), channel_id=1, source_target_pairs={{0,6},{2,4},{4,2},{6,0},{8,14},{10,12},{12,10},{14,8},{1,7},{3,5},... | collective-permute-start | bytes 393224 | tf_op jit(solution)/shard_map/ppermute | solution.py:144
  (47 other events, 883.5 us)

commit v4 on v2

--- a/solution.py
+++ b/solution.py
@@ -148,56 +148,96 @@
     return lax.ppermute(array, axis, [(0, 1), (1, 0)])
 
 
-def product_kernel(*refs, heights, parts, groups, summed):
+def product_kernel(*refs, heights, parts, groups, narrow, others):
     step = pl.program_id(0)
-    lefts, refs = refs[: heights * parts], refs[heights * parts :]
-    out = refs[-1]
-    rows, depth = lefts[0].shape
-
-    def group_of(rights):
-        def compute():
-            for height in range(heights):
-                total = None
-                for part in range(parts):
-                    span = slice(part * depth, (part + 1) * depth)
-                    right = jnp.concatenate([ref[span, :] for ref in rights], axis=1)
-                    term = jnp.dot(
-                        lefts[height * parts + part][...], right,
-                        preferred_element_type=jnp.float32,
-                    )
-                    total = term if total is None else total + term
-                at = slice(height * rows, (height + 1) * rows)
-                if summed:
-                    total = total + refs[-2][at, :].astype(jnp.float32)
-                out[at, :] = total.astype(out.dtype)
-        return compute
-
-    first = 0
-    for steps, count in groups:
-        compute = group_of(refs[:count])
-        refs = refs[count:]
+    held, sems = refs[-2 - narrow : -2], refs[-1]
+    lefts = refs[-2]
+    count = heights * parts
+    left_refs, refs = refs[:count], refs[count : -2 - narrow]
+    sources, wide, at = [], [], 0
+    for steps, size in groups:
+        wide.append(refs[at] if size == 0 else None)
+        if size:
+            sources.extend(refs[at : at + size])
+        at += max(size, 1)
+    out, summands = refs[at + others], refs[at : at + others]
+    rows, depth = left_refs[0].shape
+    copies = [
+        pltpu.make_async_copy(ref, lefts.at[n], sems.at[n]) for n, ref in enumerate(left_refs)
+    ]
+    narrow_copies = [
+        pltpu.make_async_copy(ref, held[n], sems.at[count + n]) for n, ref in enumerate(sources)
+    ]
+
+    def start():
+        order = copies + narrow_copies if groups[0][1] == 0 else narrow_copies + copies
+        for copy in order:
+            copy.start()
+
+    def compute(right_of, arrived, first):
+        for copy in arrived:
+            copy.wait()
+        for height in range(heights):
+            total = None
+            for part in range(parts):
+                if first == 0:
+                    wait = copies[height * parts + part].wait
+                    if groups[0][0] == 1:
+                        wait()
+                    else:
+                        pl.when(step == 0)(wait)
+                term = jnp.dot(
+                    lefts[height * parts + part], right_of(part),
+                    preferred_element_type=jnp.float32,
+                )
+                total = term if total is None else total + term
+            at = slice(height * rows, (height + 1) * rows)
+            for other in summands:
+                total = total + other[at, :].astype(jnp.float32)
+            out[at, :] = total.astype(out.dtype)
+
+    def within(ref, part):
+        return ref[part * depth : (part + 1) * depth, :]
+
+    first, used = 0, 0
+    if sum(steps for steps, _ in groups) == 1:
+        start()
+    else:
+        pl.when(step == 0)(start)
+    for (steps, size), ref in zip(groups, wide):
+        if size == 0:
+            arrived = []
+            right_of = lambda part, ref=ref: within(ref, part)
+        else:
+            arrived = narrow_copies[used : used + size]
+            mine = held[used : used + size]
+            right_of = lambda part, mine=mine: jnp.concatenate(
+                [within(ref, part) for ref in mine], axis=1
+            )
+            used += size
+        body = functools.partial(compute, right_of, arrived, first)
         if len(groups) == 1:
-            compute()
+            body()
         else:
-            pl.when((step >= first) & (step < first + steps))(compute)
+            pl.when((step >= first) & (step < first + steps))(body)
         first += steps
 
 
-def product(lefts, rights, other=None):
+def product(lefts, rights, *others, dtype=jnp.bfloat16):
     rows, depth = lefts[0][0].shape
-    block = 2 * WIDTH
-    operands, specs, groups = [], [], []
-    for left in lefts:
-        for part in left:
-            operands.append(part)
-            specs.append(pl.BlockSpec((rows, depth), lambda n: (0, 0)))
+    sizes = [len(right) * WIDTH for right in rights if isinstance(right, tuple)]
+    block = sizes[0] if sizes else 4 * WIDTH
+    operands = [part for left in lefts for part in left]
+    anywhere = pl.BlockSpec(memory_space=pl.ANY)
+    specs = [anywhere] * len(operands)
+    count, groups, held = len(operands), [], []
     first = 0
     for right in rights:
         if isinstance(right, tuple):
             steps = 1
-            for piece in right:
-                operands.append(piece)
-                specs.append(pl.BlockSpec(piece.shape, lambda n: (0, 0)))
+            operands += right
+            specs += [anywhere] * len(right)
+            held += [pltpu.VMEM(piece.shape, piece.dtype) for piece in right]
             groups.append((1, len(right)))
         else:
             steps = right.shape[1] // block
@@ -208,22 +248,25 @@
                     lambda n, first=first, steps=steps: (0, jnp.clip(n - first, 0, steps - 1)),
                 )
             )
-            groups.append((steps, 1))
+            groups.append((steps, 0))
         first += steps
     height = rows * len(lefts)
     out_spec = pl.BlockSpec((height, block), lambda n: (0, n))
-    if other is not None:
-        operands.append(other)
-        specs.append(out_spec)
+    operands += others
+    specs += [out_spec] * len(others)
     return pl.pallas_call(
         functools.partial(
             product_kernel, heights=len(lefts), parts=len(lefts[0]), groups=groups,
-            summed=other is not None,
+            narrow=len(held), others=len(others),
         ),
         grid=(first,),
         in_specs=specs,
         out_specs=out_spec,
-        out_shape=jax.ShapeDtypeStruct((height, first * block), operands[0].dtype),
+        out_shape=jax.ShapeDtypeStruct((height, first * block), dtype),
+        scratch_shapes=held + [
+            pltpu.VMEM((count, rows, depth), operands[0].dtype),
+            pltpu.SemaphoreType.DMA((count + len(held),)),
+        ],
         compiler_params=pltpu.CompilerParams(vmem_limit_bytes=56 << 20),
         cost_estimate=LIGHT,
         name="product",
@@ -345,14 +388,7 @@
         lefts[0][0] = gated(lefts[0][0])
         return masks, rights, product([left[:kv_parts] for left in lefts], rights)
 
-    def end_sum(begun, *earlier):
-        masks, rights, given = begun
-        given = after(given, *earlier) if earlier else given
-        if tp_count == 2:
-            lefts = [blocks[mask][kv_parts:] for mask in masks]
-            total = product(lefts, rights, swap(given, "tp"))
-        else:
-            total = given
+    def shares_of(total, masks):
         rows = total.shape[0] // len(masks)
         shares = {mask: total[n * rows : (n + 1) * rows] for n, mask in enumerate(masks)}
         if tp_count != 2:
@@ -361,6 +397,14 @@
                     shares[mask], "tp", scatter_dimension=0, tiled=True
                 )
         return total, shares
+
+    def end_sum(begun, *earlier):
+        masks, rights, given = begun
+        total = after(given, *earlier) if earlier else given
+        if tp_count == 2:
+            lefts = [blocks[mask][kv_parts:] for mask in masks]
+            total = product(lefts, rights, swap(total, "tp"))
+        return shares_of(total, masks)
 
     def group_sum(masks, rights, *earlier):
         return end_sum(begin_sum(masks, rights), *earlier)
@@ -426,12 +470,12 @@
     own_shares.update(shares)
     gate = moved + (ready,)
 
-    def pair(n):
-        return (along[n], across[n])
+    def two_pairs(n):
+        return (along[n], across[n], along[n + 1], across[n + 1])
 
     moved = weights() + spread(NEXT, own[3:], NEXT) + spread(NEXT | SIDE, near[2:3], SIDE)
     pages_side = hop(gated(pages_given), SIDE)
-    ready, shares = group_sum((0, SIDE), [pair(0), pair(1)], moved[0])
+    ready, shares = group_sum((0, SIDE), [two_pairs(0)], moved[0])
     gate = moved + (pages_side, ready)
 
     first_columns = own_columns + pair_columns(0, 2)
@@ -446,14 +490,18 @@
         lax.dynamic_index_in_dim(pages, 1 - next_here, axis=1, keepdims=False), NEXT
     )
     pages = lax.dynamic_index_in_dim(pages, next_here, axis=1, keepdims=False)
-    ready, shares = group_sum((NEXT,), [out_weight, pair(0), pair(1)], moved[0])
-    gate = moved + (pages_next, ready)
-
-    moved = weights() + (hand_out(NEXT, gated(shares[NEXT]), first_columns),)
-    begun = begin_sum((NEXT | SIDE,), [out_weight, pair(0), pair(1), pair(2), pair(3)])
-    begun_near = begin_sum((SIDE, NEXT, 0), [pair(2), pair(3)])
-    far_shares = end_sum(begun, begun_near[2], *moved)[1]
-    shares = end_sum(begun_near, *moved)[1]
+    ready, shares = group_sum((NEXT,), [out_weight, two_pairs(0)], moved[0])
+    begun_near = begin_sum((SIDE, NEXT, 0), [tuple(after(two_pairs(2), ready))])
+    gate = moved + (pages_next, begun_near[2])
+
+    last_piece = [
+        sliced[pairs - 1][part * depth // kv_parts : (part + 1) * depth // kv_parts]
+        for part in range(kv_parts)
+    ]
+    across.append(swap(gated(along[-1]), "grp"))
+    last_along = [hop(gated(last_piece[0]), FAR)]
+    moved = (across[-1], last_along[0], hand_out(NEXT, gated(shares[NEXT]), first_columns))
+    begun = begin_sum((NEXT | SIDE,), [out_weight, two_pairs(0), two_pairs(2)])
     pages = jnp.concatenate([pages, gated(pages_next)], axis=0)
     order = [mask ^ far for mask in (0, SIDE) for far in (0, FAR)]
     order = order + [at ^ NEXT for at in order]
@@ -463,20 +511,55 @@
     lens = jnp.take(pages[:, limit * PAGE, :REQ_INST].astype(jnp.int32), block_of, axis=0)
     page_of = slot_pages(lens, placement, page_table, block_of, limit)
     cache = cache_of(pages.reshape(-1, kv_width), page_of)
-    gate = moved + (begun_near[2],)
-
-    moved = weights()
+    near_ready, shares = end_sum(begun_near, begun[2], last_along[0])
+    moved += tuple(
+        hand_out(mask, shares[mask], pair_columns(2, 4)) for mask in (NEXT, SIDE, 0)
+    )
+    ready, far_shares = end_sum(begun, begun[2], last_along[0])
+    last_across = []
+    for part in range(1, kv_parts):
+        last_along.append(hop(after(last_piece[part], last_along[-1], across[-1]), FAR))
+        last_across.append(swap(after(last_along[part - 1], across[-1]), "grp"))
+    gate = moved + (cache, ready, near_ready) + tuple(last_along) + tuple(last_across)
+
+    last_across.append(swap(gated(last_along[-1]), "grp"))
     hand_out(NEXT | SIDE, gated(far_shares[NEXT | SIDE]), own_columns + pair_columns(0, 4))
-    for mask in (NEXT, SIDE, 0):
-        hand_out(mask, gated(shares[mask]), pair_columns(2, 4))
     masks = (NEXT | SIDE, NEXT, SIDE, 0)
-    ready, shares = group_sum(masks, [pair(4)])
+    ready = gate
+
+    def last_product(chunk, parts, rights, *others, dtype=jnp.float32):
+        lefts = [[blocks[mask][chunk * kv_parts + part] for part in parts] for mask in masks]
+        return product(lefts, [after(rights, *ready)], *others, dtype=dtype)
+
+    def begin(chunk):
+        nonlocal ready
+        fourth = last_product(
+            chunk, range(kv_parts), (along[4], across[4]),
+            dtype=jnp.float32 if chunk else jnp.bfloat16,
+        )
+        ready = (fourth,)
+        sums = ()
+        for part in range(kv_parts - 1):
+            sums = (last_product(chunk, [part], (last_along[part], last_across[part]), *sums),)
+            ready = sums
+        return fourth, sums
+
+    begun = [begin(chunk) for chunk in range(len(chunks))]
+    rights = (last_along[-1], last_across[-1])
+    last = [kv_parts - 1]
+    fourth, sums = begun[0]
+    fifth = last_product(0, last, rights, *sums, dtype=jnp.bfloat16)
+    if tp_count == 2:
+        other_fourth = swap(after(fourth, fifth), "tp")
+        other_fifth = swap(fifth, "tp")
+        fourth, sums = begun[1]
+        ready = (other_fifth,)
+        fifth = last_product(1, last, rights, *sums, other_fifth, dtype=jnp.bfloat16)
+        fourth = (fourth + other_fourth.astype(jnp.float32)).astype(jnp.bfloat16)
+    total = jnp.concatenate([fourth, fifth], axis=1)
+    shares = shares_of(total, masks)[1]
     for mask in masks:
-        hand_out(mask, shares[mask], pair_columns(4, 5))
-    gate = moved + (ready,)
-    ready, shares = group_sum(masks, [pair(5)])
-    for mask in masks:
-        hand_out(mask, shares[mask], pair_columns(5, 6))
+        hand_out(mask, shares[mask], pair_columns(4, 6))
     projected = place(pieces, segments, offsets, inst_count * own_cols)
     return (projected, cache)
 

time: 611 us -> 606 us (level)
  waiting for transfers between devices: 260 us -> 239 us
  Pallas kernels: 233 us -> 248 us
  starting transfers between devices: 50.1 us -> 43.4 us
  local copies, waits for them, and re-layouts: 37.3 us -> 43.5 us
    ppermute x32 -> x30, waiting for transfers between devices: 194 us -> 171 us  [hop(): return lax.ppermute(array, 'inst', [(i, i ^ mask) for i in range(count)])]
    pallas_call x16 -> x18, Pallas kernels: 201 us -> 214 us  [product(): pl.pallas_call(functools.partial(product_kernel, heights=len(lefts), part...]
    unnamed x70 -> x84, local copies, waits for them, and re-layouts: 13.3 us -> 20.9 us
    ppermute x32 -> x30, starting transfers between devices: 39 us -> 34.6 us  [hop(): return lax.ppermute(array, 'inst', [(i, i ^ mask) for i in range(count)])]
    dynamic_slice x6 -> x5, local copies, waits for them, and re-layouts: 16.4 us -> 13.6 us  [cut(): lax.dynamic_slice(weight, (jnp.int32(0), grp_here * half_cols + n * WIDTH...]
    ppermute x14 -> x15, waiting for transfers between devices: 66 us -> 68.1 us  [swap(): return lax.ppermute(array, axis, [(0, 1), (1, 0)])]
  transfers between devices with their start and end apart: 46 -> 45, of which waited for: 24 -> 23; matrix products, arithmetic and copies ran while one was open for 6% -> 6% of each run, Pallas kernels for 38% -> 40%
where the time goes in v4:
time: 606 us; the launch traced here: 597 us
  Pallas kernels  248 us (41%)
  waiting for transfers between devices  239 us (39%)
  local copies, waits for them, and re-layouts  43.5 us (7%)
  starting transfers between devices  43.4 us (7%)
  other arithmetic  13.4 us (2%)
  matrix products  7.47 us (1%)
    pallas_call x18, Pallas kernels, product(): pl.pallas_call(functools.partial(product_kernel, heights=len(lefts), part...  214 us
    ppermute x30, waiting for transfers between devices, hop(): return lax.ppermute(array, 'inst', [(i, i ^ mask) for i in range(count)])  171 us
    ppermute x15, waiting for transfers between devices, swap(): return lax.ppermute(array, axis, [(0, 1), (1, 0)])  68.1 us
    ppermute x30, starting transfers between devices, hop(): return lax.ppermute(array, 'inst', [(i, i ^ mask) for i in range(count)])  34.6 us
    pallas_call x4, Pallas kernels, attention(): pl.pallas_call(functools.partial(attention_kernel, heads=heads, row_block...  24.4 us
    unnamed x84, local copies, waits for them, and re-layouts  20.9 us
    dynamic_slice x5, local copies, waits for them, and re-layouts, cut(): lax.dynamic_slice(weight, (jnp.int32(0), grp_here * half_cols + n * WIDTH...  13.6 us
  transfers between devices with their start and end apart: 45, of which 23 were waited for; matrix products, arithmetic and copies ran while one was open for 6% of the time, Pallas kernels for 40%

profile of v4, /device:TPU:0, one launch (start us, length us, event | category | flops | bytes accessed | tf_op | source)
XLA Modules:
  0.0 596.6 jit_solution(6394940455838746712)
XLA Ops:
  2.2 2.8 constant_dynamic-slice_fusion.8
  6.3 2.8 copy-done.2
  9.1 6.3 %attention.4.refs_0_.refs_4_.refs_6_.refs_3_ = bf16[256,3072]{1,0:T(8,128)(2,1)} custom-call(s32[6]{0:T(128)S(1)} %get-tuple-element.206.info, bf16[512,6144]{1,0:T(8,128)(2,1)S(1)} %copy-done.2, bf16[512,2048]{1,0:T(8,128)(2,1)S(1)} %copy-done.1, bf16[512,2048]{1,0:T(8,128)(2,1)S(1)} %copy-done.1), custom_call_target="tpu_custom_call" | custom-call | tf_op jit(solution)/shard_map/attention/pallas_call | solution.py:62
  15.4 3.0 collective-permute-start
  22.9 6.3 %attention.5.refs_1_.refs_5_.refs_7_.refs_3_ = bf16[256,3072]{1,0:T(8,128)(2,1)} custom-call(s32[6]{0:T(128)S(1)} %get-tuple-element.207.info, bf16[512,6144]{1,0:T(8,128)(2,1)S(1)} %copy-done.2, bf16[512,2048]{1,0:T(8,128)(2,1)S(1)} %copy-done.1, bf16[512,2048]{1,0:T(8,128)(2,1)S(1)} %copy-done.1), custom_call_target="tpu_custom_call" | custom-call | tf_op jit(solution)/shard_map/attention/pallas_call | solution.py:62
  29.8 2.8 copy-done.3
  32.6 6.3 %attention.6.refs_0_.refs_4_.refs_6_.refs_3_ = bf16[256,3072]{1,0:T(8,128)(2,1)} custom-call(s32[6]{0:T(128)S(1)} %add_add_fusion.1.info, bf16[512,6144]{1,0:T(8,128)(2,1)S(1)} %copy-done.3, bf16[512,2048]{1,0:T(8,128)(2,1)S(1)} %copy-done.1, bf16[512,2048]{1,0:T(8,128)(2,1)S(1)} %copy-done.1), custom_call_target="tpu_custom_call" | custom-call | tf_op jit(solution)/shard_map/attention/pallas_call | solution.py:62
  38.8 5.5 attention.7.refs_1_.refs_5_.refs_7_.refs_3_
  45.5 2.7 constant_dynamic-slice_fusion.6
  48.1 2.6 constant_dynamic-slice_fusion.5
  50.8 2.7 constant_dynamic-slice_fusion.4
  53.4 2.9 constant_dynamic-slice_fusion.3
  56.4 80.4 %collective-permute-done.4 = bf16[528,1024]{1,0:T(8,128)(2,1)} collective-permute-done((bf16[528,1024]{1,0:T(8,128)(2,1)S(1)}, bf16[528,1024]{1,0:T(8,128)(2,1)}, u32[]{:S(2)}, u32[]{:S(2)}) %collective-permute-start.4) | collective-permute-done | bytes 1081376 | tf_op jit(solution)/shard_map/ppermute | solution.py:144
  141.8 3.0 collective-permute-start.9
  147.3 13.5 %product.18 = bf16[256,1536]{1,0:T(8,128)(2,1)} custom-call(bf16[256,3072]{1,0:T(8,128)(2,1)} %attention.4.refs_0_.refs_4_.refs_6_.refs_3_, bf16[256,3072]{1,0:T(8,128)(2,1)} %attention.5.refs_1_.refs_5_.refs_7_.refs_3_, bf16[6144,1536]{1,0:T(8,128)(2,1)} %refs_2_.15), custom_call_target="tpu_custom_call" | custom-call | tf_op jit(solution)/shard_map/product/pallas_call | solution.py:257
  163.7 10.9 %collective-permute-done.7.refs_5_.refs_4_ = bf16[6144,128]{1,0:T(8,128)(2,1)S(1)} collective-permute-done((bf16[6144,128]{1,0:T(8,128)(2,1)}, bf16[6144,128]{1,0:T(8,128)(2,1)S(1)}, u32[]{:S(2)}, u32[]{:S(2)}) %collective-permute-start.7) | collective-permute-done | bytes 1572896 | tf_op jit(solution)/shard_map/ppermute | solution.py:148
  178.0 2.9 convolution_convert_fusion
  181.8 13.4 %product.19.refs_1_ = bf16[256,1536]{1,0:T(8,128)(2,1)} custom-call(bf16[256,3072]{1,0:T(8,128)(2,1)} %attention.6.refs_0_.refs_4_.refs_6_.refs_3_, bf16[256,3072]{1,0:T(8,128)(2,1)} %copy-done.4, bf16[6144,1536]{1,0:T(8,128)(2,1)} %refs_2_.15, bf16[256,1536]{1,0:T(8,128)(2,1)} %copy-done.34), custom_call_target="tpu_custom_call" | custom-call | tf_op jit(solution)/shard_map/product/pallas_call | solution.py:257
  195.2 11.7 %collective-permute-done.6.refs_1_.refs_3_.refs_5_.refs_2_ = bf16[256,3072]{1,0:T(8,128)(2,1)} collective-permute-done((bf16[256,3072]{1,0:T(8,128)(2,1)S(1)}, bf16[256,3072]{1,0:T(8,128)(2,1)}, u32[]{:S(2)}, u32[]{:S(2)}) %collective-permute-start.6) | collective-permute-done | bytes 1572896 | tf_op jit(solution)/shard_map/ppermute | solution.py:144
  206.9 3.5 collective-permute-done.8.refs_6_.refs_5_
  215.2 13.2 %product.20 = bf16[256,1536]{1,0:T(8,128)(2,1)} custom-call(bf16[256,3072]{1,0:T(8,128)(2,1)} %collective-permute-done.1.refs_0_.refs_2_.refs_4_, bf16[256,3072]{1,0:T(8,128)(2,1)} %collective-permute-done.2.refs_1_.refs_3_.refs_5_.refs_2_, bf16[6144,1536]{1,0:T(8,128)(2,1)} %refs_2_.15), custom_call_target="tpu_custom_call" | custom-call | tf_op jit(solution)/shard_map/product/pallas_call | solution.py:257
  228.5 18.5 %collective-permute-done.11.refs_7_.refs_6_ = bf16[6144,128]{1,0:T(8,128)(2,1)S(1)} collective-permute-done((bf16[6144,128]{1,0:T(8,128)(2,1)}, bf16[6144,128]{1,0:T(8,128)(2,1)S(1)}, u32[]{:S(2)}, u32[]{:S(2)}) %collective-permute-start.11) | collective-permute-done | bytes 1572896 | tf_op jit(solution)/shard_map/ppermute | solution.py:148
  249.6 13.6 %product.21 = bf16[256,1536]{1,0:T(8,128)(2,1)} custom-call(bf16[256,3072]{1,0:T(8,128)(2,1)} %collective-permute-done.5.refs_0_.refs_2_.refs_4_, bf16[256,3072]{1,0:T(8,128)(2,1)} %collective-permute-done.6.refs_1_.refs_3_.refs_5_.refs_2_, bf16[6144,1536]{1,0:T(8,128)(2,1)} %refs_2_.15, bf16[256,1536]{1,0:T(8,128)(2,1)} %collective-permute-done.12.refs_3_), custom_call_target="tpu_custom_call" | custom-call | tf_op jit(solution)/shard_map/product/pallas_call | solution.py:257
  263.2 17.4 %collective-permute-done.13.refs_6_.refs_7_ = bf16[6144,128]{1,0:T(8,128)(2,1)S(1)} collective-permute-done((bf16[6144,128]{1,0:T(8,128)(2,1)}, bf16[6144,128]{1,0:T(8,128)(2,1)S(1)}, u32[]{:S(2)}, u32[]{:S(2)}) %collective-permute-start.13) | collective-permute-done | bytes 1572896 | tf_op jit(solution)/shard_map/ppermute | solution.py:144
  288.9 8.5 %product.22 = bf16[512,512]{1,0:T(8,128)(2,1)} custom-call(bf16[256,3072]{1,0:T(8,128)(2,1)} %attention.4.refs_0_.refs_4_.refs_6_.refs_3_, bf16[256,3072]{1,0:T(8,128)(2,1)} %attention.5.refs_1_.refs_5_.refs_7_.refs_3_, bf16[256,3072]{1,0:T(8,128)(2,1)} %collective-permute-done.1.refs_0_.refs_2_.refs_4_, ...), custom_call_target="tpu_custom_call" | custom-call | tf_op jit(solution)/shard_map/product/pallas_call | solution.py:257
  297.5 19.4 %collective-permute-done.17.refs_7_.refs_8_ = bf16[6144,128]{1,0:T(8,128)(2,1)S(1)} collective-permute-done((bf16[6144,128]{1,0:T(8,128)(2,1)S(1)}, bf16[6144,128]{1,0:T(8,128)(2,1)S(1)}, u32[]{:S(2)}, u32[]{:S(2)}) %collective-permute-start.17) | collective-permute-done | bytes 1572896 | tf_op jit(solution)/shard_map/ppermute | solution.py:148
  319.9 9.6 %product.23 = bf16[512,512]{1,0:T(8,128)(2,1)} custom-call(bf16[256,3072]{1,0:T(8,128)(2,1)} %attention.6.refs_0_.refs_4_.refs_6_.refs_3_, bf16[256,3072]{1,0:T(8,128)(2,1)} %copy-done.4, bf16[256,3072]{1,0:T(8,128)(2,1)} %collective-permute-done.5.refs_0_.refs_2_.refs_4_, bf16[256,3072]{1,0:T(8,128)(2,1)} %collective-permute-done.6.refs_1_.refs_3_.refs_5_.refs_2_, ...), custom_call_target="tpu_custom_call" | custom-call | tf_op jit(solution)/shard_map/product/pallas_call | solution.py:257
  329.5 23.5 %collective-permute-done.19.refs_8_.refs_9_ = bf16[6144,128]{1,0:T(8,128)(2,1)} collective-permute-done((bf16[6144,128]{1,0:T(8,128)(2,1)}, bf16[6144,128]{1,0:T(8,128)(2,1)}, u32[]{:S(2)}, u32[]{:S(2)}) %collective-permute-start.19) | collective-permute-done | bytes 1572896 | tf_op jit(solution)/shard_map/ppermute | solution.py:144
  362.1 15.2 %product.24 = bf16[256,2048]{1,0:T(8,128)(2,1)} custom-call(bf16[256,3072]{1,0:T(8,128)(2,1)} %collective-permute-done.refs_0_.refs_2_.refs_1_, bf16[256,3072]{1,0:T(8,128)(2,1)} %collective-permute-done.9.refs_1_.refs_3_, bf16[6144,1536]{1,0:T(8,128)(2,1)} %refs_2_.15, bf16[6144,128]{1,0:T(8,128)(2,1)} %collective-permute-done.3.refs_4_.refs_3_, ...), custom_call_target="tpu_custom_call" | custom-call | tf_op jit(solution)/shard_map/product/pallas_call | solution.py:257
  377.3 12.2 %collective-permute-done.24.refs_9_.refs_10_ = bf16[6144,128]{1,0:T(8,128)(2,1)S(1)} collective-permute-done((bf16[6144,128]{1,0:T(8,128)(2,1)}, bf16[6144,128]{1,0:T(8,128)(2,1)S(1)}, u32[]{:S(2)}, u32[]{:S(2)}) %collective-permute-start.24) | collective-permute-done | bytes 1572896 | tf_op jit(solution)/shard_map/ppermute | solution.py:148
  390.4 2.7 fusion.39
  394.0 15.6 %product.25 = bf16[256,2048]{1,0:T(8,128)(2,1)} custom-call(bf16[256,3072]{1,0:T(8,128)(2,1)} %copy-done.22, bf16[256,3072]{1,0:T(8,128)(2,1)} %collective-permute-done.20.refs_1_.refs_3_, bf16[6144,1536]{1,0:T(8,128)(2,1)} %refs_2_.15, bf16[6144,128]{1,0:T(8,128)(2,1)} %collective-permute-done.3.refs_4_.refs_3_, bf16[6144,128]{1,0:T(8,128)(2,1)} %copy-done.17, ...), custom_call_target="tpu_custom_call" | custom-call | tf_op jit(solution)/shard_map/product/pallas_call | solution.py:257
  409.7 10.9 %product.26 = bf16[768,512]{1,0:T(8,128)(2,1)} custom-call(bf16[256,3072]{1,0:T(8,128)(2,1)} %collective-permute-done.1.refs_0_.refs_2_.refs_4_, bf16[256,3072]{1,0:T(8,128)(2,1)} %collective-permute-done.2.refs_1_.refs_3_.refs_5_.refs_2_, bf16[256,3072]{1,0:T(8,128)(2,1)} %collective-permute-done.refs_0_.refs_2_.refs_1_, ...), custom_call_target="tpu_custom_call" | custom-call | tf_op jit(solution)/shard_map/product/pallas_call | solution.py:257
  420.6 5.7 collective-permute-done.26.refs_8_
  434.6 18.0 %product.27 = bf16[256,2560]{1,0:T(8,128)(2,1)} custom-call(bf16[256,3072]{1,0:T(8,128)(2,1)} %collective-permute-done.15.refs_0_, bf16[256,3072]{1,0:T(8,128)(2,1)} %collective-permute-done.16.refs_1_.refs_0_, bf16[6144,1536]{1,0:T(8,128)(2,1)} %refs_2_.15, bf16[6144,128]{1,0:T(8,128)(2,1)} %collective-permute-done.3.refs_4_.refs_3_, ...), custom_call_target="tpu_custom_call" | custom-call | tf_op jit(solution)/shard_map/product/pallas_call | solution.py:257
  452.7 11.2 %collective-permute-done.30.refs_4_ = bf16[3072,128]{1,0:T(8,128)(2,1)S(1)} collective-permute-done((bf16[3072,128]{1,0:T(8,128)(2,1)}, bf16[3072,128]{1,0:T(8,128)(2,1)S(1)}, u32[]{:S(2)}, u32[]{:S(2)}) %collective-permute-start.30) | collective-permute-done | bytes 786464 | tf_op jit(solution)/shard_map/ppermute | solution.py:144
  468.4 11.9 %product.28 = bf16[768,512]{1,0:T(8,128)(2,1)} custom-call(bf16[256,3072]{1,0:T(8,128)(2,1)} %collective-permute-done.5.refs_0_.refs_2_.refs_4_, bf16[256,3072]{1,0:T(8,128)(2,1)} %collective-permute-done.6.refs_1_.refs_3_.refs_5_.refs_2_, bf16[256,3072]{1,0:T(8,128)(2,1)} %copy-done.22, bf16[256,3072]{1,0:T(8,128)(2,1)} %collective-permute-done.20.refs_1_.refs_3_, ...), custom_call_target="tpu_custom_call" | custom-call | tf_op jit(solution)/shard_map/product/pallas_call | solution.py:257
  485.4 4.2 cache.1
  489.6 18.3 %product.29 = bf16[256,2560]{1,0:T(8,128)(2,1)} custom-call(bf16[256,3072]{1,0:T(8,128)(2,1)} %collective-permute-done.21.refs_0_, bf16[256,3072]{1,0:T(8,128)(2,1)} %collective-permute-done.27.refs_1_.refs_0_, bf16[6144,1536]{1,0:T(8,128)(2,1)} %refs_2_.15, bf16[6144,128]{1,0:T(8,128)(2,1)} %collective-permute-done.3.refs_4_.refs_3_, ...), custom_call_target="tpu_custom_call" | custom-call | tf_op jit(solution)/shard_map/product/pallas_call | solution.py:257
  512.2 11.5 %product.30 = bf16[1024,256]{1,0:T(8,128)(2,1)} custom-call(bf16[256,3072]{1,0:T(8,128)(2,1)} %collective-permute-done.15.refs_0_, bf16[256,3072]{1,0:T(8,128)(2,1)} %collective-permute-done.16.refs_1_.refs_0_, bf16[256,3072]{1,0:T(8,128)(2,1)} %collective-permute-done.refs_0_.refs_2_.refs_1_, bf16[256,3072]{1,0:T(8,128)(2,1)} %collective-permute-done.9.refs_1_.refs_3_, ...), custom_call_target="tpu_custom_call" | custom-call | tf_op jit(solution)/shard_map/product/pallas_call | solution.py:257
  523.7 6.8 %product.31.refs_6_ = f32[1024,256]{1,0:T(8,128)} custom-call(bf16[256,3072]{1,0:T(8,128)(2,1)} %collective-permute-done.15.refs_0_, bf16[256,3072]{1,0:T(8,128)(2,1)} %collective-permute-done.refs_0_.refs_2_.refs_1_, bf16[256,3072]{1,0:T(8,128)(2,1)} %collective-permute-done.1.refs_0_.refs_2_.refs_4_, ...), custom_call_target="tpu_custom_call" | custom-call | tf_op jit(solution)/shard_map/product/pallas_call | solution.py:257
  530.5 11.7 %product.32 = f32[1024,256]{1,0:T(8,128)} custom-call(bf16[256,3072]{1,0:T(8,128)(2,1)} %collective-permute-done.21.refs_0_, bf16[256,3072]{1,0:T(8,128)(2,1)} %collective-permute-done.27.refs_1_.refs_0_, bf16[256,3072]{1,0:T(8,128)(2,1)} %copy-done.22, bf16[256,3072]{1,0:T(8,128)(2,1)} %collective-permute-done.20.refs_1_.refs_3_, ...), custom_call_target="tpu_custom_call" | custom-call | tf_op jit(solution)/shard_map/product/pallas_call | solution.py:257
  542.2 7.0 %product.33.refs_6_ = f32[1024,256]{1,0:T(8,128)} custom-call(bf16[256,3072]{1,0:T(8,128)(2,1)} %collective-permute-done.21.refs_0_, bf16[256,3072]{1,0:T(8,128)(2,1)} %copy-done.22, bf16[256,3072]{1,0:T(8,128)(2,1)} %collective-permute-done.5.refs_0_.refs_2_.refs_4_, bf16[256,3072]{1,0:T(8,128)(2,1)} %attention.6.refs_0_.refs_4_.refs_6_.refs_3_, ...), custom_call_target="tpu_custom_call" | custom-call | tf_op jit(solution)/shard_map/product/pallas_call | solution.py:257
  550.1 7.8 %product.34 = bf16[1024,256]{1,0:T(8,128)(2,1)} custom-call(bf16[256,3072]{1,0:T(8,128)(2,1)} %collective-permute-done.16.refs_1_.refs_0_, bf16[256,3072]{1,0:T(8,128)(2,1)} %collective-permute-done.9.refs_1_.refs_3_, bf16[256,3072]{1,0:T(8,128)(2,1)} %collective-permute-done.2.refs_1_.refs_3_.refs_5_.refs_2_, ...), custom_call_target="tpu_custom_call" | custom-call | tf_op jit(solution)/shard_map/product/pallas_call | solution.py:257
  560.9 7.9 %product.35 = bf16[1024,256]{1,0:T(8,128)(2,1)} custom-call(bf16[256,3072]{1,0:T(8,128)(2,1)} %collective-permute-done.27.refs_1_.refs_0_, bf16[256,3072]{1,0:T(8,128)(2,1)} %collective-permute-done.20.refs_1_.refs_3_, bf16[256,3072]{1,0:T(8,128)(2,1)} %collective-permute-done.6.refs_1_.refs_3_.refs_5_.refs_2_, bf16[256,3072]{1,0:T(8,128)(2,1)} %copy-done.4, ...), custom_call_target="tpu_custom_call" | custom-call | tf_op jit(solution)/shard_map/product/pallas_call | solution.py:257
  574.5 6.8 %collective-permute-done.42.refs_8_ = bf16[256,512]{1,0:T(8,128)(2,1)} collective-permute-done((bf16[256,512]{1,0:T(8,128)(2,1)}, bf16[256,512]{1,0:T(8,128)(2,1)}, u32[]{:S(2)}, u32[]{:S(2)}) %collective-permute-start.42) | collective-permute-done | bytes 262176 | tf_op jit(solution)/shard_map/ppermute | solution.py:144
  581.3 4.4 collective-permute-done.43.refs_9_
  591.1 5.1 place.1
  (227 shorter events, 90.2 us)
Async XLA Ops:
  0.6 429.5 %copy-start = (s32[32,16]{0,1:T(8,128)S(1)}, s32[32,16]{0,1:T(8,128)}, u32[]{:S(2)}) copy-start(s32[32,16]{0,1:T(8,128)} %param.14) | copy-start | bytes 6148
  15.4 121.4 %collective-permute-start = (bf16[256,3072]{1,0:T(8,128)(2,1)}, bf16[256,3072]{1,0:T(8,128)(2,1)}, u32[]{:S(2)}, u32[]{:S(2)}) collective-permute-start(bf16[256,3072]{1,0:T(8,128)(2,1)} %attention.4.refs_0_.refs_4_.refs_6_.refs_3_), channel_id=1, source_target_pairs={{0,4},{2,6},{4,0},{6,2},{8,12},{10,14},{12,8},{14,10},{1,5},{3,7},... | collective-permute-start | bytes 4718600 | tf_op jit(solution)/shard_map/ppermute | solution.py:144
  18.4 118.4 %collective-permute-start.1 = (bf16[256,3072]{1,0:T(8,128)(2,1)}, bf16[256,3072]{1,0:T(8,128)(2,1)}, u32[]{:S(2)}, u32[]{:S(2)}) collective-permute-start(bf16[256,3072]{1,0:T(8,128)(2,1)} %attention.4.refs_0_.refs_4_.refs_6_.refs_3_), channel_id=1, source_target_pairs={{0,2},{2,0},{4,6},{6,4},{8,10},{10,8},{12,14},{14,12},{1,3},{3,1},... | collective-permute-start | bytes 4718600 | tf_op jit(solution)/shard_map/ppermute | solution.py:144
  19.9 116.9 %collective-permute-start.3 = (bf16[6144,128]{1,0:T(8,128)(2,1)}, bf16[6144,128]{1,0:T(8,128)(2,1)}, u32[]{:S(2)}, u32[]{:S(2)}) collective-permute-start(bf16[6144,128]{1,0:T(8,128)(2,1)} %constant_dynamic-slice_fusion.8), channel_id=1, source_target_pairs={{0,8},{2,10},{4,12},{6,14},{8,0},{10,2},{12,4},{14,6},{1,9},{3,11}... | collective-permute-start | bytes 4718600 | tf_op jit(solution)/shard_map/ppermute | solution.py:144
  22.5 114.3 %collective-permute-start.4 = (bf16[528,1024]{1,0:T(8,128)(2,1)S(1)}, bf16[528,1024]{1,0:T(8,128)(2,1)}, u32[]{:S(2)}, u32[]{:S(2)}) collective-permute-start(bf16[528,1024]{1,0:T(8,128)(2,1)S(1)} %fusion.1), channel_id=1, source_target_pairs={{0,8},{2,10},{4,12},{6,14},{8,0},{10,2},{12,4},{14,6},{1,9},{3,11}... | collective-permute-start | bytes 3244040 | tf_op jit(solution)/shard_map/ppermute | solution.py:144
  29.2 107.7 %collective-permute-start.2 = (bf16[256,3072]{1,0:T(8,128)(2,1)}, bf16[256,3072]{1,0:T(8,128)(2,1)}, u32[]{:S(2)}, u32[]{:S(2)}) collective-permute-start(bf16[256,3072]{1,0:T(8,128)(2,1)} %attention.5.refs_1_.refs_5_.refs_7_.refs_3_), channel_id=1, source_target_pairs={{0,2},{2,0},{4,6},{6,4},{8,10},{10,8},{12,14},{14,12},{1,3},{3,1},... | collective-permute-start | bytes 4718600 | tf_op jit(solution)/shard_map/ppermute | solution.py:144
  53.4 85.3 %copy-start.5 = (bf16[256,3072]{1,0:T(8,128)(2,1)S(1)}, bf16[256,3072]{1,0:T(8,128)(2,1)}, u32[]{:S(2)}) copy-start(bf16[256,3072]{1,0:T(8,128)(2,1)} %copy-done.4) | copy-start | bytes 4718596
  138.2 57.0 %collective-permute-start.5 = (bf16[256,3072]{1,0:T(8,128)(2,1)}, bf16[256,3072]{1,0:T(8,128)(2,1)}, u32[]{:S(2)}, u32[]{:S(2)}) collective-permute-start(bf16[256,3072]{1,0:T(8,128)(2,1)} %attention.6.refs_0_.refs_4_.refs_6_.refs_3_), channel_id=1, source_target_pairs={{0,2},{2,0},{4,6},{6,4},{8,10},{10,8},{12,14},{14,12},{1,3},{3,1},... | collective-permute-start | bytes 4718600 | tf_op jit(solution)/shard_map/ppermute | solution.py:144
  138.7 68.2 %collective-permute-start.6 = (bf16[256,3072]{1,0:T(8,128)(2,1)S(1)}, bf16[256,3072]{1,0:T(8,128)(2,1)}, u32[]{:S(2)}, u32[]{:S(2)}) collective-permute-start(bf16[256,3072]{1,0:T(8,128)(2,1)S(1)} %copy-done.5), channel_id=1, source_target_pairs={{0,2},{2,0},{4,6},{6,4},{8,10},{10,8},{12,14},{14,12},{1,3},{3,1},... | collective-permute-start | bytes 4718600 | tf_op jit(solution)/shard_map/ppermute | solution.py:144
  140.2 34.4 %collective-permute-start.7 = (bf16[6144,128]{1,0:T(8,128)(2,1)}, bf16[6144,128]{1,0:T(8,128)(2,1)S(1)}, u32[]{:S(2)}, u32[]{:S(2)}) collective-permute-start(bf16[6144,128]{1,0:T(8,128)(2,1)} %collective-permute-done.3.refs_4_.refs_3_), channel_id=1, source_target_pairs={{0,16},{16,0},{1,17},{17,1},{2,18},{18,2},{3,19},{19,3},{4,20},{20... | collective-permute-start | bytes 4718600 | tf_op jit(solution)/shard_map/ppermute | solution.py:148
  141.8 68.7 %collective-permute-start.8 = (bf16[6144,128]{1,0:T(8,128)(2,1)}, bf16[6144,128]{1,0:T(8,128)(2,1)}, u32[]{:S(2)}, u32[]{:S(2)}) collective-permute-start(bf16[6144,128]{1,0:T(8,128)(2,1)} %constant_dynamic-slice_fusion.6), channel_id=1, source_target_pairs={{0,8},{2,10},{4,12},{6,14},{8,0},{10,2},{12,4},{14,6},{1,9},{3,11}... | collective-permute-start | bytes 4718600 | tf_op jit(solution)/shard_map/ppermute | solution.py:144
  141.8 68.9 %collective-permute-start.9 = (bf16[256,3072]{1,0:T(8,128)(2,1)}, bf16[256,3072]{1,0:T(8,128)(2,1)}, u32[]{:S(2)}, u32[]{:S(2)}) collective-permute-start(bf16[256,3072]{1,0:T(8,128)(2,1)} %attention.5.refs_1_.refs_5_.refs_7_.refs_3_), channel_id=1, source_target_pairs={{0,4},{2,6},{4,0},{6,2},{8,12},{10,14},{12,8},{14,10},{1,5},{3,7},... | collective-permute-start | bytes 4718600 | tf_op jit(solution)/shard_map/ppermute | solution.py:144
  174.6 6.3 %collective-permute-start.10 = (bf16[256,1536]{1,0:T(8,128)(2,1)S(1)}, bf16[256,1536]{1,0:T(8,128)(2,1)S(1)}, u32[]{:S(2)}, u32[]{:S(2)}) collective-permute-start(bf16[256,1536]{1,0:T(8,128)(2,1)S(1)} %copy-done.33), channel_id=1, source_target_pairs={{0,1},{1,0},{2,3},{3,2},{4,5},{5,4},{6,7},{7,6},{8,9},{9,8},{10,11... | collective-permute-start | bytes 2359304 | tf_op jit(solution)/shard_map/ppermute | solution.py:148
  210.6 36.3 %collective-permute-start.11 = (bf16[6144,128]{1,0:T(8,128)(2,1)}, bf16[6144,128]{1,0:T(8,128)(2,1)S(1)}, u32[]{:S(2)}, u32[]{:S(2)}) collective-permute-start(bf16[6144,128]{1,0:T(8,128)(2,1)} %collective-permute-done.8.refs_6_.refs_5_), channel_id=1, source_target_pairs={{0,16},{16,0},{1,17},{17,1},{2,18},{18,2},{3,19},{19,3},{4,20},{20... | collective-permute-start | bytes 4718600 | tf_op jit(solution)/shard_map/ppermute | solution.py:148
  211.1 69.5 %collective-permute-start.13 = (bf16[6144,128]{1,0:T(8,128)(2,1)}, bf16[6144,128]{1,0:T(8,128)(2,1)S(1)}, u32[]{:S(2)}, u32[]{:S(2)}) collective-permute-start(bf16[6144,128]{1,0:T(8,128)(2,1)} %constant_dynamic-slice_fusion.5), channel_id=1, source_target_pairs={{0,8},{2,10},{4,12},{6,14},{8,0},{10,2},{12,4},{14,6},{1,9},{3,11}... | collective-permute-start | bytes 4718600 | tf_op jit(solution)/shard_map/ppermute | solution.py:144
  211.5 69.4 %collective-permute-start.14 = (bf16[256,3072]{1,0:T(8,128)(2,1)}, bf16[256,3072]{1,0:T(8,128)(2,1)S(1)}, u32[]{:S(2)}, u32[]{:S(2)}) collective-permute-start(bf16[256,3072]{1,0:T(8,128)(2,1)} %attention.6.refs_0_.refs_4_.refs_6_.refs_3_), channel_id=1, source_target_pairs={{0,4},{2,6},{4,0},{6,2},{8,12},{10,14},{12,8},{14,10},{1,5},{3,7},... | collective-permute-start | bytes 4718600 | tf_op jit(solution)/shard_map/ppermute | solution.py:144
  213.2 67.7 %collective-permute-start.15 = (bf16[256,3072]{1,0:T(8,128)(2,1)}, bf16[256,3072]{1,0:T(8,128)(2,1)}, u32[]{:S(2)}, u32[]{:S(2)}) collective-permute-start(bf16[256,3072]{1,0:T(8,128)(2,1)} %collective-permute-done.refs_0_.refs_2_.refs_1_), channel_id=1, source_target_pairs={{0,2},{2,0},{4,6},{6,4},{8,10},{10,8},{12,14},{14,12},{1,3},{3,1},... | collective-permute-start | bytes 4718600 | tf_op jit(solution)/shard_map/ppermute | solution.py:144
  213.7 68.6 %collective-permute-start.16 = (bf16[256,3072]{1,0:T(8,128)(2,1)}, bf16[256,3072]{1,0:T(8,128)(2,1)}, u32[]{:S(2)}, u32[]{:S(2)}) collective-permute-start(bf16[256,3072]{1,0:T(8,128)(2,1)} %collective-permute-done.9.refs_1_.refs_3_), channel_id=1, source_target_pairs={{0,2},{2,0},{4,6},{6,4},{8,10},{10,8},{12,14},{14,12},{1,3},{3,1},... | collective-permute-start | bytes 4718600 | tf_op jit(solution)/shard_map/ppermute | solution.py:144
  228.5 59.0 %copy-start.31 = (bf16[2,2,192,1024]{3,2,1,0:T(8,128)(2,1)S(1)}, bf16[2,2,192,1024]{3,2,1,0:T(8,128)(2,1)}, u32[]{:S(2)}) copy-start(bf16[2,2,192,1024]{3,2,1,0:T(8,128)(2,1)} %pad_maximum_fusion.2) | copy-start | bytes 4718596
  246.9 2.6 collective-permute-start.12
  282.3 34.6 %collective-permute-start.17 = (bf16[6144,128]{1,0:T(8,128)(2,1)S(1)}, bf16[6144,128]{1,0:T(8,128)(2,1)S(1)}, u32[]{:S(2)}, u32[]{:S(2)}) collective-permute-start(bf16[6144,128]{1,0:T(8,128)(2,1)S(1)} %collective-permute-done.13.refs_6_.refs_7_), channel_id=1, source_target_pairs={{0,16},{16,0},{1,17},{17,1},{2,18},{18,2},{3,19},{19,3},{4,20},{20... | collective-permute-start | bytes 4718600 | tf_op jit(solution)/shard_map/ppermute | solution.py:148
  283.9 69.1 %collective-permute-start.19 = (bf16[6144,128]{1,0:T(8,128)(2,1)}, bf16[6144,128]{1,0:T(8,128)(2,1)}, u32[]{:S(2)}, u32[]{:S(2)}) collective-permute-start(bf16[6144,128]{1,0:T(8,128)(2,1)} %constant_dynamic-slice_fusion.4), channel_id=1, source_target_pairs={{0,8},{2,10},{4,12},{6,14},{8,0},{10,2},{12,4},{14,6},{1,9},{3,11}... | collective-permute-start | bytes 4718600 | tf_op jit(solution)/shard_map/ppermute | solution.py:144
  285.1 67.9 %collective-permute-start.20 = (bf16[256,3072]{1,0:T(8,128)(2,1)S(1)}, bf16[256,3072]{1,0:T(8,128)(2,1)}, u32[]{:S(2)}, u32[]{:S(2)}) collective-permute-start(bf16[256,3072]{1,0:T(8,128)(2,1)S(1)} %copy-done.6), channel_id=1, source_target_pairs={{0,4},{2,6},{4,0},{6,2},{8,12},{10,14},{12,8},{14,10},{1,5},{3,7},... | collective-permute-start | bytes 4718600 | tf_op jit(solution)/shard_map/ppermute | solution.py:144
  286.9 66.1 %collective-permute-start.21 = (bf16[256,3072]{1,0:T(8,128)(2,1)S(1)}, bf16[256,3072]{1,0:T(8,128)(2,1)}, u32[]{:S(2)}, u32[]{:S(2)}) collective-permute-start(bf16[256,3072]{1,0:T(8,128)(2,1)S(1)} %collective-permute-done.14.refs_0_.refs_2_.refs_1_), channel_id=1, source_target_pairs={{0,2},{2,0},{4,6},{6,4},{8,10},{10,8},{12,14},{14,12},{1,3},{3,1},... | collective-permute-start | bytes 4718600 | tf_op jit(solution)/shard_map/ppermute | solution.py:144
  287.4 67.0 %collective-permute-start.22 = (bf16[2,2,192,1024]{3,2,1,0:T(8,128)(2,1)S(1)}, bf16[2,2,192,1024]{3,2,1,0:T(8,128)(2,1)}, u32[]{:S(2)}, u32[]{:S(2)}) collective-permute-start(bf16[2,2,192,1024]{3,2,1,0:T(8,128)(2,1)S(1)} %copy-done.31), channel_id=1, source_target_pairs={{0,2},{2,0},{4,6},{6,4},{8,10},{10,8},{12,14},{14,12},{1,3},{3,1},... | collective-permute-start | bytes 4718600 | tf_op jit(solution)/shard_map/ppermute | solution.py:144
  316.9 2.1 collective-permute-start.18
  354.5 35.1 %collective-permute-start.24 = (bf16[6144,128]{1,0:T(8,128)(2,1)}, bf16[6144,128]{1,0:T(8,128)(2,1)S(1)}, u32[]{:S(2)}, u32[]{:S(2)}) collective-permute-start(bf16[6144,128]{1,0:T(8,128)(2,1)} %collective-permute-done.19.refs_8_.refs_9_), channel_id=1, source_target_pairs={{0,16},{16,0},{1,17},{17,1},{2,18},{18,2},{3,19},{19,3},{4,20},{20... | collective-permute-start | bytes 4718600 | tf_op jit(solution)/shard_map/ppermute | solution.py:148
  356.9 69.4 %collective-permute-start.26 = (bf16[6144,128]{1,0:T(8,128)(2,1)}, bf16[6144,128]{1,0:T(8,128)(2,1)}, u32[]{:S(2)}, u32[]{:S(2)}) collective-permute-start(bf16[6144,128]{1,0:T(8,128)(2,1)} %constant_dynamic-slice_fusion.3), channel_id=1, source_target_pairs={{0,8},{2,10},{4,12},{6,14},{8,0},{10,2},{12,4},{14,6},{1,9},{3,11}... | collective-permute-start | bytes 4718600 | tf_op jit(solution)/shard_map/ppermute | solution.py:144
  357.2 69.0 %collective-permute-start.27 = (bf16[256,3072]{1,0:T(8,128)(2,1)}, bf16[256,3072]{1,0:T(8,128)(2,1)}, u32[]{:S(2)}, u32[]{:S(2)}) collective-permute-start(bf16[256,3072]{1,0:T(8,128)(2,1)} %collective-permute-done.20.refs_1_.refs_3_), channel_id=1, source_target_pairs={{0,2},{2,0},{4,6},{6,4},{8,10},{10,8},{12,14},{14,12},{1,3},{3,1},... | collective-permute-start | bytes 4718600 | tf_op jit(solution)/shard_map/ppermute | solution.py:144
  359.8 68.8 %collective-permute-start.28 = (bf16[4,192,1024]{2,1,0:T(8,128)(2,1)}, bf16[4,192,1024]{2,1,0:T(8,128)(2,1)}, u32[]{:S(2)}, u32[]{:S(2)}) collective-permute-start(bf16[4,192,1024]{2,1,0:T(8,128)(2,1)} %get-tuple-element.175), channel_id=1, source_target_pairs={{0,4},{2,6},{4,0},{6,2},{8,12},{10,14},{12,8},{14,10},{1,5},{3,7},... | collective-permute-start | bytes 4718600 | tf_op jit(solution)/shard_map/ppermute | solution.py:144
  389.6 3.5 collective-permute-start.25
  389.7 30.9 %collective-permute-start.23 = (bf16[256,2048]{1,0:T(8,128)(2,1)S(1)}, bf16[256,2048]{1,0:T(8,128)(2,1)S(1)}, u32[]{:S(2)}, u32[]{:S(2)}) collective-permute-start(bf16[256,2048]{1,0:T(8,128)(2,1)S(1)} %pad_maximum_fusion.4), channel_id=1, source_target_pairs={{0,2},{2,0},{4,6},{6,4},{8,10},{10,8},{12,14},{14,12},{1,3},{3,1},... | collective-permute-start | bytes 3145736 | tf_op jit(solution)/shard_map/ppermute | solution.py:144
  428.6 36.1 %collective-permute-start.35 = (bf16[6144,128]{1,0:T(8,128)(2,1)}, bf16[6144,128]{1,0:T(8,128)(2,1)}, u32[]{:S(2)}, u32[]{:S(2)}) collective-permute-start(bf16[6144,128]{1,0:T(8,128)(2,1)} %collective-permute-done.26.refs_8_), channel_id=1, source_target_pairs={{0,16},{16,0},{1,17},{17,1},{2,18},{18,2},{3,19},{19,3},{4,20},{20... | collective-permute-start | bytes 4718600 | tf_op jit(solution)/shard_map/ppermute | solution.py:148
  430.2 33.7 %collective-permute-start.30 = (bf16[3072,128]{1,0:T(8,128)(2,1)}, bf16[3072,128]{1,0:T(8,128)(2,1)S(1)}, u32[]{:S(2)}, u32[]{:S(2)}) collective-permute-start(bf16[3072,128]{1,0:T(8,128)(2,1)} %get-tuple-element.128), channel_id=1, source_target_pairs={{0,8},{2,10},{4,12},{6,14},{8,0},{10,2},{12,4},{14,6},{1,9},{3,11}... | collective-permute-start | bytes 2359304 | tf_op jit(solution)/shard_map/ppermute | solution.py:144
  430.6 77.3 %collective-permute-start.29 = (bf16[256,2048]{1,0:T(8,128)(2,1)}, bf16[256,2048]{1,0:T(8,128)(2,1)S(1)}, u32[]{:S(2)}, u32[]{:S(2)}) collective-permute-start(bf16[256,2048]{1,0:T(8,128)(2,1)} %product.25), channel_id=1, source_target_pairs={{0,4},{2,6},{4,0},{6,2},{8,12},{10,14},{12,8},{14,10},{1,5},{3,7},... | collective-permute-start | bytes 3145736 | tf_op jit(solution)/shard_map/ppermute | solution.py:144
  463.9 20.4 %collective-permute-start.34 = (bf16[256,2560]{1,0:T(8,128)(2,1)}, bf16[256,2560]{1,0:T(8,128)(2,1)}, u32[]{:S(2)}, u32[]{:S(2)}) collective-permute-start(bf16[256,2560]{1,0:T(8,128)(2,1)} %product.27), channel_id=1, source_target_pairs={{0,1},{1,0},{2,3},{3,2},{4,5},{5,4},{6,7},{7,6},{8,9},{9,8},{10,11... | collective-permute-start | bytes 3932168 | tf_op jit(solution)/shard_map/ppermute | solution.py:148
  463.9 4.5 collective-permute-start.31
  464.7 45.6 %collective-permute-start.36 = (bf16[3072,128]{1,0:T(8,128)(2,1)}, bf16[3072,128]{1,0:T(8,128)(2,1)}, u32[]{:S(2)}, u32[]{:S(2)}) collective-permute-start(bf16[3072,128]{1,0:T(8,128)(2,1)} %get-tuple-element.133), channel_id=1, source_target_pairs={{0,8},{2,10},{4,12},{6,14},{8,0},{10,2},{12,4},{14,6},{1,9},{3,11}... | collective-permute-start | bytes 2359304 | tf_op jit(solution)/shard_map/ppermute | solution.py:144
  464.8 45.5 %collective-permute-start.37 = (bf16[3072,128]{1,0:T(8,128)(2,1)S(1)}, bf16[3072,128]{1,0:T(8,128)(2,1)}, u32[]{:S(2)}, u32[]{:S(2)}) collective-permute-start(bf16[3072,128]{1,0:T(8,128)(2,1)S(1)} %collective-permute-done.30.refs_4_), channel_id=1, source_target_pairs={{0,16},{16,0},{1,17},{17,1},{2,18},{18,2},{3,19},{19,3},{4,20},{20... | collective-permute-start | bytes 2359304 | tf_op jit(solution)/shard_map/ppermute | solution.py:148
  482.1 26.8 %collective-permute-start.32 = (bf16[256,512]{1,0:T(8,128)(2,1)S(1)}, bf16[256,512]{1,0:T(8,128)(2,1)S(1)}, u32[]{:S(2)}, u32[]{:S(2)}) collective-permute-start(bf16[256,512]{1,0:T(8,128)(2,1)S(1)} %get-tuple-element.184), channel_id=1, source_target_pairs={{0,4},{2,6},{4,0},{6,2},{8,12},{10,14},{12,8},{14,10},{1,5},{3,7},... | collective-permute-start | bytes 786440 | tf_op jit(solution)/shard_map/ppermute | solution.py:144
  484.3 25.3 %collective-permute-start.33 = (bf16[256,512]{1,0:T(8,128)(2,1)S(1)}, bf16[256,512]{1,0:T(8,128)(2,1)S(1)}, u32[]{:S(2)}, u32[]{:S(2)}) collective-permute-start(bf16[256,512]{1,0:T(8,128)(2,1)S(1)} %get-tuple-element.183), channel_id=1, source_target_pairs={{0,2},{2,0},{4,6},{6,4},{8,10},{10,8},{12,14},{14,12},{1,3},{3,1},... | collective-permute-start | bytes 786440 | tf_op jit(solution)/shard_map/ppermute | solution.py:144
  510.3 38.9 %collective-permute-start.39 = (bf16[3072,128]{1,0:T(8,128)(2,1)}, bf16[3072,128]{1,0:T(8,128)(2,1)S(1)}, u32[]{:S(2)}, u32[]{:S(2)}) collective-permute-start(bf16[3072,128]{1,0:T(8,128)(2,1)} %collective-permute-done.36.refs_4_), channel_id=1, source_target_pairs={{0,16},{16,0},{1,17},{17,1},{2,18},{18,2},{3,19},{19,3},{4,20},{20... | collective-permute-start | bytes 2359304 | tf_op jit(solution)/shard_map/ppermute | solution.py:148
  511.8 62.6 %collective-permute-start.38 = (bf16[256,2560]{1,0:T(8,128)(2,1)}, bf16[256,2560]{1,0:T(8,128)(2,1)S(1)}, u32[]{:S(2)}, u32[]{:S(2)}) collective-permute-start(bf16[256,2560]{1,0:T(8,128)(2,1)} %product.29), channel_id=1, source_target_pairs={{0,6},{2,4},{4,2},{6,0},{8,14},{10,12},{12,10},{14,8},{1,7},{3,5},... | collective-permute-start | bytes 3932168 | tf_op jit(solution)/shard_map/ppermute | solution.py:144
  557.9 2.2 collective-permute-start.41
  558.0 10.8 %collective-permute-start.40 = (bf16[1024,256]{1,0:T(8,128)(2,1)S(1)}, bf16[1024,256]{1,0:T(8,128)(2,1)S(1)}, u32[]{:S(2)}, u32[]{:S(2)}) collective-permute-start(bf16[1024,256]{1,0:T(8,128)(2,1)S(1)} %copy-done.36), channel_id=1, source_target_pairs={{0,1},{1,0},{2,3},{3,2},{4,5},{5,4},{6,7},{7,6},{8,9},{9,8},{10,11... | collective-permute-start | bytes 1572872 | tf_op jit(solution)/shard_map/ppermute | solution.py:148
  570.9 10.4 %collective-permute-start.42 = (bf16[256,512]{1,0:T(8,128)(2,1)}, bf16[256,512]{1,0:T(8,128)(2,1)}, u32[]{:S(2)}, u32[]{:S(2)}) collective-permute-start(bf16[256,512]{1,0:T(8,128)(2,1)} %get-tuple-element.179), channel_id=1, source_target_pairs={{0,6},{2,4},{4,2},{6,0},{8,14},{10,12},{12,10},{14,8},{1,7},{3,5},... | collective-permute-start | bytes 786440 | tf_op jit(solution)/shard_map/ppermute | solution.py:144
  573.4 12.3 %collective-permute-start.43 = (bf16[256,512]{1,0:T(8,128)(2,1)}, bf16[256,512]{1,0:T(8,128)(2,1)}, u32[]{:S(2)}, u32[]{:S(2)}) collective-permute-start(bf16[256,512]{1,0:T(8,128)(2,1)} %get-tuple-element.180), channel_id=1, source_target_pairs={{0,4},{2,6},{4,0},{6,2},{8,12},{10,14},{12,8},{14,10},{1,5},{3,7},... | collective-permute-start | bytes 786440 | tf_op jit(solution)/shard_map/ppermute | solution.py:144
  573.4 12.7 %collective-permute-start.44 = (bf16[256,512]{1,0:T(8,128)(2,1)}, bf16[256,512]{1,0:T(8,128)(2,1)}, u32[]{:S(2)}, u32[]{:S(2)}) collective-permute-start(bf16[256,512]{1,0:T(8,128)(2,1)} %get-tuple-element.181), channel_id=1, source_target_pairs={{0,2},{2,0},{4,6},{6,4},{8,10},{10,8},{12,14},{14,12},{1,3},{3,1},... | collective-permute-start | bytes 786440 | tf_op jit(solution)/shard_map/ppermute | solution.py:144
  (38 other events, 307.6 us)

commit v5 on v2

--- a/solution.py
+++ b/solution.py
@@ -110,6 +110,26 @@
     )(jnp.stack(offsets).astype(jnp.int32), *pieces)
 
 
+def cut_kernel(places, weight_ref, o_ref):
+    o_ref[...] = weight_ref[...]
+
+
+def cut_out(weight, row, height, column, width, block):
+    return pl.pallas_call(
+        cut_kernel,
+        grid_spec=pltpu.PrefetchScalarGridSpec(
+            num_scalar_prefetch=1,
+            grid=(height // block,),
+            in_specs=[pl.BlockSpec((block, width), lambda n, places: (places[0] + n, places[1]))],
+            out_specs=pl.BlockSpec((block, width), lambda n, places: (n, 0)),
+        ),
+        out_shape=jax.ShapeDtypeStruct((height, width), weight.dtype),
+        compiler_params=pltpu.CompilerParams(vmem_limit_bytes=16 << 20),
+        cost_estimate=LIGHT,
+        name="cut",
+    )(jnp.stack([jnp.int32(row // block), column // width]).astype(jnp.int32), weight)
+
+
 def cache_kernel(page_of, pages_ref, o_ref):
     slots = o_ref.shape[0]
     first = pl.program_id(0) * slots
@@ -148,56 +168,116 @@
     return lax.ppermute(array, axis, [(0, 1), (1, 0)])
 
 
-def product_kernel(*refs, heights, parts, groups, summed):
+def product_kernel(*refs, masks, chunks, segments, groups, summands):
     step = pl.program_id(0)
-    lefts, refs = refs[: heights * parts], refs[heights * parts :]
-    out = refs[-1]
-    rows, depth = lefts[0].shape
-
-    def group_of(rights):
-        def compute():
-            for height in range(heights):
-                total = None
-                for part in range(parts):
-                    span = slice(part * depth, (part + 1) * depth)
-                    right = jnp.concatenate([ref[span, :] for ref in rights], axis=1)
-                    term = jnp.dot(
-                        lefts[height * parts + part][...], right,
-                        preferred_element_type=jnp.float32,
+    parts = 1 + max(part for part, _, _ in segments)
+    count = masks * chunks * parts
+    left_refs, rest = refs[:count], refs[count:]
+    sources, wide = [], []
+    for _, size in groups:
+        taken = max(size, 1)
+        if size:
+            sources.extend(rest[:taken])
+        wide.append(None if size else rest[0])
+        rest = rest[taken:]
+    others, rest = rest[: summands * chunks], rest[summands * chunks :]
+    outs, rest = rest[:chunks], rest[chunks:]
+    held, rest = rest[: len(sources)], rest[len(sources) :]
+    lefts, sems = rest[:-1], rest[-1]
+    rows = left_refs[0].shape[0]
+
+    copies, narrow_copies = [], []
+    for mask in range(masks):
+        mine = []
+        for chunk in range(chunks):
+            block = mask * chunks + chunk
+            for n, (part, start, size) in enumerate(segments):
+                mine.append(
+                    pltpu.make_async_copy(
+                        left_refs[block * parts + part].at[:, start : start + size],
+                        lefts[n].at[block * rows : (block + 1) * rows, :],
+                        sems.at[block * len(segments) + n],
                     )
-                    total = term if total is None else total + term
-                at = slice(height * rows, (height + 1) * rows)
-                if summed:
-                    total = total + refs[-2][at, :].astype(jnp.float32)
-                out[at, :] = total.astype(out.dtype)
-        return compute
-
-    first = 0
-    for steps, count in groups:
-        compute = group_of(refs[:count])
-        refs = refs[count:]
+                )
+        copies.append(mine)
+    used = masks * chunks * len(segments)
+    for n, ref in enumerate(sources):
+        narrow_copies.append(pltpu.make_async_copy(ref, held[n], sems.at[used + n]))
+
+    def start():
+        mine = [copy for group in copies for copy in group]
+        for copy in narrow_copies + mine if groups[0][1] else mine + narrow_copies:
+            copy.start()
+
+    def compute(rights, arrived, first, alone):
+        for copy in arrived:
+            copy.wait()
+        for mask in range(masks):
+            if first == 0:
+                for copy in copies[mask]:
+                    if alone:
+                        copy.wait()
+                    else:
+                        pl.when(step == 0)(copy.wait)
+            total, at = None, 0
+            span = slice(mask * chunks * rows, (mask + 1) * chunks * rows)
+            for n, (_, _, size) in enumerate(segments):
+                right = jnp.concatenate([ref[at : at + size, :] for ref in rights], axis=1)
+                term = jnp.dot(lefts[n][span, :], right, preferred_element_type=jnp.float32)
+                total = term if total is None else total + term
+                at += size
+            span = slice(mask * rows, (mask + 1) * rows)
+            for chunk in range(chunks):
+                result = total[chunk * rows : (chunk + 1) * rows, :]
+                for other in others[chunk::chunks]:
+                    result = result + other[span, :].astype(jnp.float32)
+                outs[chunk][span, :] = result.astype(outs[chunk].dtype)
+
+    if sum(steps for steps, _ in groups) == 1:
+        start()
+    else:
+        pl.when(step == 0)(start)
+    first, at = 0, 0
+    for (steps, size), ref in zip(groups, wide):
+        rights = held[at : at + size] if size else [ref]
+        body = functools.partial(
+            compute, rights, narrow_copies[at : at + size], first, steps == 1
+        )
+        at += size
         if len(groups) == 1:
-            compute()
+            body()
         else:
-            pl.when((step >= first) & (step < first + steps))(compute)
+            pl.when((step >= first) & (step < first + steps))(body)
         first += steps
 
 
-def product(lefts, rights, other=None):
-    rows, depth = lefts[0][0].shape
-    block = 2 * WIDTH
-    operands, specs, groups = [], [], []
-    for left in lefts:
-        for part in left:
-            operands.append(part)
-            specs.append(pl.BlockSpec((rows, depth), lambda n: (0, 0)))
-    first = 0
+def product(blocks, rights, span, summands=(), dtype=jnp.bfloat16):
+    masks, chunks, parts = len(blocks), len(blocks[0]), len(blocks[0][0])
+    rows, depth = blocks[0][0][0].shape
+    segments = []
+    for part in range(parts):
+        low, high = max(span[0] - part * depth, 0), min(span[1] - part * depth, depth)
+        if low < high:
+            segments.append((part, low, high - low))
+    skipped = segments[0][0]
+    segments = [(part - skipped, low, size) for part, low, size in segments]
+    block = 4 * WIDTH
+    anywhere = pl.BlockSpec(memory_space=pl.ANY)
+    operands = [
+        array
+        for mask in blocks
+        for chunk in mask
+        for array in chunk[skipped : skipped + 1 + segments[-1][0]]
+    ]
+    specs = [anywhere] * len(operands)
+    copies = masks * chunks * len(segments)
+    groups, held, first = [], [], 0
     for right in rights:
         if isinstance(right, tuple):
             steps = 1
-            for piece in right:
-                operands.append(piece)
-                specs.append(pl.BlockSpec(piece.shape, lambda n: (0, 0)))
+            operands += right
+            specs += [anywhere] * len(right)
+            held += [pltpu.VMEM(piece.shape, piece.dtype) for piece in right]
             groups.append((1, len(right)))
         else:
             steps = right.shape[1] // block
@@ -208,23 +288,26 @@
                     lambda n, first=first, steps=steps: (0, jnp.clip(n - first, 0, steps - 1)),
                 )
             )
-            groups.append((steps, 1))
+            groups.append((steps, 0))
         first += steps
-    height = rows * len(lefts)
-    out_spec = pl.BlockSpec((height, block), lambda n: (0, n))
-    if other is not None:
-        operands.append(other)
-        specs.append(out_spec)
+    out_spec = pl.BlockSpec((rows * masks, block), lambda n: (0, n))
+    for summand in summands:
+        operands += summand
+        specs += [out_spec] * chunks
+    scratch = [
+        pltpu.VMEM((masks * chunks * rows, size), operands[0].dtype) for _, _, size in segments
+    ]
     return pl.pallas_call(
         functools.partial(
-            product_kernel, heights=len(lefts), parts=len(lefts[0]), groups=groups,
-            summed=other is not None,
+            product_kernel, masks=masks, chunks=chunks, segments=segments, groups=groups,
+            summands=len(summands),
         ),
         grid=(first,),
         in_specs=specs,
-        out_specs=out_spec,
-        out_shape=jax.ShapeDtypeStruct((height, first * block), operands[0].dtype),
-        compiler_params=pltpu.CompilerParams(vmem_limit_bytes=56 << 20),
+        out_specs=[out_spec] * chunks,
+        out_shape=[jax.ShapeDtypeStruct((rows * masks, first * block), dtype)] * chunks,
+        scratch_shapes=held + scratch + [pltpu.SemaphoreType.DMA((copies + len(held),))],
+        compiler_params=pltpu.CompilerParams(vmem_limit_bytes=60 << 20),
         cost_estimate=LIGHT,
         name="product",
     )(*operands)
@@ -300,7 +383,14 @@
     half_cols = own_cols // 2
     kv_width = keys_values.shape[1] // tp_count
 
-    pairs = half_cols // WIDTH
+    narrow = 4
+    parts = 4 if depth % 512 == 0 else 2
+    spans = [(0, depth // 2)] + [
+        (n * depth // parts, (n + 1) * depth // parts) for n in range(parts // 2, parts)
+    ]
+    cuts = [(0, depth, n * WIDTH, WIDTH) for n in range(narrow)] + [
+        (low, high - low, narrow * WIDTH, half_cols - narrow * WIDTH) for low, high in spans
+    ]
 
     gate = ()
 
@@ -309,20 +399,19 @@
 
     def cut(n, *earlier):
         weight = after(out_weight, *earlier) if earlier else out_weight
-        return lax.dynamic_slice(
-            weight, (jnp.int32(0), grp_here * half_cols + n * WIDTH), (depth, WIDTH)
+        row, height, column, width = cuts[n]
+        return cut_out(
+            weight, row, height, grp_here * half_cols + column, width, depth // parts
         )
 
     pieces, segments, offsets = [], [], []
     own_columns = [(own_cols, lambda inst: inst * own_cols)]
 
-    def pair_columns(first, last):
+    def far_columns(first, last):
         return [
             (
-                WIDTH,
-                lambda inst, n=n, half=half: (
-                    (inst ^ FAR) * own_cols + half * half_cols + n * WIDTH
-                ),
+                cuts[n][3],
+                lambda inst, n=n, half=half: (inst ^ FAR) * own_cols + half * half_cols + cuts[n][2],
             )
             for n in range(first, last)
             for half in (grp_here, 1 - grp_here)
@@ -340,30 +429,27 @@
     kv_parts = 2 if local_heads % (2 * (NH // KVH)) == 0 else 1
     blocks = {mask: [] for mask in MASKS}
 
-    def begin_sum(masks, rights):
-        lefts = [list(blocks[mask]) for mask in masks]
-        lefts[0][0] = gated(lefts[0][0])
-        return masks, rights, product([left[:kv_parts] for left in lefts], rights)
-
-    def end_sum(begun, *earlier):
-        masks, rights, given = begun
-        given = after(given, *earlier) if earlier else given
+    def products(masks, rights, span=(0, depth), summands=(), dtype=jnp.bfloat16):
+        groups = []
+        for mask in masks:
+            rows = blocks[mask]
+            groups.append([rows[n : n + kv_parts] for n in range(0, len(rows), kv_parts)])
+        groups[0][0] = [gated(array) for array in groups[0][0]]
+        return product(groups, rights, span, summands, dtype)
+
+    def finish(totals, masks, *earlier):
+        given = after(totals[0], *earlier) if earlier else totals[0]
+        rows = given.shape[0] // len(masks)
         if tp_count == 2:
-            lefts = [blocks[mask][kv_parts:] for mask in masks]
-            total = product(lefts, rights, swap(given, "tp"))
-        else:
-            total = given
-        rows = total.shape[0] // len(masks)
-        shares = {mask: total[n * rows : (n + 1) * rows] for n, mask in enumerate(masks)}
-        if tp_count != 2:
-            for mask in masks:
-                shares[mask] = lax.psum_scatter(
-                    shares[mask], "tp", scatter_dimension=0, tiled=True
-                )
-        return total, shares
-
-    def group_sum(masks, rights, *earlier):
-        return end_sum(begin_sum(masks, rights), *earlier)
+            other = swap(given, "tp")
+            total = (totals[1].astype(jnp.float32) + other.astype(jnp.float32)).astype(other.dtype)
+            return {mask: total[n * rows : (n + 1) * rows] for n, mask in enumerate(masks)}
+        return {
+            mask: lax.psum_scatter(
+                given[n * rows : (n + 1) * rows], "tp", scatter_dimension=0, tiled=True
+            )
+            for n, mask in enumerate(masks)
+        }
 
     sliced, along, across = [cut(0)], [], []
     along.append(hop(sliced[0], FAR))
@@ -391,20 +477,11 @@
         return tuple(sent)
 
     moved = spread(NEXT, own[:1], NEXT) + spread(SIDE, own[:2], SIDE)
-    for n in range(1, pairs):
+    for n in range(1, len(cuts)):
         ready = cut(n, ready)
         sliced.append(ready)
-    gate = moved + (along[0], held_far, ready)
-
-    def weights():
-        n = len(across)
-        across.append(swap(gated(along[n]), "grp"))
-        if n + 1 < pairs:
-            along.append(hop(gated(sliced[n + 1]), FAR))
-        return (across[-1], along[-1])
-
-    moved = weights() + spread(NEXT, own[1:2], NEXT) + spread(SIDE, own[2:], SIDE)
-    held_far = gated(held_far)
+
+    held_far = after(held_far, ready)
     pages_given, pages_kept = (
         jnp.stack(
             [
@@ -417,44 +494,64 @@
         )
         for residues in ([1 - side_here, 3 - side_here], [side_here, 2 + side_here])
     )
-    ready, own_shares = group_sum((0,), [out_weight], moved[0])
-    gate = moved + (pages_given, pages_kept, ready)
+    gate = moved + (along[0], pages_given, pages_kept)
+
+    def weights():
+        n = len(across)
+        across.append(swap(gated(along[n]), "grp"))
+        along.append(hop(gated(sliced[n + 1]), FAR))
+        return (across[-1], along[-1])
+
+    moved = weights() + spread(NEXT, own[1:2], NEXT) + spread(SIDE, own[2:], SIDE)
+    own_shares = finish(products((0,), [out_weight]), (0,), moved[0])
+    gate = moved + (own_shares[0],)
 
     near = blocks[NEXT]
     moved = weights() + spread(NEXT, own[2:3], NEXT) + spread(NEXT | SIDE, near[:2], SIDE)
-    ready, shares = group_sum((SIDE,), [out_weight], moved[0])
-    own_shares.update(shares)
-    gate = moved + (ready,)
-
-    def pair(n):
-        return (along[n], across[n])
+    own_shares.update(finish(products((SIDE,), [out_weight]), (SIDE,), moved[0]))
+    gate = moved + (own_shares[SIDE],)
+
+    def two_pairs(n):
+        return (along[n], across[n], along[n + 1], across[n + 1])
 
     moved = weights() + spread(NEXT, own[3:], NEXT) + spread(NEXT | SIDE, near[2:3], SIDE)
     pages_side = hop(gated(pages_given), SIDE)
-    ready, shares = group_sum((0, SIDE), [pair(0), pair(1)], moved[0])
-    gate = moved + (pages_side, ready)
-
-    first_columns = own_columns + pair_columns(0, 2)
+    shares = finish(products((0, SIDE), [two_pairs(0)]), (0, SIDE), moved[0])
+    gate = moved + (pages_side, shares[0])
+
+    first_columns = own_columns + far_columns(0, 2)
     moved = weights() + spread(NEXT | SIDE, near[3:], SIDE)
-    moved += (
-        hand_out(SIDE, gated(jnp.concatenate([own_shares[SIDE], shares[SIDE]], axis=1)), first_columns),
-    )
+    side_share = jnp.concatenate([own_shares[SIDE], shares[SIDE]], axis=1)
     hand_out(0, own_shares[0], own_columns)
-    hand_out(0, shares[0], pair_columns(0, 2))
+    hand_out(0, shares[0], far_columns(0, 2))
     pages = gated(jnp.concatenate([pages_kept, pages_side], axis=0))
     pages_next = hop(
         lax.dynamic_index_in_dim(pages, 1 - next_here, axis=1, keepdims=False), NEXT
     )
     pages = lax.dynamic_index_in_dim(pages, next_here, axis=1, keepdims=False)
-    ready, shares = group_sum((NEXT,), [out_weight, pair(0), pair(1)], moved[0])
-    gate = moved + (pages_next, ready)
-
-    moved = weights() + (hand_out(NEXT, gated(shares[NEXT]), first_columns),)
-    begun = begin_sum((NEXT | SIDE,), [out_weight, pair(0), pair(1), pair(2), pair(3)])
-    begun_near = begin_sum((SIDE, NEXT, 0), [pair(2), pair(3)])
-    far_shares = end_sum(begun, begun_near[2], *moved)[1]
-    shares = end_sum(begun_near, *moved)[1]
-    pages = jnp.concatenate([pages, gated(pages_next)], axis=0)
+    begun = products((NEXT,), [out_weight, two_pairs(0)])
+    shares = finish(begun, (NEXT,))
+    begun_near = products((SIDE, NEXT, 0), [after(two_pairs(2), begun[0])])
+    gate = moved + (pages_next, begun_near[0])
+
+    moved = weights() + (
+        hand_out(NEXT, gated(shares[NEXT]), first_columns),
+        hand_out(SIDE, gated(side_share), first_columns),
+    )
+    begun = products((NEXT | SIDE,), [out_weight, two_pairs(0), two_pairs(2)])
+    near_shares = finish(begun_near, (SIDE, NEXT, 0), begun[0], moved[1])
+    far_shares = finish(begun, (NEXT | SIDE,), begun[0], moved[1])
+    gate = moved
+    for n in range(narrow + 2, len(cuts)):
+        moved += weights()
+        gate = moved
+    far_share = hand_out(
+        NEXT | SIDE, far_shares[NEXT | SIDE], own_columns + far_columns(0, 4)
+    )
+    moved += tuple(
+        hand_out(mask, near_shares[mask], far_columns(2, 4)) for mask in (NEXT, SIDE, 0)
+    )
+    pages = jnp.concatenate([pages, after(pages_next, near_shares[0])], axis=0)
     order = [mask ^ far for mask in (0, SIDE) for far in (0, FAR)]
     order = order + [at ^ NEXT for at in order]
     block_of = jnp.asarray([order.index(i) for i in range(inst_count)], jnp.int32)
@@ -463,20 +560,23 @@
     lens = jnp.take(pages[:, limit * PAGE, :REQ_INST].astype(jnp.int32), block_of, axis=0)
     page_of = slot_pages(lens, placement, page_table, block_of, limit)
     cache = cache_of(pages.reshape(-1, kv_width), page_of)
-    gate = moved + (begun_near[2],)
-
-    moved = weights()
-    hand_out(NEXT | SIDE, gated(far_shares[NEXT | SIDE]), own_columns + pair_columns(0, 4))
-    for mask in (NEXT, SIDE, 0):
-        hand_out(mask, gated(shares[mask]), pair_columns(2, 4))
+    gate = moved + (cache, far_shares[NEXT | SIDE])
+
+    across.append(swap(gated(along[-1]), "grp"))
     masks = (NEXT | SIDE, NEXT, SIDE, 0)
-    ready, shares = group_sum(masks, [pair(4)])
+    sums = []
+    for n, span in enumerate(spans):
+        last = n == len(spans) - 1
+        if last:
+            gate = (far_share,)
+        rights = (along[narrow + n], across[narrow + n])
+        sums = [
+            products(masks, [rights], span, sums, jnp.bfloat16 if last else jnp.float32)
+        ]
+    sums = sums[0]
+    shares = finish(sums, masks)
     for mask in masks:
-        hand_out(mask, shares[mask], pair_columns(4, 5))
-    gate = moved + (ready,)
-    ready, shares = group_sum(masks, [pair(5)])
-    for mask in masks:
-        hand_out(mask, shares[mask], pair_columns(5, 6))
+        hand_out(mask, shares[mask], far_columns(narrow, narrow + 1))
     projected = place(pieces, segments, offsets, inst_count * own_cols)
     return (projected, cache)
 

time: 611 us -> 577 us (0.944)
  Pallas kernels: 233 us -> 187 us
  other arithmetic: 11.5 us -> 28.2 us
  waiting for transfers between devices: 260 us -> 250 us
  local copies, waits for them, and re-layouts: 37.3 us -> 45.8 us
    pallas_call x16, Pallas kernels: 201 us -> 152 us  [the longest x9 142 us: product(): pl.pallas_call(functools.partial(product_kernel, masks=masks, chunks=chun...]
    unnamed x70, local copies, waits for them, and re-layouts: 13.3 us -> 37.6 us
    dynamic_slice x6 -> x0, local copies, waits for them, and re-layouts: 16.4 us -> none  [cut(): lax.dynamic_slice(weight, (jnp.int32(0), grp_here * half_cols + n * WIDTH...]
    convert_element_type x0 -> x7, other arithmetic: none -> 13.4 us  [finish(): (totals[1].astype(jnp.float32) + other.astype(jnp.float32)).astype(other....]
    ppermute x14, waiting for transfers between devices: 66 us -> 57 us  [swap(): return lax.ppermute(array, axis, [(0, 1), (1, 0)])]
    ppermute x32 -> x30, waiting for transfers between devices: 194 us -> 193 us  [hop(): return lax.ppermute(array, 'inst', [(i, i ^ mask) for i in range(count)])]
    ppermute x32 -> x30, starting transfers between devices: 39 us -> 38.7 us  [hop(): return lax.ppermute(array, 'inst', [(i, i ^ mask) for i in range(count)])]
  transfers between devices with their start and end apart: 46 -> 44, of which waited for: 24 -> 28; matrix products, arithmetic and copies ran while one was open for 6% -> 7% of each run, Pallas kernels for 38% -> 30%
where the time goes in v5:
time: 577 us; the launch traced here: 568 us
  waiting for transfers between devices  250 us (43%)
  Pallas kernels  187 us (32%)
  starting transfers between devices  46 us (8%)
  local copies, waits for them, and re-layouts  45.8 us (8%)
  other arithmetic  28.2 us (5%)
  matrix products  9.99 us (2%)
    ppermute x30, waiting for transfers between devices, hop(): return lax.ppermute(array, 'inst', [(i, i ^ mask) for i in range(count)])  193 us
    pallas_call x9, Pallas kernels, product(): pl.pallas_call(functools.partial(product_kernel, masks=masks, chunks=chun...  142 us
    ppermute x14, waiting for transfers between devices, swap(): return lax.ppermute(array, axis, [(0, 1), (1, 0)])  57 us
    ppermute x30, starting transfers between devices, hop(): return lax.ppermute(array, 'inst', [(i, i ^ mask) for i in range(count)])  38.7 us
    unnamed x70, local copies, waits for them, and re-layouts  37.6 us
    pallas_call x4, Pallas kernels, attention(): pl.pallas_call(functools.partial(attention_kernel, heads=heads, row_block...  24.7 us
    convert_element_type x7, other arithmetic, finish(): (totals[1].astype(jnp.float32) + other.astype(jnp.float32)).astype(other....  13.4 us
  transfers between devices with their start and end apart: 44, of which 28 were waited for; matrix products, arithmetic and copies ran while one was open for 7% of the time, Pallas kernels for 30%

profile of v5, /device:TPU:0, one launch (start us, length us, event | category | flops | bytes accessed | tf_op | source)
XLA Modules:
  0.0 568.0 jit_solution(6896177278867143283)
XLA Ops:
  1.5 6.4 %copy-done.1 = bf16[6144,1536]{1,0:T(8,128)(2,1)S(1)} copy-done((bf16[6144,1536]{1,0:T(8,128)(2,1)S(1)}, bf16[6144,1536]{1,0:T(8,128)(2,1)}, u32[]{:S(2)}) %copy-start.1) | copy-done | bytes 18874392
  13.7 4.0 collective-permute-start.4
  18.0 2.8 copy-done.5
  20.8 6.4 %attention.4.refs_0_.refs_8_.refs_6_ = bf16[256,3072]{1,0:T(8,128)(2,1)} custom-call(s32[6]{0:T(128)S(1)} %add_add_fusion.1.info, bf16[512,6144]{1,0:T(8,128)(2,1)S(1)} %copy-done.5, bf16[512,2048]{1,0:T(8,128)(2,1)S(1)} %copy-done.4, bf16[512,2048]{1,0:T(8,128)(2,1)S(1)} %copy-done.4), custom_call_target="tpu_custom_call" | custom-call | tf_op jit(solution)/shard_map/attention/pallas_call | solution.py:62
  30.7 2.8 copy-done.6
  33.5 6.4 %attention.5.refs_1_.refs_9_.refs_6_ = bf16[256,3072]{1,0:T(8,128)(2,1)} custom-call(s32[6]{0:T(128)S(1)} %get-tuple-element.228.info, bf16[512,6144]{1,0:T(8,128)(2,1)S(1)} %copy-done.6, bf16[512,2048]{1,0:T(8,128)(2,1)S(1)} %copy-done.4, bf16[512,2048]{1,0:T(8,128)(2,1)S(1)} %copy-done.4), custom_call_target="tpu_custom_call" | custom-call | tf_op jit(solution)/shard_map/attention/pallas_call | solution.py:62
  40.5 2.8 copy-done.7
  43.2 6.3 %attention.6.refs_2_.refs_10_.refs_7_ = bf16[256,3072]{1,0:T(8,128)(2,1)} custom-call(s32[6]{0:T(128)S(1)} %get-tuple-element.227.info, bf16[512,6144]{1,0:T(8,128)(2,1)S(1)} %copy-done.7, bf16[512,2048]{1,0:T(8,128)(2,1)S(1)} %copy-done.4, bf16[512,2048]{1,0:T(8,128)(2,1)S(1)} %copy-done.4), custom_call_target="tpu_custom_call" | custom-call | tf_op jit(solution)/shard_map/attention/pallas_call | solution.py:62
  49.6 5.5 attention.7.refs_3_.refs_11_.refs_7_
  56.3 6.4 %copy-done.2 = bf16[6144,1536]{1,0:T(8,128)(2,1)S(1)} copy-done((bf16[6144,1536]{1,0:T(8,128)(2,1)S(1)}, bf16[6144,1536]{1,0:T(8,128)(2,1)}, u32[]{:S(2)}) %copy-start.2) | copy-done | bytes 18874392
  63.8 6.4 %copy-done.3 = bf16[6144,1536]{1,0:T(8,128)(2,1)S(1)} copy-done((bf16[6144,1536]{1,0:T(8,128)(2,1)S(1)}, bf16[6144,1536]{1,0:T(8,128)(2,1)}, u32[]{:S(2)}) %copy-start.3) | copy-done | bytes 18874392
  88.9 2.9 convolution_convert_fusion.1
  91.8 3.1 convolution_convert_fusion
  98.3 34.2 %collective-permute-done.3.refs_8_.refs_5_ = bf16[6144,128]{1,0:T(8,128)(2,1)} collective-permute-done((bf16[6144,128]{1,0:T(8,128)(2,1)}, bf16[6144,128]{1,0:T(8,128)(2,1)}, u32[]{:S(2)}, u32[]{:S(2)}) %collective-permute-start.3) | collective-permute-done | bytes 1572896 | tf_op jit(solution)/shard_map/ppermute | solution.py:164
  134.8 3.4 collective-permute-start.7
  140.2 17.7 %product.9 = (bf16[256,1536]{1,0:T(8,128)(2,1)}, bf16[256,1536]{1,0:T(8,128)(2,1)}) custom-call(bf16[256,3072]{1,0:T(8,128)(2,1)} %attention.4.refs_0_.refs_8_.refs_6_, bf16[256,3072]{1,0:T(8,128)(2,1)} %attention.5.refs_1_.refs_9_.refs_6_, bf16[256,3072]{1,0:T(8,128)(2,1)} %attention.6.refs_2_.refs_10_.refs_7_, bf16[256,3072]{1,0:T(8,128)(2,1)} %copy-done.8, ...), custom_call_target="tpu_custom_call" | custom-call | tf_op jit(solution)/shard_map/product/pallas_call | solution.py:300
  157.9 10.6 %collective-permute-done.5.refs_9_.refs_6_ = bf16[6144,128]{1,0:T(8,128)(2,1)} collective-permute-done((bf16[6144,128]{1,0:T(8,128)(2,1)}, bf16[6144,128]{1,0:T(8,128)(2,1)}, u32[]{:S(2)}, u32[]{:S(2)}) %collective-permute-start.5) | collective-permute-done | bytes 1572896 | tf_op jit(solution)/shard_map/ppermute | solution.py:168
  168.5 2.5 collective-permute-done.6
  172.3 30.8 %collective-permute-done.8.refs_1_.refs_5_.refs_2_ = bf16[256,3072]{1,0:T(8,128)(2,1)} collective-permute-done((bf16[256,3072]{1,0:T(8,128)(2,1)}, bf16[256,3072]{1,0:T(8,128)(2,1)}, u32[]{:S(2)}, u32[]{:S(2)}) %collective-permute-start.8) | collective-permute-done | bytes 1572896 | tf_op jit(solution)/shard_map/ppermute | solution.py:164
  203.1 2.9 collective-permute-done.7.refs_10_.refs_7_
  211.5 17.8 %product.10 = (bf16[256,1536]{1,0:T(8,128)(2,1)}, bf16[256,1536]{1,0:T(8,128)(2,1)}) custom-call(bf16[256,3072]{1,0:T(8,128)(2,1)} %collective-permute-done.1.refs_0_.refs_4_, bf16[256,3072]{1,0:T(8,128)(2,1)} %collective-permute-done.2.refs_1_.refs_5_.refs_4_, bf16[256,3072]{1,0:T(8,128)(2,1)} %collective-permute-done.9.refs_2_.refs_6_.refs_5_, ...), custom_call_target="tpu_custom_call" | custom-call | tf_op jit(solution)/shard_map/product/pallas_call | solution.py:300
  229.4 13.2 %collective-permute-done.11.refs_11_.refs_8_ = bf16[6144,128]{1,0:T(8,128)(2,1)} collective-permute-done((bf16[6144,128]{1,0:T(8,128)(2,1)}, bf16[6144,128]{1,0:T(8,128)(2,1)}, u32[]{:S(2)}, u32[]{:S(2)}) %collective-permute-start.11) | collective-permute-done | bytes 1572896 | tf_op jit(solution)/shard_map/ppermute | solution.py:168
  242.5 2.5 collective-permute-done.16
  247.3 30.1 %collective-permute-done.12.refs_12_.refs_9_ = bf16[6144,128]{1,0:T(8,128)(2,1)} collective-permute-done((bf16[6144,128]{1,0:T(8,128)(2,1)}, bf16[6144,128]{1,0:T(8,128)(2,1)}, u32[]{:S(2)}, u32[]{:S(2)}) %collective-permute-start.12) | collective-permute-done | bytes 1572896 | tf_op jit(solution)/shard_map/ppermute | solution.py:164
  284.4 12.4 %product.11 = (bf16[512,512]{1,0:T(8,128)(2,1)}, bf16[512,512]{1,0:T(8,128)(2,1)}) custom-call(bf16[256,3072]{1,0:T(8,128)(2,1)} %attention.4.refs_0_.refs_8_.refs_6_, bf16[256,3072]{1,0:T(8,128)(2,1)} %attention.5.refs_1_.refs_9_.refs_6_, bf16[256,3072]{1,0:T(8,128)(2,1)} %attention.6.refs_2_.refs_10_.refs_7_, bf16[256,3072]{1,0:T(8,128)(2,1)} %copy-done.8, ...), custom_call_target="tpu_custom_call" | custom-call | tf_op jit(solution)/shard_map/product/pallas_call | solution.py:300
  296.8 17.2 %collective-permute-done.17.refs_13_.refs_10_ = bf16[6144,128]{1,0:T(8,128)(2,1)} collective-permute-done((bf16[6144,128]{1,0:T(8,128)(2,1)}, bf16[6144,128]{1,0:T(8,128)(2,1)}, u32[]{:S(2)}, u32[]{:S(2)}) %collective-permute-start.17) | collective-permute-done | bytes 1572896 | tf_op jit(solution)/shard_map/ppermute | solution.py:168
  314.0 3.0 collective-permute-done.22
  320.9 29.0 %collective-permute-done.19.refs_14_.refs_11_ = bf16[6144,128]{1,0:T(8,128)(2,1)} collective-permute-done((bf16[6144,128]{1,0:T(8,128)(2,1)}, bf16[6144,128]{1,0:T(8,128)(2,1)}, u32[]{:S(2)}, u32[]{:S(2)}) %collective-permute-start.19) | collective-permute-done | bytes 1572896 | tf_op jit(solution)/shard_map/ppermute | solution.py:164
  356.0 21.5 %product.12 = (bf16[256,2048]{1,0:T(8,128)(2,1)}, bf16[256,2048]{1,0:T(8,128)(2,1)}) custom-call(bf16[256,3072]{1,0:T(8,128)(2,1)} %collective-permute-done.refs_0_.refs_4_.refs_2_, bf16[256,3072]{1,0:T(8,128)(2,1)} %collective-permute-done.8.refs_1_.refs_5_.refs_2_, bf16[256,3072]{1,0:T(8,128)(2,1)} %collective-permute-done.13.refs_2_.refs_6_.refs_3_, ...), custom_call_target="tpu_custom_call" | custom-call | tf_op jit(solution)/shard_map/product/pallas_call | solution.py:300
  378.3 8.3 %collective-permute-done.24.refs_15_.refs_12_ = bf16[6144,128]{1,0:T(8,128)(2,1)} collective-permute-done((bf16[6144,128]{1,0:T(8,128)(2,1)}, bf16[6144,128]{1,0:T(8,128)(2,1)}, u32[]{:S(2)}, u32[]{:S(2)}) %collective-permute-start.24) | collective-permute-done | bytes 1572896 | tf_op jit(solution)/shard_map/ppermute | solution.py:168
  386.6 16.1 %product.13 = (bf16[768,512]{1,0:T(8,128)(2,1)}, bf16[768,512]{1,0:T(8,128)(2,1)}) custom-call(bf16[256,3072]{1,0:T(8,128)(2,1)} %collective-permute-done.1.refs_0_.refs_4_, bf16[256,3072]{1,0:T(8,128)(2,1)} %collective-permute-done.2.refs_1_.refs_5_.refs_4_, bf16[256,3072]{1,0:T(8,128)(2,1)} %collective-permute-done.9.refs_2_.refs_6_.refs_5_, ...), custom_call_target="tpu_custom_call" | custom-call | tf_op jit(solution)/shard_map/product/pallas_call | solution.py:300
  402.7 19.8 %collective-permute-done.27 = bf16[4,192,1024]{2,1,0:T(8,128)(2,1)} collective-permute-done((bf16[4,192,1024]{2,1,0:T(8,128)(2,1)}, bf16[4,192,1024]{2,1,0:T(8,128)(2,1)}, u32[]{:S(2)}, u32[]{:S(2)}) %collective-permute-start.27) | collective-permute-done | bytes 1572896 | tf_op jit(solution)/shard_map/ppermute | solution.py:164
  426.4 2.5 add_convert_fusion.2
  428.9 2.5 collective-permute-start.28
  432.0 25.1 %product.14 = (bf16[256,2560]{1,0:T(8,128)(2,1)}, bf16[256,2560]{1,0:T(8,128)(2,1)}) custom-call(bf16[256,3072]{1,0:T(8,128)(2,1)} %collective-permute-done.14.refs_0_, bf16[256,3072]{1,0:T(8,128)(2,1)} %collective-permute-done.15.refs_1_.refs_0_, bf16[256,3072]{1,0:T(8,128)(2,1)} %collective-permute-done.21.refs_2_.refs_1_, ...), custom_call_target="tpu_custom_call" | custom-call | tf_op jit(solution)/shard_map/product/pallas_call | solution.py:300
  460.3 7.9 %collective-permute-done.28.refs_2_ = bf16[256,2048]{1,0:T(8,128)(2,1)S(1)} collective-permute-done((bf16[256,2048]{1,0:T(8,128)(2,1)}, bf16[256,2048]{1,0:T(8,128)(2,1)S(1)}, u32[]{:S(2)}, u32[]{:S(2)}) %collective-permute-start.28) | collective-permute-done | bytes 1048608 | tf_op jit(solution)/shard_map/ppermute | solution.py:164
  478.6 2.9 add_convert_fusion
  484.3 4.5 cache.1
  489.5 4.6 collective-permute-done.34.refs_5_
  494.8 7.9 %collective-permute-done.37.refs_8_ = bf16[1536,256]{1,0:T(8,128)(2,1)} collective-permute-done((bf16[1536,256]{1,0:T(8,128)(2,1)}, bf16[1536,256]{1,0:T(8,128)(2,1)}, u32[]{:S(2)}, u32[]{:S(2)}) %collective-permute-start.37) | collective-permute-done | bytes 786464 | tf_op jit(solution)/shard_map/ppermute | solution.py:164
  503.2 12.1 %product.15 = (f32[1024,512]{1,0:T(8,128)}, f32[1024,512]{1,0:T(8,128)}) custom-call(bf16[256,3072]{1,0:T(8,128)(2,1)} %collective-permute-done.14.refs_0_, bf16[256,3072]{1,0:T(8,128)(2,1)} %collective-permute-done.21.refs_2_.refs_1_, bf16[256,3072]{1,0:T(8,128)(2,1)} %collective-permute-done.refs_0_.refs_4_.refs_2_, ...), custom_call_target="tpu_custom_call" | custom-call | tf_op jit(solution)/shard_map/product/pallas_call | solution.py:300
  515.2 10.0 %product.16 = (f32[1024,512]{1,0:T(8,128)}, f32[1024,512]{1,0:T(8,128)}) custom-call(bf16[256,3072]{1,0:T(8,128)(2,1)} %collective-permute-done.15.refs_1_.refs_0_, bf16[256,3072]{1,0:T(8,128)(2,1)} %collective-permute-done.26.refs_3_.refs_1_, bf16[256,3072]{1,0:T(8,128)(2,1)} %collective-permute-done.8.refs_1_.refs_5_.refs_2_, ...), custom_call_target="tpu_custom_call" | custom-call | tf_op jit(solution)/shard_map/product/pallas_call | solution.py:300
  527.2 9.4 %product.17 = (bf16[1024,512]{1,0:T(8,128)(2,1)}, bf16[1024,512]{1,0:T(8,128)(2,1)}) custom-call(bf16[256,3072]{1,0:T(8,128)(2,1)} %collective-permute-done.15.refs_1_.refs_0_, bf16[256,3072]{1,0:T(8,128)(2,1)} %collective-permute-done.26.refs_3_.refs_1_, bf16[256,3072]{1,0:T(8,128)(2,1)} %collective-permute-done.8.refs_1_.refs_5_.refs_2_, ...), custom_call_target="tpu_custom_call" | custom-call | tf_op jit(solution)/shard_map/product/pallas_call | solution.py:300
  536.6 2.9 collective-permute-done.40
  542.4 3.1 collective-permute-start.41
  545.6 5.1 collective-permute-done.43.refs_10_
  551.9 5.5 collective-permute-done.41.refs_8_
  562.5 5.0 place.1
  (214 shorter events, 100.4 us)
Async XLA Ops:
  0.6 458.9 %copy-start = (s32[32,16]{0,1:T(8,128)S(1)}, s32[32,16]{0,1:T(8,128)}, u32[]{:S(2)}) copy-start(s32[32,16]{0,1:T(8,128)} %param.14) | copy-start | bytes 6148
  13.7 66.0 %collective-permute-start.4 = (bf16[528,1024]{1,0:T(8,128)(2,1)}, bf16[528,1024]{1,0:T(8,128)(2,1)}, u32[]{:S(2)}, u32[]{:S(2)}) collective-permute-start(bf16[528,1024]{1,0:T(8,128)(2,1)} %fusion.1), channel_id=1, source_target_pairs={{0,8},{2,10},{4,12},{6,14},{8,0},{10,2},{12,4},{14,6},{1,9},{3,11}... | collective-permute-start | bytes 3244040 | tf_op jit(solution)/shard_map/ppermute | solution.py:164
  27.2 69.9 %collective-permute-start.1 = (bf16[256,3072]{1,0:T(8,128)(2,1)}, bf16[256,3072]{1,0:T(8,128)(2,1)}, u32[]{:S(2)}, u32[]{:S(2)}) collective-permute-start(bf16[256,3072]{1,0:T(8,128)(2,1)} %attention.4.refs_0_.refs_8_.refs_6_), channel_id=1, source_target_pairs={{0,2},{2,0},{4,6},{6,4},{8,10},{10,8},{12,14},{14,12},{1,3},{3,1},... | collective-permute-start | bytes 4718600 | tf_op jit(solution)/shard_map/ppermute | solution.py:164
  28.7 69.6 %collective-permute-start = (bf16[256,3072]{1,0:T(8,128)(2,1)}, bf16[256,3072]{1,0:T(8,128)(2,1)}, u32[]{:S(2)}, u32[]{:S(2)}) collective-permute-start(bf16[256,3072]{1,0:T(8,128)(2,1)} %attention.4.refs_0_.refs_8_.refs_6_), channel_id=1, source_target_pairs={{0,4},{2,6},{4,0},{6,2},{8,12},{10,14},{12,8},{14,10},{1,5},{3,7},... | collective-permute-start | bytes 4718600 | tf_op jit(solution)/shard_map/ppermute | solution.py:164
  30.3 102.3 %collective-permute-start.3 = (bf16[6144,128]{1,0:T(8,128)(2,1)}, bf16[6144,128]{1,0:T(8,128)(2,1)}, u32[]{:S(2)}, u32[]{:S(2)}) collective-permute-start(bf16[6144,128]{1,0:T(8,128)(2,1)} %cut.7), channel_id=1, source_target_pairs={{0,8},{2,10},{4,12},{6,14},{8,0},{10,2},{12,4},{14,6},{1,9},{3,11}... | collective-permute-start | bytes 4718600 | tf_op jit(solution)/shard_map/ppermute | solution.py:164
  39.9 57.2 %collective-permute-start.2 = (bf16[256,3072]{1,0:T(8,128)(2,1)}, bf16[256,3072]{1,0:T(8,128)(2,1)}, u32[]{:S(2)}, u32[]{:S(2)}) collective-permute-start(bf16[256,3072]{1,0:T(8,128)(2,1)} %attention.5.refs_1_.refs_9_.refs_6_), channel_id=1, source_target_pairs={{0,2},{2,0},{4,6},{6,4},{8,10},{10,8},{12,14},{14,12},{1,3},{3,1},... | collective-permute-start | bytes 4718600 | tf_op jit(solution)/shard_map/ppermute | solution.py:164
  91.8 47.9 %copy-start.9 = (bf16[256,3072]{1,0:T(8,128)(2,1)S(1)}, bf16[256,3072]{1,0:T(8,128)(2,1)}, u32[]{:S(2)}) copy-start(bf16[256,3072]{1,0:T(8,128)(2,1)} %copy-done.8) | copy-start | bytes 4718596
  132.6 35.9 %collective-permute-start.5 = (bf16[6144,128]{1,0:T(8,128)(2,1)}, bf16[6144,128]{1,0:T(8,128)(2,1)}, u32[]{:S(2)}, u32[]{:S(2)}) collective-permute-start(bf16[6144,128]{1,0:T(8,128)(2,1)} %collective-permute-done.3.refs_8_.refs_5_), channel_id=1, source_target_pairs={{0,16},{16,0},{1,17},{17,1},{2,18},{18,2},{3,19},{19,3},{4,20},{20... | collective-permute-start | bytes 4718600 | tf_op jit(solution)/shard_map/ppermute | solution.py:168
  134.1 69.0 %collective-permute-start.8 = (bf16[256,3072]{1,0:T(8,128)(2,1)}, bf16[256,3072]{1,0:T(8,128)(2,1)}, u32[]{:S(2)}, u32[]{:S(2)}) collective-permute-start(bf16[256,3072]{1,0:T(8,128)(2,1)} %attention.5.refs_1_.refs_9_.refs_6_), channel_id=1, source_target_pairs={{0,4},{2,6},{4,0},{6,2},{8,12},{10,14},{12,8},{14,10},{1,5},{3,7},... | collective-permute-start | bytes 4718600 | tf_op jit(solution)/shard_map/ppermute | solution.py:164
  134.8 71.3 %collective-permute-start.7 = (bf16[6144,128]{1,0:T(8,128)(2,1)S(1)}, bf16[6144,128]{1,0:T(8,128)(2,1)}, u32[]{:S(2)}, u32[]{:S(2)}) collective-permute-start(bf16[6144,128]{1,0:T(8,128)(2,1)S(1)} %cut.8), channel_id=1, source_target_pairs={{0,8},{2,10},{4,12},{6,14},{8,0},{10,2},{12,4},{14,6},{1,9},{3,11}... | collective-permute-start | bytes 4718600 | tf_op jit(solution)/shard_map/ppermute | solution.py:164
  138.2 67.9 %collective-permute-start.9 = (bf16[256,3072]{1,0:T(8,128)(2,1)}, bf16[256,3072]{1,0:T(8,128)(2,1)}, u32[]{:S(2)}, u32[]{:S(2)}) collective-permute-start(bf16[256,3072]{1,0:T(8,128)(2,1)} %attention.6.refs_2_.refs_10_.refs_7_), channel_id=1, source_target_pairs={{0,2},{2,0},{4,6},{6,4},{8,10},{10,8},{12,14},{14,12},{1,3},{3,1},... | collective-permute-start | bytes 4718600 | tf_op jit(solution)/shard_map/ppermute | solution.py:164
  139.7 68.0 %collective-permute-start.10 = (bf16[256,3072]{1,0:T(8,128)(2,1)S(1)}, bf16[256,3072]{1,0:T(8,128)(2,1)}, u32[]{:S(2)}, u32[]{:S(2)}) collective-permute-start(bf16[256,3072]{1,0:T(8,128)(2,1)S(1)} %copy-done.9), channel_id=1, source_target_pairs={{0,2},{2,0},{4,6},{6,4},{8,10},{10,8},{12,14},{14,12},{1,3},{3,1},... | collective-permute-start | bytes 4718600 | tf_op jit(solution)/shard_map/ppermute | solution.py:164
  168.5 2.5 collective-permute-start.6
  207.7 34.8 %collective-permute-start.11 = (bf16[6144,128]{1,0:T(8,128)(2,1)}, bf16[6144,128]{1,0:T(8,128)(2,1)}, u32[]{:S(2)}, u32[]{:S(2)}) collective-permute-start(bf16[6144,128]{1,0:T(8,128)(2,1)} %collective-permute-done.7.refs_10_.refs_7_), channel_id=1, source_target_pairs={{0,16},{16,0},{1,17},{17,1},{2,18},{18,2},{3,19},{19,3},{4,20},{20... | collective-permute-start | bytes 4718600 | tf_op jit(solution)/shard_map/ppermute | solution.py:168
  208.2 69.2 %collective-permute-start.12 = (bf16[6144,128]{1,0:T(8,128)(2,1)}, bf16[6144,128]{1,0:T(8,128)(2,1)}, u32[]{:S(2)}, u32[]{:S(2)}) collective-permute-start(bf16[6144,128]{1,0:T(8,128)(2,1)} %cut.9), channel_id=1, source_target_pairs={{0,8},{2,10},{4,12},{6,14},{8,0},{10,2},{12,4},{14,6},{1,9},{3,11}... | collective-permute-start | bytes 4718600 | tf_op jit(solution)/shard_map/ppermute | solution.py:164
  208.5 68.9 %collective-permute-start.13 = (bf16[256,3072]{1,0:T(8,128)(2,1)}, bf16[256,3072]{1,0:T(8,128)(2,1)}, u32[]{:S(2)}, u32[]{:S(2)}) collective-permute-start(bf16[256,3072]{1,0:T(8,128)(2,1)} %attention.6.refs_2_.refs_10_.refs_7_), channel_id=1, source_target_pairs={{0,4},{2,6},{4,0},{6,2},{8,12},{10,14},{12,8},{14,10},{1,5},{3,7},... | collective-permute-start | bytes 4718600 | tf_op jit(solution)/shard_map/ppermute | solution.py:164
  209.5 67.9 %collective-permute-start.14 = (bf16[256,3072]{1,0:T(8,128)(2,1)}, bf16[256,3072]{1,0:T(8,128)(2,1)}, u32[]{:S(2)}, u32[]{:S(2)}) collective-permute-start(bf16[256,3072]{1,0:T(8,128)(2,1)} %collective-permute-done.refs_0_.refs_4_.refs_2_), channel_id=1, source_target_pairs={{0,2},{2,0},{4,6},{6,4},{8,10},{10,8},{12,14},{14,12},{1,3},{3,1},... | collective-permute-start | bytes 4718600 | tf_op jit(solution)/shard_map/ppermute | solution.py:164
  211.0 66.9 %collective-permute-start.15 = (bf16[256,3072]{1,0:T(8,128)(2,1)}, bf16[256,3072]{1,0:T(8,128)(2,1)}, u32[]{:S(2)}, u32[]{:S(2)}) collective-permute-start(bf16[256,3072]{1,0:T(8,128)(2,1)} %collective-permute-done.8.refs_1_.refs_5_.refs_2_), channel_id=1, source_target_pairs={{0,2},{2,0},{4,6},{6,4},{8,10},{10,8},{12,14},{14,12},{1,3},{3,1},... | collective-permute-start | bytes 4718600 | tf_op jit(solution)/shard_map/ppermute | solution.py:164
  229.4 53.1 %copy-start.10 = (bf16[256,3072]{1,0:T(8,128)(2,1)S(1)}, bf16[256,3072]{1,0:T(8,128)(2,1)}, u32[]{:S(2)}) copy-start(bf16[256,3072]{1,0:T(8,128)(2,1)} %copy-done.8) | copy-start | bytes 4718596
  242.5 2.5 collective-permute-start.16
  247.3 69.8 %copy-start.30 = (bf16[384,1024]{1,0:T(8,128)(2,1)S(1)}, bf16[384,1024]{1,0:T(8,128)(2,1)}, u32[]{:S(2)}) copy-start(bf16[384,1024]{1,0:T(8,128)(2,1)} %convolution_convert_fusion.1) | copy-start | bytes 2359300
  277.9 36.2 %collective-permute-start.17 = (bf16[6144,128]{1,0:T(8,128)(2,1)}, bf16[6144,128]{1,0:T(8,128)(2,1)}, u32[]{:S(2)}, u32[]{:S(2)}) collective-permute-start(bf16[6144,128]{1,0:T(8,128)(2,1)} %collective-permute-done.12.refs_12_.refs_9_), channel_id=1, source_target_pairs={{0,16},{16,0},{1,17},{17,1},{2,18},{18,2},{3,19},{19,3},{4,20},{20... | collective-permute-start | bytes 4718600 | tf_op jit(solution)/shard_map/ppermute | solution.py:168
  279.4 37.7 %collective-permute-start.22 = (bf16[2,2,192,1024]{3,2,1,0:T(8,128)(2,1)}, bf16[2,2,192,1024]{3,2,1,0:T(8,128)(2,1)}, u32[]{:S(2)}, u32[]{:S(2)}) collective-permute-start(bf16[2,2,192,1024]{3,2,1,0:T(8,128)(2,1)} %pad_maximum_fusion.2), channel_id=1, source_target_pairs={{0,2},{2,0},{4,6},{6,4},{8,10},{10,8},{12,14},{14,12},{1,3},{3,1},... | collective-permute-start | bytes 4718600 | tf_op jit(solution)/shard_map/ppermute | solution.py:164
  280.9 69.1 %collective-permute-start.19 = (bf16[6144,128]{1,0:T(8,128)(2,1)}, bf16[6144,128]{1,0:T(8,128)(2,1)}, u32[]{:S(2)}, u32[]{:S(2)}) collective-permute-start(bf16[6144,128]{1,0:T(8,128)(2,1)} %copy-done.13), channel_id=1, source_target_pairs={{0,8},{2,10},{4,12},{6,14},{8,0},{10,2},{12,4},{14,6},{1,9},{3,11}... | collective-permute-start | bytes 4718600 | tf_op jit(solution)/shard_map/ppermute | solution.py:164
  282.4 67.6 %collective-permute-start.20 = (bf16[256,3072]{1,0:T(8,128)(2,1)S(1)}, bf16[256,3072]{1,0:T(8,128)(2,1)}, u32[]{:S(2)}, u32[]{:S(2)}) collective-permute-start(bf16[256,3072]{1,0:T(8,128)(2,1)S(1)} %copy-done.10), channel_id=1, source_target_pairs={{0,4},{2,6},{4,0},{6,2},{8,12},{10,14},{12,8},{14,10},{1,5},{3,7},... | collective-permute-start | bytes 4718600 | tf_op jit(solution)/shard_map/ppermute | solution.py:164
  283.9 66.2 %collective-permute-start.21 = (bf16[256,3072]{1,0:T(8,128)(2,1)}, bf16[256,3072]{1,0:T(8,128)(2,1)}, u32[]{:S(2)}, u32[]{:S(2)}) collective-permute-start(bf16[256,3072]{1,0:T(8,128)(2,1)} %collective-permute-done.13.refs_2_.refs_6_.refs_3_), channel_id=1, source_target_pairs={{0,2},{2,0},{4,6},{6,4},{8,10},{10,8},{12,14},{14,12},{1,3},{3,1},... | collective-permute-start | bytes 4718600 | tf_op jit(solution)/shard_map/ppermute | solution.py:164
  314.0 4.9 collective-permute-start.18
  350.1 36.6 %collective-permute-start.24 = (bf16[6144,128]{1,0:T(8,128)(2,1)}, bf16[6144,128]{1,0:T(8,128)(2,1)}, u32[]{:S(2)}, u32[]{:S(2)}) collective-permute-start(bf16[6144,128]{1,0:T(8,128)(2,1)} %collective-permute-done.19.refs_14_.refs_11_), channel_id=1, source_target_pairs={{0,16},{16,0},{1,17},{17,1},{2,18},{18,2},{3,19},{19,3},{4,20},{20... | collective-permute-start | bytes 4718600 | tf_op jit(solution)/shard_map/ppermute | solution.py:168
  352.5 70.0 %collective-permute-start.27 = (bf16[4,192,1024]{2,1,0:T(8,128)(2,1)}, bf16[4,192,1024]{2,1,0:T(8,128)(2,1)}, u32[]{:S(2)}, u32[]{:S(2)}) collective-permute-start(bf16[4,192,1024]{2,1,0:T(8,128)(2,1)} %get-tuple-element.197), channel_id=1, source_target_pairs={{0,4},{2,6},{4,0},{6,2},{8,12},{10,14},{12,8},{14,10},{1,5},{3,7},... | collective-permute-start | bytes 4718600 | tf_op jit(solution)/shard_map/ppermute | solution.py:164
  353.1 70.3 %collective-permute-start.25 = (bf16[3072,256]{1,0:T(8,128)(2,1)S(1)}, bf16[3072,256]{1,0:T(8,128)(2,1)}, u32[]{:S(2)}, u32[]{:S(2)}) collective-permute-start(bf16[3072,256]{1,0:T(8,128)(2,1)S(1)} %copy-done.12), channel_id=1, source_target_pairs={{0,8},{2,10},{4,12},{6,14},{8,0},{10,2},{12,4},{14,6},{1,9},{3,11}... | collective-permute-start | bytes 4718600 | tf_op jit(solution)/shard_map/ppermute | solution.py:164
  355.5 67.8 %collective-permute-start.26 = (bf16[256,3072]{1,0:T(8,128)(2,1)}, bf16[256,3072]{1,0:T(8,128)(2,1)}, u32[]{:S(2)}, u32[]{:S(2)}) collective-permute-start(bf16[256,3072]{1,0:T(8,128)(2,1)} %collective-permute-done.20.refs_3_.refs_7_), channel_id=1, source_target_pairs={{0,2},{2,0},{4,6},{6,4},{8,10},{10,8},{12,14},{14,12},{1,3},{3,1},... | collective-permute-start | bytes 4718600 | tf_op jit(solution)/shard_map/ppermute | solution.py:164
  377.5 48.9 %collective-permute-start.23 = (bf16[256,2048]{1,0:T(8,128)(2,1)}, bf16[256,2048]{1,0:T(8,128)(2,1)}, u32[]{:S(2)}, u32[]{:S(2)}) collective-permute-start(bf16[256,2048]{1,0:T(8,128)(2,1)} %get-tuple-element.138), channel_id=1, source_target_pairs={{0,1},{1,0},{2,3},{3,2},{4,5},{5,4},{6,7},{7,6},{8,9},{9,8},{10,11... | collective-permute-start | bytes 3145736 | tf_op jit(solution)/shard_map/ppermute | solution.py:168
  423.3 36.0 %collective-permute-start.30 = (bf16[1536,256]{1,0:T(8,128)(2,1)}, bf16[1536,256]{1,0:T(8,128)(2,1)}, u32[]{:S(2)}, u32[]{:S(2)}) collective-permute-start(bf16[1536,256]{1,0:T(8,128)(2,1)} %cut.12), channel_id=1, source_target_pairs={{0,8},{2,10},{4,12},{6,14},{8,0},{10,2},{12,4},{14,6},{1,9},{3,11}... | collective-permute-start | bytes 2359304 | tf_op jit(solution)/shard_map/ppermute | solution.py:164
  424.9 43.3 %collective-permute-start.36 = (bf16[3072,256]{1,0:T(8,128)(2,1)}, bf16[3072,256]{1,0:T(8,128)(2,1)}, u32[]{:S(2)}, u32[]{:S(2)}) collective-permute-start(bf16[3072,256]{1,0:T(8,128)(2,1)} %collective-permute-done.25.refs_8_), channel_id=1, source_target_pairs={{0,16},{16,0},{1,17},{17,1},{2,18},{18,2},{3,19},{19,3},{4,20},{20... | collective-permute-start | bytes 4718600 | tf_op jit(solution)/shard_map/ppermute | solution.py:168
  428.9 39.3 %collective-permute-start.28 = (bf16[256,2048]{1,0:T(8,128)(2,1)}, bf16[256,2048]{1,0:T(8,128)(2,1)S(1)}, u32[]{:S(2)}, u32[]{:S(2)}) collective-permute-start(bf16[256,2048]{1,0:T(8,128)(2,1)} %add_convert_fusion.2), channel_id=1, source_target_pairs={{0,4},{2,6},{4,0},{6,2},{8,12},{10,14},{12,8},{14,10},{1,5},{3,7},... | collective-permute-start | bytes 3145736 | tf_op jit(solution)/shard_map/ppermute | solution.py:164
  431.5 36.7 %collective-permute-start.29 = (bf16[256,2048]{1,0:T(8,128)(2,1)}, bf16[256,2048]{1,0:T(8,128)(2,1)S(1)}, u32[]{:S(2)}, u32[]{:S(2)}) collective-permute-start(bf16[256,2048]{1,0:T(8,128)(2,1)} %pad_maximum_fusion.4), channel_id=1, source_target_pairs={{0,2},{2,0},{4,6},{6,4},{8,10},{10,8},{12,14},{14,12},{1,3},{3,1},... | collective-permute-start | bytes 3145736 | tf_op jit(solution)/shard_map/ppermute | solution.py:164
  459.3 11.3 %collective-permute-start.33 = (bf16[768,512]{1,0:T(8,128)(2,1)}, bf16[768,512]{1,0:T(8,128)(2,1)}, u32[]{:S(2)}, u32[]{:S(2)}) collective-permute-start(bf16[768,512]{1,0:T(8,128)(2,1)} %get-tuple-element.159), channel_id=1, source_target_pairs={{0,1},{1,0},{2,3},{3,2},{4,5},{5,4},{6,7},{7,6},{8,9},{9,8},{10,11... | collective-permute-start | bytes 2359304 | tf_op jit(solution)/shard_map/ppermute | solution.py:168
  459.7 18.8 %collective-permute-start.31 = (bf16[256,2560]{1,0:T(8,128)(2,1)}, bf16[256,2560]{1,0:T(8,128)(2,1)}, u32[]{:S(2)}, u32[]{:S(2)}) collective-permute-start(bf16[256,2560]{1,0:T(8,128)(2,1)} %get-tuple-element.157), channel_id=1, source_target_pairs={{0,1},{1,0},{2,3},{3,2},{4,5},{5,4},{6,7},{7,6},{8,9},{9,8},{10,11... | collective-permute-start | bytes 3932168 | tf_op jit(solution)/shard_map/ppermute | solution.py:168
  468.2 34.5 %collective-permute-start.37 = (bf16[1536,256]{1,0:T(8,128)(2,1)}, bf16[1536,256]{1,0:T(8,128)(2,1)}, u32[]{:S(2)}, u32[]{:S(2)}) collective-permute-start(bf16[1536,256]{1,0:T(8,128)(2,1)} %copy-done.18), channel_id=1, source_target_pairs={{0,8},{2,10},{4,12},{6,14},{8,0},{10,2},{12,4},{14,6},{1,9},{3,11}... | collective-permute-start | bytes 2359304 | tf_op jit(solution)/shard_map/ppermute | solution.py:164
  470.2 32.6 %collective-permute-start.38 = (bf16[1536,256]{1,0:T(8,128)(2,1)}, bf16[1536,256]{1,0:T(8,128)(2,1)}, u32[]{:S(2)}, u32[]{:S(2)}) collective-permute-start(bf16[1536,256]{1,0:T(8,128)(2,1)} %collective-permute-done.30.refs_8_), channel_id=1, source_target_pairs={{0,16},{16,0},{1,17},{17,1},{2,18},{18,2},{3,19},{19,3},{4,20},{20... | collective-permute-start | bytes 2359304 | tf_op jit(solution)/shard_map/ppermute | solution.py:168
  475.7 13.1 %collective-permute-start.35 = (bf16[256,512]{1,0:T(8,128)(2,1)}, bf16[256,512]{1,0:T(8,128)(2,1)S(1)}, u32[]{:S(2)}, u32[]{:S(2)}) collective-permute-start(bf16[256,512]{1,0:T(8,128)(2,1)} %get-tuple-element.205), channel_id=1, source_target_pairs={{0,2},{2,0},{4,6},{6,4},{8,10},{10,8},{12,14},{14,12},{1,3},{3,1},... | collective-permute-start | bytes 786440 | tf_op jit(solution)/shard_map/ppermute | solution.py:164
  476.1 17.9 %collective-permute-start.34 = (bf16[256,512]{1,0:T(8,128)(2,1)}, bf16[256,512]{1,0:T(8,128)(2,1)S(1)}, u32[]{:S(2)}, u32[]{:S(2)}) collective-permute-start(bf16[256,512]{1,0:T(8,128)(2,1)} %get-tuple-element.206), channel_id=1, source_target_pairs={{0,4},{2,6},{4,0},{6,2},{8,12},{10,14},{12,8},{14,10},{1,5},{3,7},... | collective-permute-start | bytes 786440 | tf_op jit(solution)/shard_map/ppermute | solution.py:164
  481.4 45.7 %collective-permute-start.32 = (bf16[256,2560]{1,0:T(8,128)(2,1)}, bf16[256,2560]{1,0:T(8,128)(2,1)S(1)}, u32[]{:S(2)}, u32[]{:S(2)}) collective-permute-start(bf16[256,2560]{1,0:T(8,128)(2,1)} %add_convert_fusion), channel_id=1, source_target_pairs={{0,6},{2,4},{4,2},{6,0},{8,14},{10,12},{12,10},{14,8},{1,7},{3,5},... | collective-permute-start | bytes 3932168 | tf_op jit(solution)/shard_map/ppermute | solution.py:164
  502.7 24.4 %collective-permute-start.39 = (bf16[1536,256]{1,0:T(8,128)(2,1)}, bf16[1536,256]{1,0:T(8,128)(2,1)}, u32[]{:S(2)}, u32[]{:S(2)}) collective-permute-start(bf16[1536,256]{1,0:T(8,128)(2,1)} %collective-permute-done.37.refs_8_), channel_id=1, source_target_pairs={{0,16},{16,0},{1,17},{17,1},{2,18},{18,2},{3,19},{19,3},{4,20},{20... | collective-permute-start | bytes 2359304 | tf_op jit(solution)/shard_map/ppermute | solution.py:168
  536.5 2.9 collective-permute-start.40
  542.0 8.7 %collective-permute-start.43 = (bf16[256,512]{1,0:T(8,128)(2,1)}, bf16[256,512]{1,0:T(8,128)(2,1)}, u32[]{:S(2)}, u32[]{:S(2)}) collective-permute-start(bf16[256,512]{1,0:T(8,128)(2,1)} %get-tuple-element.201), channel_id=1, source_target_pairs={{0,2},{2,0},{4,6},{6,4},{8,10},{10,8},{12,14},{14,12},{1,3},{3,1},... | collective-permute-start | bytes 786440 | tf_op jit(solution)/shard_map/ppermute | solution.py:164
  542.4 9.5 %collective-permute-start.42 = (bf16[256,512]{1,0:T(8,128)(2,1)}, bf16[256,512]{1,0:T(8,128)(2,1)}, u32[]{:S(2)}, u32[]{:S(2)}) collective-permute-start(bf16[256,512]{1,0:T(8,128)(2,1)} %get-tuple-element.202), channel_id=1, source_target_pairs={{0,4},{2,6},{4,0},{6,2},{8,12},{10,14},{12,8},{14,10},{1,5},{3,7},... | collective-permute-start | bytes 786440 | tf_op jit(solution)/shard_map/ppermute | solution.py:164
  542.4 15.0 %collective-permute-start.41 = (bf16[256,512]{1,0:T(8,128)(2,1)}, bf16[256,512]{1,0:T(8,128)(2,1)}, u32[]{:S(2)}, u32[]{:S(2)}) collective-permute-start(bf16[256,512]{1,0:T(8,128)(2,1)} %get-tuple-element.203), channel_id=1, source_target_pairs={{0,6},{2,4},{4,2},{6,0},{8,14},{10,12},{12,10},{14,8},{1,7},{3,5},... | collective-permute-start | bytes 786440 | tf_op jit(solution)/shard_map/ppermute | solution.py:164
  (30 other events, 248.1 us)

commit v6 on v5

--- a/solution.py
+++ b/solution.py
@@ -76,7 +76,7 @@
             out_specs=pl.BlockSpec((chunk_rows, heads * HD), lambda g, info: (0, g)),
         ),
         out_shape=jax.ShapeDtypeStruct((chunk_rows, width // parts), jnp.bfloat16),
-        compiler_params=pltpu.CompilerParams(vmem_limit_bytes=32 << 20),
+        compiler_params=pltpu.CompilerParams(vmem_limit_bytes=60 << 20),
         cost_estimate=LIGHT,
         name="attention",
     )(info, queries, keys_values, keys_values)
@@ -104,7 +104,7 @@
             out_specs=pl.BlockSpec((block, columns), lambda i, offsets: (i, 0)),
         ),
         out_shape=jax.ShapeDtypeStruct((rows, columns), pieces[0].dtype),
-        compiler_params=pltpu.CompilerParams(vmem_limit_bytes=32 << 20),
+        compiler_params=pltpu.CompilerParams(vmem_limit_bytes=60 << 20),
         cost_estimate=LIGHT,
         name="place",
     )(jnp.stack(offsets).astype(jnp.int32), *pieces)
@@ -124,24 +124,28 @@
             out_specs=pl.BlockSpec((block, width), lambda n, places: (n, 0)),
         ),
         out_shape=jax.ShapeDtypeStruct((height, width), weight.dtype),
-        compiler_params=pltpu.CompilerParams(vmem_limit_bytes=16 << 20),
+        compiler_params=pltpu.CompilerParams(vmem_limit_bytes=60 << 20),
         cost_estimate=LIGHT,
         name="cut",
     )(jnp.stack([jnp.int32(row // block), column // width]).astype(jnp.int32), weight)
 
 
-def cache_kernel(page_of, pages_ref, o_ref):
+def cache_kernel(page_of, near_ref, far_ref, o_ref):
     slots = o_ref.shape[0]
     first = pl.program_id(0) * slots
+    count = near_ref.shape[0] // PAGE
     for n in range(slots):
         page = page_of[first + n]
-        start = pl.multiple_of(jnp.maximum(page, 0) * PAGE, PAGE)
-        rows = pages_ref[pl.ds(start, PAGE), :]
+        near = pl.multiple_of(jnp.clip(page, 0, count - 1) * PAGE, PAGE)
+        far = pl.multiple_of(jnp.clip(page - count, 0, count - 1) * PAGE, PAGE)
+        rows = jnp.where(
+            page < count, near_ref[pl.ds(near, PAGE), :], far_ref[pl.ds(far, PAGE), :]
+        )
         o_ref[n] = jnp.where(page >= 0, rows, jnp.zeros_like(rows))
 
 
-def cache_of(pages, page_of):
-    rows, width = pages.shape
+def cache_of(near, far, page_of):
+    rows, width = near.shape
     count = page_of.shape[0]
     block = 16 if count % 16 == 0 else count
     return pl.pallas_call(
@@ -149,14 +153,14 @@
         grid_spec=pltpu.PrefetchScalarGridSpec(
             num_scalar_prefetch=1,
             grid=(count // block,),
-            in_specs=[pl.BlockSpec((rows, width), lambda i, page_of: (0, 0))],
+            in_specs=[pl.BlockSpec((rows, width), lambda i, page_of: (0, 0))] * 2,
             out_specs=pl.BlockSpec((block, PAGE, width), lambda i, page_of: (i, 0, 0)),
         ),
-        out_shape=jax.ShapeDtypeStruct((count, PAGE, width), pages.dtype),
-        compiler_params=pltpu.CompilerParams(vmem_limit_bytes=32 << 20),
+        out_shape=jax.ShapeDtypeStruct((count, PAGE, width), near.dtype),
+        compiler_params=pltpu.CompilerParams(vmem_limit_bytes=60 << 20),
         cost_estimate=LIGHT,
         name="cache",
-    )(page_of, pages)
+    )(page_of, near, far)
 
 
 def hop(array, mask):
@@ -437,11 +441,14 @@
         groups[0][0] = [gated(array) for array in groups[0][0]]
         return product(groups, rights, span, summands, dtype)
 
-    def finish(totals, masks, *earlier):
+    def finish(totals, masks, *earlier, swaps=1):
         given = after(totals[0], *earlier) if earlier else totals[0]
         rows = given.shape[0] // len(masks)
         if tp_count == 2:
-            other = swap(given, "tp")
+            some = given.shape[0] // swaps
+            other = jnp.concatenate(
+                [swap(given[n * some : (n + 1) * some], "tp") for n in range(swaps)], axis=0
+            )
             total = (totals[1].astype(jnp.float32) + other.astype(jnp.float32)).astype(other.dtype)
             return {mask: total[n * rows : (n + 1) * rows] for n, mask in enumerate(masks)}
         return {
@@ -453,16 +460,9 @@
 
     sliced, along, across = [cut(0)], [], []
     along.append(hop(sliced[0], FAR))
-    held = lax.dynamic_slice_in_dim(
-        after(keys_values, sliced[0]), tp_here * kv_width, kv_width, 1
-    )
-    lens_rows = jnp.zeros((PAGE, kv_width), held.dtype)
-    lens_rows = lens_rows.at[0, :REQ_INST].set(lengths[0].astype(held.dtype))
-    held = jnp.concatenate([held, lens_rows], axis=0)
-    held_far = hop(held, FAR)
     chunks = [1 - tp_here, tp_here] if tp_count == 2 else [jnp.int32(0)]
     own = blocks[0]
-    ready = held
+    ready = sliced[0]
     for chunk in chunks:
         for part in range(kv_parts):
             ready = attention(
@@ -481,20 +481,8 @@
         ready = cut(n, ready)
         sliced.append(ready)
 
-    held_far = after(held_far, ready)
-    pages_given, pages_kept = (
-        jnp.stack(
-            [
-                packed_pages(rows, lens, residues, tok_rows)
-                for rows, lens in (
-                    (held, lengths[0]),
-                    (held_far, held_far[tok_rows, :REQ_INST].astype(jnp.int32)),
-                )
-            ]
-        )
-        for residues in ([1 - side_here, 3 - side_here], [side_here, 2 + side_here])
-    )
-    gate = moved + (along[0], pages_given, pages_kept)
+    seen = jnp.sum(along[0].astype(jnp.float32), axis=0)
+    gate = moved + (along[0], seen, ready)
 
     def weights():
         n = len(across)
@@ -503,8 +491,18 @@
         return (across[-1], along[-1])
 
     moved = weights() + spread(NEXT, own[1:2], NEXT) + spread(SIDE, own[2:], SIDE)
+    held = lax.dynamic_slice_in_dim(
+        gated(keys_values), tp_here * kv_width, kv_width, 1
+    )
+    lens_rows = jnp.zeros((PAGE, kv_width), held.dtype)
+    lens_rows = lens_rows.at[0, :REQ_INST].set(lengths[0].astype(held.dtype))
+    held = jnp.concatenate([held, lens_rows], axis=0)
+    pages = packed_pages(
+        held, lengths[0], [1 - side_here, 3 - side_here, side_here, 2 + side_here], tok_rows
+    )
+    pages_given, pages_kept = pages[None, :2], pages[None, 2:]
     own_shares = finish(products((0,), [out_weight]), (0,), moved[0])
-    gate = moved + (own_shares[0],)
+    gate = moved + (own_shares[0], pages_given, pages_kept)
 
     near = blocks[NEXT]
     moved = weights() + spread(NEXT, own[2:3], NEXT) + spread(NEXT | SIDE, near[:2], SIDE)
@@ -538,6 +536,10 @@
         hand_out(NEXT, gated(shares[NEXT]), first_columns),
         hand_out(SIDE, gated(side_share), first_columns),
     )
+    pages = gated(jnp.concatenate([pages, pages_next], axis=0))
+    limit = data_pages(tok_rows)
+    near_lens = pages[:, limit * PAGE, :REQ_INST].astype(jnp.int32)
+    far_lens = hop(near_lens, FAR)
     begun = products((NEXT | SIDE,), [out_weight, two_pairs(0), two_pairs(2)])
     near_shares = finish(begun_near, (SIDE, NEXT, 0), begun[0], moved[1])
     far_shares = finish(begun, (NEXT | SIDE,), begun[0], moved[1])
@@ -551,33 +553,32 @@
     moved += tuple(
         hand_out(mask, near_shares[mask], far_columns(2, 4)) for mask in (NEXT, SIDE, 0)
     )
-    pages = jnp.concatenate([pages, after(pages_next, near_shares[0])], axis=0)
-    order = [mask ^ far for mask in (0, SIDE) for far in (0, FAR)]
-    order = order + [at ^ NEXT for at in order]
+    order = [0, SIDE, NEXT, NEXT | SIDE]
+    order = order + [at ^ FAR for at in order]
     block_of = jnp.asarray([order.index(i) for i in range(inst_count)], jnp.int32)
     block_of = jnp.take(block_of, jnp.arange(inst_count, dtype=jnp.int32) ^ inst_here)
-    limit = data_pages(tok_rows)
-    lens = jnp.take(pages[:, limit * PAGE, :REQ_INST].astype(jnp.int32), block_of, axis=0)
+    lens = jnp.take(jnp.concatenate([near_lens, far_lens], axis=0), block_of, axis=0)
     page_of = slot_pages(lens, placement, page_table, block_of, limit)
-    cache = cache_of(pages.reshape(-1, kv_width), page_of)
-    gate = moved + (cache, far_shares[NEXT | SIDE])
+    gate = moved + (page_of, far_shares[NEXT | SIDE])
 
     across.append(swap(gated(along[-1]), "grp"))
+    pages_far = hop(gated(pages), FAR)
     masks = (NEXT | SIDE, NEXT, SIDE, 0)
     sums = []
     for n, span in enumerate(spans):
         last = n == len(spans) - 1
-        if last:
-            gate = (far_share,)
         rights = (along[narrow + n], across[narrow + n])
         sums = [
             products(masks, [rights], span, sums, jnp.bfloat16 if last else jnp.float32)
         ]
     sums = sums[0]
-    shares = finish(sums, masks)
+    shares = finish(sums, masks, far_share, swaps=2)
     for mask in masks:
         hand_out(mask, shares[mask], far_columns(narrow, narrow + 1))
     projected = place(pieces, segments, offsets, inst_count * own_cols)
+    cache = cache_of(
+        pages.reshape(-1, kv_width), after(pages_far, projected).reshape(-1, kv_width), page_of
+    )
     return (projected, cache)
 
 

time: 577 us -> 614 us (1.064)
  waiting for transfers between devices: 250 us -> 303 us
  local copies, waits for them, and re-layouts: 45.8 us -> 15.5 us
  Pallas kernels: 187 us -> 211 us
  matrix products: 9.99 us -> 1.3 us
    ppermute x30 -> x31, waiting for transfers between devices: 193 us -> 259 us  [hop(): return lax.ppermute(array, 'inst', [(i, i ^ mask) for i in range(count)])]
    unnamed x70 -> x43, local copies, waits for them, and re-layouts: 37.6 us -> 1.23 us
    pallas_call x7, Pallas kernels: 10.4 us -> 25.7 us  [cut_out(): pl.pallas_call(cut_kernel, grid_spec=pltpu.PrefetchScalarGridSpec(num_sca...]
    ppermute x14 -> x15, waiting for transfers between devices: 57 us -> 44.7 us  [swap(): return lax.ppermute(array, axis, [(0, 1), (1, 0)])]
    dot_general x4 -> x1, matrix products: 9.99 us -> 1.3 us  [packed_pages(): jnp.dot(chosen.astype(held.dtype), held, preferred_element_type=jnp.float32)]
    ppermute x30 -> x31, starting transfers between devices: 38.7 us -> 38.9 us  [hop(): return lax.ppermute(array, 'inst', [(i, i ^ mask) for i in range(count)])]
  transfers between devices with their start and end apart: 44 -> 46, of which waited for: 28 -> 21; matrix products, arithmetic and copies ran while one was open for 7% -> 6% of each run, Pallas kernels for 30% -> 33%
where the time goes in v6:
time: 614 us; the launch traced here: 605 us
  waiting for transfers between devices  303 us (49%)
  Pallas kernels  211 us (34%)
  starting transfers between devices  48.2 us (8%)
  other arithmetic  24.4 us (4%)
  local copies, waits for them, and re-layouts  15.5 us (3%)
    ppermute x31, waiting for transfers between devices, hop(): return lax.ppermute(array, 'inst', [(i, i ^ mask) for i in range(count)])  259 us
    pallas_call x9, Pallas kernels, product(): pl.pallas_call(functools.partial(product_kernel, masks=masks, chunks=chun...  142 us
    ppermute x15, waiting for transfers between devices, swap(): return lax.ppermute(array, axis, [(0, 1), (1, 0)])  44.7 us
    ppermute x31, starting transfers between devices, hop(): return lax.ppermute(array, 'inst', [(i, i ^ mask) for i in range(count)])  38.9 us
    pallas_call x4, Pallas kernels, attention(): pl.pallas_call(functools.partial(attention_kernel, heads=heads, row_block...  29.9 us
    pallas_call x7, Pallas kernels, cut_out(): pl.pallas_call(cut_kernel, grid_spec=pltpu.PrefetchScalarGridSpec(num_sca...  25.7 us
  transfers between devices with their start and end apart: 46, of which 21 were waited for; matrix products, arithmetic and copies ran while one was open for 6% of the time, Pallas kernels for 33%

profile of v6, /device:TPU:0, one launch (start us, length us, event | category | flops | bytes accessed | tf_op | source)
XLA Modules:
  0.0 605.0 jit_solution(13415747505886273048)
XLA Ops:
  1.3 4.4 cut.7
  5.6 4.0 collective-permute-start.3
  10.4 7.5 %attention.4.refs_0_.refs_8_.refs_6_ = bf16[256,3072]{1,0:T(8,128)(2,1)} custom-call(s32[6]{0:T(128)} %add_add_fusion.1.info, bf16[512,6144]{1,0:T(8,128)(2,1)} %q_ref.3, bf16[512,2048]{1,0:T(8,128)(2,1)} %v_ref.7, bf16[512,2048]{1,0:T(8,128)(2,1)} %v_ref.7), custom_call_target="tpu_custom_call" | custom-call | tf_op jit(solution)/shard_map/attention/pallas_call | solution.py:62
  21.7 7.5 %attention.5.refs_1_.refs_9_.refs_6_ = bf16[256,3072]{1,0:T(8,128)(2,1)} custom-call(s32[6]{0:T(128)} %get-tuple-element.204.info, bf16[512,6144]{1,0:T(8,128)(2,1)} %q_ref.3, bf16[512,2048]{1,0:T(8,128)(2,1)} %v_ref.7, bf16[512,2048]{1,0:T(8,128)(2,1)} %v_ref.7), custom_call_target="tpu_custom_call" | custom-call | tf_op jit(solution)/shard_map/attention/pallas_call | solution.py:62
  29.7 7.4 %attention.6.refs_2_.refs_10_.refs_7_ = bf16[256,3072]{1,0:T(8,128)(2,1)} custom-call(s32[6]{0:T(128)} %get-tuple-element.203.info, bf16[512,6144]{1,0:T(8,128)(2,1)} %q_ref.3, bf16[512,2048]{1,0:T(8,128)(2,1)} %v_ref.7, bf16[512,2048]{1,0:T(8,128)(2,1)} %v_ref.7), custom_call_target="tpu_custom_call" | custom-call | tf_op jit(solution)/shard_map/attention/pallas_call | solution.py:62
  37.1 7.4 %attention.7.refs_3_.refs_11_.refs_7_ = bf16[256,3072]{1,0:T(8,128)(2,1)} custom-call(s32[6]{0:T(128)} %get-tuple-element.205.info, bf16[512,6144]{1,0:T(8,128)(2,1)} %q_ref.3, bf16[512,2048]{1,0:T(8,128)(2,1)} %v_ref.7, bf16[512,2048]{1,0:T(8,128)(2,1)} %v_ref.7), custom_call_target="tpu_custom_call" | custom-call | tf_op jit(solution)/shard_map/attention/pallas_call | solution.py:62
  45.2 4.2 cut.8
  50.1 4.2 cut.9
  54.4 4.3 cut.10
  58.6 3.1 cut.11
  62.3 2.7 cut.12
  65.1 2.7 cut.13
  67.8 10.4 %collective-permute-done.3.refs_8_.refs_5_ = bf16[6144,128]{1,0:T(8,128)(2,1)} collective-permute-done((bf16[6144,128]{1,0:T(8,128)(2,1)}, bf16[6144,128]{1,0:T(8,128)(2,1)}, u32[]{:S(2)}, u32[]{:S(2)}) %collective-permute-start.3) | collective-permute-done | bytes 1572896 | tf_op jit(solution)/shard_map/ppermute | solution.py:168
  78.2 8.5 %collective-permute-done.refs_0_.refs_4_.refs_2_ = bf16[256,3072]{1,0:T(8,128)(2,1)} collective-permute-done((bf16[256,3072]{1,0:T(8,128)(2,1)}, bf16[256,3072]{1,0:T(8,128)(2,1)}, u32[]{:S(2)}, u32[]{:S(2)}) %collective-permute-start) | collective-permute-done | bytes 1572896 | tf_op jit(solution)/shard_map/ppermute | solution.py:168
  86.7 2.4 collective-permute-done.2.refs_1_.refs_5_.refs_4_
  94.0 18.1 %product.9 = (bf16[256,1536]{1,0:T(8,128)(2,1)}, bf16[256,1536]{1,0:T(8,128)(2,1)}) custom-call(bf16[256,3072]{1,0:T(8,128)(2,1)} %attention.4.refs_0_.refs_8_.refs_6_, bf16[256,3072]{1,0:T(8,128)(2,1)} %attention.5.refs_1_.refs_9_.refs_6_, bf16[256,3072]{1,0:T(8,128)(2,1)} %attention.6.refs_2_.refs_10_.refs_7_, ...), custom_call_target="tpu_custom_call" | custom-call | tf_op jit(solution)/shard_map/product/pallas_call | solution.py:304
  112.2 11.9 %collective-permute-done.4.refs_9_.refs_6_ = bf16[6144,128]{1,0:T(8,128)(2,1)} collective-permute-done((bf16[6144,128]{1,0:T(8,128)(2,1)}, bf16[6144,128]{1,0:T(8,128)(2,1)}, u32[]{:S(2)}, u32[]{:S(2)}) %collective-permute-start.4) | collective-permute-done | bytes 1572896 | tf_op jit(solution)/shard_map/ppermute | solution.py:172
  128.1 32.3 %collective-permute-done.6.refs_10_.refs_7_ = bf16[6144,128]{1,0:T(8,128)(2,1)} collective-permute-done((bf16[6144,128]{1,0:T(8,128)(2,1)}, bf16[6144,128]{1,0:T(8,128)(2,1)}, u32[]{:S(2)}, u32[]{:S(2)}) %collective-permute-start.6) | collective-permute-done | bytes 1572896 | tf_op jit(solution)/shard_map/ppermute | solution.py:168
  166.5 17.7 %product.10 = (bf16[256,1536]{1,0:T(8,128)(2,1)}, bf16[256,1536]{1,0:T(8,128)(2,1)}) custom-call(bf16[256,3072]{1,0:T(8,128)(2,1)} %copy-done.4, bf16[256,3072]{1,0:T(8,128)(2,1)} %copy-done.3, bf16[256,3072]{1,0:T(8,128)(2,1)} %collective-permute-done.8.refs_2_.refs_6_.refs_5_, bf16[256,3072]{1,0:T(8,128)(2,1)} %collective-permute-done.9.refs_3_.refs_7_.refs_5_, ...), custom_call_target="tpu_custom_call" | custom-call | tf_op jit(solution)/shard_map/product/pallas_call | solution.py:304
  184.2 12.8 %collective-permute-done.10.refs_11_.refs_8_ = bf16[6144,128]{1,0:T(8,128)(2,1)S(1)} collective-permute-done((bf16[6144,128]{1,0:T(8,128)(2,1)}, bf16[6144,128]{1,0:T(8,128)(2,1)S(1)}, u32[]{:S(2)}, u32[]{:S(2)}) %collective-permute-start.10) | collective-permute-done | bytes 1572896 | tf_op jit(solution)/shard_map/ppermute | solution.py:172
  197.0 2.5 collective-permute-done.15
  201.7 27.7 %collective-permute-done.11.refs_12_.refs_9_ = bf16[6144,128]{1,0:T(8,128)(2,1)} collective-permute-done((bf16[6144,128]{1,0:T(8,128)(2,1)}, bf16[6144,128]{1,0:T(8,128)(2,1)}, u32[]{:S(2)}, u32[]{:S(2)}) %collective-permute-start.11) | collective-permute-done | bytes 1572896 | tf_op jit(solution)/shard_map/ppermute | solution.py:168
  232.6 2.5 collective-permute-start.18
  238.3 12.5 %product.11 = (bf16[512,512]{1,0:T(8,128)(2,1)}, bf16[512,512]{1,0:T(8,128)(2,1)}) custom-call(bf16[256,3072]{1,0:T(8,128)(2,1)} %attention.4.refs_0_.refs_8_.refs_6_, bf16[256,3072]{1,0:T(8,128)(2,1)} %attention.5.refs_1_.refs_9_.refs_6_, bf16[256,3072]{1,0:T(8,128)(2,1)} %attention.6.refs_2_.refs_10_.refs_7_, ...), custom_call_target="tpu_custom_call" | custom-call | tf_op jit(solution)/shard_map/product/pallas_call | solution.py:304
  250.8 15.2 %collective-permute-done.16.refs_13_.refs_10_ = bf16[6144,128]{1,0:T(8,128)(2,1)} collective-permute-done((bf16[6144,128]{1,0:T(8,128)(2,1)}, bf16[6144,128]{1,0:T(8,128)(2,1)}, u32[]{:S(2)}, u32[]{:S(2)}) %collective-permute-start.16) | collective-permute-done | bytes 1572896 | tf_op jit(solution)/shard_map/ppermute | solution.py:172
  270.1 17.5 %collective-permute-done.21 = bf16[1,2,192,1024]{3,2,1,0:T(8,128)(2,1)S(1)} collective-permute-done((bf16[1,2,192,1024]{3,2,1,0:T(8,128)(2,1)}, bf16[1,2,192,1024]{3,2,1,0:T(8,128)(2,1)S(1)}, u32[]{:S(2)}, u32[]{:S(2)}) %collective-permute-start.21) | collective-permute-done | bytes 786464 | tf_op jit(solution)/shard_map/ppermute | solution.py:168
  287.6 14.1 %collective-permute-done.18.refs_14_.refs_11_ = bf16[6144,128]{1,0:T(8,128)(2,1)} collective-permute-done((bf16[6144,128]{1,0:T(8,128)(2,1)}, bf16[6144,128]{1,0:T(8,128)(2,1)}, u32[]{:S(2)}, u32[]{:S(2)}) %collective-permute-start.18) | collective-permute-done | bytes 1572896 | tf_op jit(solution)/shard_map/ppermute | solution.py:168
  305.7 2.7 pad_maximum_fusion
  308.4 21.5 %product.12 = (bf16[256,2048]{1,0:T(8,128)(2,1)}, bf16[256,2048]{1,0:T(8,128)(2,1)}) custom-call(bf16[256,3072]{1,0:T(8,128)(2,1)} %collective-permute-done.refs_0_.refs_4_.refs_2_, bf16[256,3072]{1,0:T(8,128)(2,1)} %collective-permute-done.7.refs_1_.refs_5_.refs_2_, bf16[256,3072]{1,0:T(8,128)(2,1)} %collective-permute-done.12.refs_2_.refs_6_.refs_3_, ...), custom_call_target="tpu_custom_call" | custom-call | tf_op jit(solution)/shard_map/product/pallas_call | solution.py:304
  336.2 49.0 %collective-permute-done.26 = bf16[2,192,1024]{2,0,1:T(2,128)(2,1)S(1)} collective-permute-done((bf16[2,192,1024]{2,0,1:T(2,128)(2,1)S(1)}, bf16[2,192,1024]{2,0,1:T(2,128)(2,1)S(1)}, u32[]{:S(2)}, u32[]{:S(2)}) %collective-permute-start.26) | collective-permute-done | bytes 786464 | tf_op jit(solution)/shard_map/ppermute | solution.py:168
  385.1 2.8 pad_maximum_fusion.1
  387.9 16.1 %product.13 = (bf16[768,512]{1,0:T(8,128)(2,1)}, bf16[768,512]{1,0:T(8,128)(2,1)}) custom-call(bf16[256,3072]{1,0:T(8,128)(2,1)} %copy-done.4, bf16[256,3072]{1,0:T(8,128)(2,1)} %copy-done.3, bf16[256,3072]{1,0:T(8,128)(2,1)} %collective-permute-done.8.refs_2_.refs_6_.refs_5_, bf16[256,3072]{1,0:T(8,128)(2,1)} %collective-permute-done.9.refs_3_.refs_7_.refs_5_, ...), custom_call_target="tpu_custom_call" | custom-call | tf_op jit(solution)/shard_map/product/pallas_call | solution.py:304
  406.1 3.0 add_convert_fusion.2
  409.2 2.5 collective-permute-start.27
  412.3 25.0 %product.14 = (bf16[256,2560]{1,0:T(8,128)(2,1)}, bf16[256,2560]{1,0:T(8,128)(2,1)}) custom-call(bf16[256,3072]{1,0:T(8,128)(2,1)} %collective-permute-done.13.refs_0_, bf16[256,3072]{1,0:T(8,128)(2,1)} %copy-done.6, bf16[256,3072]{1,0:T(8,128)(2,1)} %collective-permute-done.20.refs_2_.refs_1_, bf16[256,3072]{1,0:T(8,128)(2,1)} %copy-done.7, ...), custom_call_target="tpu_custom_call" | custom-call | tf_op jit(solution)/shard_map/product/pallas_call | solution.py:304
  437.3 6.8 %collective-permute-done.38 = s32[4,4]{1,0:T(4,128)S(1)} collective-permute-done((s32[4,4]{1,0:T(4,128)S(1)}, s32[4,4]{1,0:T(4,128)S(1)}, u32[]{:S(2)}, u32[]{:S(2)}) %collective-permute-start.38) | collective-permute-done | bytes 96 | tf_op jit(solution)/shard_map/ppermute | solution.py:168
  446.1 5.1 collective-permute-done.27.refs_2_
  453.2 2.8 add_convert_fusion
  455.9 2.4 collective-permute-start.31
  461.2 47.0 %collective-permute-done.33.refs_5_ = bf16[256,512]{1,0:T(8,128)(2,1)S(1)} collective-permute-done((bf16[256,512]{1,0:T(8,128)(2,1)S(1)}, bf16[256,512]{1,0:T(8,128)(2,1)S(1)}, u32[]{:S(2)}, u32[]{:S(2)}) %collective-permute-start.33) | collective-permute-done | bytes 262176 | tf_op jit(solution)/shard_map/ppermute | solution.py:168
  511.0 12.0 %product.15 = (f32[1024,512]{1,0:T(8,128)}, f32[1024,512]{1,0:T(8,128)}) custom-call(bf16[256,3072]{1,0:T(8,128)(2,1)} %collective-permute-done.13.refs_0_, bf16[256,3072]{1,0:T(8,128)(2,1)} %collective-permute-done.20.refs_2_.refs_1_, bf16[256,3072]{1,0:T(8,128)(2,1)} %collective-permute-done.refs_0_.refs_4_.refs_2_, ...), custom_call_target="tpu_custom_call" | custom-call | tf_op jit(solution)/shard_map/product/pallas_call | solution.py:304
  523.0 10.0 %product.16 = (f32[1024,512]{1,0:T(8,128)}, f32[1024,512]{1,0:T(8,128)}) custom-call(bf16[256,3072]{1,0:T(8,128)(2,1)} %copy-done.6, bf16[256,3072]{1,0:T(8,128)(2,1)} %copy-done.7, bf16[256,3072]{1,0:T(8,128)(2,1)} %collective-permute-done.7.refs_1_.refs_5_.refs_2_, bf16[256,3072]{1,0:T(8,128)(2,1)} %copy-done.5, bf16[256,3072]{1,0:T(8,128)(2,1)} %copy-done.3, ...), custom_call_target="tpu_custom_call" | custom-call | tf_op jit(solution)/shard_map/product/pallas_call | solution.py:304
  533.0 9.3 %product.17 = (bf16[1024,512]{1,0:T(8,128)(2,1)}, bf16[1024,512]{1,0:T(8,128)(2,1)}) custom-call(bf16[256,3072]{1,0:T(8,128)(2,1)} %copy-done.6, bf16[256,3072]{1,0:T(8,128)(2,1)} %copy-done.7, bf16[256,3072]{1,0:T(8,128)(2,1)} %collective-permute-done.7.refs_1_.refs_5_.refs_2_, bf16[256,3072]{1,0:T(8,128)(2,1)} %copy-done.5, bf16[256,3072]{1,0:T(8,128)(2,1)} %copy-done.3, ...), custom_call_target="tpu_custom_call" | custom-call | tf_op jit(solution)/shard_map/product/pallas_call | solution.py:304
  547.8 2.3 collective-permute-start.42
  553.8 30.7 %collective-permute-done.42.refs_8_ = bf16[256,512]{1,0:T(8,128)(2,1)S(1)} collective-permute-done((bf16[256,512]{1,0:T(8,128)(2,1)}, bf16[256,512]{1,0:T(8,128)(2,1)S(1)}, u32[]{:S(2)}, u32[]{:S(2)}) %collective-permute-start.42) | collective-permute-done | bytes 262176 | tf_op jit(solution)/shard_map/ppermute | solution.py:168
  584.5 5.5 collective-permute-done.43.refs_9_
  590.0 6.6 %place.1 = bf16[256,12288]{1,0:T(8,128)(2,1)} custom-call(s32[44]{0:T(128)} %stack.248.offsets, bf16[256,1536]{1,0:T(8,128)(2,1)} %add_convert_fusion.5.refs_0_, bf16[256,512]{1,0:T(8,128)(2,1)} %get-tuple-element.198.refs_1_, bf16[256,2048]{1,0:T(8,128)(2,1)} %collective-permute-done.27.refs_2_, bf16[256,2048]{1,0:T(8,128)(2,1)} %collective-permute-done.28.refs_3_, ...), custom_call_target="tpu_custom_call" | custom-call | tf_op jit(solution)/shard_map/place/pallas_call | solution.py:95
  598.2 6.5 %cache.1 = bf16[128,16,1024]{2,1,0:T(8,128)(2,1)} custom-call(s32[128]{0:T(128)} %broadcast_add_fusion.page_of, bf16[768,1024]{1,0:T(8,128)(2,1)} %bitcast.89, bf16[768,1024]{1,0:T(8,128)(2,1)} %bitcast.90), custom_call_target="tpu_custom_call" | custom-call | tf_op jit(solution)/shard_map/cache/pallas_call | solution.py:151
  (178 shorter events, 68.6 us)
Async XLA Ops:
  0.6 304.8 %copy-start = (s32[32,16]{0,1:T(8,128)S(1)}, s32[32,16]{0,1:T(8,128)}, u32[]{:S(2)}) copy-start(s32[32,16]{0,1:T(8,128)} %param.14) | copy-start | bytes 6148
  5.6 72.6 %collective-permute-start.3 = (bf16[6144,128]{1,0:T(8,128)(2,1)}, bf16[6144,128]{1,0:T(8,128)(2,1)}, u32[]{:S(2)}, u32[]{:S(2)}) collective-permute-start(bf16[6144,128]{1,0:T(8,128)(2,1)} %cut.7), channel_id=1, source_target_pairs={{0,8},{2,10},{4,12},{6,14},{8,0},{10,2},{12,4},{14,6},{1,9},{3,11}... | collective-permute-start | bytes 4718600 | tf_op jit(solution)/shard_map/ppermute | solution.py:168
  18.0 68.7 %collective-permute-start = (bf16[256,3072]{1,0:T(8,128)(2,1)}, bf16[256,3072]{1,0:T(8,128)(2,1)}, u32[]{:S(2)}, u32[]{:S(2)}) collective-permute-start(bf16[256,3072]{1,0:T(8,128)(2,1)} %attention.4.refs_0_.refs_8_.refs_6_), channel_id=1, source_target_pairs={{0,4},{2,6},{4,0},{6,2},{8,12},{10,14},{12,8},{14,10},{1,5},{3,7},... | collective-permute-start | bytes 4718600 | tf_op jit(solution)/shard_map/ppermute | solution.py:168
  19.6 67.1 %collective-permute-start.1 = (bf16[256,3072]{1,0:T(8,128)(2,1)}, bf16[256,3072]{1,0:T(8,128)(2,1)S(1)}, u32[]{:S(2)}, u32[]{:S(2)}) collective-permute-start(bf16[256,3072]{1,0:T(8,128)(2,1)} %attention.4.refs_0_.refs_8_.refs_6_), channel_id=1, source_target_pairs={{0,2},{2,0},{4,6},{6,4},{8,10},{10,8},{12,14},{14,12},{1,3},{3,1},... | collective-permute-start | bytes 4718600 | tf_op jit(solution)/shard_map/ppermute | solution.py:168
  29.2 59.8 %collective-permute-start.2 = (bf16[256,3072]{1,0:T(8,128)(2,1)}, bf16[256,3072]{1,0:T(8,128)(2,1)S(1)}, u32[]{:S(2)}, u32[]{:S(2)}) collective-permute-start(bf16[256,3072]{1,0:T(8,128)(2,1)} %attention.5.refs_1_.refs_9_.refs_6_), channel_id=1, source_target_pairs={{0,2},{2,0},{4,6},{6,4},{8,10},{10,8},{12,14},{14,12},{1,3},{3,1},... | collective-permute-start | bytes 4718600 | tf_op jit(solution)/shard_map/ppermute | solution.py:168
  89.1 35.0 %collective-permute-start.4 = (bf16[6144,128]{1,0:T(8,128)(2,1)}, bf16[6144,128]{1,0:T(8,128)(2,1)}, u32[]{:S(2)}, u32[]{:S(2)}) collective-permute-start(bf16[6144,128]{1,0:T(8,128)(2,1)} %collective-permute-done.3.refs_8_.refs_5_), channel_id=1, source_target_pairs={{0,16},{16,0},{1,17},{17,1},{2,18},{18,2},{3,19},{19,3},{4,20},{20... | collective-permute-start | bytes 4718600 | tf_op jit(solution)/shard_map/ppermute | solution.py:172
  91.1 69.2 %collective-permute-start.6 = (bf16[6144,128]{1,0:T(8,128)(2,1)}, bf16[6144,128]{1,0:T(8,128)(2,1)}, u32[]{:S(2)}, u32[]{:S(2)}) collective-permute-start(bf16[6144,128]{1,0:T(8,128)(2,1)} %cut.8), channel_id=1, source_target_pairs={{0,8},{2,10},{4,12},{6,14},{8,0},{10,2},{12,4},{14,6},{1,9},{3,11}... | collective-permute-start | bytes 4718600 | tf_op jit(solution)/shard_map/ppermute | solution.py:168
  91.5 68.8 %collective-permute-start.7 = (bf16[256,3072]{1,0:T(8,128)(2,1)}, bf16[256,3072]{1,0:T(8,128)(2,1)}, u32[]{:S(2)}, u32[]{:S(2)}) collective-permute-start(bf16[256,3072]{1,0:T(8,128)(2,1)} %attention.5.refs_1_.refs_9_.refs_6_), channel_id=1, source_target_pairs={{0,4},{2,6},{4,0},{6,2},{8,12},{10,14},{12,8},{14,10},{1,5},{3,7},... | collective-permute-start | bytes 4718600 | tf_op jit(solution)/shard_map/ppermute | solution.py:168
  92.0 68.4 %collective-permute-start.8 = (bf16[256,3072]{1,0:T(8,128)(2,1)}, bf16[256,3072]{1,0:T(8,128)(2,1)}, u32[]{:S(2)}, u32[]{:S(2)}) collective-permute-start(bf16[256,3072]{1,0:T(8,128)(2,1)} %attention.6.refs_2_.refs_10_.refs_7_), channel_id=1, source_target_pairs={{0,2},{2,0},{4,6},{6,4},{8,10},{10,8},{12,14},{14,12},{1,3},{3,1},... | collective-permute-start | bytes 4718600 | tf_op jit(solution)/shard_map/ppermute | solution.py:168
  93.5 66.9 %collective-permute-start.9 = (bf16[256,3072]{1,0:T(8,128)(2,1)}, bf16[256,3072]{1,0:T(8,128)(2,1)}, u32[]{:S(2)}, u32[]{:S(2)}) collective-permute-start(bf16[256,3072]{1,0:T(8,128)(2,1)} %attention.7.refs_3_.refs_11_.refs_7_), channel_id=1, source_target_pairs={{0,2},{2,0},{4,6},{6,4},{8,10},{10,8},{12,14},{14,12},{1,3},{3,1},... | collective-permute-start | bytes 4718600 | tf_op jit(solution)/shard_map/ppermute | solution.py:168
  124.0 2.9 collective-permute-start.5
  160.4 36.6 %collective-permute-start.10 = (bf16[6144,128]{1,0:T(8,128)(2,1)}, bf16[6144,128]{1,0:T(8,128)(2,1)S(1)}, u32[]{:S(2)}, u32[]{:S(2)}) collective-permute-start(bf16[6144,128]{1,0:T(8,128)(2,1)} %collective-permute-done.6.refs_10_.refs_7_), channel_id=1, source_target_pairs={{0,16},{16,0},{1,17},{17,1},{2,18},{18,2},{3,19},{19,3},{4,20},{20... | collective-permute-start | bytes 4718600 | tf_op jit(solution)/shard_map/ppermute | solution.py:172
  160.9 68.4 %collective-permute-start.11 = (bf16[6144,128]{1,0:T(8,128)(2,1)}, bf16[6144,128]{1,0:T(8,128)(2,1)}, u32[]{:S(2)}, u32[]{:S(2)}) collective-permute-start(bf16[6144,128]{1,0:T(8,128)(2,1)} %cut.9), channel_id=1, source_target_pairs={{0,8},{2,10},{4,12},{6,14},{8,0},{10,2},{12,4},{14,6},{1,9},{3,11}... | collective-permute-start | bytes 4718600 | tf_op jit(solution)/shard_map/ppermute | solution.py:168
  162.9 68.1 %collective-permute-start.12 = (bf16[256,3072]{1,0:T(8,128)(2,1)}, bf16[256,3072]{1,0:T(8,128)(2,1)}, u32[]{:S(2)}, u32[]{:S(2)}) collective-permute-start(bf16[256,3072]{1,0:T(8,128)(2,1)} %attention.6.refs_2_.refs_10_.refs_7_), channel_id=1, source_target_pairs={{0,4},{2,6},{4,0},{6,2},{8,12},{10,14},{12,8},{14,10},{1,5},{3,7},... | collective-permute-start | bytes 4718600 | tf_op jit(solution)/shard_map/ppermute | solution.py:168
  164.5 66.5 %collective-permute-start.13 = (bf16[256,3072]{1,0:T(8,128)(2,1)}, bf16[256,3072]{1,0:T(8,128)(2,1)}, u32[]{:S(2)}, u32[]{:S(2)}) collective-permute-start(bf16[256,3072]{1,0:T(8,128)(2,1)} %collective-permute-done.refs_0_.refs_4_.refs_2_), channel_id=1, source_target_pairs={{0,2},{2,0},{4,6},{6,4},{8,10},{10,8},{12,14},{14,12},{1,3},{3,1},... | collective-permute-start | bytes 4718600 | tf_op jit(solution)/shard_map/ppermute | solution.py:168
  166.0 65.0 %collective-permute-start.14 = (bf16[256,3072]{1,0:T(8,128)(2,1)}, bf16[256,3072]{1,0:T(8,128)(2,1)S(1)}, u32[]{:S(2)}, u32[]{:S(2)}) collective-permute-start(bf16[256,3072]{1,0:T(8,128)(2,1)} %collective-permute-done.7.refs_1_.refs_5_.refs_2_), channel_id=1, source_target_pairs={{0,2},{2,0},{4,6},{6,4},{8,10},{10,8},{12,14},{14,12},{1,3},{3,1},... | collective-permute-start | bytes 4718600 | tf_op jit(solution)/shard_map/ppermute | solution.py:168
  197.0 35.6 %copy-start.8 = (bf16[6144,128]{1,0:T(8,128)(2,1)}, bf16[6144,128]{1,0:T(8,128)(2,1)S(1)}, u32[]{:S(2)}) copy-start(bf16[6144,128]{1,0:T(8,128)(2,1)S(1)} %collective-permute-done.10.refs_11_.refs_8_) | copy-start | bytes 4718596
  197.0 2.5 collective-permute-start.15
  231.0 35.0 %collective-permute-start.16 = (bf16[6144,128]{1,0:T(8,128)(2,1)}, bf16[6144,128]{1,0:T(8,128)(2,1)}, u32[]{:S(2)}, u32[]{:S(2)}) collective-permute-start(bf16[6144,128]{1,0:T(8,128)(2,1)} %collective-permute-done.11.refs_12_.refs_9_), channel_id=1, source_target_pairs={{0,16},{16,0},{1,17},{17,1},{2,18},{18,2},{3,19},{19,3},{4,20},{20... | collective-permute-start | bytes 4718600 | tf_op jit(solution)/shard_map/ppermute | solution.py:172
  232.6 69.1 %collective-permute-start.18 = (bf16[6144,128]{1,0:T(8,128)(2,1)}, bf16[6144,128]{1,0:T(8,128)(2,1)}, u32[]{:S(2)}, u32[]{:S(2)}) collective-permute-start(bf16[6144,128]{1,0:T(8,128)(2,1)} %cut.10), channel_id=1, source_target_pairs={{0,8},{2,10},{4,12},{6,14},{8,0},{10,2},{12,4},{14,6},{1,9},{3,11}... | collective-permute-start | bytes 4718600 | tf_op jit(solution)/shard_map/ppermute | solution.py:168
  235.1 66.6 %collective-permute-start.19 = (bf16[256,3072]{1,0:T(8,128)(2,1)}, bf16[256,3072]{1,0:T(8,128)(2,1)S(1)}, u32[]{:S(2)}, u32[]{:S(2)}) collective-permute-start(bf16[256,3072]{1,0:T(8,128)(2,1)} %attention.7.refs_3_.refs_11_.refs_7_), channel_id=1, source_target_pairs={{0,4},{2,6},{4,0},{6,2},{8,12},{10,14},{12,8},{14,10},{1,5},{3,7},... | collective-permute-start | bytes 4718600 | tf_op jit(solution)/shard_map/ppermute | solution.py:168
  236.8 64.9 %collective-permute-start.20 = (bf16[256,3072]{1,0:T(8,128)(2,1)}, bf16[256,3072]{1,0:T(8,128)(2,1)}, u32[]{:S(2)}, u32[]{:S(2)}) collective-permute-start(bf16[256,3072]{1,0:T(8,128)(2,1)} %collective-permute-done.12.refs_2_.refs_6_.refs_3_), channel_id=1, source_target_pairs={{0,2},{2,0},{4,6},{6,4},{8,10},{10,8},{12,14},{14,12},{1,3},{3,1},... | collective-permute-start | bytes 4718600 | tf_op jit(solution)/shard_map/ppermute | solution.py:168
  266.0 2.1 collective-permute-start.17
  266.0 21.5 %collective-permute-start.21 = (bf16[1,2,192,1024]{3,2,1,0:T(8,128)(2,1)}, bf16[1,2,192,1024]{3,2,1,0:T(8,128)(2,1)S(1)}, u32[]{:S(2)}, u32[]{:S(2)}) collective-permute-start(bf16[1,2,192,1024]{3,2,1,0:T(8,128)(2,1)} %bitcast.94), channel_id=1, source_target_pairs={{0,2},{2,0},{4,6},{6,4},{8,10},{10,8},{12,14},{14,12},{1,3},{3,1},... | collective-permute-start | bytes 2359304 | tf_op jit(solution)/shard_map/ppermute | solution.py:168
  301.7 86.2 %collective-permute-start.23 = (bf16[6144,128]{1,0:T(8,128)(2,1)}, bf16[6144,128]{1,0:T(8,128)(2,1)}, u32[]{:S(2)}, u32[]{:S(2)}) collective-permute-start(bf16[6144,128]{1,0:T(8,128)(2,1)} %collective-permute-done.18.refs_14_.refs_11_), channel_id=1, source_target_pairs={{0,16},{16,0},{1,17},{17,1},{2,18},{18,2},{3,19},{19,3},{4,20},{20... | collective-permute-start | bytes 4718600 | tf_op jit(solution)/shard_map/ppermute | solution.py:172
  302.6 101.5 %collective-permute-start.24 = (bf16[3072,256]{1,0:T(8,128)(2,1)}, bf16[3072,256]{1,0:T(8,128)(2,1)}, u32[]{:S(2)}, u32[]{:S(2)}) collective-permute-start(bf16[3072,256]{1,0:T(8,128)(2,1)} %cut.11), channel_id=1, source_target_pairs={{0,8},{2,10},{4,12},{6,14},{8,0},{10,2},{12,4},{14,6},{1,9},{3,11}... | collective-permute-start | bytes 4718600 | tf_op jit(solution)/shard_map/ppermute | solution.py:168
  303.8 100.2 %collective-permute-start.25 = (bf16[256,3072]{1,0:T(8,128)(2,1)S(1)}, bf16[256,3072]{1,0:T(8,128)(2,1)S(1)}, u32[]{:S(2)}, u32[]{:S(2)}) collective-permute-start(bf16[256,3072]{1,0:T(8,128)(2,1)S(1)} %collective-permute-done.19.refs_3_.refs_7_), channel_id=1, source_target_pairs={{0,2},{2,0},{4,6},{6,4},{8,10},{10,8},{12,14},{14,12},{1,3},{3,1},... | collective-permute-start | bytes 4718600 | tf_op jit(solution)/shard_map/ppermute | solution.py:168
  329.8 76.3 %collective-permute-start.22 = (bf16[256,2048]{1,0:T(8,128)(2,1)}, bf16[256,2048]{1,0:T(8,128)(2,1)}, u32[]{:S(2)}, u32[]{:S(2)}) collective-permute-start(bf16[256,2048]{1,0:T(8,128)(2,1)} %get-tuple-element.138), channel_id=1, source_target_pairs={{0,1},{1,0},{2,3},{3,2},{4,5},{5,4},{6,7},{7,6},{8,9},{9,8},{10,11... | collective-permute-start | bytes 3145736 | tf_op jit(solution)/shard_map/ppermute | solution.py:172
  332.3 52.9 %collective-permute-start.26 = (bf16[2,192,1024]{2,0,1:T(2,128)(2,1)S(1)}, bf16[2,192,1024]{2,0,1:T(2,128)(2,1)S(1)}, u32[]{:S(2)}, u32[]{:S(2)}) collective-permute-start(bf16[2,192,1024]{2,0,1:T(2,128)(2,1)S(1)} %bitcast.93), channel_id=1, source_target_pairs={{0,4},{2,6},{4,0},{6,2},{8,12},{10,14},{12,8},{14,10},{1,5},{3,7},... | collective-permute-start | bytes 2359304 | tf_op jit(solution)/shard_map/ppermute | solution.py:168
  404.0 40.7 %collective-permute-start.29 = (bf16[1536,256]{1,0:T(8,128)(2,1)}, bf16[1536,256]{1,0:T(8,128)(2,1)}, u32[]{:S(2)}, u32[]{:S(2)}) collective-permute-start(bf16[1536,256]{1,0:T(8,128)(2,1)} %cut.12), channel_id=1, source_target_pairs={{0,8},{2,10},{4,12},{6,14},{8,0},{10,2},{12,4},{14,6},{1,9},{3,11}... | collective-permute-start | bytes 2359304 | tf_op jit(solution)/shard_map/ppermute | solution.py:168
  404.6 46.6 %collective-permute-start.35 = (bf16[3072,256]{1,0:T(8,128)(2,1)}, bf16[3072,256]{1,0:T(8,128)(2,1)}, u32[]{:S(2)}, u32[]{:S(2)}) collective-permute-start(bf16[3072,256]{1,0:T(8,128)(2,1)} %collective-permute-done.24.refs_8_), channel_id=1, source_target_pairs={{0,16},{16,0},{1,17},{17,1},{2,18},{18,2},{3,19},{19,3},{4,20},{20... | collective-permute-start | bytes 4718600 | tf_op jit(solution)/shard_map/ppermute | solution.py:172
  409.2 42.1 %collective-permute-start.27 = (bf16[256,2048]{1,0:T(8,128)(2,1)}, bf16[256,2048]{1,0:T(8,128)(2,1)}, u32[]{:S(2)}, u32[]{:S(2)}) collective-permute-start(bf16[256,2048]{1,0:T(8,128)(2,1)} %add_convert_fusion.2), channel_id=1, source_target_pairs={{0,4},{2,6},{4,0},{6,2},{8,12},{10,14},{12,8},{14,10},{1,5},{3,7},... | collective-permute-start | bytes 3145736 | tf_op jit(solution)/shard_map/ppermute | solution.py:168
  411.7 39.6 %collective-permute-start.28 = (bf16[256,2048]{1,0:T(8,128)(2,1)}, bf16[256,2048]{1,0:T(8,128)(2,1)}, u32[]{:S(2)}, u32[]{:S(2)}) collective-permute-start(bf16[256,2048]{1,0:T(8,128)(2,1)} %pad_maximum_fusion.2), channel_id=1, source_target_pairs={{0,2},{2,0},{4,6},{6,4},{8,10},{10,8},{12,14},{14,12},{1,3},{3,1},... | collective-permute-start | bytes 3145736 | tf_op jit(solution)/shard_map/ppermute | solution.py:168
  412.2 31.9 %collective-permute-start.38 = (s32[4,4]{1,0:T(4,128)S(1)}, s32[4,4]{1,0:T(4,128)S(1)}, u32[]{:S(2)}, u32[]{:S(2)}) collective-permute-start(s32[4,4]{1,0:T(4,128)S(1)} %bitcast_convert_fusion), channel_id=1, source_target_pairs={{0,8},{2,10},{4,12},{6,14},{8,0},{10,2},{12,4},{14,6},{1,9},{3,11}... | collective-permute-start | bytes 200 | tf_op jit(solution)/shard_map/ppermute | solution.py:168
  444.7 8.4 %collective-permute-start.30 = (bf16[256,2560]{1,0:T(8,128)(2,1)}, bf16[256,2560]{1,0:T(8,128)(2,1)}, u32[]{:S(2)}, u32[]{:S(2)}) collective-permute-start(bf16[256,2560]{1,0:T(8,128)(2,1)} %get-tuple-element.157), channel_id=1, source_target_pairs={{0,1},{1,0},{2,3},{3,2},{4,5},{5,4},{6,7},{7,6},{8,9},{9,8},{10,11... | collective-permute-start | bytes 3932168 | tf_op jit(solution)/shard_map/ppermute | solution.py:172
  445.2 6.4 %collective-permute-start.32 = (bf16[768,512]{1,0:T(8,128)(2,1)}, bf16[768,512]{1,0:T(8,128)(2,1)}, u32[]{:S(2)}, u32[]{:S(2)}) collective-permute-start(bf16[768,512]{1,0:T(8,128)(2,1)} %get-tuple-element.159), channel_id=1, source_target_pairs={{0,1},{1,0},{2,3},{3,2},{4,5},{5,4},{6,7},{7,6},{8,9},{9,8},{10,11... | collective-permute-start | bytes 2359304 | tf_op jit(solution)/shard_map/ppermute | solution.py:172
  451.2 57.0 %collective-permute-start.36 = (bf16[1536,256]{1,0:T(8,128)(2,1)}, bf16[1536,256]{1,0:T(8,128)(2,1)S(1)}, u32[]{:S(2)}, u32[]{:S(2)}) collective-permute-start(bf16[1536,256]{1,0:T(8,128)(2,1)} %collective-permute-done.29.refs_8_), channel_id=1, source_target_pairs={{0,16},{16,0},{1,17},{17,1},{2,18},{18,2},{3,19},{19,3},{4,20},{20... | collective-permute-start | bytes 2359304 | tf_op jit(solution)/shard_map/ppermute | solution.py:172
  451.5 56.7 %collective-permute-start.37 = (bf16[1536,256]{1,0:T(8,128)(2,1)}, bf16[1536,256]{1,0:T(8,128)(2,1)}, u32[]{:S(2)}, u32[]{:S(2)}) collective-permute-start(bf16[1536,256]{1,0:T(8,128)(2,1)} %cut.13), channel_id=1, source_target_pairs={{0,8},{2,10},{4,12},{6,14},{8,0},{10,2},{12,4},{14,6},{1,9},{3,11}... | collective-permute-start | bytes 2359304 | tf_op jit(solution)/shard_map/ppermute | solution.py:168
  455.9 86.5 %collective-permute-start.31 = (bf16[256,2560]{1,0:T(8,128)(2,1)}, bf16[256,2560]{1,0:T(8,128)(2,1)}, u32[]{:S(2)}, u32[]{:S(2)}) collective-permute-start(bf16[256,2560]{1,0:T(8,128)(2,1)} %add_convert_fusion), channel_id=1, source_target_pairs={{0,6},{2,4},{4,2},{6,0},{8,14},{10,12},{12,10},{14,8},{1,7},{3,5},... | collective-permute-start | bytes 3932168 | tf_op jit(solution)/shard_map/ppermute | solution.py:168
  459.0 49.2 %collective-permute-start.33 = (bf16[256,512]{1,0:T(8,128)(2,1)S(1)}, bf16[256,512]{1,0:T(8,128)(2,1)S(1)}, u32[]{:S(2)}, u32[]{:S(2)}) collective-permute-start(bf16[256,512]{1,0:T(8,128)(2,1)S(1)} %get-tuple-element.196), channel_id=1, source_target_pairs={{0,4},{2,6},{4,0},{6,2},{8,12},{10,14},{12,8},{14,10},{1,5},{3,7},... | collective-permute-start | bytes 786440 | tf_op jit(solution)/shard_map/ppermute | solution.py:168
  459.1 49.2 %collective-permute-start.34 = (bf16[256,512]{1,0:T(8,128)(2,1)S(1)}, bf16[256,512]{1,0:T(8,128)(2,1)S(1)}, u32[]{:S(2)}, u32[]{:S(2)}) collective-permute-start(bf16[256,512]{1,0:T(8,128)(2,1)S(1)} %get-tuple-element.195), channel_id=1, source_target_pairs={{0,2},{2,0},{4,6},{6,4},{8,10},{10,8},{12,14},{14,12},{1,3},{3,1},... | collective-permute-start | bytes 786440 | tf_op jit(solution)/shard_map/ppermute | solution.py:168
  509.2 23.8 %collective-permute-start.39 = (bf16[1536,256]{1,0:T(8,128)(2,1)}, bf16[1536,256]{1,0:T(8,128)(2,1)}, u32[]{:S(2)}, u32[]{:S(2)}) collective-permute-start(bf16[1536,256]{1,0:T(8,128)(2,1)} %collective-permute-done.37.refs_8_), channel_id=1, source_target_pairs={{0,16},{16,0},{1,17},{17,1},{2,18},{18,2},{3,19},{19,3},{4,20},{20... | collective-permute-start | bytes 2359304 | tf_op jit(solution)/shard_map/ppermute | solution.py:172
  511.0 85.6 %collective-permute-start.45 = (bf16[4,192,1024]{2,0,1:T(4,128)(2,1)S(1)}, bf16[4,192,1024]{2,0,1:T(4,128)(2,1)S(1)}, u32[]{:S(2)}, u32[]{:S(2)}) collective-permute-start(bf16[4,192,1024]{2,0,1:T(4,128)(2,1)S(1)} %copy-done.9), channel_id=1, source_target_pairs={{0,8},{2,10},{4,12},{6,14},{8,0},{10,2},{12,4},{14,6},{1,9},{3,11}... | collective-permute-start | bytes 4718600 | tf_op jit(solution)/shard_map/ppermute | solution.py:168
  543.8 2.0 collective-permute-start.41
  543.8 2.6 collective-permute-start.40
  547.8 36.7 %collective-permute-start.42 = (bf16[256,512]{1,0:T(8,128)(2,1)}, bf16[256,512]{1,0:T(8,128)(2,1)S(1)}, u32[]{:S(2)}, u32[]{:S(2)}) collective-permute-start(bf16[256,512]{1,0:T(8,128)(2,1)} %get-tuple-element.191), channel_id=1, source_target_pairs={{0,6},{2,4},{4,2},{6,0},{8,14},{10,12},{12,10},{14,8},{1,7},{3,5},... | collective-permute-start | bytes 786440 | tf_op jit(solution)/shard_map/ppermute | solution.py:168
  550.1 39.9 %collective-permute-start.43 = (bf16[256,512]{1,0:T(8,128)(2,1)}, bf16[256,512]{1,0:T(8,128)(2,1)}, u32[]{:S(2)}, u32[]{:S(2)}) collective-permute-start(bf16[256,512]{1,0:T(8,128)(2,1)} %get-tuple-element.190), channel_id=1, source_target_pairs={{0,4},{2,6},{4,0},{6,2},{8,12},{10,14},{12,8},{14,10},{1,5},{3,7},... | collective-permute-start | bytes 786440 | tf_op jit(solution)/shard_map/ppermute | solution.py:168
  550.1 39.9 %collective-permute-start.44 = (bf16[256,512]{1,0:T(8,128)(2,1)}, bf16[256,512]{1,0:T(8,128)(2,1)}, u32[]{:S(2)}, u32[]{:S(2)}) collective-permute-start(bf16[256,512]{1,0:T(8,128)(2,1)} %get-tuple-element.189), channel_id=1, source_target_pairs={{0,2},{2,0},{4,6},{6,4},{8,10},{10,8},{12,14},{14,12},{1,3},{3,1},... | collective-permute-start | bytes 786440 | tf_op jit(solution)/shard_map/ppermute | solution.py:168
  (19 other events, 159.7 us)

commit v7 on v5

--- a/solution.py
+++ b/solution.py
@@ -76,7 +76,7 @@
             out_specs=pl.BlockSpec((chunk_rows, heads * HD), lambda g, info: (0, g)),
         ),
         out_shape=jax.ShapeDtypeStruct((chunk_rows, width // parts), jnp.bfloat16),
-        compiler_params=pltpu.CompilerParams(vmem_limit_bytes=32 << 20),
+        compiler_params=pltpu.CompilerParams(vmem_limit_bytes=60 << 20),
         cost_estimate=LIGHT,
         name="attention",
     )(info, queries, keys_values, keys_values)
@@ -104,7 +104,7 @@
             out_specs=pl.BlockSpec((block, columns), lambda i, offsets: (i, 0)),
         ),
         out_shape=jax.ShapeDtypeStruct((rows, columns), pieces[0].dtype),
-        compiler_params=pltpu.CompilerParams(vmem_limit_bytes=32 << 20),
+        compiler_params=pltpu.CompilerParams(vmem_limit_bytes=60 << 20),
         cost_estimate=LIGHT,
         name="place",
     )(jnp.stack(offsets).astype(jnp.int32), *pieces)
@@ -124,7 +124,7 @@
             out_specs=pl.BlockSpec((block, width), lambda n, places: (n, 0)),
         ),
         out_shape=jax.ShapeDtypeStruct((height, width), weight.dtype),
-        compiler_params=pltpu.CompilerParams(vmem_limit_bytes=16 << 20),
+        compiler_params=pltpu.CompilerParams(vmem_limit_bytes=60 << 20),
         cost_estimate=LIGHT,
         name="cut",
     )(jnp.stack([jnp.int32(row // block), column // width]).astype(jnp.int32), weight)
@@ -153,7 +153,7 @@
             out_specs=pl.BlockSpec((block, PAGE, width), lambda i, page_of: (i, 0, 0)),
         ),
         out_shape=jax.ShapeDtypeStruct((count, PAGE, width), pages.dtype),
-        compiler_params=pltpu.CompilerParams(vmem_limit_bytes=32 << 20),
+        compiler_params=pltpu.CompilerParams(vmem_limit_bytes=60 << 20),
         cost_estimate=LIGHT,
         name="cache",
     )(page_of, pages)
@@ -174,7 +174,7 @@
     count = masks * chunks * parts
     left_refs, rest = refs[:count], refs[count:]
     sources, wide = [], []
-    for _, size in groups:
+    for _, size, _ in groups:
         taken = max(size, 1)
         if size:
             sources.extend(rest[:taken])
@@ -209,7 +209,7 @@
         for copy in narrow_copies + mine if groups[0][1] else mine + narrow_copies:
             copy.start()
 
-    def compute(rights, arrived, first, alone):
+    def compute(rights, stacked, arrived, first, alone):
         for copy in arrived:
             copy.wait()
         for mask in range(masks):
@@ -222,7 +222,11 @@
             total, at = None, 0
             span = slice(mask * chunks * rows, (mask + 1) * chunks * rows)
             for n, (_, _, size) in enumerate(segments):
-                right = jnp.concatenate([ref[at : at + size, :] for ref in rights], axis=1)
+                if stacked > 1:
+                    mine = rights[n * len(rights) // stacked : (n + 1) * len(rights) // stacked]
+                    right = jnp.concatenate([ref[...] for ref in mine], axis=1)
+                else:
+                    right = jnp.concatenate([ref[at : at + size, :] for ref in rights], axis=1)
                 term = jnp.dot(lefts[n][span, :], right, preferred_element_type=jnp.float32)
                 total = term if total is None else total + term
                 at += size
@@ -233,15 +237,15 @@
                     result = result + other[span, :].astype(jnp.float32)
                 outs[chunk][span, :] = result.astype(outs[chunk].dtype)
 
-    if sum(steps for steps, _ in groups) == 1:
+    if sum(steps for steps, _, _ in groups) == 1:
         start()
     else:
         pl.when(step == 0)(start)
     first, at = 0, 0
-    for (steps, size), ref in zip(groups, wide):
+    for (steps, size, stacked), ref in zip(groups, wide):
         rights = held[at : at + size] if size else [ref]
         body = functools.partial(
-            compute, rights, narrow_copies[at : at + size], first, steps == 1
+            compute, rights, stacked, narrow_copies[at : at + size], first, steps == 1
         )
         at += size
         if len(groups) == 1:
@@ -273,12 +277,15 @@
     copies = masks * chunks * len(segments)
     groups, held, first = [], [], 0
     for right in rights:
-        if isinstance(right, tuple):
-            steps = 1
+        if isinstance(right, (tuple, list)):
+            steps, stacked = 1, 1
+            if isinstance(right, list):
+                stacked = len(right)
+                right = [piece for pieces in right for piece in pieces]
             operands += right
             specs += [anywhere] * len(right)
             held += [pltpu.VMEM(piece.shape, piece.dtype) for piece in right]
-            groups.append((1, len(right)))
+            groups.append((1, len(right), stacked))
         else:
             steps = right.shape[1] // block
             operands.append(right)
@@ -288,7 +295,7 @@
                     lambda n, first=first, steps=steps: (0, jnp.clip(n - first, 0, steps - 1)),
                 )
             )
-            groups.append((steps, 0))
+            groups.append((steps, 0, 1))
         first += steps
     out_spec = pl.BlockSpec((rows * masks, block), lambda n: (0, n))
     for summand in summands:
@@ -481,7 +488,18 @@
         ready = cut(n, ready)
         sliced.append(ready)
 
-    held_far = after(held_far, ready)
+    seen = jnp.sum(along[0].astype(jnp.float32), axis=0)
+    seen_far = jnp.sum(held_far.astype(jnp.float32), axis=0)
+    gate = moved + (along[0], held_far, seen, seen_far, ready)
+
+    def weights():
+        n = len(across)
+        across.append(swap(gated(along[n]), "grp"))
+        along.append(hop(gated(sliced[n + 1]), FAR))
+        return (across[-1], along[-1])
+
+    moved = weights() + spread(NEXT, own[1:2], NEXT) + spread(SIDE, own[2:], SIDE)
+    held_far = gated(held_far)
     pages_given, pages_kept = (
         jnp.stack(
             [
@@ -494,17 +512,8 @@
         )
         for residues in ([1 - side_here, 3 - side_here], [side_here, 2 + side_here])
     )
-    gate = moved + (along[0], pages_given, pages_kept)
-
-    def weights():
-        n = len(across)
-        across.append(swap(gated(along[n]), "grp"))
-        along.append(hop(gated(sliced[n + 1]), FAR))
-        return (across[-1], along[-1])
-
-    moved = weights() + spread(NEXT, own[1:2], NEXT) + spread(SIDE, own[2:], SIDE)
     own_shares = finish(products((0,), [out_weight]), (0,), moved[0])
-    gate = moved + (own_shares[0],)
+    gate = moved + (own_shares[0], pages_given, pages_kept)
 
     near = blocks[NEXT]
     moved = weights() + spread(NEXT, own[2:3], NEXT) + spread(NEXT | SIDE, near[:2], SIDE)
@@ -564,16 +573,11 @@
 
     across.append(swap(gated(along[-1]), "grp"))
     masks = (NEXT | SIDE, NEXT, SIDE, 0)
-    sums = []
-    for n, span in enumerate(spans):
-        last = n == len(spans) - 1
-        if last:
-            gate = (far_share,)
-        rights = (along[narrow + n], across[narrow + n])
-        sums = [
-            products(masks, [rights], span, sums, jnp.bfloat16 if last else jnp.float32)
-        ]
-    sums = sums[0]
+    far_pairs = [(along[narrow + n], across[narrow + n]) for n in range(len(spans))]
+    early = far_pairs[0] if len(spans) == 2 else far_pairs[:-1]
+    sums = products(masks, [early], (0, spans[-1][0]))
+    gate = (far_share,)
+    sums = products(masks, [after(far_pairs[-1], sums[0])], spans[-1], [sums])
     shares = finish(sums, masks)
     for mask in masks:
         hand_out(mask, shares[mask], far_columns(narrow, narrow + 1))

time: 577 us -> 591 us (1.024)
  local copies, waits for them, and re-layouts: 45.8 us -> 10.6 us
  waiting for transfers between devices: 250 us -> 279 us
  Pallas kernels: 187 us -> 204 us
    unnamed x70 -> x62, local copies, waits for them, and re-layouts: 37.6 us -> 3.11 us
    ppermute x30, waiting for transfers between devices: 193 us -> 227 us  [hop(): return lax.ppermute(array, 'inst', [(i, i ^ mask) for i in range(count)])]
    pallas_call x7, Pallas kernels: 10.4 us -> 25.8 us  [cut_out(): pl.pallas_call(cut_kernel, grid_spec=pltpu.PrefetchScalarGridSpec(num_sca...]
    pallas_call x9 -> x8, Pallas kernels: 142 us -> 136 us  [product(): pl.pallas_call(functools.partial(product_kernel, masks=masks, chunks=chun...]
  transfers between devices with their start and end apart: 44 -> 44, of which waited for: 28 -> 25; matrix products, arithmetic and copies ran while one was open for 7% -> 7% of each run, Pallas kernels for 30% -> 32%
where the time goes in v7:
time: 591 us; the launch traced here: 581 us
  waiting for transfers between devices  279 us (47%)
  Pallas kernels  204 us (35%)
  starting transfers between devices  45.8 us (8%)
  other arithmetic  33 us (6%)
  local copies, waits for them, and re-layouts  10.6 us (2%)
  matrix products  7.55 us (1%)
    ppermute x30, waiting for transfers between devices, hop(): return lax.ppermute(array, 'inst', [(i, i ^ mask) for i in range(count)])  227 us
    pallas_call x8, Pallas kernels, product(): pl.pallas_call(functools.partial(product_kernel, masks=masks, chunks=chun...  136 us
    ppermute x14, waiting for transfers between devices, swap(): return lax.ppermute(array, axis, [(0, 1), (1, 0)])  51.9 us
    ppermute x30, starting transfers between devices, hop(): return lax.ppermute(array, 'inst', [(i, i ^ mask) for i in range(count)])  38.5 us
    pallas_call x4, Pallas kernels, attention(): pl.pallas_call(functools.partial(attention_kernel, heads=heads, row_block...  30 us
    pallas_call x7, Pallas kernels, cut_out(): pl.pallas_call(cut_kernel, grid_spec=pltpu.PrefetchScalarGridSpec(num_sca...  25.8 us
    convert_element_type x7, other arithmetic, finish(): (totals[1].astype(jnp.float32) + other.astype(jnp.float32)).astype(other....  13.1 us
  transfers between devices with their start and end apart: 44, of which 25 were waited for; matrix products, arithmetic and copies ran while one was open for 7% of the time, Pallas kernels for 32%

profile of v7, /device:TPU:0, one launch (start us, length us, event | category | flops | bytes accessed | tf_op | source)
XLA Modules:
  0.0 581.4 jit_solution(12428636806831013163)
XLA Ops:
  1.3 4.4 cut.7
  5.6 4.0 collective-permute-start.3
  12.8 7.5 %attention.4.refs_0_.refs_8_.refs_12_ = bf16[256,3072]{1,0:T(8,128)(2,1)} custom-call(s32[6]{0:T(128)} %add_add_fusion.1.info, bf16[512,6144]{1,0:T(8,128)(2,1)} %q_ref.3, bf16[512,2048]{1,0:T(8,128)(2,1)} %v_ref.7, bf16[512,2048]{1,0:T(8,128)(2,1)} %v_ref.7), custom_call_target="tpu_custom_call" | custom-call | tf_op jit(solution)/shard_map/attention/pallas_call | solution.py:62
  20.9 7.6 %attention.5.refs_1_.refs_9_.refs_13_.refs_6_ = bf16[256,3072]{1,0:T(8,128)(2,1)} custom-call(s32[6]{0:T(128)} %get-tuple-element.228.info, bf16[512,6144]{1,0:T(8,128)(2,1)} %q_ref.3, bf16[512,2048]{1,0:T(8,128)(2,1)} %v_ref.7, bf16[512,2048]{1,0:T(8,128)(2,1)} %v_ref.7), custom_call_target="tpu_custom_call" | custom-call | tf_op jit(solution)/shard_map/attention/pallas_call | solution.py:62
  32.4 7.5 %attention.6.refs_2_.refs_10_.refs_14_ = bf16[256,3072]{1,0:T(8,128)(2,1)} custom-call(s32[6]{0:T(128)} %get-tuple-element.227.info, bf16[512,6144]{1,0:T(8,128)(2,1)} %q_ref.3, bf16[512,2048]{1,0:T(8,128)(2,1)} %v_ref.7, bf16[512,2048]{1,0:T(8,128)(2,1)} %v_ref.7), custom_call_target="tpu_custom_call" | custom-call | tf_op jit(solution)/shard_map/attention/pallas_call | solution.py:62
  39.8 7.5 %attention.7.refs_3_.refs_11_.refs_15_.refs_7_ = bf16[256,3072]{1,0:T(8,128)(2,1)} custom-call(s32[6]{0:T(128)} %get-tuple-element.229.info, bf16[512,6144]{1,0:T(8,128)(2,1)} %q_ref.3, bf16[512,2048]{1,0:T(8,128)(2,1)} %v_ref.7, bf16[512,2048]{1,0:T(8,128)(2,1)} %v_ref.7), custom_call_target="tpu_custom_call" | custom-call | tf_op jit(solution)/shard_map/attention/pallas_call | solution.py:62
  48.0 4.2 cut.8
  52.8 4.3 cut.9
  57.1 4.3 cut.10
  61.4 3.0 cut.11
  65.0 2.7 cut.12
  67.7 2.9 cut.13
  70.7 53.8 %collective-permute-done.4 = bf16[528,1024]{1,0:T(8,128)(2,1)} collective-permute-done((bf16[528,1024]{1,0:T(8,128)(2,1)}, bf16[528,1024]{1,0:T(8,128)(2,1)}, u32[]{:S(2)}, u32[]{:S(2)}) %collective-permute-start.4) | collective-permute-done | bytes 1081376 | tf_op jit(solution)/shard_map/ppermute | solution.py:164
  130.7 18.2 %product.8 = (bf16[256,1536]{1,0:T(8,128)(2,1)}, bf16[256,1536]{1,0:T(8,128)(2,1)}) custom-call(bf16[256,3072]{1,0:T(8,128)(2,1)} %attention.4.refs_0_.refs_8_.refs_12_, bf16[256,3072]{1,0:T(8,128)(2,1)} %attention.5.refs_1_.refs_9_.refs_13_.refs_6_, bf16[256,3072]{1,0:T(8,128)(2,1)} %attention.6.refs_2_.refs_10_.refs_14_, ...), custom_call_target="tpu_custom_call" | custom-call | tf_op jit(solution)/shard_map/product/pallas_call | solution.py:307
  148.9 3.4 collective-permute-start.7
  157.3 6.2 %collective-permute-done.5.refs_9_.refs_6_ = bf16[6144,128]{1,0:T(8,128)(2,1)} collective-permute-done((bf16[6144,128]{1,0:T(8,128)(2,1)}, bf16[6144,128]{1,0:T(8,128)(2,1)}, u32[]{:S(2)}, u32[]{:S(2)}) %collective-permute-start.5) | collective-permute-done | bytes 1572896 | tf_op jit(solution)/shard_map/ppermute | solution.py:168
  166.4 3.1 convolution_convert_fusion
  170.5 9.7 %collective-permute-done.8.refs_1_.refs_5_.refs_2_ = bf16[256,3072]{1,0:T(8,128)(2,1)} collective-permute-done((bf16[256,3072]{1,0:T(8,128)(2,1)S(1)}, bf16[256,3072]{1,0:T(8,128)(2,1)}, u32[]{:S(2)}, u32[]{:S(2)}) %collective-permute-start.8) | collective-permute-done | bytes 1572896 | tf_op jit(solution)/shard_map/ppermute | solution.py:164
  180.2 40.2 %collective-permute-done.7.refs_10_.refs_7_ = bf16[6144,128]{1,0:T(8,128)(2,1)} collective-permute-done((bf16[6144,128]{1,0:T(8,128)(2,1)}, bf16[6144,128]{1,0:T(8,128)(2,1)}, u32[]{:S(2)}, u32[]{:S(2)}) %collective-permute-start.7) | collective-permute-done | bytes 1572896 | tf_op jit(solution)/shard_map/ppermute | solution.py:164
  227.2 17.7 %product.9 = (bf16[256,1536]{1,0:T(8,128)(2,1)}, bf16[256,1536]{1,0:T(8,128)(2,1)}) custom-call(bf16[256,3072]{1,0:T(8,128)(2,1)} %collective-permute-done.1.refs_0_.refs_4_.refs_8_, bf16[256,3072]{1,0:T(8,128)(2,1)} %collective-permute-done.2.refs_1_.refs_5_.refs_9_.refs_4_, bf16[256,3072]{1,0:T(8,128)(2,1)} %copy-done.7, bf16[256,3072]{1,0:T(8,128)(2,1)} %copy-done.6, ...), custom_call_target="tpu_custom_call" | custom-call | tf_op jit(solution)/shard_map/product/pallas_call | solution.py:307
  244.9 12.9 %collective-permute-done.11.refs_11_.refs_8_ = bf16[6144,128]{1,0:T(8,128)(2,1)} collective-permute-done((bf16[6144,128]{1,0:T(8,128)(2,1)}, bf16[6144,128]{1,0:T(8,128)(2,1)}, u32[]{:S(2)}, u32[]{:S(2)}) %collective-permute-start.11) | collective-permute-done | bytes 1572896 | tf_op jit(solution)/shard_map/ppermute | solution.py:168
  257.8 2.5 collective-permute-done.16
  262.6 30.0 %collective-permute-done.12.refs_12_.refs_9_ = bf16[6144,128]{1,0:T(8,128)(2,1)} collective-permute-done((bf16[6144,128]{1,0:T(8,128)(2,1)}, bf16[6144,128]{1,0:T(8,128)(2,1)}, u32[]{:S(2)}, u32[]{:S(2)}) %collective-permute-start.12) | collective-permute-done | bytes 1572896 | tf_op jit(solution)/shard_map/ppermute | solution.py:164
  299.6 12.5 %product.10 = (bf16[512,512]{1,0:T(8,128)(2,1)}, bf16[512,512]{1,0:T(8,128)(2,1)}) custom-call(bf16[256,3072]{1,0:T(8,128)(2,1)} %attention.4.refs_0_.refs_8_.refs_12_, bf16[256,3072]{1,0:T(8,128)(2,1)} %attention.5.refs_1_.refs_9_.refs_13_.refs_6_, bf16[256,3072]{1,0:T(8,128)(2,1)} %attention.6.refs_2_.refs_10_.refs_14_, ...), custom_call_target="tpu_custom_call" | custom-call | tf_op jit(solution)/shard_map/product/pallas_call | solution.py:307
  312.1 17.3 %collective-permute-done.17.refs_13_.refs_10_ = bf16[6144,128]{1,0:T(8,128)(2,1)} collective-permute-done((bf16[6144,128]{1,0:T(8,128)(2,1)}, bf16[6144,128]{1,0:T(8,128)(2,1)}, u32[]{:S(2)}, u32[]{:S(2)}) %collective-permute-start.17) | collective-permute-done | bytes 1572896 | tf_op jit(solution)/shard_map/ppermute | solution.py:168
  329.3 3.3 collective-permute-done.22
  336.7 28.7 %collective-permute-done.19.refs_14_.refs_11_ = bf16[6144,128]{1,0:T(8,128)(2,1)} collective-permute-done((bf16[6144,128]{1,0:T(8,128)(2,1)}, bf16[6144,128]{1,0:T(8,128)(2,1)}, u32[]{:S(2)}, u32[]{:S(2)}) %collective-permute-start.19) | collective-permute-done | bytes 1572896 | tf_op jit(solution)/shard_map/ppermute | solution.py:164
  368.3 2.6 collective-permute-start.25
  372.0 21.4 %product.11 = (bf16[256,2048]{1,0:T(8,128)(2,1)}, bf16[256,2048]{1,0:T(8,128)(2,1)}) custom-call(bf16[256,3072]{1,0:T(8,128)(2,1)} %collective-permute-done.refs_0_.refs_4_, bf16[256,3072]{1,0:T(8,128)(2,1)} %collective-permute-done.8.refs_1_.refs_5_.refs_2_, bf16[256,3072]{1,0:T(8,128)(2,1)} %collective-permute-done.13.refs_2_.refs_6_, ...), custom_call_target="tpu_custom_call" | custom-call | tf_op jit(solution)/shard_map/product/pallas_call | solution.py:307
  394.2 7.8 %collective-permute-done.24.refs_15_.refs_12_ = bf16[6144,128]{1,0:T(8,128)(2,1)} collective-permute-done((bf16[6144,128]{1,0:T(8,128)(2,1)}, bf16[6144,128]{1,0:T(8,128)(2,1)}, u32[]{:S(2)}, u32[]{:S(2)}) %collective-permute-start.24) | collective-permute-done | bytes 1572896 | tf_op jit(solution)/shard_map/ppermute | solution.py:168
  402.0 16.1 %product.12 = (bf16[768,512]{1,0:T(8,128)(2,1)}, bf16[768,512]{1,0:T(8,128)(2,1)}) custom-call(bf16[256,3072]{1,0:T(8,128)(2,1)} %collective-permute-done.1.refs_0_.refs_4_.refs_8_, bf16[256,3072]{1,0:T(8,128)(2,1)} %collective-permute-done.2.refs_1_.refs_5_.refs_9_.refs_4_, bf16[256,3072]{1,0:T(8,128)(2,1)} %copy-done.7, bf16[256,3072]{1,0:T(8,128)(2,1)} %copy-done.6, ...), custom_call_target="tpu_custom_call" | custom-call | tf_op jit(solution)/shard_map/product/pallas_call | solution.py:307
  418.2 19.6 %collective-permute-done.27 = bf16[4,192,1024]{2,1,0:T(8,128)(2,1)} collective-permute-done((bf16[4,192,1024]{2,1,0:T(8,128)(2,1)}, bf16[4,192,1024]{2,1,0:T(8,128)(2,1)}, u32[]{:S(2)}, u32[]{:S(2)}) %collective-permute-start.27) | collective-permute-done | bytes 1572896 | tf_op jit(solution)/shard_map/ppermute | solution.py:164
  439.3 2.5 pad_maximum_fusion.4
  448.6 25.1 %product.13 = (bf16[256,2560]{1,0:T(8,128)(2,1)}, bf16[256,2560]{1,0:T(8,128)(2,1)}) custom-call(bf16[256,3072]{1,0:T(8,128)(2,1)} %collective-permute-done.14.refs_0_, bf16[256,3072]{1,0:T(8,128)(2,1)} %copy-done.9, bf16[256,3072]{1,0:T(8,128)(2,1)} %collective-permute-done.21.refs_2_, bf16[256,3072]{1,0:T(8,128)(2,1)} %copy-done.10, ...), custom_call_target="tpu_custom_call" | custom-call | tf_op jit(solution)/shard_map/product/pallas_call | solution.py:307
  475.5 9.4 %collective-permute-done.28.refs_2_ = bf16[256,2048]{1,0:T(8,128)(2,1)} collective-permute-done((bf16[256,2048]{1,0:T(8,128)(2,1)}, bf16[256,2048]{1,0:T(8,128)(2,1)}, u32[]{:S(2)}, u32[]{:S(2)}) %collective-permute-start.28) | collective-permute-done | bytes 1048608 | tf_op jit(solution)/shard_map/ppermute | solution.py:164
  492.8 2.5 collective-permute-start.34
  495.3 2.8 add_convert_fusion
  498.5 3.3 pad_maximum_fusion
  502.6 6.4 %cache.1 = bf16[128,16,1024]{2,1,0:T(8,128)(2,1)} custom-call(s32[128]{0:T(128)} %broadcast_add_fusion.page_of, bf16[1536,1024]{1,0:T(8,128)(2,1)} %bitcast.100), custom_call_target="tpu_custom_call" | custom-call | tf_op jit(solution)/shard_map/cache/pallas_call | solution.py:147
  510.0 9.3 %collective-permute-done.37.refs_8_ = bf16[1536,256]{1,0:T(8,128)(2,1)} collective-permute-done((bf16[1536,256]{1,0:T(8,128)(2,1)}, bf16[1536,256]{1,0:T(8,128)(2,1)}, u32[]{:S(2)}, u32[]{:S(2)}) %collective-permute-start.37) | collective-permute-done | bytes 786464 | tf_op jit(solution)/shard_map/ppermute | solution.py:164
  519.9 15.5 %product.14 = (bf16[1024,512]{1,0:T(8,128)(2,1)}, bf16[1024,512]{1,0:T(8,128)(2,1)}) custom-call(bf16[256,3072]{1,0:T(8,128)(2,1)} %collective-permute-done.14.refs_0_, bf16[256,3072]{1,0:T(8,128)(2,1)} %copy-done.9, bf16[256,3072]{1,0:T(8,128)(2,1)} %collective-permute-done.21.refs_2_, bf16[256,3072]{1,0:T(8,128)(2,1)} %copy-done.10, ...), custom_call_target="tpu_custom_call" | custom-call | tf_op jit(solution)/shard_map/product/pallas_call | solution.py:307
  537.8 6.4 %collective-permute-done.32.refs_4_ = bf16[256,2560]{1,0:T(8,128)(2,1)S(1)} collective-permute-done((bf16[256,2560]{1,0:T(8,128)(2,1)}, bf16[256,2560]{1,0:T(8,128)(2,1)S(1)}, u32[]{:S(2)}, u32[]{:S(2)}) %collective-permute-start.32) | collective-permute-done | bytes 1310752 | tf_op jit(solution)/shard_map/ppermute | solution.py:164
  544.2 9.1 %product.15 = (bf16[1024,512]{1,0:T(8,128)(2,1)}, bf16[1024,512]{1,0:T(8,128)(2,1)}) custom-call(bf16[256,3072]{1,0:T(8,128)(2,1)} %copy-done.9, bf16[256,3072]{1,0:T(8,128)(2,1)} %copy-done.10, bf16[256,3072]{1,0:T(8,128)(2,1)} %collective-permute-done.8.refs_1_.refs_5_.refs_2_, bf16[256,3072]{1,0:T(8,128)(2,1)} %copy-done.8, ...), custom_call_target="tpu_custom_call" | custom-call | tf_op jit(solution)/shard_map/product/pallas_call | solution.py:307
  553.4 2.9 collective-permute-done.40
  559.5 2.6 collective-permute-start.41
  562.7 4.2 collective-permute-done.43.refs_10_
  568.7 5.1 collective-permute-done.41.refs_8_
  574.5 6.5 %place.1 = bf16[256,12288]{1,0:T(8,128)(2,1)} custom-call(s32[44]{0:T(128)} %stack.263.offsets, bf16[256,1536]{1,0:T(8,128)(2,1)} %add_convert_fusion.5.refs_0_, bf16[256,512]{1,0:T(8,128)(2,1)} %get-tuple-element.208.refs_1_, bf16[256,2048]{1,0:T(8,128)(2,1)} %collective-permute-done.28.refs_2_, bf16[256,2048]{1,0:T(8,128)(2,1)} %copy-done.17, ...), custom_call_target="tpu_custom_call" | custom-call | tf_op jit(solution)/shard_map/place/pallas_call | solution.py:95
  (204 shorter events, 79.6 us)
Async XLA Ops:
  0.6 474.0 %copy-start = (s32[32,16]{0,1:T(8,128)S(1)}, s32[32,16]{0,1:T(8,128)}, u32[]{:S(2)}) copy-start(s32[32,16]{0,1:T(8,128)} %param.14) | copy-start | bytes 6148
  5.6 118.8 %collective-permute-start.3 = (bf16[6144,128]{1,0:T(8,128)(2,1)}, bf16[6144,128]{1,0:T(8,128)(2,1)}, u32[]{:S(2)}, u32[]{:S(2)}) collective-permute-start(bf16[6144,128]{1,0:T(8,128)(2,1)} %cut.7), channel_id=1, source_target_pairs={{0,8},{2,10},{4,12},{6,14},{8,0},{10,2},{12,4},{14,6},{1,9},{3,11}... | collective-permute-start | bytes 4718600 | tf_op jit(solution)/shard_map/ppermute | solution.py:164
  28.4 96.1 %collective-permute-start.2 = (bf16[256,3072]{1,0:T(8,128)(2,1)}, bf16[256,3072]{1,0:T(8,128)(2,1)}, u32[]{:S(2)}, u32[]{:S(2)}) collective-permute-start(bf16[256,3072]{1,0:T(8,128)(2,1)} %attention.5.refs_1_.refs_9_.refs_13_.refs_6_), channel_id=1, source_target_pairs={{0,2},{2,0},{4,6},{6,4},{8,10},{10,8},{12,14},{14,12},{1,3},{3,1},... | collective-permute-start | bytes 4718600 | tf_op jit(solution)/shard_map/ppermute | solution.py:164
  29.9 94.6 %collective-permute-start.1 = (bf16[256,3072]{1,0:T(8,128)(2,1)S(1)}, bf16[256,3072]{1,0:T(8,128)(2,1)}, u32[]{:S(2)}, u32[]{:S(2)}) collective-permute-start(bf16[256,3072]{1,0:T(8,128)(2,1)S(1)} %copy-done.5), channel_id=1, source_target_pairs={{0,2},{2,0},{4,6},{6,4},{8,10},{10,8},{12,14},{14,12},{1,3},{3,1},... | collective-permute-start | bytes 4718600 | tf_op jit(solution)/shard_map/ppermute | solution.py:164
  30.5 94.0 %collective-permute-start = (bf16[256,3072]{1,0:T(8,128)(2,1)S(1)}, bf16[256,3072]{1,0:T(8,128)(2,1)}, u32[]{:S(2)}, u32[]{:S(2)}) collective-permute-start(bf16[256,3072]{1,0:T(8,128)(2,1)S(1)} %copy-done.5), channel_id=1, source_target_pairs={{0,4},{2,6},{4,0},{6,2},{8,12},{10,14},{12,8},{14,10},{1,5},{3,7},... | collective-permute-start | bytes 4718600 | tf_op jit(solution)/shard_map/ppermute | solution.py:164
  32.0 92.4 %collective-permute-start.4 = (bf16[528,1024]{1,0:T(8,128)(2,1)}, bf16[528,1024]{1,0:T(8,128)(2,1)}, u32[]{:S(2)}, u32[]{:S(2)}) collective-permute-start(bf16[528,1024]{1,0:T(8,128)(2,1)} %fusion.1), channel_id=1, source_target_pairs={{0,8},{2,10},{4,12},{6,14},{8,0},{10,2},{12,4},{14,6},{1,9},{3,11}... | collective-permute-start | bytes 3244040 | tf_op jit(solution)/shard_map/ppermute | solution.py:164
  67.7 62.3 %copy-start.3 = (bf16[256,3072]{1,0:T(8,128)(2,1)S(1)}, bf16[256,3072]{1,0:T(8,128)(2,1)}, u32[]{:S(2)}) copy-start(bf16[256,3072]{1,0:T(8,128)(2,1)} %attention.5.refs_1_.refs_9_.refs_13_.refs_6_) | copy-start | bytes 4718596
  127.5 35.9 %collective-permute-start.5 = (bf16[6144,128]{1,0:T(8,128)(2,1)}, bf16[6144,128]{1,0:T(8,128)(2,1)}, u32[]{:S(2)}, u32[]{:S(2)}) collective-permute-start(bf16[6144,128]{1,0:T(8,128)(2,1)} %collective-permute-done.3.refs_8_.refs_5_), channel_id=1, source_target_pairs={{0,16},{16,0},{1,17},{17,1},{2,18},{18,2},{3,19},{19,3},{4,20},{20... | collective-permute-start | bytes 4718600 | tf_op jit(solution)/shard_map/ppermute | solution.py:168
  130.0 50.2 %collective-permute-start.8 = (bf16[256,3072]{1,0:T(8,128)(2,1)S(1)}, bf16[256,3072]{1,0:T(8,128)(2,1)}, u32[]{:S(2)}, u32[]{:S(2)}) collective-permute-start(bf16[256,3072]{1,0:T(8,128)(2,1)S(1)} %copy-done.3), channel_id=1, source_target_pairs={{0,4},{2,6},{4,0},{6,2},{8,12},{10,14},{12,8},{14,10},{1,5},{3,7},... | collective-permute-start | bytes 4718600 | tf_op jit(solution)/shard_map/ppermute | solution.py:164
  148.9 71.5 %collective-permute-start.7 = (bf16[6144,128]{1,0:T(8,128)(2,1)}, bf16[6144,128]{1,0:T(8,128)(2,1)}, u32[]{:S(2)}, u32[]{:S(2)}) collective-permute-start(bf16[6144,128]{1,0:T(8,128)(2,1)} %cut.8), channel_id=1, source_target_pairs={{0,8},{2,10},{4,12},{6,14},{8,0},{10,2},{12,4},{14,6},{1,9},{3,11}... | collective-permute-start | bytes 4718600 | tf_op jit(solution)/shard_map/ppermute | solution.py:164
  152.3 68.1 %collective-permute-start.9 = (bf16[256,3072]{1,0:T(8,128)(2,1)}, bf16[256,3072]{1,0:T(8,128)(2,1)S(1)}, u32[]{:S(2)}, u32[]{:S(2)}) collective-permute-start(bf16[256,3072]{1,0:T(8,128)(2,1)} %attention.6.refs_2_.refs_10_.refs_14_), channel_id=1, source_target_pairs={{0,2},{2,0},{4,6},{6,4},{8,10},{10,8},{12,14},{14,12},{1,3},{3,1},... | collective-permute-start | bytes 4718600 | tf_op jit(solution)/shard_map/ppermute | solution.py:164
  153.8 67.9 %collective-permute-start.10 = (bf16[256,3072]{1,0:T(8,128)(2,1)S(1)}, bf16[256,3072]{1,0:T(8,128)(2,1)S(1)}, u32[]{:S(2)}, u32[]{:S(2)}) collective-permute-start(bf16[256,3072]{1,0:T(8,128)(2,1)S(1)} %copy-done.4), channel_id=1, source_target_pairs={{0,2},{2,0},{4,6},{6,4},{8,10},{10,8},{12,14},{14,12},{1,3},{3,1},... | collective-permute-start | bytes 4718600 | tf_op jit(solution)/shard_map/ppermute | solution.py:164
  163.4 6.0 %collective-permute-start.6 = (bf16[256,1536]{1,0:T(8,128)(2,1)S(1)}, bf16[256,1536]{1,0:T(8,128)(2,1)S(1)}, u32[]{:S(2)}, u32[]{:S(2)}) collective-permute-start(bf16[256,1536]{1,0:T(8,128)(2,1)S(1)} %copy-done.28), channel_id=1, source_target_pairs={{0,1},{1,0},{2,3},{3,2},{4,5},{5,4},{6,7},{7,6},{8,9},{9,8},{10,11... | collective-permute-start | bytes 2359304 | tf_op jit(solution)/shard_map/ppermute | solution.py:168
  222.9 34.9 %collective-permute-start.11 = (bf16[6144,128]{1,0:T(8,128)(2,1)}, bf16[6144,128]{1,0:T(8,128)(2,1)}, u32[]{:S(2)}, u32[]{:S(2)}) collective-permute-start(bf16[6144,128]{1,0:T(8,128)(2,1)} %collective-permute-done.7.refs_10_.refs_7_), channel_id=1, source_target_pairs={{0,16},{16,0},{1,17},{17,1},{2,18},{18,2},{3,19},{19,3},{4,20},{20... | collective-permute-start | bytes 4718600 | tf_op jit(solution)/shard_map/ppermute | solution.py:168
  223.4 69.3 %collective-permute-start.12 = (bf16[6144,128]{1,0:T(8,128)(2,1)}, bf16[6144,128]{1,0:T(8,128)(2,1)}, u32[]{:S(2)}, u32[]{:S(2)}) collective-permute-start(bf16[6144,128]{1,0:T(8,128)(2,1)} %cut.9), channel_id=1, source_target_pairs={{0,8},{2,10},{4,12},{6,14},{8,0},{10,2},{12,4},{14,6},{1,9},{3,11}... | collective-permute-start | bytes 4718600 | tf_op jit(solution)/shard_map/ppermute | solution.py:164
  223.8 68.9 %collective-permute-start.13 = (bf16[256,3072]{1,0:T(8,128)(2,1)}, bf16[256,3072]{1,0:T(8,128)(2,1)}, u32[]{:S(2)}, u32[]{:S(2)}) collective-permute-start(bf16[256,3072]{1,0:T(8,128)(2,1)} %attention.6.refs_2_.refs_10_.refs_14_), channel_id=1, source_target_pairs={{0,4},{2,6},{4,0},{6,2},{8,12},{10,14},{12,8},{14,10},{1,5},{3,7},... | collective-permute-start | bytes 4718600 | tf_op jit(solution)/shard_map/ppermute | solution.py:164
  225.2 67.5 %collective-permute-start.14 = (bf16[256,3072]{1,0:T(8,128)(2,1)}, bf16[256,3072]{1,0:T(8,128)(2,1)}, u32[]{:S(2)}, u32[]{:S(2)}) collective-permute-start(bf16[256,3072]{1,0:T(8,128)(2,1)} %collective-permute-done.refs_0_.refs_4_), channel_id=1, source_target_pairs={{0,2},{2,0},{4,6},{6,4},{8,10},{10,8},{12,14},{14,12},{1,3},{3,1},... | collective-permute-start | bytes 4718600 | tf_op jit(solution)/shard_map/ppermute | solution.py:164
  226.7 67.0 %collective-permute-start.15 = (bf16[256,3072]{1,0:T(8,128)(2,1)}, bf16[256,3072]{1,0:T(8,128)(2,1)S(1)}, u32[]{:S(2)}, u32[]{:S(2)}) collective-permute-start(bf16[256,3072]{1,0:T(8,128)(2,1)} %collective-permute-done.8.refs_1_.refs_5_.refs_2_), channel_id=1, source_target_pairs={{0,2},{2,0},{4,6},{6,4},{8,10},{10,8},{12,14},{14,12},{1,3},{3,1},... | collective-permute-start | bytes 4718600 | tf_op jit(solution)/shard_map/ppermute | solution.py:164
  257.8 2.5 collective-permute-start.16
  293.7 35.7 %collective-permute-start.17 = (bf16[6144,128]{1,0:T(8,128)(2,1)}, bf16[6144,128]{1,0:T(8,128)(2,1)}, u32[]{:S(2)}, u32[]{:S(2)}) collective-permute-start(bf16[6144,128]{1,0:T(8,128)(2,1)} %collective-permute-done.12.refs_12_.refs_9_), channel_id=1, source_target_pairs={{0,16},{16,0},{1,17},{17,1},{2,18},{18,2},{3,19},{19,3},{4,20},{20... | collective-permute-start | bytes 4718600 | tf_op jit(solution)/shard_map/ppermute | solution.py:168
  295.0 37.6 %collective-permute-start.22 = (bf16[2,2,192,1024]{3,2,1,0:T(8,128)(2,1)}, bf16[2,2,192,1024]{3,2,1,0:T(8,128)(2,1)}, u32[]{:S(2)}, u32[]{:S(2)}) collective-permute-start(bf16[2,2,192,1024]{3,2,1,0:T(8,128)(2,1)} %pad_maximum_fusion.2), channel_id=1, source_target_pairs={{0,2},{2,0},{4,6},{6,4},{8,10},{10,8},{12,14},{14,12},{1,3},{3,1},... | collective-permute-start | bytes 4718600 | tf_op jit(solution)/shard_map/ppermute | solution.py:164
  296.5 68.9 %collective-permute-start.19 = (bf16[6144,128]{1,0:T(8,128)(2,1)}, bf16[6144,128]{1,0:T(8,128)(2,1)}, u32[]{:S(2)}, u32[]{:S(2)}) collective-permute-start(bf16[6144,128]{1,0:T(8,128)(2,1)} %cut.10), channel_id=1, source_target_pairs={{0,8},{2,10},{4,12},{6,14},{8,0},{10,2},{12,4},{14,6},{1,9},{3,11}... | collective-permute-start | bytes 4718600 | tf_op jit(solution)/shard_map/ppermute | solution.py:164
  297.7 67.7 %collective-permute-start.20 = (bf16[256,3072]{1,0:T(8,128)(2,1)S(1)}, bf16[256,3072]{1,0:T(8,128)(2,1)S(1)}, u32[]{:S(2)}, u32[]{:S(2)}) collective-permute-start(bf16[256,3072]{1,0:T(8,128)(2,1)S(1)} %copy-done.4), channel_id=1, source_target_pairs={{0,4},{2,6},{4,0},{6,2},{8,12},{10,14},{12,8},{14,10},{1,5},{3,7},... | collective-permute-start | bytes 4718600 | tf_op jit(solution)/shard_map/ppermute | solution.py:164
  299.1 66.3 %collective-permute-start.21 = (bf16[256,3072]{1,0:T(8,128)(2,1)}, bf16[256,3072]{1,0:T(8,128)(2,1)}, u32[]{:S(2)}, u32[]{:S(2)}) collective-permute-start(bf16[256,3072]{1,0:T(8,128)(2,1)} %collective-permute-done.13.refs_2_.refs_6_), channel_id=1, source_target_pairs={{0,2},{2,0},{4,6},{6,4},{8,10},{10,8},{12,14},{14,12},{1,3},{3,1},... | collective-permute-start | bytes 4718600 | tf_op jit(solution)/shard_map/ppermute | solution.py:164
  329.3 5.4 collective-permute-start.18
  365.4 36.6 %collective-permute-start.24 = (bf16[6144,128]{1,0:T(8,128)(2,1)}, bf16[6144,128]{1,0:T(8,128)(2,1)}, u32[]{:S(2)}, u32[]{:S(2)}) collective-permute-start(bf16[6144,128]{1,0:T(8,128)(2,1)} %collective-permute-done.19.refs_14_.refs_11_), channel_id=1, source_target_pairs={{0,16},{16,0},{1,17},{17,1},{2,18},{18,2},{3,19},{19,3},{4,20},{20... | collective-permute-start | bytes 4718600 | tf_op jit(solution)/shard_map/ppermute | solution.py:168
  368.0 69.7 %collective-permute-start.27 = (bf16[4,192,1024]{2,1,0:T(8,128)(2,1)}, bf16[4,192,1024]{2,1,0:T(8,128)(2,1)}, u32[]{:S(2)}, u32[]{:S(2)}) collective-permute-start(bf16[4,192,1024]{2,1,0:T(8,128)(2,1)} %get-tuple-element.197), channel_id=1, source_target_pairs={{0,4},{2,6},{4,0},{6,2},{8,12},{10,14},{12,8},{14,10},{1,5},{3,7},... | collective-permute-start | bytes 4718600 | tf_op jit(solution)/shard_map/ppermute | solution.py:164
  368.3 70.6 %collective-permute-start.25 = (bf16[3072,256]{1,0:T(8,128)(2,1)}, bf16[3072,256]{1,0:T(8,128)(2,1)}, u32[]{:S(2)}, u32[]{:S(2)}) collective-permute-start(bf16[3072,256]{1,0:T(8,128)(2,1)} %cut.11), channel_id=1, source_target_pairs={{0,8},{2,10},{4,12},{6,14},{8,0},{10,2},{12,4},{14,6},{1,9},{3,11}... | collective-permute-start | bytes 4718600 | tf_op jit(solution)/shard_map/ppermute | solution.py:164
  370.9 68.1 %collective-permute-start.26 = (bf16[256,3072]{1,0:T(8,128)(2,1)S(1)}, bf16[256,3072]{1,0:T(8,128)(2,1)S(1)}, u32[]{:S(2)}, u32[]{:S(2)}) collective-permute-start(bf16[256,3072]{1,0:T(8,128)(2,1)S(1)} %collective-permute-done.20.refs_3_.refs_7_), channel_id=1, source_target_pairs={{0,2},{2,0},{4,6},{6,4},{8,10},{10,8},{12,14},{14,12},{1,3},{3,1},... | collective-permute-start | bytes 4718600 | tf_op jit(solution)/shard_map/ppermute | solution.py:164
  393.4 49.8 %collective-permute-start.23 = (bf16[256,2048]{1,0:T(8,128)(2,1)}, bf16[256,2048]{1,0:T(8,128)(2,1)}, u32[]{:S(2)}, u32[]{:S(2)}) collective-permute-start(bf16[256,2048]{1,0:T(8,128)(2,1)} %get-tuple-element.138), channel_id=1, source_target_pairs={{0,1},{1,0},{2,3},{3,2},{4,5},{5,4},{6,7},{7,6},{8,9},{9,8},{10,11... | collective-permute-start | bytes 3145736 | tf_op jit(solution)/shard_map/ppermute | solution.py:168
  439.0 35.5 %collective-permute-start.30 = (bf16[1536,256]{1,0:T(8,128)(2,1)}, bf16[1536,256]{1,0:T(8,128)(2,1)}, u32[]{:S(2)}, u32[]{:S(2)}) collective-permute-start(bf16[1536,256]{1,0:T(8,128)(2,1)} %cut.12), channel_id=1, source_target_pairs={{0,8},{2,10},{4,12},{6,14},{8,0},{10,2},{12,4},{14,6},{1,9},{3,11}... | collective-permute-start | bytes 2359304 | tf_op jit(solution)/shard_map/ppermute | solution.py:164
  441.8 43.1 %collective-permute-start.36 = (bf16[3072,256]{1,0:T(8,128)(2,1)}, bf16[3072,256]{1,0:T(8,128)(2,1)S(1)}, u32[]{:S(2)}, u32[]{:S(2)}) collective-permute-start(bf16[3072,256]{1,0:T(8,128)(2,1)} %collective-permute-done.25.refs_16_), channel_id=1, source_target_pairs={{0,16},{16,0},{1,17},{17,1},{2,18},{18,2},{3,19},{19,3},{4,20},{20... | collective-permute-start | bytes 4718600 | tf_op jit(solution)/shard_map/ppermute | solution.py:168
  445.7 39.2 %collective-permute-start.28 = (bf16[256,2048]{1,0:T(8,128)(2,1)}, bf16[256,2048]{1,0:T(8,128)(2,1)}, u32[]{:S(2)}, u32[]{:S(2)}) collective-permute-start(bf16[256,2048]{1,0:T(8,128)(2,1)} %add_convert_fusion.2), channel_id=1, source_target_pairs={{0,4},{2,6},{4,0},{6,2},{8,12},{10,14},{12,8},{14,10},{1,5},{3,7},... | collective-permute-start | bytes 3145736 | tf_op jit(solution)/shard_map/ppermute | solution.py:164
  448.0 36.9 %collective-permute-start.29 = (bf16[256,2048]{1,0:T(8,128)(2,1)}, bf16[256,2048]{1,0:T(8,128)(2,1)S(1)}, u32[]{:S(2)}, u32[]{:S(2)}) collective-permute-start(bf16[256,2048]{1,0:T(8,128)(2,1)} %pad_maximum_fusion.4), channel_id=1, source_target_pairs={{0,2},{2,0},{4,6},{6,4},{8,10},{10,8},{12,14},{14,12},{1,3},{3,1},... | collective-permute-start | bytes 3145736 | tf_op jit(solution)/shard_map/ppermute | solution.py:164
  448.6 26.3 %copy-start.29 = (s32[32]{0:T(128)S(1)}, s32[32]{0:T(128)}, u32[]{:S(2)}) copy-start(s32[32]{0:T(128)} %param.13) | copy-start | bytes 388
  474.5 12.2 %collective-permute-start.33 = (bf16[768,512]{1,0:T(8,128)(2,1)}, bf16[768,512]{1,0:T(8,128)(2,1)}, u32[]{:S(2)}, u32[]{:S(2)}) collective-permute-start(bf16[768,512]{1,0:T(8,128)(2,1)} %get-tuple-element.159), channel_id=1, source_target_pairs={{0,1},{1,0},{2,3},{3,2},{4,5},{5,4},{6,7},{7,6},{8,9},{9,8},{10,11... | collective-permute-start | bytes 2359304 | tf_op jit(solution)/shard_map/ppermute | solution.py:168
  474.9 20.3 %collective-permute-start.31 = (bf16[256,2560]{1,0:T(8,128)(2,1)}, bf16[256,2560]{1,0:T(8,128)(2,1)}, u32[]{:S(2)}, u32[]{:S(2)}) collective-permute-start(bf16[256,2560]{1,0:T(8,128)(2,1)} %get-tuple-element.157), channel_id=1, source_target_pairs={{0,1},{1,0},{2,3},{3,2},{4,5},{5,4},{6,7},{7,6},{8,9},{9,8},{10,11... | collective-permute-start | bytes 3932168 | tf_op jit(solution)/shard_map/ppermute | solution.py:168
  484.9 34.4 %collective-permute-start.37 = (bf16[1536,256]{1,0:T(8,128)(2,1)}, bf16[1536,256]{1,0:T(8,128)(2,1)}, u32[]{:S(2)}, u32[]{:S(2)}) collective-permute-start(bf16[1536,256]{1,0:T(8,128)(2,1)} %cut.13), channel_id=1, source_target_pairs={{0,8},{2,10},{4,12},{6,14},{8,0},{10,2},{12,4},{14,6},{1,9},{3,11}... | collective-permute-start | bytes 2359304 | tf_op jit(solution)/shard_map/ppermute | solution.py:164
  486.1 33.2 %collective-permute-start.38 = (bf16[1536,256]{1,0:T(8,128)(2,1)}, bf16[1536,256]{1,0:T(8,128)(2,1)}, u32[]{:S(2)}, u32[]{:S(2)}) collective-permute-start(bf16[1536,256]{1,0:T(8,128)(2,1)} %collective-permute-done.30.refs_18_), channel_id=1, source_target_pairs={{0,16},{16,0},{1,17},{17,1},{2,18},{18,2},{3,19},{19,3},{4,20},{20... | collective-permute-start | bytes 2359304 | tf_op jit(solution)/shard_map/ppermute | solution.py:168
  491.7 17.3 %collective-permute-start.35 = (bf16[256,512]{1,0:T(8,128)(2,1)}, bf16[256,512]{1,0:T(8,128)(2,1)S(1)}, u32[]{:S(2)}, u32[]{:S(2)}) collective-permute-start(bf16[256,512]{1,0:T(8,128)(2,1)} %get-tuple-element.205), channel_id=1, source_target_pairs={{0,2},{2,0},{4,6},{6,4},{8,10},{10,8},{12,14},{14,12},{1,3},{3,1},... | collective-permute-start | bytes 786440 | tf_op jit(solution)/shard_map/ppermute | solution.py:164
  492.8 17.3 %collective-permute-start.34 = (bf16[256,512]{1,0:T(8,128)(2,1)}, bf16[256,512]{1,0:T(8,128)(2,1)S(1)}, u32[]{:S(2)}, u32[]{:S(2)}) collective-permute-start(bf16[256,512]{1,0:T(8,128)(2,1)} %get-tuple-element.206), channel_id=1, source_target_pairs={{0,4},{2,6},{4,0},{6,2},{8,12},{10,14},{12,8},{14,10},{1,5},{3,7},... | collective-permute-start | bytes 786440 | tf_op jit(solution)/shard_map/ppermute | solution.py:164
  498.1 46.1 %collective-permute-start.32 = (bf16[256,2560]{1,0:T(8,128)(2,1)}, bf16[256,2560]{1,0:T(8,128)(2,1)S(1)}, u32[]{:S(2)}, u32[]{:S(2)}) collective-permute-start(bf16[256,2560]{1,0:T(8,128)(2,1)} %add_convert_fusion), channel_id=1, source_target_pairs={{0,6},{2,4},{4,2},{6,0},{8,14},{10,12},{12,10},{14,8},{1,7},{3,5},... | collective-permute-start | bytes 3932168 | tf_op jit(solution)/shard_map/ppermute | solution.py:164
  509.0 26.4 %copy-start.22 = (bf16[256,512]{1,0:T(8,128)(2,1)}, bf16[256,512]{1,0:T(8,128)(2,1)S(1)}, u32[]{:S(2)}) copy-start(bf16[256,512]{1,0:T(8,128)(2,1)S(1)} %collective-permute-done.35.refs_6_) | copy-start | bytes 786436
  519.3 18.5 %collective-permute-start.39 = (bf16[1536,256]{1,0:T(8,128)(2,1)}, bf16[1536,256]{1,0:T(8,128)(2,1)S(1)}, u32[]{:S(2)}, u32[]{:S(2)}) collective-permute-start(bf16[1536,256]{1,0:T(8,128)(2,1)} %collective-permute-done.37.refs_8_), channel_id=1, source_target_pairs={{0,16},{16,0},{1,17},{17,1},{2,18},{18,2},{3,19},{19,3},{4,20},{20... | collective-permute-start | bytes 2359304 | tf_op jit(solution)/shard_map/ppermute | solution.py:168
  553.4 2.9 collective-permute-start.40
  558.6 8.3 %collective-permute-start.43 = (bf16[256,512]{1,0:T(8,128)(2,1)S(1)}, bf16[256,512]{1,0:T(8,128)(2,1)S(1)}, u32[]{:S(2)}, u32[]{:S(2)}) collective-permute-start(bf16[256,512]{1,0:T(8,128)(2,1)S(1)} %get-tuple-element.201), channel_id=1, source_target_pairs={{0,2},{2,0},{4,6},{6,4},{8,10},{10,8},{12,14},{14,12},{1,3},{3,1},... | collective-permute-start | bytes 786440 | tf_op jit(solution)/shard_map/ppermute | solution.py:164
  559.5 9.2 %collective-permute-start.42 = (bf16[256,512]{1,0:T(8,128)(2,1)S(1)}, bf16[256,512]{1,0:T(8,128)(2,1)S(1)}, u32[]{:S(2)}, u32[]{:S(2)}) collective-permute-start(bf16[256,512]{1,0:T(8,128)(2,1)S(1)} %get-tuple-element.202), channel_id=1, source_target_pairs={{0,4},{2,6},{4,0},{6,2},{8,12},{10,14},{12,8},{14,10},{1,5},{3,7},... | collective-permute-start | bytes 786440 | tf_op jit(solution)/shard_map/ppermute | solution.py:164
  559.5 14.3 %collective-permute-start.41 = (bf16[256,512]{1,0:T(8,128)(2,1)S(1)}, bf16[256,512]{1,0:T(8,128)(2,1)S(1)}, u32[]{:S(2)}, u32[]{:S(2)}) collective-permute-start(bf16[256,512]{1,0:T(8,128)(2,1)S(1)} %get-tuple-element.203), channel_id=1, source_target_pairs={{0,6},{2,4},{4,2},{6,0},{8,14},{10,12},{12,10},{14,8},{1,7},{3,5},... | collective-permute-start | bytes 786440 | tf_op jit(solution)/shard_map/ppermute | solution.py:164
  (26 other events, 212.0 us)

commit v8 on v7

--- a/solution.py
+++ b/solution.py
@@ -512,8 +512,9 @@
         )
         for residues in ([1 - side_here, 3 - side_here], [side_here, 2 + side_here])
     )
+    gate += (pages_given, pages_kept)
     own_shares = finish(products((0,), [out_weight]), (0,), moved[0])
-    gate = moved + (own_shares[0], pages_given, pages_kept)
+    gate = moved + (own_shares[0],)
 
     near = blocks[NEXT]
     moved = weights() + spread(NEXT, own[2:3], NEXT) + spread(NEXT | SIDE, near[:2], SIDE)

time: 591 us -> 572 us (0.968)
  waiting for transfers between devices: 279 us -> 263 us
    ppermute x30, waiting for transfers between devices: 227 us -> 213 us  [hop(): return lax.ppermute(array, 'inst', [(i, i ^ mask) for i in range(count)])]
  transfers between devices with their start and end apart: 44 -> 44, of which waited for: 25 -> 22; matrix products, arithmetic and copies ran while one was open for 7% -> 8% of each run, Pallas kernels for 32% -> 33%
where the time goes in v8:
time: 572 us; the launch traced here: 564 us
  waiting for transfers between devices  263 us (46%)
  Pallas kernels  205 us (36%)
  starting transfers between devices  42.5 us (7%)
  other arithmetic  34.2 us (6%)
  local copies, waits for them, and re-layouts  9.46 us (2%)
  matrix products  8.67 us (2%)
    ppermute x30, waiting for transfers between devices, hop(): return lax.ppermute(array, 'inst', [(i, i ^ mask) for i in range(count)])  213 us
    pallas_call x8, Pallas kernels, product(): pl.pallas_call(functools.partial(product_kernel, masks=masks, chunks=chun...  136 us
    ppermute x14, waiting for transfers between devices, swap(): return lax.ppermute(array, axis, [(0, 1), (1, 0)])  49.7 us
    ppermute x30, starting transfers between devices, hop(): return lax.ppermute(array, 'inst', [(i, i ^ mask) for i in range(count)])  36 us
    pallas_call x4, Pallas kernels, attention(): pl.pallas_call(functools.partial(attention_kernel, heads=heads, row_block...  29.8 us
    pallas_call x7, Pallas kernels, cut_out(): pl.pallas_call(cut_kernel, grid_spec=pltpu.PrefetchScalarGridSpec(num_sca...  26.1 us
    convert_element_type x7, other arithmetic, finish(): (totals[1].astype(jnp.float32) + other.astype(jnp.float32)).astype(other....  14 us
  transfers between devices with their start and end apart: 44, of which 22 were waited for; matrix products, arithmetic and copies ran while one was open for 8% of the time, Pallas kernels for 33%

profile of v8, /device:TPU:0, one launch (start us, length us, event | category | flops | bytes accessed | tf_op | source)
XLA Modules:
  0.0 563.8 jit_solution(3953283067873926266)
XLA Ops:
  1.3 4.4 cut.7
  5.7 4.0 collective-permute-start.3
  12.7 7.5 %attention.4.refs_0_.refs_8_.refs_12_ = bf16[256,3072]{1,0:T(8,128)(2,1)} custom-call(s32[6]{0:T(128)} %add_add_fusion.1.info, bf16[512,6144]{1,0:T(8,128)(2,1)} %q_ref.3, bf16[512,2048]{1,0:T(8,128)(2,1)} %v_ref.7, bf16[512,2048]{1,0:T(8,128)(2,1)} %v_ref.7), custom_call_target="tpu_custom_call" | custom-call | tf_op jit(solution)/shard_map/attention/pallas_call | solution.py:62
  20.8 7.4 %attention.5.refs_1_.refs_9_.refs_13_.refs_6_ = bf16[256,3072]{1,0:T(8,128)(2,1)} custom-call(s32[6]{0:T(128)} %get-tuple-element.230.info, bf16[512,6144]{1,0:T(8,128)(2,1)} %q_ref.3, bf16[512,2048]{1,0:T(8,128)(2,1)} %v_ref.7, bf16[512,2048]{1,0:T(8,128)(2,1)} %v_ref.7), custom_call_target="tpu_custom_call" | custom-call | tf_op jit(solution)/shard_map/attention/pallas_call | solution.py:62
  32.2 7.5 %attention.6.refs_2_.refs_10_.refs_14_ = bf16[256,3072]{1,0:T(8,128)(2,1)} custom-call(s32[6]{0:T(128)} %get-tuple-element.229.info, bf16[512,6144]{1,0:T(8,128)(2,1)} %q_ref.3, bf16[512,2048]{1,0:T(8,128)(2,1)} %v_ref.7, bf16[512,2048]{1,0:T(8,128)(2,1)} %v_ref.7), custom_call_target="tpu_custom_call" | custom-call | tf_op jit(solution)/shard_map/attention/pallas_call | solution.py:62
  39.7 7.5 %attention.7.refs_3_.refs_11_.refs_15_.refs_7_ = bf16[256,3072]{1,0:T(8,128)(2,1)} custom-call(s32[6]{0:T(128)} %get-tuple-element.231.info, bf16[512,6144]{1,0:T(8,128)(2,1)} %q_ref.3, bf16[512,2048]{1,0:T(8,128)(2,1)} %v_ref.7, bf16[512,2048]{1,0:T(8,128)(2,1)} %v_ref.7), custom_call_target="tpu_custom_call" | custom-call | tf_op jit(solution)/shard_map/attention/pallas_call | solution.py:62
  47.8 4.2 cut.8
  52.7 4.3 cut.9
  57.0 4.2 cut.10
  61.2 3.2 cut.11
  65.0 2.7 cut.12
  67.8 3.0 cut.13
  70.9 53.6 %collective-permute-done.4 = bf16[528,1024]{1,0:T(8,128)(2,1)} collective-permute-done((bf16[528,1024]{1,0:T(8,128)(2,1)}, bf16[528,1024]{1,0:T(8,128)(2,1)}, u32[]{:S(2)}, u32[]{:S(2)}) %collective-permute-start.4) | collective-permute-done | bytes 1081376 | tf_op jit(solution)/shard_map/ppermute | solution.py:164
  129.9 4.0 collective-permute-start.8
  139.7 3.0 convolution_convert_fusion
  146.0 17.7 %product.8 = (bf16[256,1536]{1,0:T(8,128)(2,1)}, bf16[256,1536]{1,0:T(8,128)(2,1)}) custom-call(bf16[256,3072]{1,0:T(8,128)(2,1)} %attention.4.refs_0_.refs_8_.refs_12_, bf16[256,3072]{1,0:T(8,128)(2,1)} %attention.5.refs_1_.refs_9_.refs_13_.refs_6_, bf16[256,3072]{1,0:T(8,128)(2,1)} %attention.6.refs_2_.refs_10_.refs_14_, ...), custom_call_target="tpu_custom_call" | custom-call | tf_op jit(solution)/shard_map/product/pallas_call | solution.py:307
  163.8 2.5 collective-permute-done.6
  168.6 31.3 %collective-permute-done.7.refs_10_.refs_7_ = bf16[6144,128]{1,0:T(8,128)(2,1)} collective-permute-done((bf16[6144,128]{1,0:T(8,128)(2,1)}, bf16[6144,128]{1,0:T(8,128)(2,1)}, u32[]{:S(2)}, u32[]{:S(2)}) %collective-permute-start.7) | collective-permute-done | bytes 1572896 | tf_op jit(solution)/shard_map/ppermute | solution.py:164
  199.9 3.6 collective-permute-done.10.refs_3_.refs_7_.refs_11_.refs_5_
  206.7 17.9 %product.9 = (bf16[256,1536]{1,0:T(8,128)(2,1)}, bf16[256,1536]{1,0:T(8,128)(2,1)}) custom-call(bf16[256,3072]{1,0:T(8,128)(2,1)} %collective-permute-done.1.refs_0_.refs_4_.refs_8_, bf16[256,3072]{1,0:T(8,128)(2,1)} %collective-permute-done.2.refs_1_.refs_5_.refs_9_.refs_4_, bf16[256,3072]{1,0:T(8,128)(2,1)} %collective-permute-done.9.refs_2_.refs_6_.refs_10_, ...), custom_call_target="tpu_custom_call" | custom-call | tf_op jit(solution)/shard_map/product/pallas_call | solution.py:307
  224.7 13.6 %collective-permute-done.11.refs_11_.refs_8_ = bf16[6144,128]{1,0:T(8,128)(2,1)} collective-permute-done((bf16[6144,128]{1,0:T(8,128)(2,1)}, bf16[6144,128]{1,0:T(8,128)(2,1)}, u32[]{:S(2)}, u32[]{:S(2)}) %collective-permute-start.11) | collective-permute-done | bytes 1572896 | tf_op jit(solution)/shard_map/ppermute | solution.py:168
  238.3 2.5 collective-permute-done.16
  243.1 30.0 %collective-permute-done.12.refs_12_.refs_9_ = bf16[6144,128]{1,0:T(8,128)(2,1)} collective-permute-done((bf16[6144,128]{1,0:T(8,128)(2,1)}, bf16[6144,128]{1,0:T(8,128)(2,1)}, u32[]{:S(2)}, u32[]{:S(2)}) %collective-permute-start.12) | collective-permute-done | bytes 1572896 | tf_op jit(solution)/shard_map/ppermute | solution.py:164
  280.3 12.4 %product.10 = (bf16[512,512]{1,0:T(8,128)(2,1)}, bf16[512,512]{1,0:T(8,128)(2,1)}) custom-call(bf16[256,3072]{1,0:T(8,128)(2,1)} %attention.4.refs_0_.refs_8_.refs_12_, bf16[256,3072]{1,0:T(8,128)(2,1)} %attention.5.refs_1_.refs_9_.refs_13_.refs_6_, bf16[256,3072]{1,0:T(8,128)(2,1)} %attention.6.refs_2_.refs_10_.refs_14_, ...), custom_call_target="tpu_custom_call" | custom-call | tf_op jit(solution)/shard_map/product/pallas_call | solution.py:307
  292.7 17.1 %collective-permute-done.17.refs_13_.refs_10_ = bf16[6144,128]{1,0:T(8,128)(2,1)} collective-permute-done((bf16[6144,128]{1,0:T(8,128)(2,1)}, bf16[6144,128]{1,0:T(8,128)(2,1)}, u32[]{:S(2)}, u32[]{:S(2)}) %collective-permute-start.17) | collective-permute-done | bytes 1572896 | tf_op jit(solution)/shard_map/ppermute | solution.py:168
  309.8 2.5 collective-permute-done.22
  316.4 27.9 %collective-permute-done.19.refs_14_.refs_11_ = bf16[6144,128]{1,0:T(8,128)(2,1)} collective-permute-done((bf16[6144,128]{1,0:T(8,128)(2,1)}, bf16[6144,128]{1,0:T(8,128)(2,1)}, u32[]{:S(2)}, u32[]{:S(2)}) %collective-permute-start.19) | collective-permute-done | bytes 1572896 | tf_op jit(solution)/shard_map/ppermute | solution.py:164
  350.6 21.8 %product.11 = (bf16[256,2048]{1,0:T(8,128)(2,1)}, bf16[256,2048]{1,0:T(8,128)(2,1)}) custom-call(bf16[256,3072]{1,0:T(8,128)(2,1)} %collective-permute-done.refs_0_.refs_4_, bf16[256,3072]{1,0:T(8,128)(2,1)} %collective-permute-done.8.refs_1_.refs_5_.refs_2_, bf16[256,3072]{1,0:T(8,128)(2,1)} %collective-permute-done.13.refs_2_.refs_6_, ...), custom_call_target="tpu_custom_call" | custom-call | tf_op jit(solution)/shard_map/product/pallas_call | solution.py:307
  373.2 7.9 %collective-permute-done.24.refs_15_.refs_12_ = bf16[6144,128]{1,0:T(8,128)(2,1)} collective-permute-done((bf16[6144,128]{1,0:T(8,128)(2,1)}, bf16[6144,128]{1,0:T(8,128)(2,1)}, u32[]{:S(2)}, u32[]{:S(2)}) %collective-permute-start.24) | collective-permute-done | bytes 1572896 | tf_op jit(solution)/shard_map/ppermute | solution.py:168
  381.0 16.1 %product.12 = (bf16[768,512]{1,0:T(8,128)(2,1)}, bf16[768,512]{1,0:T(8,128)(2,1)}) custom-call(bf16[256,3072]{1,0:T(8,128)(2,1)} %collective-permute-done.1.refs_0_.refs_4_.refs_8_, bf16[256,3072]{1,0:T(8,128)(2,1)} %collective-permute-done.2.refs_1_.refs_5_.refs_9_.refs_4_, bf16[256,3072]{1,0:T(8,128)(2,1)} %collective-permute-done.9.refs_2_.refs_6_.refs_10_, ...), custom_call_target="tpu_custom_call" | custom-call | tf_op jit(solution)/shard_map/product/pallas_call | solution.py:307
  397.1 18.0 %collective-permute-done.27 = bf16[4,192,1024]{2,1,0:T(8,128)(2,1)} collective-permute-done((bf16[4,192,1024]{2,1,0:T(8,128)(2,1)}, bf16[4,192,1024]{2,1,0:T(8,128)(2,1)}, u32[]{:S(2)}, u32[]{:S(2)}) %collective-permute-start.27) | collective-permute-done | bytes 1572896 | tf_op jit(solution)/shard_map/ppermute | solution.py:164
  415.1 16.5 %collective-permute-done.25.refs_16_ = bf16[3072,256]{1,0:T(8,128)(2,1)} collective-permute-done((bf16[3072,256]{1,0:T(8,128)(2,1)}, bf16[3072,256]{1,0:T(8,128)(2,1)}, u32[]{:S(2)}, u32[]{:S(2)}) %collective-permute-start.25) | collective-permute-done | bytes 1572896 | tf_op jit(solution)/shard_map/ppermute | solution.py:164
  431.6 2.8 pad_maximum_fusion.4
  435.9 2.5 add_convert_fusion.2
  440.3 25.1 %product.13 = (bf16[256,2560]{1,0:T(8,128)(2,1)}, bf16[256,2560]{1,0:T(8,128)(2,1)}) custom-call(bf16[256,3072]{1,0:T(8,128)(2,1)} %collective-permute-done.14.refs_0_, bf16[256,3072]{1,0:T(8,128)(2,1)} %copy-done.7, bf16[256,3072]{1,0:T(8,128)(2,1)} %collective-permute-done.21.refs_2_, bf16[256,3072]{1,0:T(8,128)(2,1)} %copy-done.8, ...), custom_call_target="tpu_custom_call" | custom-call | tf_op jit(solution)/shard_map/product/pallas_call | solution.py:307
  476.5 2.8 add_convert_fusion
  480.1 3.3 pad_maximum_fusion
  484.1 6.4 %cache.1 = bf16[128,16,1024]{2,1,0:T(8,128)(2,1)} custom-call(s32[128]{0:T(128)} %broadcast_add_fusion.page_of, bf16[1536,1024]{1,0:T(8,128)(2,1)} %bitcast.100), custom_call_target="tpu_custom_call" | custom-call | tf_op jit(solution)/shard_map/cache/pallas_call | solution.py:147
  492.8 11.4 %collective-permute-done.37.refs_8_ = bf16[1536,256]{1,0:T(8,128)(2,1)} collective-permute-done((bf16[1536,256]{1,0:T(8,128)(2,1)}, bf16[1536,256]{1,0:T(8,128)(2,1)}, u32[]{:S(2)}, u32[]{:S(2)}) %collective-permute-start.37) | collective-permute-done | bytes 786464 | tf_op jit(solution)/shard_map/ppermute | solution.py:164
  504.2 15.5 %product.14 = (bf16[1024,512]{1,0:T(8,128)(2,1)}, bf16[1024,512]{1,0:T(8,128)(2,1)}) custom-call(bf16[256,3072]{1,0:T(8,128)(2,1)} %collective-permute-done.14.refs_0_, bf16[256,3072]{1,0:T(8,128)(2,1)} %copy-done.7, bf16[256,3072]{1,0:T(8,128)(2,1)} %collective-permute-done.21.refs_2_, bf16[256,3072]{1,0:T(8,128)(2,1)} %copy-done.8, ...), custom_call_target="tpu_custom_call" | custom-call | tf_op jit(solution)/shard_map/product/pallas_call | solution.py:307
  519.8 3.2 collective-permute-done.39.refs_9_
  523.0 3.8 collective-permute-done.32.refs_4_
  526.8 9.2 %product.15 = (bf16[1024,512]{1,0:T(8,128)(2,1)}, bf16[1024,512]{1,0:T(8,128)(2,1)}) custom-call(bf16[256,3072]{1,0:T(8,128)(2,1)} %copy-done.7, bf16[256,3072]{1,0:T(8,128)(2,1)} %copy-done.8, bf16[256,3072]{1,0:T(8,128)(2,1)} %collective-permute-done.8.refs_1_.refs_5_.refs_2_, bf16[256,3072]{1,0:T(8,128)(2,1)} %copy-done.6, ...), custom_call_target="tpu_custom_call" | custom-call | tf_op jit(solution)/shard_map/product/pallas_call | solution.py:307
  536.1 2.9 collective-permute-done.40
  541.6 3.1 collective-permute-start.41
  545.4 4.1 collective-permute-done.43.refs_10_
  550.8 5.6 collective-permute-done.41.refs_8_
  557.0 6.5 %place.1 = bf16[256,12288]{1,0:T(8,128)(2,1)} custom-call(s32[44]{0:T(128)} %stack.263.offsets, bf16[256,1536]{1,0:T(8,128)(2,1)} %add_convert_fusion.5.refs_0_, bf16[256,512]{1,0:T(8,128)(2,1)} %get-tuple-element.210.refs_1_, bf16[256,2048]{1,0:T(8,128)(2,1)} %collective-permute-done.28.refs_2_, bf16[256,2048]{1,0:T(8,128)(2,1)} %copy-done.15, ...), custom_call_target="tpu_custom_call" | custom-call | tf_op jit(solution)/shard_map/place/pallas_call | solution.py:95
  (198 shorter events, 74.3 us)
Async XLA Ops:
  0.6 465.0 %copy-start = (s32[32,16]{0,1:T(8,128)S(1)}, s32[32,16]{0,1:T(8,128)}, u32[]{:S(2)}) copy-start(s32[32,16]{0,1:T(8,128)} %param.14) | copy-start | bytes 6148
  5.7 118.8 %collective-permute-start.3 = (bf16[6144,128]{1,0:T(8,128)(2,1)}, bf16[6144,128]{1,0:T(8,128)(2,1)}, u32[]{:S(2)}, u32[]{:S(2)}) collective-permute-start(bf16[6144,128]{1,0:T(8,128)(2,1)} %cut.7), channel_id=1, source_target_pairs={{0,8},{2,10},{4,12},{6,14},{8,0},{10,2},{12,4},{14,6},{1,9},{3,11}... | collective-permute-start | bytes 4718600 | tf_op jit(solution)/shard_map/ppermute | solution.py:164
  28.3 96.2 %collective-permute-start.2 = (bf16[256,3072]{1,0:T(8,128)(2,1)}, bf16[256,3072]{1,0:T(8,128)(2,1)}, u32[]{:S(2)}, u32[]{:S(2)}) collective-permute-start(bf16[256,3072]{1,0:T(8,128)(2,1)} %attention.5.refs_1_.refs_9_.refs_13_.refs_6_), channel_id=1, source_target_pairs={{0,2},{2,0},{4,6},{6,4},{8,10},{10,8},{12,14},{14,12},{1,3},{3,1},... | collective-permute-start | bytes 4718600 | tf_op jit(solution)/shard_map/ppermute | solution.py:164
  29.8 94.7 %collective-permute-start.1 = (bf16[256,3072]{1,0:T(8,128)(2,1)}, bf16[256,3072]{1,0:T(8,128)(2,1)}, u32[]{:S(2)}, u32[]{:S(2)}) collective-permute-start(bf16[256,3072]{1,0:T(8,128)(2,1)} %attention.4.refs_0_.refs_8_.refs_12_), channel_id=1, source_target_pairs={{0,2},{2,0},{4,6},{6,4},{8,10},{10,8},{12,14},{14,12},{1,3},{3,1},... | collective-permute-start | bytes 4718600 | tf_op jit(solution)/shard_map/ppermute | solution.py:164
  30.3 94.2 %collective-permute-start = (bf16[256,3072]{1,0:T(8,128)(2,1)}, bf16[256,3072]{1,0:T(8,128)(2,1)}, u32[]{:S(2)}, u32[]{:S(2)}) collective-permute-start(bf16[256,3072]{1,0:T(8,128)(2,1)} %attention.4.refs_0_.refs_8_.refs_12_), channel_id=1, source_target_pairs={{0,4},{2,6},{4,0},{6,2},{8,12},{10,14},{12,8},{14,10},{1,5},{3,7},... | collective-permute-start | bytes 4718600 | tf_op jit(solution)/shard_map/ppermute | solution.py:164
  31.9 92.6 %collective-permute-start.4 = (bf16[528,1024]{1,0:T(8,128)(2,1)}, bf16[528,1024]{1,0:T(8,128)(2,1)}, u32[]{:S(2)}, u32[]{:S(2)}) collective-permute-start(bf16[528,1024]{1,0:T(8,128)(2,1)} %fusion.1), channel_id=1, source_target_pairs={{0,8},{2,10},{4,12},{6,14},{8,0},{10,2},{12,4},{14,6},{1,9},{3,11}... | collective-permute-start | bytes 3244040 | tf_op jit(solution)/shard_map/ppermute | solution.py:164
  67.8 62.1 %copy-start.3 = (bf16[256,3072]{1,0:T(8,128)(2,1)S(1)}, bf16[256,3072]{1,0:T(8,128)(2,1)}, u32[]{:S(2)}) copy-start(bf16[256,3072]{1,0:T(8,128)(2,1)} %attention.5.refs_1_.refs_9_.refs_13_.refs_6_) | copy-start | bytes 4718596
  67.8 67.7 %copy-start.4 = (bf16[256,3072]{1,0:T(8,128)(2,1)S(1)}, bf16[256,3072]{1,0:T(8,128)(2,1)}, u32[]{:S(2)}) copy-start(bf16[256,3072]{1,0:T(8,128)(2,1)} %attention.7.refs_3_.refs_11_.refs_15_.refs_7_) | copy-start | bytes 4718596
  127.4 36.3 %collective-permute-start.5 = (bf16[6144,128]{1,0:T(8,128)(2,1)}, bf16[6144,128]{1,0:T(8,128)(2,1)}, u32[]{:S(2)}, u32[]{:S(2)}) collective-permute-start(bf16[6144,128]{1,0:T(8,128)(2,1)} %collective-permute-done.3.refs_8_.refs_5_), channel_id=1, source_target_pairs={{0,16},{16,0},{1,17},{17,1},{2,18},{18,2},{3,19},{19,3},{4,20},{20... | collective-permute-start | bytes 4718600 | tf_op jit(solution)/shard_map/ppermute | solution.py:168
  129.9 70.0 %collective-permute-start.7 = (bf16[6144,128]{1,0:T(8,128)(2,1)}, bf16[6144,128]{1,0:T(8,128)(2,1)}, u32[]{:S(2)}, u32[]{:S(2)}) collective-permute-start(bf16[6144,128]{1,0:T(8,128)(2,1)} %cut.8), channel_id=1, source_target_pairs={{0,8},{2,10},{4,12},{6,14},{8,0},{10,2},{12,4},{14,6},{1,9},{3,11}... | collective-permute-start | bytes 4718600 | tf_op jit(solution)/shard_map/ppermute | solution.py:164
  129.9 69.9 %collective-permute-start.8 = (bf16[256,3072]{1,0:T(8,128)(2,1)S(1)}, bf16[256,3072]{1,0:T(8,128)(2,1)}, u32[]{:S(2)}, u32[]{:S(2)}) collective-permute-start(bf16[256,3072]{1,0:T(8,128)(2,1)S(1)} %copy-done.3), channel_id=1, source_target_pairs={{0,4},{2,6},{4,0},{6,2},{8,12},{10,14},{12,8},{14,10},{1,5},{3,7},... | collective-permute-start | bytes 4718600 | tf_op jit(solution)/shard_map/ppermute | solution.py:164
  134.0 65.9 %collective-permute-start.9 = (bf16[256,3072]{1,0:T(8,128)(2,1)}, bf16[256,3072]{1,0:T(8,128)(2,1)}, u32[]{:S(2)}, u32[]{:S(2)}) collective-permute-start(bf16[256,3072]{1,0:T(8,128)(2,1)} %attention.6.refs_2_.refs_10_.refs_14_), channel_id=1, source_target_pairs={{0,2},{2,0},{4,6},{6,4},{8,10},{10,8},{12,14},{14,12},{1,3},{3,1},... | collective-permute-start | bytes 4718600 | tf_op jit(solution)/shard_map/ppermute | solution.py:164
  135.5 68.0 %collective-permute-start.10 = (bf16[256,3072]{1,0:T(8,128)(2,1)S(1)}, bf16[256,3072]{1,0:T(8,128)(2,1)}, u32[]{:S(2)}, u32[]{:S(2)}) collective-permute-start(bf16[256,3072]{1,0:T(8,128)(2,1)S(1)} %copy-done.4), channel_id=1, source_target_pairs={{0,2},{2,0},{4,6},{6,4},{8,10},{10,8},{12,14},{14,12},{1,3},{3,1},... | collective-permute-start | bytes 4718600 | tf_op jit(solution)/shard_map/ppermute | solution.py:164
  163.7 2.6 collective-permute-start.6
  203.5 34.8 %collective-permute-start.11 = (bf16[6144,128]{1,0:T(8,128)(2,1)}, bf16[6144,128]{1,0:T(8,128)(2,1)}, u32[]{:S(2)}, u32[]{:S(2)}) collective-permute-start(bf16[6144,128]{1,0:T(8,128)(2,1)} %collective-permute-done.7.refs_10_.refs_7_), channel_id=1, source_target_pairs={{0,16},{16,0},{1,17},{17,1},{2,18},{18,2},{3,19},{19,3},{4,20},{20... | collective-permute-start | bytes 4718600 | tf_op jit(solution)/shard_map/ppermute | solution.py:168
  204.0 69.2 %collective-permute-start.12 = (bf16[6144,128]{1,0:T(8,128)(2,1)}, bf16[6144,128]{1,0:T(8,128)(2,1)}, u32[]{:S(2)}, u32[]{:S(2)}) collective-permute-start(bf16[6144,128]{1,0:T(8,128)(2,1)} %cut.9), channel_id=1, source_target_pairs={{0,8},{2,10},{4,12},{6,14},{8,0},{10,2},{12,4},{14,6},{1,9},{3,11}... | collective-permute-start | bytes 4718600 | tf_op jit(solution)/shard_map/ppermute | solution.py:164
  204.3 68.8 %collective-permute-start.13 = (bf16[256,3072]{1,0:T(8,128)(2,1)}, bf16[256,3072]{1,0:T(8,128)(2,1)}, u32[]{:S(2)}, u32[]{:S(2)}) collective-permute-start(bf16[256,3072]{1,0:T(8,128)(2,1)} %attention.6.refs_2_.refs_10_.refs_14_), channel_id=1, source_target_pairs={{0,4},{2,6},{4,0},{6,2},{8,12},{10,14},{12,8},{14,10},{1,5},{3,7},... | collective-permute-start | bytes 4718600 | tf_op jit(solution)/shard_map/ppermute | solution.py:164
  204.7 68.4 %collective-permute-start.14 = (bf16[256,3072]{1,0:T(8,128)(2,1)}, bf16[256,3072]{1,0:T(8,128)(2,1)}, u32[]{:S(2)}, u32[]{:S(2)}) collective-permute-start(bf16[256,3072]{1,0:T(8,128)(2,1)} %collective-permute-done.refs_0_.refs_4_), channel_id=1, source_target_pairs={{0,2},{2,0},{4,6},{6,4},{8,10},{10,8},{12,14},{14,12},{1,3},{3,1},... | collective-permute-start | bytes 4718600 | tf_op jit(solution)/shard_map/ppermute | solution.py:164
  206.2 67.0 %collective-permute-start.15 = (bf16[256,3072]{1,0:T(8,128)(2,1)}, bf16[256,3072]{1,0:T(8,128)(2,1)S(1)}, u32[]{:S(2)}, u32[]{:S(2)}) collective-permute-start(bf16[256,3072]{1,0:T(8,128)(2,1)} %collective-permute-done.8.refs_1_.refs_5_.refs_2_), channel_id=1, source_target_pairs={{0,2},{2,0},{4,6},{6,4},{8,10},{10,8},{12,14},{14,12},{1,3},{3,1},... | collective-permute-start | bytes 4718600 | tf_op jit(solution)/shard_map/ppermute | solution.py:164
  224.7 53.5 %copy-start.5 = (bf16[256,3072]{1,0:T(8,128)(2,1)S(1)}, bf16[256,3072]{1,0:T(8,128)(2,1)}, u32[]{:S(2)}) copy-start(bf16[256,3072]{1,0:T(8,128)(2,1)} %attention.7.refs_3_.refs_11_.refs_15_.refs_7_) | copy-start | bytes 4718596
  238.3 2.5 collective-permute-start.16
  273.2 36.7 %collective-permute-start.17 = (bf16[6144,128]{1,0:T(8,128)(2,1)}, bf16[6144,128]{1,0:T(8,128)(2,1)}, u32[]{:S(2)}, u32[]{:S(2)}) collective-permute-start(bf16[6144,128]{1,0:T(8,128)(2,1)} %collective-permute-done.12.refs_12_.refs_9_), channel_id=1, source_target_pairs={{0,16},{16,0},{1,17},{17,1},{2,18},{18,2},{3,19},{19,3},{4,20},{20... | collective-permute-start | bytes 4718600 | tf_op jit(solution)/shard_map/ppermute | solution.py:168
  274.7 37.6 %collective-permute-start.22 = (bf16[2,2,192,1024]{3,2,1,0:T(8,128)(2,1)}, bf16[2,2,192,1024]{3,2,1,0:T(8,128)(2,1)}, u32[]{:S(2)}, u32[]{:S(2)}) collective-permute-start(bf16[2,2,192,1024]{3,2,1,0:T(8,128)(2,1)} %pad_maximum_fusion.2), channel_id=1, source_target_pairs={{0,2},{2,0},{4,6},{6,4},{8,10},{10,8},{12,14},{14,12},{1,3},{3,1},... | collective-permute-start | bytes 4718600 | tf_op jit(solution)/shard_map/ppermute | solution.py:164
  276.3 68.1 %collective-permute-start.19 = (bf16[6144,128]{1,0:T(8,128)(2,1)}, bf16[6144,128]{1,0:T(8,128)(2,1)}, u32[]{:S(2)}, u32[]{:S(2)}) collective-permute-start(bf16[6144,128]{1,0:T(8,128)(2,1)} %cut.10), channel_id=1, source_target_pairs={{0,8},{2,10},{4,12},{6,14},{8,0},{10,2},{12,4},{14,6},{1,9},{3,11}... | collective-permute-start | bytes 4718600 | tf_op jit(solution)/shard_map/ppermute | solution.py:164
  278.1 67.7 %collective-permute-start.20 = (bf16[256,3072]{1,0:T(8,128)(2,1)S(1)}, bf16[256,3072]{1,0:T(8,128)(2,1)S(1)}, u32[]{:S(2)}, u32[]{:S(2)}) collective-permute-start(bf16[256,3072]{1,0:T(8,128)(2,1)S(1)} %copy-done.5), channel_id=1, source_target_pairs={{0,4},{2,6},{4,0},{6,2},{8,12},{10,14},{12,8},{14,10},{1,5},{3,7},... | collective-permute-start | bytes 4718600 | tf_op jit(solution)/shard_map/ppermute | solution.py:164
  279.8 66.0 %collective-permute-start.21 = (bf16[256,3072]{1,0:T(8,128)(2,1)}, bf16[256,3072]{1,0:T(8,128)(2,1)}, u32[]{:S(2)}, u32[]{:S(2)}) collective-permute-start(bf16[256,3072]{1,0:T(8,128)(2,1)} %collective-permute-done.13.refs_2_.refs_6_), channel_id=1, source_target_pairs={{0,2},{2,0},{4,6},{6,4},{8,10},{10,8},{12,14},{14,12},{1,3},{3,1},... | collective-permute-start | bytes 4718600 | tf_op jit(solution)/shard_map/ppermute | solution.py:164
  309.8 4.7 collective-permute-start.18
  345.8 35.2 %collective-permute-start.24 = (bf16[6144,128]{1,0:T(8,128)(2,1)}, bf16[6144,128]{1,0:T(8,128)(2,1)}, u32[]{:S(2)}, u32[]{:S(2)}) collective-permute-start(bf16[6144,128]{1,0:T(8,128)(2,1)} %collective-permute-done.19.refs_14_.refs_11_), channel_id=1, source_target_pairs={{0,16},{16,0},{1,17},{17,1},{2,18},{18,2},{3,19},{19,3},{4,20},{20... | collective-permute-start | bytes 4718600 | tf_op jit(solution)/shard_map/ppermute | solution.py:168
  348.3 66.8 %collective-permute-start.27 = (bf16[4,192,1024]{2,1,0:T(8,128)(2,1)}, bf16[4,192,1024]{2,1,0:T(8,128)(2,1)}, u32[]{:S(2)}, u32[]{:S(2)}) collective-permute-start(bf16[4,192,1024]{2,1,0:T(8,128)(2,1)} %get-tuple-element.199), channel_id=1, source_target_pairs={{0,4},{2,6},{4,0},{6,2},{8,12},{10,14},{12,8},{14,10},{1,5},{3,7},... | collective-permute-start | bytes 4718600 | tf_op jit(solution)/shard_map/ppermute | solution.py:164
  348.8 82.8 %collective-permute-start.25 = (bf16[3072,256]{1,0:T(8,128)(2,1)}, bf16[3072,256]{1,0:T(8,128)(2,1)}, u32[]{:S(2)}, u32[]{:S(2)}) collective-permute-start(bf16[3072,256]{1,0:T(8,128)(2,1)} %cut.11), channel_id=1, source_target_pairs={{0,8},{2,10},{4,12},{6,14},{8,0},{10,2},{12,4},{14,6},{1,9},{3,11}... | collective-permute-start | bytes 4718600 | tf_op jit(solution)/shard_map/ppermute | solution.py:164
  349.5 82.1 %collective-permute-start.26 = (bf16[256,3072]{1,0:T(8,128)(2,1)S(1)}, bf16[256,3072]{1,0:T(8,128)(2,1)S(1)}, u32[]{:S(2)}, u32[]{:S(2)}) collective-permute-start(bf16[256,3072]{1,0:T(8,128)(2,1)S(1)} %collective-permute-done.20.refs_3_.refs_7_), channel_id=1, source_target_pairs={{0,2},{2,0},{4,6},{6,4},{8,10},{10,8},{12,14},{14,12},{1,3},{3,1},... | collective-permute-start | bytes 4718600 | tf_op jit(solution)/shard_map/ppermute | solution.py:164
  372.4 63.5 %collective-permute-start.23 = (bf16[256,2048]{1,0:T(8,128)(2,1)}, bf16[256,2048]{1,0:T(8,128)(2,1)}, u32[]{:S(2)}, u32[]{:S(2)}) collective-permute-start(bf16[256,2048]{1,0:T(8,128)(2,1)} %get-tuple-element.140), channel_id=1, source_target_pairs={{0,1},{1,0},{2,3},{3,2},{4,5},{5,4},{6,7},{7,6},{8,9},{9,8},{10,11... | collective-permute-start | bytes 3145736 | tf_op jit(solution)/shard_map/ppermute | solution.py:168
  431.6 33.8 %collective-permute-start.30 = (bf16[1536,256]{1,0:T(8,128)(2,1)}, bf16[1536,256]{1,0:T(8,128)(2,1)}, u32[]{:S(2)}, u32[]{:S(2)}) collective-permute-start(bf16[1536,256]{1,0:T(8,128)(2,1)} %cut.12), channel_id=1, source_target_pairs={{0,8},{2,10},{4,12},{6,14},{8,0},{10,2},{12,4},{14,6},{1,9},{3,11}... | collective-permute-start | bytes 2359304 | tf_op jit(solution)/shard_map/ppermute | solution.py:164
  434.4 32.0 %collective-permute-start.36 = (bf16[3072,256]{1,0:T(8,128)(2,1)}, bf16[3072,256]{1,0:T(8,128)(2,1)S(1)}, u32[]{:S(2)}, u32[]{:S(2)}) collective-permute-start(bf16[3072,256]{1,0:T(8,128)(2,1)} %collective-permute-done.25.refs_16_), channel_id=1, source_target_pairs={{0,16},{16,0},{1,17},{17,1},{2,18},{18,2},{3,19},{19,3},{4,20},{20... | collective-permute-start | bytes 4718600 | tf_op jit(solution)/shard_map/ppermute | solution.py:168
  438.4 28.1 %collective-permute-start.28 = (bf16[256,2048]{1,0:T(8,128)(2,1)}, bf16[256,2048]{1,0:T(8,128)(2,1)}, u32[]{:S(2)}, u32[]{:S(2)}) collective-permute-start(bf16[256,2048]{1,0:T(8,128)(2,1)} %add_convert_fusion.2), channel_id=1, source_target_pairs={{0,4},{2,6},{4,0},{6,2},{8,12},{10,14},{12,8},{14,10},{1,5},{3,7},... | collective-permute-start | bytes 3145736 | tf_op jit(solution)/shard_map/ppermute | solution.py:164
  438.4 28.1 %collective-permute-start.29 = (bf16[256,2048]{1,0:T(8,128)(2,1)}, bf16[256,2048]{1,0:T(8,128)(2,1)S(1)}, u32[]{:S(2)}, u32[]{:S(2)}) collective-permute-start(bf16[256,2048]{1,0:T(8,128)(2,1)} %pad_maximum_fusion.4), channel_id=1, source_target_pairs={{0,2},{2,0},{4,6},{6,4},{8,10},{10,8},{12,14},{14,12},{1,3},{3,1},... | collective-permute-start | bytes 3145736 | tf_op jit(solution)/shard_map/ppermute | solution.py:164
  465.4 3.5 collective-permute-start.33
  465.9 10.6 %collective-permute-start.31 = (bf16[256,2560]{1,0:T(8,128)(2,1)}, bf16[256,2560]{1,0:T(8,128)(2,1)}, u32[]{:S(2)}, u32[]{:S(2)}) collective-permute-start(bf16[256,2560]{1,0:T(8,128)(2,1)} %get-tuple-element.159), channel_id=1, source_target_pairs={{0,1},{1,0},{2,3},{3,2},{4,5},{5,4},{6,7},{7,6},{8,9},{9,8},{10,11... | collective-permute-start | bytes 3932168 | tf_op jit(solution)/shard_map/ppermute | solution.py:168
  466.5 37.7 %collective-permute-start.37 = (bf16[1536,256]{1,0:T(8,128)(2,1)}, bf16[1536,256]{1,0:T(8,128)(2,1)}, u32[]{:S(2)}, u32[]{:S(2)}) collective-permute-start(bf16[1536,256]{1,0:T(8,128)(2,1)} %cut.13), channel_id=1, source_target_pairs={{0,8},{2,10},{4,12},{6,14},{8,0},{10,2},{12,4},{14,6},{1,9},{3,11}... | collective-permute-start | bytes 2359304 | tf_op jit(solution)/shard_map/ppermute | solution.py:164
  468.9 35.3 %collective-permute-start.38 = (bf16[1536,256]{1,0:T(8,128)(2,1)}, bf16[1536,256]{1,0:T(8,128)(2,1)}, u32[]{:S(2)}, u32[]{:S(2)}) collective-permute-start(bf16[1536,256]{1,0:T(8,128)(2,1)} %collective-permute-done.30.refs_18_), channel_id=1, source_target_pairs={{0,16},{16,0},{1,17},{17,1},{2,18},{18,2},{3,19},{19,3},{4,20},{20... | collective-permute-start | bytes 2359304 | tf_op jit(solution)/shard_map/ppermute | solution.py:168
  473.7 16.8 %collective-permute-start.35 = (bf16[256,512]{1,0:T(8,128)(2,1)}, bf16[256,512]{1,0:T(8,128)(2,1)S(1)}, u32[]{:S(2)}, u32[]{:S(2)}) collective-permute-start(bf16[256,512]{1,0:T(8,128)(2,1)} %get-tuple-element.207), channel_id=1, source_target_pairs={{0,2},{2,0},{4,6},{6,4},{8,10},{10,8},{12,14},{14,12},{1,3},{3,1},... | collective-permute-start | bytes 786440 | tf_op jit(solution)/shard_map/ppermute | solution.py:164
  474.5 18.4 %collective-permute-start.34 = (bf16[256,512]{1,0:T(8,128)(2,1)}, bf16[256,512]{1,0:T(8,128)(2,1)S(1)}, u32[]{:S(2)}, u32[]{:S(2)}) collective-permute-start(bf16[256,512]{1,0:T(8,128)(2,1)} %get-tuple-element.208), channel_id=1, source_target_pairs={{0,4},{2,6},{4,0},{6,2},{8,12},{10,14},{12,8},{14,10},{1,5},{3,7},... | collective-permute-start | bytes 786440 | tf_op jit(solution)/shard_map/ppermute | solution.py:164
  479.3 47.5 %collective-permute-start.32 = (bf16[256,2560]{1,0:T(8,128)(2,1)}, bf16[256,2560]{1,0:T(8,128)(2,1)S(1)}, u32[]{:S(2)}, u32[]{:S(2)}) collective-permute-start(bf16[256,2560]{1,0:T(8,128)(2,1)} %add_convert_fusion), channel_id=1, source_target_pairs={{0,6},{2,4},{4,2},{6,0},{8,14},{10,12},{12,10},{14,8},{1,7},{3,5},... | collective-permute-start | bytes 3932168 | tf_op jit(solution)/shard_map/ppermute | solution.py:164
  504.2 18.8 %collective-permute-start.39 = (bf16[1536,256]{1,0:T(8,128)(2,1)}, bf16[1536,256]{1,0:T(8,128)(2,1)S(1)}, u32[]{:S(2)}, u32[]{:S(2)}) collective-permute-start(bf16[1536,256]{1,0:T(8,128)(2,1)} %collective-permute-done.37.refs_8_), channel_id=1, source_target_pairs={{0,16},{16,0},{1,17},{17,1},{2,18},{18,2},{3,19},{19,3},{4,20},{20... | collective-permute-start | bytes 2359304 | tf_op jit(solution)/shard_map/ppermute | solution.py:168
  536.0 2.9 collective-permute-start.40
  541.2 8.3 %collective-permute-start.43 = (bf16[256,512]{1,0:T(8,128)(2,1)S(1)}, bf16[256,512]{1,0:T(8,128)(2,1)S(1)}, u32[]{:S(2)}, u32[]{:S(2)}) collective-permute-start(bf16[256,512]{1,0:T(8,128)(2,1)S(1)} %get-tuple-element.203), channel_id=1, source_target_pairs={{0,2},{2,0},{4,6},{6,4},{8,10},{10,8},{12,14},{14,12},{1,3},{3,1},... | collective-permute-start | bytes 786440 | tf_op jit(solution)/shard_map/ppermute | solution.py:164
  541.6 9.2 %collective-permute-start.42 = (bf16[256,512]{1,0:T(8,128)(2,1)S(1)}, bf16[256,512]{1,0:T(8,128)(2,1)S(1)}, u32[]{:S(2)}, u32[]{:S(2)}) collective-permute-start(bf16[256,512]{1,0:T(8,128)(2,1)S(1)} %get-tuple-element.204), channel_id=1, source_target_pairs={{0,4},{2,6},{4,0},{6,2},{8,12},{10,14},{12,8},{14,10},{1,5},{3,7},... | collective-permute-start | bytes 786440 | tf_op jit(solution)/shard_map/ppermute | solution.py:164
  541.6 14.7 %collective-permute-start.41 = (bf16[256,512]{1,0:T(8,128)(2,1)S(1)}, bf16[256,512]{1,0:T(8,128)(2,1)S(1)}, u32[]{:S(2)}, u32[]{:S(2)}) collective-permute-start(bf16[256,512]{1,0:T(8,128)(2,1)S(1)} %get-tuple-element.205), channel_id=1, source_target_pairs={{0,6},{2,4},{4,2},{6,0},{8,14},{10,12},{12,10},{14,8},{1,7},{3,5},... | collective-permute-start | bytes 786440 | tf_op jit(solution)/shard_map/ppermute | solution.py:164
  (23 other events, 258.7 us)
